TPU v7x, 32 devices: a whole 2x2x4 slice. The times are simulated.
32 devices in a mesh: groups: 2 (over x), blk: 8 (over z, y), rep: 2 (over core).
Axes of the slice: x: 2, y: 2, z: 4, core: 2. Of those that a mesh axis runs over, the one named last changes fastest.
Arguments:
- projections: bfloat16 [512, 8, 36, 1024], P(('groups', 'blk', 'rep')), parts along dimension 0, may hold values from -6 to 6
- images: bfloat16 [512, 36, 1024], P(('groups', 'blk', 'rep')), parts along dimension 0, may hold values from -6 to 6
- transfer: bfloat16 [512, 36, 1024], P(('groups', 'blk', 'rep')), parts along dimension 0, may hold values from -1 to 1
- pose_weights: float32 [512, 8], P(('groups', 'blk', 'rep')), parts along dimension 0, may hold values from 0 to 1
- pose_of: int32 [512, 8], P(('groups', 'blk', 'rep')), parts along dimension 0, may hold values from 0 to 511
- pose_blocks: int32 [1024, 36], P('groups'), parts along dimension 0, may hold values from 0 to 63
- pose_tiles: int32 [1024, 36], P('groups'), parts along dimension 0, may hold values from 0 to 15
- weight_bank: float32 [16, 32, 1024], replicated, may hold values from -0.18 to 0.18
Outputs:
- map_gradient: float32 [128, 32, 1024], P(('groups', 'blk')), parts along dimension 0
There are 2 independent parts, one for each index of `groups`. A program takes and returns all parts, laid end to end along the dimension named above; an argument that names none is the same for every part. Nothing has to cross between parts.
All inputs are finite; a program needn't handle non-finite values.
Results may differ from a plain program's by a relative error of at most 0.0003.
Values sent between devices are 32-bit elements; how exact they have to be, the bound alone decides.
No kernel may reach another device: no remote copies, remote signals or barrier semaphores. Data moves between devices by JAX's collectives and lax.ppermute only.
A program may use at most 128 MiB of HBM per device.

v0:
```python
import jax
import jax.numpy as jnp
from jax import lax
from jax.sharding import PartitionSpec as P

NB_DEV = 8


def apply_bank(weight_bank, tile_rows):
    return jnp.einsum("tzq,btq->bzq", weight_bank, tile_rows, precision=lax.Precision.HIGHEST)


def body(
    projections, images, transfer, pose_weights, pose_of, pose_blocks, pose_tiles, weight_bank
):
    bank_size = weight_bank.shape[0]
    face_cells = projections.shape[-1]
    total_blocks = NB_DEV * lax.axis_size("blk")
    transfer_f = transfer.astype(jnp.float32)[:, None]
    residual = transfer_f * projections.astype(jnp.float32) - images.astype(jnp.float32)[:, None]
    contrib = pose_weights[:, :, None, None] * transfer_f * residual
    block_ids = jnp.take(pose_blocks, pose_of, axis=0)
    tile_ids = jnp.take(pose_tiles, pose_of, axis=0)
    segment = (block_ids * bank_size + tile_ids).reshape(-1)
    tile_sums = jax.ops.segment_sum(
        contrib.reshape(-1, face_cells), segment, num_segments=total_blocks * bank_size
    )
    tile_sums = tile_sums.reshape(total_blocks, bank_size, face_cells)
    owned = lax.psum_scatter(
        apply_bank(weight_bank, tile_sums), ("blk", "rep"), scatter_dimension=0, tiled=True
    )
    owned = lax.all_gather(owned, "rep", axis=0, tiled=True)
    return owned


def solution(mesh):
    placed = (
        P(("groups", "blk", "rep"), None, None, None),
        P(("groups", "blk", "rep"), None, None),
        P(("groups", "blk", "rep"), None, None),
        P(("groups", "blk", "rep"), None),
        P(("groups", "blk", "rep"), None),
        P("groups", None),
        P("groups", None),
        P(),
    )
    return jax.shard_map(
        body,
        mesh=mesh,
        in_specs=placed,
        out_specs=P(("groups", "blk"), None, None),
        check_vma=False,
    )
```

profile of v0, /device:TPU:0, one launch (start us, length us, event | category | flops | bytes accessed | tf_op | source)
XLA Modules:
  0.0 292.6 jit_solution(16848720831339303146)
XLA Ops:
  6.5 0.7 compare_select_fusion
  7.2 0.7 compare_and_fusion
  7.9 0.1 copy.34
  8.0 0.1 reshape.45
  8.1 1.0 copy.35
  9.1 1.0 copy.38
  10.2 0.6 gather_fusion
  10.8 0.6 gather_fusion.1
  11.5 0.1 copy.33
  11.5 0.1 fusion.2
  11.6 0.1 reshape.34
  11.7 2.0 copy.40
  13.7 3.5 %copy.41 = f32[16,36,1024]{2,1,0:T(8,128)} copy(bf16[16,36,1024]{2,0,1:T(8,128)(2,1)} %param.11) | data formatting | bytes 3538944 | tf_op jit(solution)/shard_map/convert_element_type | solution.py:20
  17.3 6.6 %subtract_multiply_fusion = f32[16,8,36,1024]{3,1,2,0:T(8,128)S(1)} fusion(bf16[16,8,36,1024]{3,1,2,0:T(8,128)(2,1)} %param.10, f32[16,36,1024]{2,1,0:T(8,128)} %copy.41, f32[16,36,1024]{2,1,0:T(8,128)S(1)} %copy.40, f32[16,8]{1,0:T(8,128)S(1)} %copy.39), kind=kLoop, calls=%fused_computation.3 | loop fusion | flops 23592960 | bytes 33030656 | tf_op jit(solution)/shard_map/mul | solution.py:21
  23.9 18.4 %copy.42 = f32[16,8,36,1024]{3,2,1,0:T(8,128)} copy(f32[16,8,36,1024]{3,1,2,0:T(8,128)S(1)} %subtract_multiply_fusion) | data formatting | bytes 37748736 | tf_op jit(solution)/shard_map/mul | solution.py:21
  42.3 19.3 %reshape.36 = f32[4608,1024]{1,0:T(8,128)} reshape(f32[16,8,36,1024]{3,2,1,0:T(8,128)} %copy.42) | data formatting | bytes 37748736 | tf_op jit(solution)/shard_map/reshape | solution.py:26
  61.6 42.9 %scatter_custom_fusion = f32[1024,1024]{1,0:T(8,128)} fusion(s32[4608]{0:T(1024)S(1)} %reshape.34, f32[4608,1024]{1,0:T(8,128)} %reshape.36, f32[]{:T(128)} %constant.1.clone.1), kind=kCustom, calls=%fused_computation.5 | custom fusion | flops 4718592 | bytes 4194816 | tf_op jit(solution)/shard_map/scatter-add | solution.py:25
  104.5 8.7 %copy.43 = f32[64,16,1024]{0,1,2:T(8,128)} copy(f32[64,16,1024]{2,1,0:T(8,128)} %bitcast.15) | data formatting | bytes 8388608 | tf_op jit(solution)/shard_map/reshape | solution.py:28
  113.2 6.2 %copy.44 = f32[16,32,1024]{1,0,2:T(8,128)} copy(f32[16,32,1024]{2,1,0:T(8,128)S(1)} %copy-done) | data formatting | bytes 4194304 | tf_op args[7]
  119.5 32.2 %convolution_bitcast_fusion = f32[64,32,1024]{0,1,2:T(8,128)} fusion(f32[64,16,1024]{0,1,2:T(8,128)} %copy.43, f32[16,32,1024]{1,0,2:T(8,128)} %copy.44), kind=kOutput, calls=%fused_computation.4 | convolution fusion | flops 402653184 | bytes 14680064 | tf_op jit(solution)/shard_map/tzq,btq->bzq/dot_general | solution.py:10
  151.7 13.8 %copy.45 = f32[64,32,1024]{2,1,0:T(8,128)} copy(f32[64,32,1024]{0,1,2:T(8,128)} %convolution_bitcast_fusion) | data formatting | bytes 16777216 | tf_op jit(solution)/shard_map/tzq,btq->bzq/transpose | solution.py:10
  165.6 107.5 %reduce-scatter.2.cloned.1.call-done = f32[4,32,1024]{2,1,0:T(8,128)} async-done(((f32[64,32,1024]{2,1,0:T(8,128)}), f32[4,32,1024]{2,1,0:T(8,128)}) %reduce-scatter.2.cloned.1.call-update) | async-done | bytes 524304 | tf_op jit(solution)/shard_map/reduce_scatter | solution.py:29
  273.1 10.3 %all-gather.2.cloned.1.call-done = f32[8,32,1024]{2,1,0:T(8,128)} async-done(((f32[4,32,1024]{2,1,0:T(8,128)}), f32[8,32,1024]{2,1,0:T(8,128)}) %all-gather.2.cloned.1.call-update) | async-done | bytes 1048592 | tf_op jit(solution)/shard_map/all_gather | solution.py:32
  283.4 2.3 copy.47
  (10 shorter events, 0.2 us)
Async XLA Ops:
  6.5 10.7 %copy-start.1 = (f32[16,8]{0,1:T(8,128)S(1)}, f32[16,8]{0,1:T(8,128)}, u32[]{:S(2)}) copy-start(f32[16,8]{0,1:T(8,128)} %param.13) | copy-start | bytes 1540
  6.5 266.5 %reduce-scatter.2.cloned.1.call-start = ((), (), s32[]{:S(2)}) async-start(), calls=%async_computation.1 | async-start | bytes 8912896 | tf_op jit(solution)/shard_map/reduce_scatter | solution.py:29
  61.6 51.6 %copy-start = (f32[16,32,1024]{2,1,0:T(8,128)S(1)}, f32[16,32,1024]{2,1,0:T(8,128)}, u32[]{:S(2)}) copy-start(f32[16,32,1024]{2,1,0:T(8,128)} %param.17) | copy-start | bytes 6291460
  165.5 117.9 %all-gather.2.cloned.1.call-start = ((), (), s32[]{:S(2)}) async-start(), calls=%async_computation.2 | async-start | bytes 1572864 | tf_op jit(solution)/shard_map/all_gather | solution.py:32
Sparse Core Ops, SparseCore 0:
  165.6 107.3 reduce-scatter.1
  274.6 8.7 all-gather.1
where the time goes:
time: 294 us; the launch traced here: 293 us
  waiting for transfers between devices  118 us (40%)
  local copies, waits for them, and re-layouts  78 us (27%)
  other arithmetic  51 us (17%)
  matrix products  32.2 us (11%)
  between operations  13.5 us (5%)
    reduce_scatter x1, waiting for transfers between devices, body(): lax.psum_scatter(apply_bank(weight_bank, tile_sums), ('blk', 'rep'), scat...  108 us
    scatter-add x1, other arithmetic, body(): jax.ops.segment_sum(contrib.reshape(-1, face_cells), segment, num_segment...  42.9 us
    dot_general x1, matrix products, apply_bank(): jnp.einsum('tzq,btq->bzq', weight_bank, tile_rows, precision=lax.Precisio...  32.2 us
    reshape x1, local copies, waits for them, and re-layouts, body(): contrib.reshape(-1, face_cells)  19.3 us
    mul x1, local copies, waits for them, and re-layouts, body(): contrib = pose_weights[:, :, None, None] * transfer_f * residual  18.4 us
    transpose x1, local copies, waits for them, and re-layouts, apply_bank(): jnp.einsum('tzq,btq->bzq', weight_bank, tile_rows, precision=lax.Precisio...  13.8 us
    unnamed x9, local copies, waits for them, and re-layouts  10.7 us
    all_gather x1, waiting for transfers between devices, body(): owned = lax.all_gather(owned, 'rep', axis=0, tiled=True)  10.3 us
  transfers between devices with their start and end apart: 2, of which 2 were waited for; matrix products, arithmetic and copies ran while one was open for 0% of the time, Pallas kernels for 0%

commit v1 on v0

v1 whole, which is shorter than its diff:
```python
import functools

import jax
import jax.numpy as jnp
from jax import lax
from jax.experimental import pallas as pl
from jax.experimental.pallas import tpu as pltpu
from jax.sharding import PartitionSpec as P

NB_DEV = 8
LANES = 128
SUB = 8
MIB = 1 << 20
UNROLL = 4


def accumulate_kernel(
    bank_size, n_acc,
    proj_hbm, img_hbm, tra_hbm, w_smem, pose_hbm, blocks_hbm, tiles_hbm,
    out_hbm,
    proj, img, tra, pose, blocks, tiles, idx_v, idx_s, square, cross, *rest,
):
    parts, accs = rest[:UNROLL], rest[UNROLL : UNROLL + n_acc]
    proj_sem, small_sem, table_sem, idx_sem, out_sem = rest[UNROLL + n_acc :]
    n_part, n_tile, n_pose, n_cell = proj.shape
    n_col = n_cell // LANES
    n_table = blocks.shape[1]
    n_row = accs[0].shape[0]

    table_copies = [
        pltpu.make_async_copy(src, dst, table_sem.at[i])
        for i, (src, dst) in enumerate(((pose_hbm, pose), (blocks_hbm, blocks), (tiles_hbm, tiles)))
    ]
    small_copies = [
        pltpu.make_async_copy(img_hbm, img, small_sem.at[0]),
        pltpu.make_async_copy(tra_hbm, tra, small_sem.at[1]),
    ]
    for copy in table_copies + small_copies:
        copy.start()

    def proj_copy(p):
        return pltpu.make_async_copy(proj_hbm.at[p], proj.at[p], proj_sem.at[p])

    for p in range(n_part):
        proj_copy(p).start()

    for copy in table_copies:
        copy.wait()
    lane = lax.broadcasted_iota(jnp.int32, (n_pose, n_table), 1)
    chosen = jnp.concatenate(
        [(pose[:, p : p + 1] == lane).astype(jnp.float32) for p in range(n_part)], axis=0
    ).astype(jnp.bfloat16)

    def look_up(table):
        return lax.dot_general(
            chosen, table[...].astype(jnp.float32).astype(jnp.bfloat16),
            (((1,), (1,)), ((), ())), preferred_element_type=jnp.float32,
        )

    idx_v[:, :n_tile] = ((look_up(blocks) * bank_size + look_up(tiles)) * SUB).astype(jnp.int32)
    idx_copy = pltpu.make_async_copy(idx_v, idx_s, idx_sem)
    idx_copy.start()

    zero = jnp.zeros((8 * SUB, LANES), jnp.float32)

    @pl.loop(0, n_row // (8 * SUB))
    def _(i):
        rows = pl.ds(pl.multiple_of(i * (8 * SUB), 8 * SUB), 8 * SUB)
        for acc in accs:
            acc[rows, :] = zero

    for copy in small_copies:
        copy.wait()

    @pl.loop(0, n_tile)
    def _(j):
        for c in range(n_col):
            cols = slice(c * LANES, (c + 1) * LANES)
            rows = slice(c * n_part, (c + 1) * n_part)
            t = tra[j, :, cols].astype(jnp.float32)
            square[j, rows, :] = t * t
            cross[j, rows, :] = t * img[j, :, cols].astype(jnp.float32)

    idx_copy.wait()

    @pl.loop(0, n_part)
    def _(p):
        proj_copy(p).wait()
        weights = [jnp.full((n_col, LANES), w_smem[k, p], jnp.float32) for k in range(n_pose)]

        @pl.loop(0, n_tile // UNROLL)
        def _(i):
            for u, part in enumerate(parts):
                j = i * UNROLL + u
                for c in range(n_col):
                    x = proj[p, j, :, c * LANES : (c + 1) * LANES].astype(jnp.float32)
                    part[c * n_pose : (c + 1) * n_pose, :] = x
                cell = pl.ds(p, n_col, stride=n_part)
                tt = square[j, cell, :]
                ti = cross[j, cell, :]
                for k in range(n_pose):
                    x = part[pl.ds(k, n_col, stride=n_pose), :]
                    row = pl.ds(pl.multiple_of(idx_s[p * n_pose + k, j], SUB), SUB)
                    acc = accs[k % n_acc]
                    acc[row, :] += (tt * x - ti) * weights[k]

    chunk = 64 * SUB
    n_chunk = n_row // chunk
    step = chunk // 16

    def out_copy(i):
        rows = pl.ds(pl.multiple_of(i * chunk, chunk), chunk)
        return pltpu.make_async_copy(accs[0].at[rows, :], out_hbm.at[rows, :], out_sem.at[i])

    @pl.loop(0, n_chunk)
    def _(i):
        @pl.loop(0, chunk // step)
        def _(h):
            rows = pl.ds(pl.multiple_of(i * chunk + h * step, step), step)
            total = accs[0][rows, :]
            for acc in accs[1:]:
                total += acc[rows, :]
            accs[0][rows, :] = total
        out_copy(i).start()

    @pl.loop(0, n_chunk)
    def _(i):
        out_copy(i).wait()


def accumulate(projections, images, transfer, pose_weights, pose_of, pose_blocks, pose_tiles, total, bank_size):
    n_part, n_pose, n_tile, n_cell = projections.shape
    n_col = n_cell // LANES
    n_acc = 4 if total * n_cell * 4 * 4 <= 16 * MIB else 2
    n_row = total * n_col
    n_idx = n_part * n_pose
    projections = jnp.transpose(projections, (0, 2, 1, 3))
    images, transfer = jnp.transpose(images, (1, 0, 2)), jnp.transpose(transfer, (1, 0, 2))
    anywhere = pl.BlockSpec(memory_space=pl.ANY)
    return pl.pallas_call(
        functools.partial(accumulate_kernel, bank_size, n_acc),
        out_shape=jax.ShapeDtypeStruct((n_row, LANES), jnp.float32),
        in_specs=[anywhere] * 3 + [pl.BlockSpec(memory_space=pltpu.SMEM)] + [anywhere] * 3,
        out_specs=anywhere,
        scratch_shapes=[
            pltpu.VMEM(projections.shape, jnp.bfloat16),
            pltpu.VMEM(images.shape, jnp.bfloat16),
            pltpu.VMEM(transfer.shape, jnp.bfloat16),
            pltpu.VMEM((n_pose, n_part), jnp.int32),
            pltpu.VMEM(pose_blocks.shape[::-1], jnp.int32),
            pltpu.VMEM(pose_tiles.shape[::-1], jnp.int32),
            pltpu.VMEM((n_idx, LANES), jnp.int32),
            pltpu.SMEM((n_idx, LANES), jnp.int32),
            pltpu.VMEM((n_tile, n_col * n_part, LANES), jnp.float32),
            pltpu.VMEM((n_tile, n_col * n_part, LANES), jnp.float32),
        ]
        + [pltpu.VMEM((n_pose * n_col, LANES), jnp.float32)] * UNROLL
        + [pltpu.VMEM((n_row, LANES), jnp.float32)] * n_acc
        + [
            pltpu.SemaphoreType.DMA((n_part,)),
            pltpu.SemaphoreType.DMA((2,)),
            pltpu.SemaphoreType.DMA((3,)),
            pltpu.SemaphoreType.DMA,
            pltpu.SemaphoreType.DMA((n_row // (64 * SUB),)),
        ],
        compiler_params=pltpu.CompilerParams(vmem_limit_bytes=60 * MIB),
        name="accumulate",
    )(projections, images, transfer, pose_weights.T, pose_of.T, pose_blocks.T, pose_tiles.T)


def bank_kernel(sums, bank, out):
    bank_size, n_z, n_cell = bank.shape
    n_blk = out.shape[0]
    group = 2 * SUB

    for c in range(n_cell // LANES):
        cols = slice(c * LANES, (c + 1) * LANES)

        @pl.loop(0, n_z // group)
        def _(g):
            rows = pl.ds(pl.multiple_of(g * group, group), group)
            weights = [bank[t, rows, cols] for t in range(bank_size)]
            for b in range(n_blk):
                total = weights[0] * sums[b * bank_size, c : c + 1, :]
                for t in range(1, bank_size):
                    total += weights[t] * sums[b * bank_size + t, c : c + 1, :]
                out[b, rows, cols] = total


def apply_bank(sums, weight_bank, n_blk):
    bank_size, n_z, n_cell = weight_bank.shape
    vmem = pl.BlockSpec(memory_space=pltpu.VMEM)
    return pl.pallas_call(
        bank_kernel,
        out_shape=jax.ShapeDtypeStruct((n_blk, n_z, n_cell), jnp.float32),
        in_specs=[vmem, vmem],
        out_specs=vmem,
        compiler_params=pltpu.CompilerParams(vmem_limit_bytes=32 * MIB),
        name="apply_bank",
    )(sums, weight_bank)


def body(
    projections, images, transfer, pose_weights, pose_of, pose_blocks, pose_tiles, weight_bank
):
    bank_size = weight_bank.shape[0]
    n_cell = projections.shape[-1]
    total = NB_DEV * lax.axis_size("blk") * bank_size
    sums = accumulate(
        projections, images, transfer, pose_weights, pose_of, pose_blocks, pose_tiles, total, bank_size
    )
    sums = sums.reshape(total, n_cell // LANES, LANES)
    owned = lax.psum_scatter(sums, ("blk", "rep"), scatter_dimension=0, tiled=True)
    owned = lax.all_gather(owned, "rep", axis=0, tiled=True)
    return apply_bank(owned, weight_bank, NB_DEV)


def solution(mesh):
    placed = (
        P(("groups", "blk", "rep"), None, None, None),
        P(("groups", "blk", "rep"), None, None),
        P(("groups", "blk", "rep"), None, None),
        P(("groups", "blk", "rep"), None),
        P(("groups", "blk", "rep"), None),
        P("groups", None),
        P("groups", None),
        P(),
    )
    return jax.shard_map(
        body,
        mesh=mesh,
        in_specs=placed,
        out_specs=P(("groups", "blk"), None, None),
        check_vma=False,
    )
```

time: 294 us -> 113 us (0.38)
  local copies, waits for them, and re-layouts: 78 us -> 0.01 us
  other arithmetic: 51 us -> 0 us
  waiting for transfers between devices: 118 us -> 75.5 us
  matrix products: 32.2 us -> 0 us
  Pallas kernels: 0 us -> 21.6 us
    scatter-add x1 -> x0, other arithmetic: 42.9 us -> none  [body(): jax.ops.segment_sum(contrib.reshape(-1, face_cells), segment, num_segment...]
    dot_general x1 -> x0, matrix products: 32.2 us -> none  [apply_bank(): jnp.einsum('tzq,btq->bzq', weight_bank, tile_rows, precision=lax.Precisio...]
    reduce_scatter x1, waiting for transfers between devices: 108 us -> 75.5 us  [body(): lax.psum_scatter(sums, ('blk', 'rep'), scatter_dimension=0, tiled=True)]
    reshape x2 -> x0, local copies, waits for them, and re-layouts: 28 us -> none  [the longest x1 19.3 us: body(): contrib.reshape(-1, face_cells)]
    pallas_call x0 -> x2, Pallas kernels: none -> 21.6 us  [the longest x1 19.2 us: accumulate(): pl.pallas_call(functools.partial(accumulate_kernel, bank_size, n_acc), ou...]
    mul x1 -> x0, local copies, waits for them, and re-layouts: 18.4 us -> none  [body(): contrib = pose_weights[:, :, None, None] * transfer_f * residual]
    transpose x1 -> x0, local copies, waits for them, and re-layouts: 13.8 us -> none  [apply_bank(): jnp.einsum('tzq,btq->bzq', weight_bank, tile_rows, precision=lax.Precisio...]
    unnamed x9 -> x2, local copies, waits for them, and re-layouts: 10.7 us -> 0.01 us
  transfers between devices with their start and end apart: 2 -> 1, of which waited for: 2 -> 1; matrix products, arithmetic and copies ran while one was open for 0% -> 0% of each run, Pallas kernels for 0% -> 0%
where the time goes in v1:
time: 113 us
  waiting for transfers between devices  75.5 us (67%)
  Pallas kernels  21.6 us (19%)
  between operations  13.4 us (12%)
  blocking collectives  2.38 us (2%)
    reduce_scatter x1, waiting for transfers between devices, body(): lax.psum_scatter(sums, ('blk', 'rep'), scatter_dimension=0, tiled=True)  75.5 us
    pallas_call x1, Pallas kernels, accumulate(): pl.pallas_call(functools.partial(accumulate_kernel, bank_size, n_acc), ou...  19.2 us
    all_gather x1, blocking collectives, body(): owned = lax.all_gather(owned, 'rep', axis=0, tiled=True)  2.38 us
    pallas_call x1, Pallas kernels, apply_bank(): pl.pallas_call(bank_kernel, out_shape=jax.ShapeDtypeStruct((n_blk, n_z, n...  2.36 us
  transfers between devices with their start and end apart: 1, of which 1 were waited for; matrix products, arithmetic and copies ran while one was open for 0% of the time, Pallas kernels for 0%

profile of v1, /device:TPU:0, one launch (start us, length us, event | category | flops | bytes accessed | tf_op | source)
XLA Modules:
  0.0 112.9 jit_solution(7949343078623199002)
XLA Ops:
  6.5 0.0 reduce-scatter.2.cloned.1.call-start
  6.5 19.2 %accumulate.1 = f32[8192,128]{1,0:T(8,128)} custom-call(bf16[16,36,8,1024]{3,2,1,0:T(8,128)(2,1)} %bitcast.9, bf16[36,16,1024]{2,1,0:T(8,128)(2,1)} %bitcast.10, bf16[36,16,1024]{2,1,0:T(8,128)(2,1)} %bitcast.11, f32[8,16]{1,0:T(8,128)} %bitcast.14, s32[8,16]{1,0:T(8,128)} %bitcast.15, s32[36,512]{1,0:T(8,128)} %bitcast.12, s32[36,512]{1,0:T(8,128)} %bitcast.13), custom_call_target="tpu_custom_call" | custom-call | tf_op jit(solution)/shard_map/accumulate/pallas_call | solution.py:140
  25.8 0.0 copy-start
  25.8 0.0 reduce-scatter.2.cloned.1.call-update
  25.8 75.5 %reduce-scatter.2.cloned.1.call-done = f32[64,8,128]{2,1,0:T(8,128)} async-done(((f32[1024,8,128]{2,1,0:T(8,128)}), f32[64,8,128]{2,1,0:T(8,128)}) %reduce-scatter.2.cloned.1.call-update) | async-done | bytes 262160 | tf_op jit(solution)/shard_map/reduce_scatter | solution.py:213
  101.3 2.4 %all_gather.3.sums = f32[128,8,128]{2,1,0:T(8,128)S(1)} all-gather(f32[64,8,128]{2,1,0:T(8,128)} %reduce-scatter.2.cloned.1.call-done), channel_id=1, replica_groups=mesh['groups'=2,'blk'=8,'rep'=2] {'rep'}, dimensions={0}, use_global_device_ids=true | all-gather | bytes 786432 | tf_op jit(solution)/shard_map/all_gather | solution.py:214
  103.7 0.0 copy-done
  103.7 2.4 %apply_bank.1 = f32[8,32,1024]{2,1,0:T(8,128)} custom-call(f32[128,8,128]{2,1,0:T(8,128)S(1)} %all_gather.3.sums, f32[16,32,1024]{2,1,0:T(8,128)S(1)} %copy-done), custom_call_target="tpu_custom_call" | custom-call | tf_op jit(solution)/shard_map/apply_bank/pallas_call | solution.py:193
Async XLA Ops:
  6.5 94.8 %reduce-scatter.2.cloned.1.call-start = ((), (), s32[]{:S(2)}) async-start(), calls=%async_computation.1 | async-start | bytes 4456448 | tf_op jit(solution)/shard_map/reduce_scatter | solution.py:213
  25.8 77.9 %copy-start = (f32[16,32,1024]{2,1,0:T(8,128)S(1)}, f32[16,32,1024]{2,1,0:T(8,128)}, u32[]{:S(2)}) copy-start(f32[16,32,1024]{2,1,0:T(8,128)} %bank.1) | copy-start | bytes 6291460
Sparse Core Ops, SparseCore 0:
  25.9 75.3 reduce-scatter.1

commit v2 on v1

v2 whole, which is shorter than its diff:
```python
import functools

import jax
import jax.numpy as jnp
from jax import lax
from jax.experimental import pallas as pl
from jax.experimental.pallas import tpu as pltpu
from jax.sharding import PartitionSpec as P

NB_DEV = 8
LANES = 128
SUB = 8
MIB = 1 << 20
N_ACC = 4
N_CHUNK = 4


def accumulate_kernel(
    bank_size, n_owner, n_chunk,
    rep_smem, proj_hbm, img_hbm, tra_hbm, w_smem, pose_hbm, blocks_hbm, tiles_hbm,
    *rest,
):
    outs, rest = rest[: 2 * n_chunk], rest[2 * n_chunk :]
    proj, img, tra, pose, blocks, tiles, idx_v, idx_s, square, cross = rest[:10]
    accs = rest[10 : 10 + N_ACC]
    proj_sem, small_sem, table_sem, idx_sem, out_sem = rest[10 + N_ACC :]
    n_pose, n_part = pose.shape
    n_tile, n_table = blocks.shape
    n_row = accs[0].shape[0]
    group = 4 * SUB * SUB

    table_copies = [
        pltpu.make_async_copy(src, dst, table_sem.at[i])
        for i, (src, dst) in enumerate(((pose_hbm, pose), (blocks_hbm, blocks), (tiles_hbm, tiles)))
    ]
    small_copies = [
        pltpu.make_async_copy(img_hbm, img, small_sem.at[0]),
        pltpu.make_async_copy(tra_hbm, tra, small_sem.at[1]),
    ]
    for copy in table_copies + small_copies:
        copy.start()

    def proj_copy(p):
        return pltpu.make_async_copy(proj_hbm.at[p], proj.at[p], proj_sem.at[p])

    for p in range(n_part):
        proj_copy(p).start()

    for copy in table_copies:
        copy.wait()
    lane = lax.broadcasted_iota(jnp.int32, (n_pose, n_table), 1)
    chosen = jnp.concatenate(
        [(pose[:, p : p + 1] == lane).astype(jnp.float32) for p in range(n_part)], axis=0
    ).astype(jnp.bfloat16)

    def look_up(table):
        return lax.dot_general(
            chosen, table[...].astype(jnp.float32).astype(jnp.bfloat16),
            (((1,), (1,)), ((), ())), preferred_element_type=jnp.float32,
        )

    idx_v[:, :n_tile] = ((look_up(blocks) * bank_size + look_up(tiles)) * SUB).astype(jnp.int32)
    idx_copy = pltpu.make_async_copy(idx_v, idx_s, idx_sem)
    idx_copy.start()

    zero = jnp.zeros((8 * SUB, LANES), jnp.float32)

    @pl.loop(0, n_row // (8 * SUB))
    def _(i):
        rows = pl.ds(pl.multiple_of(i * (8 * SUB), 8 * SUB), 8 * SUB)
        for acc in accs:
            acc[rows, :] = zero

    to = lax.broadcasted_iota(jnp.int32, (group, group), 0)
    fro = lax.broadcasted_iota(jnp.int32, (group, group), 1)
    swapped = (fro // 64) * 64 + (fro % 8) * 8 + (fro // 8) % 8
    swap = (to == swapped).astype(jnp.float32).astype(jnp.bfloat16)

    def regroup(left, right):
        both = jnp.concatenate([left, right], axis=1)
        return jnp.dot(swap, both, preferred_element_type=jnp.float32)

    for copy in small_copies:
        copy.wait()

    @pl.loop(0, tra.shape[0] // group)
    def _(i):
        rows = pl.ds(pl.multiple_of(i * group, group), group)
        both = regroup(tra[rows, :], img[rows, :])
        t = both[:, :LANES]
        square[rows, :] = t * t
        cross[rows, :] = t * both[:, LANES:]

    idx_copy.wait()

    @pl.loop(0, n_part // 2)
    def _(q):
        proj_copy(2 * q).wait()
        proj_copy(2 * q + 1).wait()
        weights = [
            [jnp.full((SUB, LANES), w_smem[k, 2 * q + h], jnp.float32) for k in range(n_pose)]
            for h in range(2)
        ]

        @pl.loop(0, n_tile // 4)
        def _(i):
            rows = pl.ds(pl.multiple_of(i * group, group), group)
            x = regroup(proj[2 * q, rows, :], proj[2 * q + 1, rows, :])
            for u in range(4):
                j = i * 4 + u
                for h in range(2):
                    p = 2 * q + h
                    cell = pl.ds(pl.multiple_of((j * n_part + p) * SUB, SUB), SUB)
                    tt = square[cell, :]
                    ti = cross[cell, :]

                    def term(k):
                        first = (u * n_pose + k) * SUB
                        value = x[first : first + SUB, h * LANES : (h + 1) * LANES]
                        return (tt * value - ti) * weights[h][k]

                    for k in range(N_ACC):
                        acc = accs[k]
                        at = idx_s[p * n_pose + k, j]
                        at2 = idx_s[p * n_pose + k + N_ACC, j]
                        here = pl.ds(pl.multiple_of(at, SUB), SUB)
                        here2 = pl.ds(pl.multiple_of(at2, SUB), SUB)
                        same = jnp.where(at == at2, 1.0, 0.0)
                        one, two = term(k), term(k + N_ACC)
                        old, old2 = acc[here, :], acc[here2, :]
                        acc[here, :] = old + one
                        acc[here2, :] = old2 + (two + same * one)

    rep = rep_smem[0]
    piece = n_row // (n_owner * 2 * n_chunk)
    step = 4 * SUB

    for c in range(n_chunk):
        for side in range(2):
            out = outs[2 * c + side]
            half = rep if side else 1 - rep

            def out_copy(o, first):
                return pltpu.make_async_copy(
                    accs[0].at[pl.ds(first, piece), :], out.at[o], out_sem.at[(2 * c + side) * n_owner + o]
                )

            @pl.loop(0, n_owner)
            def _(o):
                first = pl.multiple_of(((o * 2 + half) * n_chunk + c) * piece, piece)

                @pl.loop(0, piece // step)
                def _(h):
                    rows = pl.ds(pl.multiple_of(first + h * step, step), step)
                    total = accs[0][rows, :]
                    for acc in accs[1:]:
                        total += acc[rows, :]
                    accs[0][rows, :] = total

                out_copy(o, first).start()

    for c in range(n_chunk):
        for side in range(2):

            @pl.loop(0, n_owner)
            def _(o):
                pltpu.make_async_copy(
                    accs[0].at[pl.ds(0, piece), :],
                    outs[2 * c + side].at[o],
                    out_sem.at[(2 * c + side) * n_owner + o],
                ).wait()


def tiles_in_order(array):
    lead = array.shape[:-2]
    rows, cells = array.shape[-2:]
    array = array.reshape(lead + (rows // SUB, SUB, cells // LANES, LANES))
    return jnp.swapaxes(array, -3, -2)


def accumulate(
    projections, images, transfer, pose_weights, pose_of, pose_blocks, pose_tiles,
    bank_size, n_owner, n_chunk, rep,
):
    n_part, n_pose, n_tile, n_cell = projections.shape
    assert n_cell == SUB * LANES and n_pose == SUB and n_pose == 2 * N_ACC
    n_row = n_owner * NB_DEV * bank_size * SUB
    n_idx = n_part * n_pose
    piece = n_row // (n_owner * 2 * n_chunk)
    projections = tiles_in_order(jnp.transpose(projections, (0, 2, 1, 3)))
    projections = projections.reshape(n_part, n_tile * n_pose * SUB, LANES)
    images = tiles_in_order(jnp.transpose(images, (1, 0, 2))).reshape(n_tile * n_part * SUB, LANES)
    transfer = tiles_in_order(jnp.transpose(transfer, (1, 0, 2))).reshape(n_tile * n_part * SUB, LANES)
    anywhere = pl.BlockSpec(memory_space=pl.ANY)
    smem = pl.BlockSpec(memory_space=pltpu.SMEM)
    return pl.pallas_call(
        functools.partial(accumulate_kernel, bank_size, n_owner, n_chunk),
        out_shape=[jax.ShapeDtypeStruct((n_owner, piece, LANES), jnp.float32)] * (2 * n_chunk),
        in_specs=[smem] + [anywhere] * 3 + [smem] + [anywhere] * 3,
        out_specs=[anywhere] * (2 * n_chunk),
        scratch_shapes=[
            pltpu.VMEM(projections.shape, jnp.bfloat16),
            pltpu.VMEM(images.shape, jnp.bfloat16),
            pltpu.VMEM(transfer.shape, jnp.bfloat16),
            pltpu.VMEM((n_pose, n_part), jnp.int32),
            pltpu.VMEM(pose_blocks.shape[::-1], jnp.int32),
            pltpu.VMEM(pose_tiles.shape[::-1], jnp.int32),
            pltpu.VMEM((n_idx, LANES), jnp.int32),
            pltpu.SMEM((n_idx, LANES), jnp.int32),
            pltpu.VMEM(transfer.shape, jnp.float32),
            pltpu.VMEM(transfer.shape, jnp.float32),
        ]
        + [pltpu.VMEM((n_row, LANES), jnp.float32)] * N_ACC
        + [
            pltpu.SemaphoreType.DMA((n_part,)),
            pltpu.SemaphoreType.DMA((2,)),
            pltpu.SemaphoreType.DMA((3,)),
            pltpu.SemaphoreType.DMA,
            pltpu.SemaphoreType.DMA((2 * n_chunk * n_owner,)),
        ],
        compiler_params=pltpu.CompilerParams(vmem_limit_bytes=60 * MIB),
        name="accumulate",
    )(rep, projections, images, transfer, pose_weights.T, pose_of.T, pose_blocks.T, pose_tiles.T)


def bank_kernel(sums, bank, out):
    bank_size, n_z, n_cell = bank.shape
    n_blk = out.shape[0]
    group = 2 * SUB

    for c in range(n_cell // LANES):
        cols = slice(c * LANES, (c + 1) * LANES)

        @pl.loop(0, n_z // group)
        def _(g):
            rows = pl.ds(pl.multiple_of(g * group, group), group)
            weights = [bank[t, rows, cols] for t in range(bank_size)]
            for b in range(n_blk):
                total = weights[0] * sums[b * bank_size, c : c + 1, :]
                for t in range(1, bank_size):
                    total += weights[t] * sums[b * bank_size + t, c : c + 1, :]
                out[b, rows, cols] = total


def apply_bank(sums, weight_bank, n_blk):
    bank_size, n_z, n_cell = weight_bank.shape
    vmem = pl.BlockSpec(memory_space=pltpu.VMEM)
    return pl.pallas_call(
        bank_kernel,
        out_shape=jax.ShapeDtypeStruct((n_blk, n_z, n_cell), jnp.float32),
        in_specs=[vmem, vmem],
        out_specs=vmem,
        compiler_params=pltpu.CompilerParams(vmem_limit_bytes=32 * MIB),
        name="apply_bank",
    )(sums, weight_bank)


def body(
    projections, images, transfer, pose_weights, pose_of, pose_blocks, pose_tiles, weight_bank
):
    bank_size = weight_bank.shape[0]
    n_blk = lax.axis_size("blk")
    n_far = n_blk // 2
    here = lax.axis_index("blk")
    far, near = here // 2, here % 2
    rep = lax.axis_index("rep").astype(jnp.int32).reshape(1)
    outs = accumulate(
        projections, images, transfer, pose_weights, pose_of, pose_blocks, pose_tiles,
        bank_size, n_blk, N_CHUNK, rep,
    )
    swap_rep = [(0, 1), (1, 0)]
    swap_near = [(i, i ^ 1) for i in range(n_blk)]

    def pick(array, index, axis):
        return lax.dynamic_index_in_dim(array, index, axis, keepdims=False)

    owned = []
    for c in range(N_CHUNK):
        sent, kept = outs[2 * c], outs[2 * c + 1]
        got = lax.ppermute(sent, "rep", swap_rep)
        shape = (n_far, 2) + sent.shape[1:]
        got, kept = got.reshape(shape), kept.reshape(shape)
        away = pick(kept, 1 - near, 1) + pick(got, 1 - near, 1)
        stay = pick(kept, near, 1) + pick(got, near, 1)
        stay = stay + lax.ppermute(away, "blk", swap_near)
        total = pick(stay, far, 0)
        for d in range(1, n_far):
            pairs = [(i, i ^ (2 * d)) for i in range(n_blk)]
            total = total + lax.ppermute(pick(stay, far ^ d, 0), "blk", pairs)
        owned.append(total)
    owned = jnp.concatenate(owned, axis=0)
    owned = lax.all_gather(owned, "rep", axis=0, tiled=True)
    owned = owned.reshape(NB_DEV * bank_size, SUB, LANES)
    return apply_bank(owned, weight_bank, NB_DEV)


def solution(mesh):
    placed = (
        P(("groups", "blk", "rep"), None, None, None),
        P(("groups", "blk", "rep"), None, None),
        P(("groups", "blk", "rep"), None, None),
        P(("groups", "blk", "rep"), None),
        P(("groups", "blk", "rep"), None),
        P("groups", None),
        P("groups", None),
        P(),
    )
    return jax.shard_map(
        body,
        mesh=mesh,
        in_specs=placed,
        out_specs=P(("groups", "blk"), None, None),
        check_vma=False,
    )
```

time: 113 us -> 87.7 us (0.78)
  waiting for transfers between devices: 75.5 us -> 18.4 us
  starting transfers between devices: 0.01 us -> 29.1 us
  between operations: 13.4 us -> 0.21 us
  Pallas kernels: 21.6 us -> 34.1 us
  other arithmetic: 0 us -> 3.33 us
    reduce_scatter x1 -> x0, waiting for transfers between devices: 75.5 us -> none  [body(): lax.psum_scatter(sums, ('blk', 'rep'), scatter_dimension=0, tiled=True)]
    ppermute x0 -> x20, starting transfers between devices: none -> 29.1 us  [the longest x12 22.8 us: body(): total = total + lax.ppermute(pick(stay, far ^ d, 0), 'blk', pairs)]
    ppermute x0 -> x20, waiting for transfers between devices: none -> 18.4 us  [the longest x4 8.91 us: body(): stay = stay + lax.ppermute(away, 'blk', swap_near)]
    pallas_call x1, Pallas kernels: 19.2 us -> 31.7 us  [accumulate(): pl.pallas_call(functools.partial(accumulate_kernel, bank_size, n_owner, n...]
    add x0 -> x12, other arithmetic: none -> 3.31 us  [the longest x4 3.04 us: body(): away = pick(kept, 1 - near, 1) + pick(got, 1 - near, 1)]
  transfers between devices with their start and end apart: 1 -> 20, of which waited for: 1 -> 9; matrix products, arithmetic and copies ran while one was open for 0% -> 4% of each run, Pallas kernels for 0% -> 0%
where the time goes in v2:
time: 87.7 us; the launch traced here: 87.5 us
  Pallas kernels  34.1 us (39%)
  starting transfers between devices  29.1 us (33%)
  waiting for transfers between devices  18.4 us (21%)
  other arithmetic  3.33 us (4%)
  blocking collectives  2.18 us (2%)
    pallas_call x1, Pallas kernels, accumulate(): pl.pallas_call(functools.partial(accumulate_kernel, bank_size, n_owner, n...  31.7 us
    ppermute x12, starting transfers between devices, body(): total = total + lax.ppermute(pick(stay, far ^ d, 0), 'blk', pairs)  22.8 us
    ppermute x4, waiting for transfers between devices, body(): stay = stay + lax.ppermute(away, 'blk', swap_near)  8.91 us
    ppermute x12, waiting for transfers between devices, body(): total = total + lax.ppermute(pick(stay, far ^ d, 0), 'blk', pairs)  8.37 us
    ppermute x4, starting transfers between devices, body(): stay = stay + lax.ppermute(away, 'blk', swap_near)  5.23 us
    add x4, other arithmetic, body(): away = pick(kept, 1 - near, 1) + pick(got, 1 - near, 1)  3.04 us
    pallas_call x1, Pallas kernels, apply_bank(): pl.pallas_call(bank_kernel, out_shape=jax.ShapeDtypeStruct((n_blk, n_z, n...  2.36 us
    all_gather x1, blocking collectives, body(): owned = lax.all_gather(owned, 'rep', axis=0, tiled=True)  2.18 us
  transfers between devices with their start and end apart: 20, of which 9 were waited for; matrix products, arithmetic and copies ran while one was open for 4% of the time, Pallas kernels for 0%

profile of v2, /device:TPU:0, one launch (start us, length us, event | category | flops | bytes accessed | tf_op | source)
XLA Modules:
  0.0 87.5 jit_solution(553983147418693336)
XLA Ops:
  0.0 31.7 %accumulate.1 = (f32[8,128,128]{2,1,0:T(8,128)}, f32[8,128,128]{2,1,0:T(8,128)}, f32[8,128,128]{2,1,0:T(8,128)}, f32[8,128,128]{2,1,0:T(8,128)}, f32[8,128,128]{...) custom-call(s32[1]{0:T(128)} %bitcast.rep_smem, ...), custom_call_target="tpu_custom_call" | custom-call | tf_op jit(solution)/shard_map/accumulate/pallas_call | solution.py:196
  32.8 1.2 %collective-permute-done = f32[8,128,128]{2,1,0:T(8,128)S(1)} collective-permute-done((f32[8,128,128]{2,1,0:T(8,128)}, f32[8,128,128]{2,1,0:T(8,128)S(1)}, u32[]{:S(2)}, u32[]{:S(2)}) %collective-permute-start) | collective-permute-done | bytes 524320 | tf_op jit(solution)/shard_map/ppermute | solution.py:280
  34.0 1.0 %add_bitcast_fusion.3 = f32[4,128,128]{2,1,0:T(8,128)S(1)} fusion(f32[4,2,128,128]{3,2,1,0:T(8,128)S(1)} %bitcast.157, s32[]{:T(128)S(6)} %select_n.59, f32[4,2,128,128]{3,2,1,0:T(8,128)} %bitcast.155), kind=kLoop, calls=%fused_computation.16 | loop fusion | flops 65536 | bytes 786436 | tf_op jit(solution)/shard_map/add | solution.py:283
  35.0 2.9 %collective-permute-start.1 = (f32[4,128,128]{2,1,0:T(8,128)S(1)}, f32[4,128,128]{2,1,0:T(8,128)S(1)}, u32[]{:S(2)}, u32[]{:S(2)}) collective-permute-start(f32[4,128,128]{2,1,0:T(8,128)S(1)} %add_bitcast_fusion.3), channel_id=1, source_target_pairs={{0,2},{2,0},{4,6},{6,4},{8,10},{10,8},{12,14},{14,12},{1,3},{3,1},... | collective-permute-start | bytes 786440 | tf_op jit(solution)/shard_map/ppermute | solution.py:285
  37.9 1.0 %add_bitcast_fusion.2 = f32[4,128,128]{2,1,0:T(8,128)S(1)} fusion(f32[4,2,128,128]{3,2,1,0:T(8,128)S(1)} %bitcast.153, s32[]{:T(128)S(6)} %select_n.59, f32[4,2,128,128]{3,2,1,0:T(8,128)} %bitcast.151), kind=kLoop, calls=%fused_computation.15 | loop fusion | flops 65536 | bytes 786436 | tf_op jit(solution)/shard_map/add | solution.py:283
  39.1 1.1 %add_bitcast_fusion.1 = f32[4,128,128]{2,1,0:T(8,128)S(1)} fusion(f32[4,2,128,128]{3,2,1,0:T(8,128)S(1)} %bitcast.149, s32[]{:T(128)S(6)} %select_n.59, f32[4,2,128,128]{3,2,1,0:T(8,128)} %bitcast.145), kind=kLoop, calls=%fused_computation.14 | loop fusion | flops 65536 | bytes 786436 | tf_op jit(solution)/shard_map/add | solution.py:283
  40.1 2.0 %collective-permute-start.11 = (f32[4,128,128]{2,1,0:T(8,128)S(1)}, f32[4,128,128]{2,1,0:T(8,128)S(1)}, u32[]{:S(2)}, u32[]{:S(2)}) collective-permute-start(f32[4,128,128]{2,1,0:T(8,128)S(1)} %add_bitcast_fusion.1), channel_id=1, source_target_pairs={{0,2},{2,0},{4,6},{6,4},{8,10},{10,8},{12,14},{14,12},{1,3},{3,1},... | collective-permute-start | bytes 786440 | tf_op jit(solution)/shard_map/ppermute | solution.py:285
  42.3 2.7 %collective-permute-done.1 = f32[4,128,128]{2,1,0:T(8,128)S(1)} collective-permute-done((f32[4,128,128]{2,1,0:T(8,128)S(1)}, f32[4,128,128]{2,1,0:T(8,128)S(1)}, u32[]{:S(2)}, u32[]{:S(2)}) %collective-permute-start.1) | collective-permute-done | bytes 262176 | tf_op jit(solution)/shard_map/ppermute | solution.py:285
  45.1 2.2 %collective-permute-start.2 = (f32[128,128]{1,0:T(8,128)S(1)}, f32[128,128]{1,0:T(8,128)S(1)}, u32[]{:S(2)}, u32[]{:S(2)}) collective-permute-start(f32[128,128]{1,0:T(8,128)S(1)} %get-tuple-element.21), channel_id=1, source_target_pairs={{0,4},{2,6},{4,0},{6,2},{8,12},{10,14},{12,8},{14,10},{1,5},{3,7},... | collective-permute-start | bytes 196616 | tf_op jit(solution)/shard_map/ppermute | solution.py:289
  47.3 2.5 %collective-permute-start.4 = (f32[128,128]{1,0:T(8,128)S(1)}, f32[128,128]{1,0:T(8,128)S(1)}, u32[]{:S(2)}, u32[]{:S(2)}) collective-permute-start(f32[128,128]{1,0:T(8,128)S(1)} %get-tuple-element.22), channel_id=1, source_target_pairs={{0,12},{2,14},{4,8},{6,10},{8,4},{10,6},{12,0},{14,2},{1,13},{3,15... | collective-permute-start | bytes 196616 | tf_op jit(solution)/shard_map/ppermute | solution.py:289
  49.7 0.9 %collective-permute-done.6 = f32[4,128,128]{2,1,0:T(8,128)S(1)} collective-permute-done((f32[4,128,128]{2,1,0:T(8,128)S(1)}, f32[4,128,128]{2,1,0:T(8,128)S(1)}, u32[]{:S(2)}, u32[]{:S(2)}) %collective-permute-start.6) | collective-permute-done | bytes 262176 | tf_op jit(solution)/shard_map/ppermute | solution.py:285
  50.6 3.1 %collective-permute-start.3 = (f32[128,128]{1,0:T(8,128)S(1)}, f32[128,128]{1,0:T(8,128)S(1)}, u32[]{:S(2)}, u32[]{:S(2)}) collective-permute-start(f32[128,128]{1,0:T(8,128)S(1)} %get-tuple-element.23), channel_id=1, source_target_pairs={{0,8},{2,10},{4,12},{6,14},{8,0},{10,2},{12,4},{14,6},{1,9},{3,11}... | collective-permute-start | bytes 196616 | tf_op jit(solution)/shard_map/ppermute | solution.py:289
  53.8 2.4 %collective-permute-done.11 = f32[4,128,128]{2,1,0:T(8,128)S(1)} collective-permute-done((f32[4,128,128]{2,1,0:T(8,128)S(1)}, f32[4,128,128]{2,1,0:T(8,128)S(1)}, u32[]{:S(2)}, u32[]{:S(2)}) %collective-permute-start.11) | collective-permute-done | bytes 262176 | tf_op jit(solution)/shard_map/ppermute | solution.py:285
  56.2 2.1 %collective-permute-start.7 = (f32[128,128]{1,0:T(8,128)S(1)}, f32[128,128]{1,0:T(8,128)S(1)}, u32[]{:S(2)}, u32[]{:S(2)}) collective-permute-start(f32[128,128]{1,0:T(8,128)S(1)} %get-tuple-element.24), channel_id=1, source_target_pairs={{0,4},{2,6},{4,0},{6,2},{8,12},{10,14},{12,8},{14,10},{1,5},{3,7},... | collective-permute-start | bytes 196616 | tf_op jit(solution)/shard_map/ppermute | solution.py:289
  58.5 2.9 %collective-permute-done.16 = f32[4,128,128]{2,1,0:T(8,128)S(1)} collective-permute-done((f32[4,128,128]{2,1,0:T(8,128)S(1)}, f32[4,128,128]{2,1,0:T(8,128)S(1)}, u32[]{:S(2)}, u32[]{:S(2)}) %collective-permute-start.16) | collective-permute-done | bytes 262176 | tf_op jit(solution)/shard_map/ppermute | solution.py:285
  61.4 3.8 %collective-permute-start.9 = (f32[128,128]{1,0:T(8,128)S(1)}, f32[128,128]{1,0:T(8,128)S(1)}, u32[]{:S(2)}, u32[]{:S(2)}) collective-permute-start(f32[128,128]{1,0:T(8,128)S(1)} %get-tuple-element.25), channel_id=1, source_target_pairs={{0,12},{2,14},{4,8},{6,10},{8,4},{10,6},{12,0},{14,2},{1,13},{3,15... | collective-permute-start | bytes 196616 | tf_op jit(solution)/shard_map/ppermute | solution.py:289
  66.0 3.8 %collective-permute-start.14 = (f32[128,128]{1,0:T(8,128)S(1)}, f32[128,128]{1,0:T(8,128)S(1)}, u32[]{:S(2)}, u32[]{:S(2)}) collective-permute-start(f32[128,128]{1,0:T(8,128)S(1)} %get-tuple-element.28), channel_id=1, source_target_pairs={{0,12},{2,14},{4,8},{6,10},{8,4},{10,6},{12,0},{14,2},{1,13},{3,15... | collective-permute-start | bytes 196616 | tf_op jit(solution)/shard_map/ppermute | solution.py:289
  70.4 3.2 %collective-permute-done.8 = f32[128,128]{1,0:T(8,128)S(1)} collective-permute-done((f32[128,128]{1,0:T(8,128)S(1)}, f32[128,128]{1,0:T(8,128)S(1)}, u32[]{:S(2)}, u32[]{:S(2)}) %collective-permute-start.8) | collective-permute-done | bytes 65568 | tf_op jit(solution)/shard_map/ppermute | solution.py:289
  73.7 3.9 %collective-permute-start.19 = (f32[128,128]{1,0:T(8,128)S(1)}, f32[128,128]{1,0:T(8,128)S(1)}, u32[]{:S(2)}, u32[]{:S(2)}) collective-permute-start(f32[128,128]{1,0:T(8,128)S(1)} %get-tuple-element.31), channel_id=1, source_target_pairs={{0,12},{2,14},{4,8},{6,10},{8,4},{10,6},{12,0},{14,2},{1,13},{3,15... | collective-permute-start | bytes 196616 | tf_op jit(solution)/shard_map/ppermute | solution.py:289
  77.7 0.6 collective-permute-done.13
  78.4 1.6 %collective-permute-done.19 = f32[128,128]{1,0:T(8,128)S(1)} collective-permute-done((f32[128,128]{1,0:T(8,128)S(1)}, f32[128,128]{1,0:T(8,128)S(1)}, u32[]{:S(2)}, u32[]{:S(2)}) %collective-permute-start.19) | collective-permute-done | bytes 65568 | tf_op jit(solution)/shard_map/ppermute | solution.py:289
  80.0 2.9 %collective-permute-done.18 = f32[128,128]{1,0:T(8,128)S(1)} collective-permute-done((f32[128,128]{1,0:T(8,128)S(1)}, f32[128,128]{1,0:T(8,128)S(1)}, u32[]{:S(2)}, u32[]{:S(2)}) %collective-permute-start.18) | collective-permute-done | bytes 65568 | tf_op jit(solution)/shard_map/ppermute | solution.py:289
  82.9 2.2 %all_gather.3 = f32[1024,128]{1,0:T(8,128)S(1)} all-gather(f32[512,128]{1,0:T(8,128)S(1)} %pad_maximum_fusion), channel_id=1, replica_groups=mesh['groups'=2,'blk'=8,'rep'=2] {'rep'}, dimensions={0}, use_global_device_ids=true | all-gather | bytes 786432 | tf_op jit(solution)/shard_map/all_gather | solution.py:292
  85.1 2.4 %apply_bank.1 = f32[8,32,1024]{2,1,0:T(8,128)} custom-call(f32[128,8,128]{2,1,0:T(8,128)S(1)} %bitcast.139, f32[16,32,1024]{2,1,0:T(8,128)S(1)} %copy-done), custom_call_target="tpu_custom_call" | custom-call | tf_op jit(solution)/shard_map/apply_bank/pallas_call | solution.py:248
  (46 shorter events, 3.2 us)
Async XLA Ops:
  31.7 13.3 %copy-start.4 = (f32[8,128,128]{2,1,0:T(8,128)S(1)}, f32[8,128,128]{2,1,0:T(8,128)}, u32[]{:S(2)}) copy-start(f32[8,128,128]{2,1,0:T(8,128)} %get-tuple-element.13) | copy-start | bytes 1572868
  31.7 2.3 %collective-permute-start = (f32[8,128,128]{2,1,0:T(8,128)}, f32[8,128,128]{2,1,0:T(8,128)S(1)}, u32[]{:S(2)}, u32[]{:S(2)}) collective-permute-start(f32[8,128,128]{2,1,0:T(8,128)} %get-tuple-element.14), channel_id=1, source_target_pairs={{0,1},{1,0},{2,3},{3,2},{4,5},{5,4},{6,7},{7,6},{8,9},{9,8},{10,11... | collective-permute-start | bytes 1572872 | tf_op jit(solution)/shard_map/ppermute | solution.py:280
  32.2 5.7 %collective-permute-start.5 = (f32[8,128,128]{2,1,0:T(8,128)}, f32[8,128,128]{2,1,0:T(8,128)S(1)}, u32[]{:S(2)}, u32[]{:S(2)}) collective-permute-start(f32[8,128,128]{2,1,0:T(8,128)} %get-tuple-element.16), channel_id=1, source_target_pairs={{0,1},{1,0},{2,3},{3,2},{4,5},{5,4},{6,7},{7,6},{8,9},{9,8},{10,11... | collective-permute-start | bytes 1572872 | tf_op jit(solution)/shard_map/ppermute | solution.py:280
  32.3 6.7 %collective-permute-start.10 = (f32[8,128,128]{2,1,0:T(8,128)}, f32[8,128,128]{2,1,0:T(8,128)S(1)}, u32[]{:S(2)}, u32[]{:S(2)}) collective-permute-start(f32[8,128,128]{2,1,0:T(8,128)} %get-tuple-element.18), channel_id=1, source_target_pairs={{0,1},{1,0},{2,3},{3,2},{4,5},{5,4},{6,7},{7,6},{8,9},{9,8},{10,11... | collective-permute-start | bytes 1572872 | tf_op jit(solution)/shard_map/ppermute | solution.py:280
  32.8 9.4 %collective-permute-start.15 = (f32[8,128,128]{2,1,0:T(8,128)}, f32[8,128,128]{2,1,0:T(8,128)S(1)}, u32[]{:S(2)}, u32[]{:S(2)}) collective-permute-start(f32[8,128,128]{2,1,0:T(8,128)} %get-tuple-element.20), channel_id=1, source_target_pairs={{0,1},{1,0},{2,3},{3,2},{4,5},{5,4},{6,7},{7,6},{8,9},{9,8},{10,11... | collective-permute-start | bytes 1572872 | tf_op jit(solution)/shard_map/ppermute | solution.py:280
  35.0 18.8 %copy-start.3 = (f32[8,128,128]{2,1,0:T(8,128)S(1)}, f32[8,128,128]{2,1,0:T(8,128)}, u32[]{:S(2)}) copy-start(f32[8,128,128]{2,1,0:T(8,128)} %get-tuple-element.15) | copy-start | bytes 1572868
  35.0 10.0 %collective-permute-start.1 = (f32[4,128,128]{2,1,0:T(8,128)S(1)}, f32[4,128,128]{2,1,0:T(8,128)S(1)}, u32[]{:S(2)}, u32[]{:S(2)}) collective-permute-start(f32[4,128,128]{2,1,0:T(8,128)S(1)} %add_bitcast_fusion.3), channel_id=1, source_target_pairs={{0,2},{2,0},{4,6},{6,4},{8,10},{10,8},{12,14},{14,12},{1,3},{3,1},... | collective-permute-start | bytes 786440 | tf_op jit(solution)/shard_map/ppermute | solution.py:285
  38.9 11.7 %collective-permute-start.6 = (f32[4,128,128]{2,1,0:T(8,128)S(1)}, f32[4,128,128]{2,1,0:T(8,128)S(1)}, u32[]{:S(2)}, u32[]{:S(2)}) collective-permute-start(f32[4,128,128]{2,1,0:T(8,128)S(1)} %add_bitcast_fusion.2), channel_id=1, source_target_pairs={{0,2},{2,0},{4,6},{6,4},{8,10},{10,8},{12,14},{14,12},{1,3},{3,1},... | collective-permute-start | bytes 786440 | tf_op jit(solution)/shard_map/ppermute | solution.py:285
  39.0 19.3 %copy-start.2 = (f32[8,128,128]{2,1,0:T(8,128)S(1)}, f32[8,128,128]{2,1,0:T(8,128)}, u32[]{:S(2)}) copy-start(f32[8,128,128]{2,1,0:T(8,128)} %get-tuple-element.17) | copy-start | bytes 1572868
  40.1 16.1 %collective-permute-start.11 = (f32[4,128,128]{2,1,0:T(8,128)S(1)}, f32[4,128,128]{2,1,0:T(8,128)S(1)}, u32[]{:S(2)}, u32[]{:S(2)}) collective-permute-start(f32[4,128,128]{2,1,0:T(8,128)S(1)} %add_bitcast_fusion.1), channel_id=1, source_target_pairs={{0,2},{2,0},{4,6},{6,4},{8,10},{10,8},{12,14},{14,12},{1,3},{3,1},... | collective-permute-start | bytes 786440 | tf_op jit(solution)/shard_map/ppermute | solution.py:285
  42.2 19.2 %collective-permute-start.16 = (f32[4,128,128]{2,1,0:T(8,128)S(1)}, f32[4,128,128]{2,1,0:T(8,128)S(1)}, u32[]{:S(2)}, u32[]{:S(2)}) collective-permute-start(f32[4,128,128]{2,1,0:T(8,128)S(1)} %add_bitcast_fusion), channel_id=1, source_target_pairs={{0,2},{2,0},{4,6},{6,4},{8,10},{10,8},{12,14},{14,12},{1,3},{3,1},... | collective-permute-start | bytes 786440 | tf_op jit(solution)/shard_map/ppermute | solution.py:285
  45.1 20.2 %collective-permute-start.2 = (f32[128,128]{1,0:T(8,128)S(1)}, f32[128,128]{1,0:T(8,128)S(1)}, u32[]{:S(2)}, u32[]{:S(2)}) collective-permute-start(f32[128,128]{1,0:T(8,128)S(1)} %get-tuple-element.21), channel_id=1, source_target_pairs={{0,4},{2,6},{4,0},{6,2},{8,12},{10,14},{12,8},{14,10},{1,5},{3,7},... | collective-permute-start | bytes 196616 | tf_op jit(solution)/shard_map/ppermute | solution.py:289
  47.3 18.1 %collective-permute-start.4 = (f32[128,128]{1,0:T(8,128)S(1)}, f32[128,128]{1,0:T(8,128)S(1)}, u32[]{:S(2)}, u32[]{:S(2)}) collective-permute-start(f32[128,128]{1,0:T(8,128)S(1)} %get-tuple-element.22), channel_id=1, source_target_pairs={{0,12},{2,14},{4,8},{6,10},{8,4},{10,6},{12,0},{14,2},{1,13},{3,15... | collective-permute-start | bytes 196616 | tf_op jit(solution)/shard_map/ppermute | solution.py:289
  50.6 15.3 %collective-permute-start.3 = (f32[128,128]{1,0:T(8,128)S(1)}, f32[128,128]{1,0:T(8,128)S(1)}, u32[]{:S(2)}, u32[]{:S(2)}) collective-permute-start(f32[128,128]{1,0:T(8,128)S(1)} %get-tuple-element.23), channel_id=1, source_target_pairs={{0,8},{2,10},{4,12},{6,14},{8,0},{10,2},{12,4},{14,6},{1,9},{3,11}... | collective-permute-start | bytes 196616 | tf_op jit(solution)/shard_map/ppermute | solution.py:289
  56.2 13.6 %collective-permute-start.7 = (f32[128,128]{1,0:T(8,128)S(1)}, f32[128,128]{1,0:T(8,128)S(1)}, u32[]{:S(2)}, u32[]{:S(2)}) collective-permute-start(f32[128,128]{1,0:T(8,128)S(1)} %get-tuple-element.24), channel_id=1, source_target_pairs={{0,4},{2,6},{4,0},{6,2},{8,12},{10,14},{12,8},{14,10},{1,5},{3,7},... | collective-permute-start | bytes 196616 | tf_op jit(solution)/shard_map/ppermute | solution.py:289
  58.4 26.7 %copy-start = (f32[16,32,1024]{2,1,0:T(8,128)S(1)}, f32[16,32,1024]{2,1,0:T(8,128)}, u32[]{:S(2)}) copy-start(f32[16,32,1024]{2,1,0:T(8,128)} %bank.1) | copy-start | bytes 6291460
  61.4 8.5 %collective-permute-start.9 = (f32[128,128]{1,0:T(8,128)S(1)}, f32[128,128]{1,0:T(8,128)S(1)}, u32[]{:S(2)}, u32[]{:S(2)}) collective-permute-start(f32[128,128]{1,0:T(8,128)S(1)} %get-tuple-element.25), channel_id=1, source_target_pairs={{0,12},{2,14},{4,8},{6,10},{8,4},{10,6},{12,0},{14,2},{1,13},{3,15... | collective-permute-start | bytes 196616 | tf_op jit(solution)/shard_map/ppermute | solution.py:289
  65.3 8.4 %collective-permute-start.8 = (f32[128,128]{1,0:T(8,128)S(1)}, f32[128,128]{1,0:T(8,128)S(1)}, u32[]{:S(2)}, u32[]{:S(2)}) collective-permute-start(f32[128,128]{1,0:T(8,128)S(1)} %get-tuple-element.26), channel_id=1, source_target_pairs={{0,8},{2,10},{4,12},{6,14},{8,0},{10,2},{12,4},{14,6},{1,9},{3,11}... | collective-permute-start | bytes 196616 | tf_op jit(solution)/shard_map/ppermute | solution.py:289
  65.4 12.2 %collective-permute-start.12 = (f32[128,128]{1,0:T(8,128)S(1)}, f32[128,128]{1,0:T(8,128)S(1)}, u32[]{:S(2)}, u32[]{:S(2)}) collective-permute-start(f32[128,128]{1,0:T(8,128)S(1)} %get-tuple-element.27), channel_id=1, source_target_pairs={{0,4},{2,6},{4,0},{6,2},{8,12},{10,14},{12,8},{14,10},{1,5},{3,7},... | collective-permute-start | bytes 196616 | tf_op jit(solution)/shard_map/ppermute | solution.py:289
  66.0 11.8 %collective-permute-start.14 = (f32[128,128]{1,0:T(8,128)S(1)}, f32[128,128]{1,0:T(8,128)S(1)}, u32[]{:S(2)}, u32[]{:S(2)}) collective-permute-start(f32[128,128]{1,0:T(8,128)S(1)} %get-tuple-element.28), channel_id=1, source_target_pairs={{0,12},{2,14},{4,8},{6,10},{8,4},{10,6},{12,0},{14,2},{1,13},{3,15... | collective-permute-start | bytes 196616 | tf_op jit(solution)/shard_map/ppermute | solution.py:289
  69.8 8.6 %collective-permute-start.13 = (f32[128,128]{1,0:T(8,128)S(1)}, f32[128,128]{1,0:T(8,128)S(1)}, u32[]{:S(2)}, u32[]{:S(2)}) collective-permute-start(f32[128,128]{1,0:T(8,128)S(1)} %get-tuple-element.29), channel_id=1, source_target_pairs={{0,8},{2,10},{4,12},{6,14},{8,0},{10,2},{12,4},{14,6},{1,9},{3,11}... | collective-permute-start | bytes 196616 | tf_op jit(solution)/shard_map/ppermute | solution.py:289
  69.9 8.5 %collective-permute-start.17 = (f32[128,128]{1,0:T(8,128)S(1)}, f32[128,128]{1,0:T(8,128)S(1)}, u32[]{:S(2)}, u32[]{:S(2)}) collective-permute-start(f32[128,128]{1,0:T(8,128)S(1)} %get-tuple-element.30), channel_id=1, source_target_pairs={{0,4},{2,6},{4,0},{6,2},{8,12},{10,14},{12,8},{14,10},{1,5},{3,7},... | collective-permute-start | bytes 196616 | tf_op jit(solution)/shard_map/ppermute | solution.py:289
  73.7 6.3 %collective-permute-start.19 = (f32[128,128]{1,0:T(8,128)S(1)}, f32[128,128]{1,0:T(8,128)S(1)}, u32[]{:S(2)}, u32[]{:S(2)}) collective-permute-start(f32[128,128]{1,0:T(8,128)S(1)} %get-tuple-element.31), channel_id=1, source_target_pairs={{0,12},{2,14},{4,8},{6,10},{8,4},{10,6},{12,0},{14,2},{1,13},{3,15... | collective-permute-start | bytes 196616 | tf_op jit(solution)/shard_map/ppermute | solution.py:289
  77.6 5.2 %collective-permute-start.18 = (f32[128,128]{1,0:T(8,128)S(1)}, f32[128,128]{1,0:T(8,128)S(1)}, u32[]{:S(2)}, u32[]{:S(2)}) collective-permute-start(f32[128,128]{1,0:T(8,128)S(1)} %get-tuple-element.32), channel_id=1, source_target_pairs={{0,8},{2,10},{4,12},{6,14},{8,0},{10,2},{12,4},{14,6},{1,9},{3,11}... | collective-permute-start | bytes 196616 | tf_op jit(solution)/shard_map/ppermute | solution.py:289
  (1 other events, 10.4 us)

commit v3 on v2

--- a/solution.py
+++ b/solution.py
@@ -12,22 +12,25 @@
 SUB = 8
 MIB = 1 << 20
 N_ACC = 4
-N_CHUNK = 4
+UNROLL = 4
+STRIDE = 9
+PARTS = ((1, True), (2, False), (1, False))
 
 
 def accumulate_kernel(
-    bank_size, n_owner, n_chunk,
+    bank_size, n_owner, sizes,
     rep_smem, proj_hbm, img_hbm, tra_hbm, w_smem, pose_hbm, blocks_hbm, tiles_hbm,
     *rest,
 ):
+    n_chunk = len(sizes)
     outs, rest = rest[: 2 * n_chunk], rest[2 * n_chunk :]
     proj, img, tra, pose, blocks, tiles, idx_v, idx_s, square, cross = rest[:10]
-    accs = rest[10 : 10 + N_ACC]
-    proj_sem, small_sem, table_sem, idx_sem, out_sem = rest[10 + N_ACC :]
+    parts, rest = rest[10 : 10 + UNROLL], rest[10 + UNROLL :]
+    accs = rest[:N_ACC]
+    proj_sem, small_sem, table_sem, idx_sem, out_sem = rest[N_ACC:]
     n_pose, n_part = pose.shape
     n_tile, n_table = blocks.shape
     n_row = accs[0].shape[0]
-    group = 4 * SUB * SUB
 
     table_copies = [
         pltpu.make_async_copy(src, dst, table_sem.at[i])
@@ -71,85 +74,78 @@
         for acc in accs:
             acc[rows, :] = zero
 
-    to = lax.broadcasted_iota(jnp.int32, (group, group), 0)
-    fro = lax.broadcasted_iota(jnp.int32, (group, group), 1)
-    swapped = (fro // 64) * 64 + (fro % 8) * 8 + (fro // 8) % 8
-    swap = (to == swapped).astype(jnp.float32).astype(jnp.bfloat16)
-
-    def regroup(left, right):
-        both = jnp.concatenate([left, right], axis=1)
-        return jnp.dot(swap, both, preferred_element_type=jnp.float32)
-
     for copy in small_copies:
         copy.wait()
 
-    @pl.loop(0, tra.shape[0] // group)
+    def stage_in(part, tiles_of, first):
+        for c in range(0, SUB, 2):
+            pair = tiles_of[pl.ds(pl.multiple_of(first + c * SUB, 2 * SUB), 2 * SUB), :].astype(jnp.float32)
+            part[c * STRIDE : c * STRIDE + SUB, :] = pair[:SUB]
+            part[(c + 1) * STRIDE : (c + 1) * STRIDE + SUB, :] = pair[SUB:]
+
+    def row_of(part, k):
+        return part[pl.ds(k, SUB, stride=STRIDE), :]
+
+    @pl.loop(0, tra.shape[0] // (2 * SUB * SUB))
     def _(i):
-        rows = pl.ds(pl.multiple_of(i * group, group), group)
-        both = regroup(tra[rows, :], img[rows, :])
-        t = both[:, :LANES]
-        square[rows, :] = t * t
-        cross[rows, :] = t * both[:, LANES:]
+        for u in range(2):
+            first = (i * 2 + u) * (SUB * SUB)
+            stage_in(parts[2 * u], tra, first)
+            stage_in(parts[2 * u + 1], img, first)
+            for k in range(SUB):
+                rows = pl.ds(pl.multiple_of(first + k * SUB, SUB), SUB)
+                t = row_of(parts[2 * u], k)
+                square[rows, :] = t * t
+                cross[rows, :] = t * row_of(parts[2 * u + 1], k)
 
     idx_copy.wait()
 
-    @pl.loop(0, n_part // 2)
-    def _(q):
-        proj_copy(2 * q).wait()
-        proj_copy(2 * q + 1).wait()
-        weights = [
-            [jnp.full((SUB, LANES), w_smem[k, 2 * q + h], jnp.float32) for k in range(n_pose)]
-            for h in range(2)
-        ]
-
-        @pl.loop(0, n_tile // 4)
+    @pl.loop(0, n_part)
+    def _(p):
+        proj_copy(p).wait()
+        weights = [jnp.full((SUB, LANES), w_smem[k, p], jnp.float32) for k in range(n_pose)]
+
+        @pl.loop(0, n_tile // UNROLL)
         def _(i):
-            rows = pl.ds(pl.multiple_of(i * group, group), group)
-            x = regroup(proj[2 * q, rows, :], proj[2 * q + 1, rows, :])
-            for u in range(4):
-                j = i * 4 + u
-                for h in range(2):
-                    p = 2 * q + h
-                    cell = pl.ds(pl.multiple_of((j * n_part + p) * SUB, SUB), SUB)
-                    tt = square[cell, :]
-                    ti = cross[cell, :]
-
-                    def term(k):
-                        first = (u * n_pose + k) * SUB
-                        value = x[first : first + SUB, h * LANES : (h + 1) * LANES]
-                        return (tt * value - ti) * weights[h][k]
-
-                    for k in range(N_ACC):
-                        acc = accs[k]
-                        at = idx_s[p * n_pose + k, j]
-                        at2 = idx_s[p * n_pose + k + N_ACC, j]
-                        here = pl.ds(pl.multiple_of(at, SUB), SUB)
-                        here2 = pl.ds(pl.multiple_of(at2, SUB), SUB)
-                        same = jnp.where(at == at2, 1.0, 0.0)
-                        one, two = term(k), term(k + N_ACC)
-                        old, old2 = acc[here, :], acc[here2, :]
-                        acc[here, :] = old + one
-                        acc[here2, :] = old2 + (two + same * one)
+            for u, part in enumerate(parts):
+                j = i * UNROLL + u
+                stage_in(part, proj.at[p], j * (SUB * SUB))
+                cell = pl.ds(pl.multiple_of((j * n_part + p) * SUB, SUB), SUB)
+                tt = square[cell, :]
+                ti = cross[cell, :]
+                for k in range(N_ACC):
+                    acc = accs[k]
+                    at = idx_s[p * n_pose + k, j]
+                    at2 = idx_s[p * n_pose + k + N_ACC, j]
+                    here = pl.ds(pl.multiple_of(at, SUB), SUB)
+                    here2 = pl.ds(pl.multiple_of(at2, SUB), SUB)
+                    same = jnp.where(at == at2, 1.0, 0.0)
+                    one = (tt * row_of(part, k) - ti) * weights[k]
+                    two = (tt * row_of(part, k + N_ACC) - ti) * weights[k + N_ACC]
+                    old, old2 = acc[here, :], acc[here2, :]
+                    acc[here, :] = old + one
+                    acc[here2, :] = old2 + (two + same * one)
 
     rep = rep_smem[0]
-    piece = n_row // (n_owner * 2 * n_chunk)
     step = 4 * SUB
+    half_rows = n_row // (n_owner * 2)
+    begins = [sum(sizes[:c]) for c in range(n_chunk)]
 
     for c in range(n_chunk):
         for side in range(2):
-            out = outs[2 * c + side]
             half = rep if side else 1 - rep
 
             def out_copy(o, first):
                 return pltpu.make_async_copy(
-                    accs[0].at[pl.ds(first, piece), :], out.at[o], out_sem.at[(2 * c + side) * n_owner + o]
+                    accs[0].at[pl.ds(first, sizes[c]), :], outs[2 * c + side].at[o],
+                    out_sem.at[(2 * c + side) * n_owner + o],
                 )
 
             @pl.loop(0, n_owner)
             def _(o):
-                first = pl.multiple_of(((o * 2 + half) * n_chunk + c) * piece, piece)
-
-                @pl.loop(0, piece // step)
+                first = pl.multiple_of((o * 2 + half) * half_rows + begins[c], step)
+
+                @pl.loop(0, sizes[c] // step)
                 def _(h):
                     rows = pl.ds(pl.multiple_of(first + h * step, step), step)
                     total = accs[0][rows, :]
@@ -165,8 +161,7 @@
             @pl.loop(0, n_owner)
             def _(o):
                 pltpu.make_async_copy(
-                    accs[0].at[pl.ds(0, piece), :],
-                    outs[2 * c + side].at[o],
+                    accs[0].at[pl.ds(0, sizes[c]), :], outs[2 * c + side].at[o],
                     out_sem.at[(2 * c + side) * n_owner + o],
                 ).wait()
 
@@ -180,13 +175,14 @@
 
 def accumulate(
     projections, images, transfer, pose_weights, pose_of, pose_blocks, pose_tiles,
-    bank_size, n_owner, n_chunk, rep,
+    bank_size, n_owner, rep,
 ):
     n_part, n_pose, n_tile, n_cell = projections.shape
     assert n_cell == SUB * LANES and n_pose == SUB and n_pose == 2 * N_ACC
     n_row = n_owner * NB_DEV * bank_size * SUB
     n_idx = n_part * n_pose
-    piece = n_row // (n_owner * 2 * n_chunk)
+    sizes = [size * bank_size * SUB for size, _ in PARTS]
+    n_chunk = len(sizes)
     projections = tiles_in_order(jnp.transpose(projections, (0, 2, 1, 3)))
     projections = projections.reshape(n_part, n_tile * n_pose * SUB, LANES)
     images = tiles_in_order(jnp.transpose(images, (1, 0, 2))).reshape(n_tile * n_part * SUB, LANES)
@@ -194,8 +190,10 @@
     anywhere = pl.BlockSpec(memory_space=pl.ANY)
     smem = pl.BlockSpec(memory_space=pltpu.SMEM)
     return pl.pallas_call(
-        functools.partial(accumulate_kernel, bank_size, n_owner, n_chunk),
-        out_shape=[jax.ShapeDtypeStruct((n_owner, piece, LANES), jnp.float32)] * (2 * n_chunk),
+        functools.partial(accumulate_kernel, bank_size, n_owner, sizes),
+        out_shape=[
+            jax.ShapeDtypeStruct((n_owner, size, LANES), jnp.float32) for size in sizes for _ in range(2)
+        ],
         in_specs=[smem] + [anywhere] * 3 + [smem] + [anywhere] * 3,
         out_specs=[anywhere] * (2 * n_chunk),
         scratch_shapes=[
@@ -210,6 +208,7 @@
             pltpu.VMEM(transfer.shape, jnp.float32),
             pltpu.VMEM(transfer.shape, jnp.float32),
         ]
+        + [pltpu.VMEM((SUB * STRIDE, LANES), jnp.float32)] * UNROLL
         + [pltpu.VMEM((n_row, LANES), jnp.float32)] * N_ACC
         + [
             pltpu.SemaphoreType.DMA((n_part,)),
@@ -266,7 +265,7 @@
     rep = lax.axis_index("rep").astype(jnp.int32).reshape(1)
     outs = accumulate(
         projections, images, transfer, pose_weights, pose_of, pose_blocks, pose_tiles,
-        bank_size, n_blk, N_CHUNK, rep,
+        bank_size, n_blk, rep,
     )
     swap_rep = [(0, 1), (1, 0)]
     swap_near = [(i, i ^ 1) for i in range(n_blk)]
@@ -274,20 +273,30 @@
     def pick(array, index, axis):
         return lax.dynamic_index_in_dim(array, index, axis, keepdims=False)
 
+    def sum_near(array, got, axis):
+        away = pick(array, 1 - near, axis)
+        stay = pick(array, near, axis)
+        if got is not None:
+            away, stay = away + pick(got, 1 - near, axis), stay + pick(got, near, axis)
+        return stay + lax.ppermute(away, "blk", swap_near)
+
+    def sum_far(array):
+        total = pick(array, far, 0)
+        for d in range(1, n_far):
+            pairs = [(i, i ^ (2 * d)) for i in range(n_blk)]
+            total = total + lax.ppermute(pick(array, far ^ d, 0), "blk", pairs)
+        return total
+
     owned = []
-    for c in range(N_CHUNK):
+    for c, (_, far_first) in enumerate(PARTS):
         sent, kept = outs[2 * c], outs[2 * c + 1]
         got = lax.ppermute(sent, "rep", swap_rep)
         shape = (n_far, 2) + sent.shape[1:]
         got, kept = got.reshape(shape), kept.reshape(shape)
-        away = pick(kept, 1 - near, 1) + pick(got, 1 - near, 1)
-        stay = pick(kept, near, 1) + pick(got, near, 1)
-        stay = stay + lax.ppermute(away, "blk", swap_near)
-        total = pick(stay, far, 0)
-        for d in range(1, n_far):
-            pairs = [(i, i ^ (2 * d)) for i in range(n_blk)]
-            total = total + lax.ppermute(pick(stay, far ^ d, 0), "blk", pairs)
-        owned.append(total)
+        if far_first:
+            owned.append(sum_near(sum_far(kept + got), None, 0))
+        else:
+            owned.append(sum_far(sum_near(kept, got, 1)))
     owned = jnp.concatenate(owned, axis=0)
     owned = lax.all_gather(owned, "rep", axis=0, tiled=True)
     owned = owned.reshape(NB_DEV * bank_size, SUB, LANES)

time: 87.7 us -> 80.3 us (0.916)
  starting transfers between devices: 29.1 us -> 17.4 us
  waiting for transfers between devices: 18.4 us -> 29.6 us
  Pallas kernels: 34.1 us -> 26.5 us
    ppermute x16 -> x12, starting transfers between devices: 28 us -> 16.4 us  [the longest x9 12.6 us: sum_far(): total = total + lax.ppermute(pick(array, far ^ d, 0), 'blk', pairs)]
    ppermute x16 -> x12, waiting for transfers between devices: 17.3 us -> 28.4 us  [the longest x9 19.8 us: sum_far(): total = total + lax.ppermute(pick(array, far ^ d, 0), 'blk', pairs)]
    pallas_call x1, Pallas kernels: 31.7 us -> 24.1 us  [accumulate(): pl.pallas_call(functools.partial(accumulate_kernel, bank_size, n_owner, s...]
    add x12 -> x9, other arithmetic: 3.31 us -> 3.48 us  [the longest x3 1.19 us: sum_near(): return stay + lax.ppermute(away, 'blk', swap_near)]
  transfers between devices with their start and end apart: 20 -> 15, of which waited for: 9 -> 8; matrix products, arithmetic and copies ran while one was open for 4% -> 5% of each run, Pallas kernels for 0% -> 0%
where the time goes in v3:
time: 80.3 us; the launch traced here: 80 us
  waiting for transfers between devices  29.6 us (37%)
  Pallas kernels  26.5 us (33%)
  starting transfers between devices  17.4 us (22%)
  other arithmetic  3.5 us (4%)
  blocking collectives  2.18 us (3%)
    pallas_call x1, Pallas kernels, accumulate(): pl.pallas_call(functools.partial(accumulate_kernel, bank_size, n_owner, s...  24.1 us
    ppermute x9, waiting for transfers between devices, sum_far(): total = total + lax.ppermute(pick(array, far ^ d, 0), 'blk', pairs)  19.8 us
    ppermute x9, starting transfers between devices, sum_far(): total = total + lax.ppermute(pick(array, far ^ d, 0), 'blk', pairs)  12.6 us
    ppermute x3, waiting for transfers between devices, sum_near(): return stay + lax.ppermute(away, 'blk', swap_near)  8.56 us
    ppermute x3, starting transfers between devices, sum_near(): return stay + lax.ppermute(away, 'blk', swap_near)  3.74 us
    pallas_call x1, Pallas kernels, apply_bank(): pl.pallas_call(bank_kernel, out_shape=jax.ShapeDtypeStruct((n_blk, n_z, n...  2.36 us
    all_gather x1, blocking collectives, body(): owned = lax.all_gather(owned, 'rep', axis=0, tiled=True)  2.18 us
  transfers between devices with their start and end apart: 15, of which 8 were waited for; matrix products, arithmetic and copies ran while one was open for 5% of the time, Pallas kernels for 0%

profile of v3, /device:TPU:0, one launch (start us, length us, event | category | flops | bytes accessed | tf_op | source)
XLA Modules:
  0.0 80.0 jit_solution(2868933249732147835)
XLA Ops:
  0.0 24.1 %accumulate.1 = (f32[8,128,128]{2,1,0:T(8,128)}, f32[8,128,128]{2,1,0:T(8,128)}, f32[8,256,128]{2,1,0:T(8,128)}, f32[8,256,128]{2,1,0:T(8,128)}, f32[8,128,128]{2,1,0:T(8,128)}, /*index=5*/f32[8,128,128]{2,1,0:T(8,128)}) custom-call(s32[1]{0:T(128)} %bitcast.rep_smem, bf16[16,2304,128]{2,1,0:T(8,128)(2,1)} %bitcast.101, bf16[4608,128]{1,0:T(8,128)(2,1)} %bitcast.104, ...), custom_call_target="tpu_custom_call" | custom-call | tf_op jit(solution)/shard_map/accumulate/pallas_call | solution.py:192
  25.1 1.2 %collective-permute-done = f32[8,128,128]{2,1,0:T(8,128)S(1)} collective-permute-done((f32[8,128,128]{2,1,0:T(8,128)}, f32[8,128,128]{2,1,0:T(8,128)S(1)}, u32[]{:S(2)}, u32[]{:S(2)}) %collective-permute-start) | collective-permute-done | bytes 524320 | tf_op jit(solution)/shard_map/ppermute | solution.py:293
  26.4 1.1 %add.112 = f32[8,128,128]{2,1,0:T(8,128)S(1)} add(f32[8,128,128]{2,1,0:T(8,128)} %get-tuple-element.11, f32[8,128,128]{2,1,0:T(8,128)S(1)} %collective-permute-done) | non-fusion elementwise | flops 131072 | bytes 1572864 | tf_op jit(solution)/shard_map/add | solution.py:297
  27.5 0.7 dynamic-slice_bitcast_fusion.5
  28.2 2.9 %collective-permute-start.1 = (f32[2,128,128]{2,1,0:T(8,128)}, f32[2,128,128]{2,1,0:T(8,128)S(1)}, u32[]{:S(2)}, u32[]{:S(2)}) collective-permute-start(f32[2,128,128]{2,1,0:T(8,128)} %get-tuple-element.17), channel_id=1, source_target_pairs={{0,4},{2,6},{4,0},{6,2},{8,12},{10,14},{12,8},{14,10},{1,5},{3,7},... | collective-permute-start | bytes 393224 | tf_op jit(solution)/shard_map/ppermute | solution.py:287
  31.1 2.5 %collective-permute-start.3 = (f32[2,128,128]{2,1,0:T(8,128)S(1)}, f32[2,128,128]{2,1,0:T(8,128)S(1)}, u32[]{:S(2)}, u32[]{:S(2)}) collective-permute-start(f32[2,128,128]{2,1,0:T(8,128)S(1)} %get-tuple-element.18), channel_id=1, source_target_pairs={{0,12},{2,14},{4,8},{6,10},{8,4},{10,6},{12,0},{14,2},{1,13},{3,15... | collective-permute-start | bytes 393224 | tf_op jit(solution)/shard_map/ppermute | solution.py:287
  33.7 1.1 %add_bitcast_fusion.1 = f32[4,128,128]{2,1,0:T(8,128)S(1)} fusion(f32[4,2,128,128]{3,2,1,0:T(8,128)} %bitcast.33, s32[]{:T(128)S(6)} %select_n.58, f32[4,2,128,128]{3,2,1,0:T(8,128)} %bitcast.110), kind=kLoop, calls=%fused_computation.8 | loop fusion | flops 65536 | bytes 786436 | tf_op jit(solution)/shard_map/add | solution.py:280
  34.8 1.6 %collective-permute-start.11 = (f32[4,128,128]{2,1,0:T(8,128)S(1)}, f32[4,128,128]{2,1,0:T(8,128)S(1)}, u32[]{:S(2)}, u32[]{:S(2)}) collective-permute-start(f32[4,128,128]{2,1,0:T(8,128)S(1)} %add_bitcast_fusion.1), channel_id=1, source_target_pairs={{0,2},{2,0},{4,6},{6,4},{8,10},{10,8},{12,14},{14,12},{1,3},{3,1},... | collective-permute-start | bytes 786440 | tf_op jit(solution)/shard_map/ppermute | solution.py:281
  36.4 4.7 %collective-permute-done.3 = f32[2,128,128]{2,1,0:T(8,128)S(1)} collective-permute-done((f32[2,128,128]{2,1,0:T(8,128)S(1)}, f32[2,128,128]{2,1,0:T(8,128)S(1)}, u32[]{:S(2)}, u32[]{:S(2)}) %collective-permute-start.3) | collective-permute-done | bytes 131104 | tf_op jit(solution)/shard_map/ppermute | solution.py:287
  41.0 4.6 %collective-permute-done.2 = f32[2,128,128]{2,1,0:T(8,128)S(1)} collective-permute-done((f32[2,128,128]{2,1,0:T(8,128)S(1)}, f32[2,128,128]{2,1,0:T(8,128)S(1)}, u32[]{:S(2)}, u32[]{:S(2)}) %collective-permute-start.2) | collective-permute-done | bytes 131104 | tf_op jit(solution)/shard_map/ppermute | solution.py:287
  45.7 1.6 %collective-permute-start.4 = (f32[128,128]{1,0:T(8,128)S(1)}, f32[128,128]{1,0:T(8,128)S(1)}, u32[]{:S(2)}, u32[]{:S(2)}) collective-permute-start(f32[128,128]{1,0:T(8,128)S(1)} %dynamic-slice_bitcast_fusion.9), channel_id=1, source_target_pairs={{0,2},{2,0},{4,6},{6,4},{8,10},{10,8},{12,14},{14,12},{1,3},{3,1},... | collective-permute-start | bytes 196616 | tf_op jit(solution)/shard_map/ppermute | solution.py:281
  47.4 0.6 collective-permute-start.6
  47.9 2.8 %collective-permute-done.4 = f32[128,128]{1,0:T(8,128)S(1)} collective-permute-done((f32[128,128]{1,0:T(8,128)S(1)}, f32[128,128]{1,0:T(8,128)S(1)}, u32[]{:S(2)}, u32[]{:S(2)}) %collective-permute-start.4) | collective-permute-done | bytes 65568 | tf_op jit(solution)/shard_map/ppermute | solution.py:281
  50.8 1.1 %fusion.3 = f32[4,128,128]{2,1,0:T(8,128)S(1)} fusion(f32[4,128,128]{2,1,0:T(8,128)S(1)} %collective-permute-done.11, f32[4,2,128,128]{3,2,1,0:T(8,128)} %bitcast.33, s32[]{:T(128)S(6)} %select_n.57, f32[4,2,128,128]{3,2,1,0:T(8,128)} %bitcast.111), kind=kLoop, calls=%fused_computation.7 | loop fusion | flops 131072 | bytes 1048580 | tf_op jit(solution)/shard_map/add | solution.py:281
  52.0 2.6 %collective-permute-start.14 = (f32[128,128]{1,0:T(8,128)S(1)}, f32[128,128]{1,0:T(8,128)S(1)}, u32[]{:S(2)}, u32[]{:S(2)}) collective-permute-start(f32[128,128]{1,0:T(8,128)S(1)} %get-tuple-element.24), channel_id=1, source_target_pairs={{0,12},{2,14},{4,8},{6,10},{8,4},{10,6},{12,0},{14,2},{1,13},{3,15... | collective-permute-start | bytes 196616 | tf_op jit(solution)/shard_map/ppermute | solution.py:287
  54.6 0.8 %collective-permute-start.13 = (f32[128,128]{1,0:T(8,128)S(1)}, f32[128,128]{1,0:T(8,128)S(1)}, u32[]{:S(2)}, u32[]{:S(2)}) collective-permute-start(f32[128,128]{1,0:T(8,128)S(1)} %get-tuple-element.25), channel_id=1, source_target_pairs={{0,8},{2,10},{4,12},{6,14},{8,0},{10,2},{12,4},{14,6},{1,9},{3,11}... | collective-permute-start | bytes 196616 | tf_op jit(solution)/shard_map/ppermute | solution.py:287
  55.5 5.7 %collective-permute-done.6 = f32[4,256,128]{2,1,0:T(8,128)S(1)} collective-permute-done((f32[4,256,128]{2,1,0:T(8,128)S(1)}, f32[4,256,128]{2,1,0:T(8,128)S(1)}, u32[]{:S(2)}, u32[]{:S(2)}) %collective-permute-start.6) | collective-permute-done | bytes 524320 | tf_op jit(solution)/shard_map/ppermute | solution.py:281
  61.4 2.3 %collective-permute-start.9 = (f32[256,128]{1,0:T(8,128)S(1)}, f32[256,128]{1,0:T(8,128)S(1)}, u32[]{:S(2)}, u32[]{:S(2)}) collective-permute-start(f32[256,128]{1,0:T(8,128)S(1)} %get-tuple-element.21), channel_id=1, source_target_pairs={{0,12},{2,14},{4,8},{6,10},{8,4},{10,6},{12,0},{14,2},{1,13},{3,15... | collective-permute-start | bytes 393224 | tf_op jit(solution)/shard_map/ppermute | solution.py:287
  63.7 1.2 %collective-permute-start.8 = (f32[256,128]{1,0:T(8,128)S(1)}, f32[256,128]{1,0:T(8,128)S(1)}, u32[]{:S(2)}, u32[]{:S(2)}) collective-permute-start(f32[256,128]{1,0:T(8,128)S(1)} %get-tuple-element.22), channel_id=1, source_target_pairs={{0,8},{2,10},{4,12},{6,14},{8,0},{10,2},{12,4},{14,6},{1,9},{3,11}... | collective-permute-start | bytes 393224 | tf_op jit(solution)/shard_map/ppermute | solution.py:287
  64.9 3.2 %collective-permute-done.7 = f32[256,128]{1,0:T(8,128)S(1)} collective-permute-done((f32[256,128]{1,0:T(8,128)S(1)}, f32[256,128]{1,0:T(8,128)S(1)}, u32[]{:S(2)}, u32[]{:S(2)}) %collective-permute-start.7) | collective-permute-done | bytes 131104 | tf_op jit(solution)/shard_map/ppermute | solution.py:287
  68.2 2.4 %collective-permute-done.9 = f32[256,128]{1,0:T(8,128)S(1)} collective-permute-done((f32[256,128]{1,0:T(8,128)S(1)}, f32[256,128]{1,0:T(8,128)S(1)}, u32[]{:S(2)}, u32[]{:S(2)}) %collective-permute-start.9) | collective-permute-done | bytes 131104 | tf_op jit(solution)/shard_map/ppermute | solution.py:287
  70.5 4.9 %collective-permute-done.8 = f32[256,128]{1,0:T(8,128)S(1)} collective-permute-done((f32[256,128]{1,0:T(8,128)S(1)}, f32[256,128]{1,0:T(8,128)S(1)}, u32[]{:S(2)}, u32[]{:S(2)}) %collective-permute-start.8) | collective-permute-done | bytes 131104 | tf_op jit(solution)/shard_map/ppermute | solution.py:287
  75.5 2.2 %all_gather.3 = f32[1024,128]{1,0:T(8,128)S(1)} all-gather(f32[512,128]{1,0:T(8,128)S(1)} %pad_maximum_fusion), channel_id=1, replica_groups=mesh['groups'=2,'blk'=8,'rep'=2] {'rep'}, dimensions={0}, use_global_device_ids=true | all-gather | bytes 786432 | tf_op jit(solution)/shard_map/all_gather | solution.py:301
  77.7 2.4 %apply_bank.1 = f32[8,32,1024]{2,1,0:T(8,128)} custom-call(f32[128,8,128]{2,1,0:T(8,128)S(1)} %bitcast.100, f32[16,32,1024]{2,1,0:T(8,128)S(1)} %copy-done), custom_call_target="tpu_custom_call" | custom-call | tf_op jit(solution)/shard_map/apply_bank/pallas_call | solution.py:247
  (27 shorter events, 1.6 us)
Async XLA Ops:
  24.1 23.2 %copy-start.1 = (f32[8,256,128]{2,1,0:T(8,128)S(1)}, f32[8,256,128]{2,1,0:T(8,128)}, u32[]{:S(2)}) copy-start(f32[8,256,128]{2,1,0:T(8,128)} %get-tuple-element.13) | copy-start | bytes 3145732
  24.1 2.3 %collective-permute-start = (f32[8,128,128]{2,1,0:T(8,128)}, f32[8,128,128]{2,1,0:T(8,128)S(1)}, u32[]{:S(2)}, u32[]{:S(2)}) collective-permute-start(f32[8,128,128]{2,1,0:T(8,128)} %get-tuple-element.12), channel_id=1, source_target_pairs={{0,1},{1,0},{2,3},{3,2},{4,5},{5,4},{6,7},{7,6},{8,9},{9,8},{10,11... | collective-permute-start | bytes 1572872 | tf_op jit(solution)/shard_map/ppermute | solution.py:293
  24.6 22.7 %collective-permute-start.5 = (f32[8,256,128]{2,1,0:T(8,128)}, f32[8,256,128]{2,1,0:T(8,128)S(1)}, u32[]{:S(2)}, u32[]{:S(2)}) collective-permute-start(f32[8,256,128]{2,1,0:T(8,128)} %get-tuple-element.14), channel_id=1, source_target_pairs={{0,1},{1,0},{2,3},{3,2},{4,5},{5,4},{6,7},{7,6},{8,9},{9,8},{10,11... | collective-permute-start | bytes 3145736 | tf_op jit(solution)/shard_map/ppermute | solution.py:293
  24.7 9.0 %collective-permute-start.10 = (f32[8,128,128]{2,1,0:T(8,128)}, f32[8,128,128]{2,1,0:T(8,128)}, u32[]{:S(2)}, u32[]{:S(2)}) collective-permute-start(f32[8,128,128]{2,1,0:T(8,128)} %get-tuple-element.16), channel_id=1, source_target_pairs={{0,1},{1,0},{2,3},{3,2},{4,5},{5,4},{6,7},{7,6},{8,9},{9,8},{10,11... | collective-permute-start | bytes 1572872 | tf_op jit(solution)/shard_map/ppermute | solution.py:293
  28.2 8.2 %collective-permute-start.1 = (f32[2,128,128]{2,1,0:T(8,128)}, f32[2,128,128]{2,1,0:T(8,128)S(1)}, u32[]{:S(2)}, u32[]{:S(2)}) collective-permute-start(f32[2,128,128]{2,1,0:T(8,128)} %get-tuple-element.17), channel_id=1, source_target_pairs={{0,4},{2,6},{4,0},{6,2},{8,12},{10,14},{12,8},{14,10},{1,5},{3,7},... | collective-permute-start | bytes 393224 | tf_op jit(solution)/shard_map/ppermute | solution.py:287
  31.1 9.9 %collective-permute-start.3 = (f32[2,128,128]{2,1,0:T(8,128)S(1)}, f32[2,128,128]{2,1,0:T(8,128)S(1)}, u32[]{:S(2)}, u32[]{:S(2)}) collective-permute-start(f32[2,128,128]{2,1,0:T(8,128)S(1)} %get-tuple-element.18), channel_id=1, source_target_pairs={{0,12},{2,14},{4,8},{6,10},{8,4},{10,6},{12,0},{14,2},{1,13},{3,15... | collective-permute-start | bytes 393224 | tf_op jit(solution)/shard_map/ppermute | solution.py:287
  33.6 12.1 %collective-permute-start.2 = (f32[2,128,128]{2,1,0:T(8,128)S(1)}, f32[2,128,128]{2,1,0:T(8,128)S(1)}, u32[]{:S(2)}, u32[]{:S(2)}) collective-permute-start(f32[2,128,128]{2,1,0:T(8,128)S(1)} %get-tuple-element.19), channel_id=1, source_target_pairs={{0,8},{2,10},{4,12},{6,14},{8,0},{10,2},{12,4},{14,6},{1,9},{3,11}... | collective-permute-start | bytes 393224 | tf_op jit(solution)/shard_map/ppermute | solution.py:287
  34.8 16.0 %collective-permute-start.11 = (f32[4,128,128]{2,1,0:T(8,128)S(1)}, f32[4,128,128]{2,1,0:T(8,128)S(1)}, u32[]{:S(2)}, u32[]{:S(2)}) collective-permute-start(f32[4,128,128]{2,1,0:T(8,128)S(1)} %add_bitcast_fusion.1), channel_id=1, source_target_pairs={{0,2},{2,0},{4,6},{6,4},{8,10},{10,8},{12,14},{14,12},{1,3},{3,1},... | collective-permute-start | bytes 786440 | tf_op jit(solution)/shard_map/ppermute | solution.py:281
  45.7 5.0 %collective-permute-start.4 = (f32[128,128]{1,0:T(8,128)S(1)}, f32[128,128]{1,0:T(8,128)S(1)}, u32[]{:S(2)}, u32[]{:S(2)}) collective-permute-start(f32[128,128]{1,0:T(8,128)S(1)} %dynamic-slice_bitcast_fusion.9), channel_id=1, source_target_pairs={{0,2},{2,0},{4,6},{6,4},{8,10},{10,8},{12,14},{14,12},{1,3},{3,1},... | collective-permute-start | bytes 196616 | tf_op jit(solution)/shard_map/ppermute | solution.py:281
  47.4 13.8 %collective-permute-start.6 = (f32[4,256,128]{2,1,0:T(8,128)S(1)}, f32[4,256,128]{2,1,0:T(8,128)S(1)}, u32[]{:S(2)}, u32[]{:S(2)}) collective-permute-start(f32[4,256,128]{2,1,0:T(8,128)S(1)} %add_bitcast_fusion), channel_id=1, source_target_pairs={{0,2},{2,0},{4,6},{6,4},{8,10},{10,8},{12,14},{14,12},{1,3},{3,1},... | collective-permute-start | bytes 1572872 | tf_op jit(solution)/shard_map/ppermute | solution.py:281
  51.9 11.8 %collective-permute-start.12 = (f32[128,128]{1,0:T(8,128)S(1)}, f32[128,128]{1,0:T(8,128)S(1)}, u32[]{:S(2)}, u32[]{:S(2)}) collective-permute-start(f32[128,128]{1,0:T(8,128)S(1)} %get-tuple-element.23), channel_id=1, source_target_pairs={{0,4},{2,6},{4,0},{6,2},{8,12},{10,14},{12,8},{14,10},{1,5},{3,7},... | collective-permute-start | bytes 196616 | tf_op jit(solution)/shard_map/ppermute | solution.py:287
  52.0 12.9 %collective-permute-start.14 = (f32[128,128]{1,0:T(8,128)S(1)}, f32[128,128]{1,0:T(8,128)S(1)}, u32[]{:S(2)}, u32[]{:S(2)}) collective-permute-start(f32[128,128]{1,0:T(8,128)S(1)} %get-tuple-element.24), channel_id=1, source_target_pairs={{0,12},{2,14},{4,8},{6,10},{8,4},{10,6},{12,0},{14,2},{1,13},{3,15... | collective-permute-start | bytes 196616 | tf_op jit(solution)/shard_map/ppermute | solution.py:287
  54.6 23.1 %copy-start = (f32[16,32,1024]{2,1,0:T(8,128)S(1)}, f32[16,32,1024]{2,1,0:T(8,128)}, u32[]{:S(2)}) copy-start(f32[16,32,1024]{2,1,0:T(8,128)} %bank.1) | copy-start | bytes 6291460
  54.6 10.3 %collective-permute-start.13 = (f32[128,128]{1,0:T(8,128)S(1)}, f32[128,128]{1,0:T(8,128)S(1)}, u32[]{:S(2)}, u32[]{:S(2)}) collective-permute-start(f32[128,128]{1,0:T(8,128)S(1)} %get-tuple-element.25), channel_id=1, source_target_pairs={{0,8},{2,10},{4,12},{6,14},{8,0},{10,2},{12,4},{14,6},{1,9},{3,11}... | collective-permute-start | bytes 196616 | tf_op jit(solution)/shard_map/ppermute | solution.py:287
  61.3 6.8 %collective-permute-start.7 = (f32[256,128]{1,0:T(8,128)S(1)}, f32[256,128]{1,0:T(8,128)S(1)}, u32[]{:S(2)}, u32[]{:S(2)}) collective-permute-start(f32[256,128]{1,0:T(8,128)S(1)} %get-tuple-element.20), channel_id=1, source_target_pairs={{0,4},{2,6},{4,0},{6,2},{8,12},{10,14},{12,8},{14,10},{1,5},{3,7},... | collective-permute-start | bytes 393224 | tf_op jit(solution)/shard_map/ppermute | solution.py:287
  61.4 9.1 %collective-permute-start.9 = (f32[256,128]{1,0:T(8,128)S(1)}, f32[256,128]{1,0:T(8,128)S(1)}, u32[]{:S(2)}, u32[]{:S(2)}) collective-permute-start(f32[256,128]{1,0:T(8,128)S(1)} %get-tuple-element.21), channel_id=1, source_target_pairs={{0,12},{2,14},{4,8},{6,10},{8,4},{10,6},{12,0},{14,2},{1,13},{3,15... | collective-permute-start | bytes 393224 | tf_op jit(solution)/shard_map/ppermute | solution.py:287
  63.7 11.7 %collective-permute-start.8 = (f32[256,128]{1,0:T(8,128)S(1)}, f32[256,128]{1,0:T(8,128)S(1)}, u32[]{:S(2)}, u32[]{:S(2)}) collective-permute-start(f32[256,128]{1,0:T(8,128)S(1)} %get-tuple-element.22), channel_id=1, source_target_pairs={{0,8},{2,10},{4,12},{6,14},{8,0},{10,2},{12,4},{14,6},{1,9},{3,11}... | collective-permute-start | bytes 393224 | tf_op jit(solution)/shard_map/ppermute | solution.py:287

commit v4 on v1

v4 whole, which is shorter than its diff:
```python
import functools

import jax
import jax.numpy as jnp
from jax import lax
from jax.experimental import pallas as pl
from jax.experimental.pallas import tpu as pltpu
from jax.sharding import PartitionSpec as P

NB_DEV = 8
LANES = 128
SUB = 8
MIB = 1 << 20
FAR_FIRST = 21


def accumulate_kernel(
    bank_size, n_owner, n_acc,
    place, proj_hbm, img_hbm, tra_hbm, w_hbm, pose_hbm, blocks_hbm, tiles_hbm,
    sent_away, kept_away, sent_b, kept_b, sent_stay, kept_stay,
    proj, img, tra, w_smem, pose, blocks, tiles, idx_v, idx_s, square, cross,
    *rest,
):
    accs = rest[:n_acc]
    proj_sem, small_sem, table_sem, idx_sem = rest[n_acc:]
    n_pose, n_part = pose.shape
    n_tile, n_table = blocks.shape
    n_row = accs[0].shape[0]
    tile_rows = SUB * SUB
    part_rows = n_tile * tile_rows

    table_copies = [
        pltpu.make_async_copy(src, dst, table_sem.at[i])
        for i, (src, dst) in enumerate(((pose_hbm, pose), (blocks_hbm, blocks), (tiles_hbm, tiles)))
    ]
    small_copies = [
        pltpu.make_async_copy(img_hbm, img, small_sem.at[0]),
        pltpu.make_async_copy(tra_hbm, tra, small_sem.at[1]),
        pltpu.make_async_copy(w_hbm, w_smem, small_sem.at[2]),
    ]
    for copy in table_copies + small_copies:
        copy.start()

    def proj_copy(p):
        rows = pl.ds(pl.multiple_of(p * part_rows, part_rows), part_rows)
        return pltpu.make_async_copy(proj_hbm.at[rows, :], proj.at[rows, :], proj_sem.at[p])

    for p in range(n_part):
        proj_copy(p).start()

    for copy in table_copies:
        copy.wait()
    lane = lax.broadcasted_iota(jnp.int32, (n_pose, n_table), 1)
    chosen = jnp.concatenate(
        [(pose[:, p : p + 1] == lane).astype(jnp.float32) for p in range(n_part)], axis=0
    ).astype(jnp.bfloat16)

    def look_up(table):
        return lax.dot_general(
            chosen, table[...].astype(jnp.float32).astype(jnp.bfloat16),
            (((1,), (1,)), ((), ())), preferred_element_type=jnp.float32,
        )

    idx_v[:, :n_tile] = ((look_up(blocks) * bank_size + look_up(tiles)) * SUB).astype(jnp.int32)
    idx_copy = pltpu.make_async_copy(idx_v, idx_s, idx_sem)
    idx_copy.start()

    zero = jnp.zeros((8 * SUB, LANES), jnp.float32)

    @pl.loop(0, n_row // (8 * SUB))
    def _(i):
        rows = pl.ds(pl.multiple_of(i * (8 * SUB), 8 * SUB), 8 * SUB)
        for acc in accs:
            acc[rows, :] = zero

    def regroup(ref, first):
        block = ref[pl.ds(pl.multiple_of(first, tile_rows), tile_rows), :].astype(jnp.float32)
        return jnp.swapaxes(block.reshape(SUB, SUB, LANES), 0, 1)

    for copy in small_copies:
        copy.wait()

    @pl.loop(0, n_tile)
    def _(j):
        for h in range(n_part // SUB):
            first = (j * (n_part // SUB) + h) * tile_rows
            t, i = regroup(tra, first), regroup(img, first)
            for k in range(SUB):
                rows = pl.ds(pl.multiple_of(((h * SUB + k) * n_tile + j) * SUB, SUB), SUB)
                square[rows, :] = t[k] * t[k]
                cross[rows, :] = t[k] * i[k]

    def terms(unit):
        x = regroup(proj, unit * tile_rows)
        cell = pl.ds(pl.multiple_of(unit * SUB, SUB), SUB)
        tt, ti = square[cell, :], cross[cell, :]
        return [tt * x[k] - ti for k in range(n_pose)]

    def add_rows(p, j, values, weights):
        at = [idx_s[p * n_pose + k, j] for k in range(n_pose)]
        rows = [pl.ds(pl.multiple_of(at[k], SUB), SUB) for k in range(n_pose)]
        values = [values[k] * weights[k] for k in range(n_pose)]
        old = [accs[k % n_acc][rows[k], :] for k in range(n_pose)]
        new = []
        for k in range(n_pose):
            total = old[k] + values[k]
            for m in range(k % n_acc, k, n_acc):
                total += jnp.where(at[m] == at[k], 1.0, 0.0) * values[m]
            new.append(total)
        for k in range(n_pose):
            accs[k % n_acc][rows[k], :] = new[k]

    proj_copy(0).wait()
    idx_copy.wait()
    n_unit = n_part * n_tile

    @pl.loop(0, n_part, init_carry=tuple(terms(0) + terms(1)))
    def _(p, ready):
        @pl.when(p + 1 < n_part)
        def _():
            proj_copy(p + 1).wait()

        weights = [jnp.full((SUB, LANES), w_smem[k, p], jnp.float32) for k in range(n_pose)]

        @pl.loop(0, n_tile, step=2, init_carry=ready)
        def done(j, now):
            unit = jnp.minimum(p * n_tile + j + 2, n_unit - 2)
            later = terms(unit) + terms(unit + 1)
            add_rows(p, j, now[:n_pose], weights)
            add_rows(p, j + 1, now[n_pose:], weights)
            return tuple(later)

        return done

    rep, near = place[0], place[1]
    half_rows = n_row // (n_owner * 2)
    b_rows = sent_b.shape[1]

    def finish(out, o, owner, half, begin):
        size = out.shape[1]
        step = 8 * SUB
        first = (owner * 2 + half) * half_rows + begin

        def sum_rows(offset, count):
            rows = pl.ds(pl.multiple_of(first + offset, SUB), count)
            total = accs[0][rows, :]
            for acc in accs[1:]:
                total += acc[rows, :]
            out[o, pl.ds(pl.multiple_of(offset, SUB), count), :] = total

        @pl.loop(0, size // step)
        def _(i):
            sum_rows(i * step, step)

        if size % step:
            sum_rows(size - size % step, size % step)

    for sent, kept, side in ((sent_away, kept_away, 1 - near), (sent_stay, kept_stay, near)):

        @pl.loop(0, n_owner // 2)
        def _(o):
            finish(sent, o, o * 2 + side, 1 - rep, b_rows)
            finish(kept, o, o * 2 + side, rep, b_rows)

    @pl.loop(0, n_owner)
    def _(o):
        finish(sent_b, o, o, 1 - rep, 0)
        finish(kept_b, o, o, rep, 0)


def tiles_in_order(array):
    lead = array.shape[:-2]
    rows, cells = array.shape[-2:]
    array = array.reshape(lead + (rows // SUB, SUB, cells // LANES, LANES))
    return jnp.swapaxes(array, -3, -2).reshape(-1, LANES)


def accumulate(
    projections, images, transfer, pose_weights, pose_of, pose_blocks, pose_tiles,
    bank_size, n_owner, place,
):
    n_part, n_pose, n_tile, n_cell = projections.shape
    assert n_cell == SUB * LANES and n_pose == SUB and n_part % SUB == 0 and n_tile % 2 == 0
    n_row = n_owner * NB_DEV * bank_size * SUB
    n_acc = 4 if n_row * LANES * 4 <= 4 * MIB else 2
    b_rows = FAR_FIRST * SUB
    a_rows = n_row // (n_owner * 2) - b_rows
    projections = tiles_in_order(jnp.transpose(projections, (0, 2, 1, 3)))
    images = tiles_in_order(jnp.transpose(images, (1, 0, 2)))
    transfer = tiles_in_order(jnp.transpose(transfer, (1, 0, 2)))
    stay = functools.partial(pltpu.with_memory_space_constraint, memory_space=pltpu.HBM)
    hbm = pl.BlockSpec(memory_space=pltpu.HBM)
    smem = pl.BlockSpec(memory_space=pltpu.SMEM)
    vmem = pl.BlockSpec(memory_space=pltpu.VMEM)
    a_out = jax.ShapeDtypeStruct((n_owner // 2, a_rows, LANES), jnp.float32)
    b_out = jax.ShapeDtypeStruct((n_owner, b_rows, LANES), jnp.float32)
    return pl.pallas_call(
        functools.partial(accumulate_kernel, bank_size, n_owner, n_acc),
        out_shape=[a_out, a_out, b_out, b_out, a_out, a_out],
        in_specs=[smem] + [hbm] * 7,
        out_specs=[vmem] * 6,
        scratch_shapes=[
            pltpu.VMEM(projections.shape, jnp.bfloat16),
            pltpu.VMEM(images.shape, jnp.bfloat16),
            pltpu.VMEM(transfer.shape, jnp.bfloat16),
            pltpu.SMEM((n_pose, n_part), jnp.float32),
            pltpu.VMEM((n_pose, n_part), jnp.int32),
            pltpu.VMEM(pose_blocks.shape[::-1], jnp.int32),
            pltpu.VMEM(pose_tiles.shape[::-1], jnp.int32),
            pltpu.VMEM((n_part * n_pose, LANES), jnp.int32),
            pltpu.SMEM((n_part * n_pose, LANES), jnp.int32),
            pltpu.VMEM(transfer.shape, jnp.float32),
            pltpu.VMEM(transfer.shape, jnp.float32),
        ]
        + [pltpu.VMEM((n_row, LANES), jnp.float32)] * n_acc
        + [
            pltpu.SemaphoreType.DMA((n_part,)),
            pltpu.SemaphoreType.DMA((3,)),
            pltpu.SemaphoreType.DMA((3,)),
            pltpu.SemaphoreType.DMA,
        ],
        compiler_params=pltpu.CompilerParams(vmem_limit_bytes=(40 if n_acc == 4 else 56) * MIB),
        name="accumulate",
    )(
        place, stay(projections), stay(images), stay(transfer),
        stay(pose_weights.T), stay(pose_of.T), stay(pose_blocks.T), stay(pose_tiles.T),
    )


def in_vmem(kernel, name, out_shape, place, *operands):
    vmem = pl.BlockSpec(memory_space=pltpu.VMEM)
    return pl.pallas_call(
        kernel,
        out_shape=out_shape,
        in_specs=[pl.BlockSpec(memory_space=pltpu.SMEM)] + [vmem] * len(operands),
        out_specs=jax.tree.map(lambda _: vmem, out_shape),
        compiler_params=pltpu.CompilerParams(vmem_limit_bytes=32 * MIB),
        name=name,
    )(place, *operands)


def first_step_kernel(place, kept_away, got_away, kept_b, got_b, away, own_b, *far_b):
    far = place[2]
    away[...] = kept_away[...] + got_away[...]
    for d, out in enumerate((own_b,) + far_b):
        line = jnp.bitwise_xor(far, d)
        for y in range(2):
            out[y] = kept_b[line * 2 + y] + got_b[line * 2 + y]


def second_step_kernel(n_far, place, kept_stay, got_stay, got_near, own_b, *rest):
    got_b, (own_a, stay_b, away_b, *far_a) = rest[: n_far - 1], rest[n_far - 1 :]
    near, far = place[1], place[2]
    for d, out in enumerate([own_a] + far_a):
        line = jnp.bitwise_xor(far, d)
        out[...] = kept_stay[line] + got_stay[line] + got_near[line]
    for out, y in ((away_b, 1 - near), (stay_b, near)):
        total = own_b[y]
        for got in got_b:
            total += got[y]
        out[...] = total


def last_step_kernel(n_far, place, own_a, stay_b, got_b, *rest):
    got_a, (all_a, all_b) = rest[: n_far - 1], rest[n_far - 1 :]
    total = own_a[...]
    for got in got_a:
        total += got[...]
    all_a[...] = total
    all_b[...] = stay_b[...] + got_b[...]


def bank_kernel(mine, place, rows_b, rows_a, bank, *rest):
    out_hbm, block, sem = rest[-3:]
    bank_size, n_z, n_cell = bank.shape
    n_blk = block.shape[0]
    group = 2 * SUB
    half = place[0] if mine else 1 - place[0]

    def tile_row(row, c):
        if row < FAR_FIRST:
            return rows_b[row * SUB + c : row * SUB + c + 1, :]
        row -= FAR_FIRST
        return rows_a[row * SUB + c : row * SUB + c + 1, :]

    for c in range(n_cell // LANES):
        cols = slice(c * LANES, (c + 1) * LANES)

        @pl.loop(0, n_z // group)
        def _(g):
            rows = pl.ds(pl.multiple_of(g * group, group), group)
            weights = [bank[t, rows, cols] for t in range(bank_size)]
            for b in range(n_blk):
                total = weights[0] * tile_row(b * bank_size, c)
                for t in range(1, bank_size):
                    total += weights[t] * tile_row(b * bank_size + t, c)
                block[b, rows, cols] = total

    copy = pltpu.make_async_copy(block, out_hbm.at[pl.ds(half * n_blk, n_blk)], sem)
    copy.start()
    copy.wait()


def apply_bank(place, rows_b, rows_a, weight_bank, filled):
    bank_size, n_z, n_cell = weight_bank.shape
    vmem = pl.BlockSpec(memory_space=pltpu.VMEM)
    anywhere = pl.BlockSpec(memory_space=pl.ANY)
    mine = filled is None
    operands = (place, rows_b, rows_a, weight_bank) + (() if mine else (filled,))
    return pl.pallas_call(
        functools.partial(bank_kernel, mine),
        out_shape=jax.ShapeDtypeStruct((NB_DEV, n_z, n_cell), jnp.float32),
        in_specs=[pl.BlockSpec(memory_space=pltpu.SMEM), vmem, vmem, vmem] + ([] if mine else [anywhere]),
        out_specs=anywhere,
        scratch_shapes=[
            pltpu.VMEM((NB_DEV // 2, n_z, n_cell), jnp.float32),
            pltpu.SemaphoreType.DMA,
        ],
        input_output_aliases={} if mine else {4: 0},
        compiler_params=pltpu.CompilerParams(vmem_limit_bytes=32 * MIB),
        name="bank_of_own_half" if mine else "bank_of_other_half",
    )(*operands)


def body(
    projections, images, transfer, pose_weights, pose_of, pose_blocks, pose_tiles, weight_bank
):
    bank_size = weight_bank.shape[0]
    n_blk = lax.axis_size("blk")
    n_far = n_blk // 2
    here = lax.axis_index("blk")
    place = jnp.stack([lax.axis_index("rep"), here & 1, here >> 1]).astype(jnp.int32)
    sent_away, kept_away, sent_b, kept_b, sent_stay, kept_stay = accumulate(
        projections, images, transfer, pose_weights, pose_of, pose_blocks, pose_tiles,
        bank_size, n_blk, place,
    )

    def over_rep(array):
        return lax.ppermute(array, "rep", [(0, 1), (1, 0)])

    def over_near(array):
        return lax.ppermute(array, "blk", [(i, i ^ 1) for i in range(n_blk)])

    def over_far(array, d):
        return lax.ppermute(array, "blk", [(i, i ^ (2 * d)) for i in range(n_blk)])

    def like(*shape):
        return jax.ShapeDtypeStruct(shape, jnp.float32)

    a_rows, b_rows = sent_away.shape[1], sent_b.shape[1]
    got_away, got_b, got_stay = over_rep(sent_away), over_rep(sent_b), over_rep(sent_stay)
    away, own_b, *far_b = in_vmem(
        first_step_kernel, "first_step",
        [like(n_far, a_rows, LANES)] + [like(2, b_rows, LANES)] * n_far,
        place, kept_away, got_away, kept_b, got_b,
    )
    got_near = over_near(away)
    got_far_b = [over_far(array, d + 1) for d, array in enumerate(far_b)]
    own_a, stay_b, away_b, *far_a = in_vmem(
        functools.partial(second_step_kernel, n_far), "second_step",
        [like(a_rows, LANES)] + [like(b_rows, LANES)] * 2 + [like(a_rows, LANES)] * (n_far - 1),
        place, kept_stay, got_stay, got_near, own_b, *got_far_b,
    )
    got_far_a = [over_far(array, d + 1) for d, array in enumerate(far_a)]
    rows_a, rows_b = in_vmem(
        functools.partial(last_step_kernel, n_far), "last_step",
        [like(a_rows, LANES), like(b_rows, LANES)],
        place, own_a, stay_b, over_near(away_b), *got_far_a,
    )
    out = apply_bank(place, rows_b, rows_a, weight_bank, None)
    return apply_bank(place, over_rep(rows_b), over_rep(rows_a), weight_bank, out)


def solution(mesh):
    placed = (
        P(("groups", "blk", "rep"), None, None, None),
        P(("groups", "blk", "rep"), None, None),
        P(("groups", "blk", "rep"), None, None),
        P(("groups", "blk", "rep"), None),
        P(("groups", "blk", "rep"), None),
        P("groups", None),
        P("groups", None),
        P(),
    )
    return jax.shard_map(
        body,
        mesh=mesh,
        in_specs=placed,
        out_specs=P(("groups", "blk"), None, None),
        check_vma=False,
    )
```

time: 113 us -> 72 us (0.64)
  waiting for transfers between devices: 75.5 us -> 27.2 us
  starting transfers between devices: 0.01 us -> 14.8 us
  between operations: 13.4 us -> 0.07 us
  Pallas kernels: 21.6 us -> 29.7 us
  blocking collectives: 2.38 us -> 0 us
    reduce_scatter x1 -> x0, waiting for transfers between devices: 75.5 us -> none  [body(): lax.psum_scatter(sums, ('blk', 'rep'), scatter_dimension=0, tiled=True)]
    ppermute x0 -> x13, waiting for transfers between devices: none -> 27.2 us  [the longest x6 21 us: over_far(): return lax.ppermute(array, 'blk', [(i, i ^ 2 * d) for i in range(n_blk)])]
    ppermute x0 -> x13, starting transfers between devices: none -> 14.8 us  [the longest x6 9.77 us: over_far(): return lax.ppermute(array, 'blk', [(i, i ^ 2 * d) for i in range(n_blk)])]
    pallas_call x2 -> x6, Pallas kernels: 21.6 us -> 29.7 us  [the longest x1 23.3 us: accumulate(): pl.pallas_call(functools.partial(accumulate_kernel, bank_size, n_owner, n...]
    all_gather x1 -> x0, blocking collectives: 2.38 us -> none  [body(): owned = lax.all_gather(owned, 'rep', axis=0, tiled=True)]
  transfers between devices with their start and end apart: 1 -> 13, of which waited for: 1 -> 5; matrix products, arithmetic and copies ran while one was open for 0% -> 0% of each run, Pallas kernels for 0% -> 4%
where the time goes in v4:
time: 72 us; the launch traced here: 71.9 us
  Pallas kernels  29.7 us (41%)
  waiting for transfers between devices  27.2 us (38%)
  starting transfers between devices  14.8 us (21%)
    pallas_call x1, Pallas kernels, accumulate(): pl.pallas_call(functools.partial(accumulate_kernel, bank_size, n_owner, n...  23.3 us
    ppermute x6, waiting for transfers between devices, over_far(): return lax.ppermute(array, 'blk', [(i, i ^ 2 * d) for i in range(n_blk)])  21 us
    ppermute x6, starting transfers between devices, over_far(): return lax.ppermute(array, 'blk', [(i, i ^ 2 * d) for i in range(n_blk)])  9.77 us
    pallas_call x2, Pallas kernels, apply_bank(): pl.pallas_call(functools.partial(bank_kernel, mine), out_shape=jax.ShapeD...  4.39 us
    ppermute x2, waiting for transfers between devices, over_near(): return lax.ppermute(array, 'blk', [(i, i ^ 1) for i in range(n_blk)])  3.99 us
    ppermute x2, starting transfers between devices, over_near(): return lax.ppermute(array, 'blk', [(i, i ^ 1) for i in range(n_blk)])  3.45 us
    ppermute x5, waiting for transfers between devices, over_rep(): return lax.ppermute(array, 'rep', [(0, 1), (1, 0)])  2.28 us
    pallas_call x3, Pallas kernels, in_vmem(): pl.pallas_call(kernel, out_shape=out_shape, in_specs=[pl.BlockSpec(memory...  2 us
  transfers between devices with their start and end apart: 13, of which 5 were waited for; matrix products, arithmetic and copies ran while one was open for 0% of the time, Pallas kernels for 4%

profile of v4, /device:TPU:0, one launch (start us, length us, event | category | flops | bytes accessed | tf_op | source)
XLA Modules:
  0.0 71.9 jit_solution(9061590761080565781)
XLA Ops:
  0.0 0.1 pad_add_fusion.place
  0.1 23.3 %accumulate.1 = (f32[4,344,128]{2,1,0:T(8,128)S(1)}, f32[4,344,128]{2,1,0:T(8,128)S(1)}, f32[8,168,128]{2,1,0:T(8,128)S(1)}, f32[8,168,128]{2,1,0:T(8,128)S(1)},...) custom-call(s32[3]{0:T(128)S(1)} %pad_add_fusion.place, bf16[36864,128]{1,0:T(8,128)(2,1)} %bitcast.28, ...), custom_call_target="tpu_custom_call" | custom-call | tf_op jit(solution)/shard_map/accumulate/pallas_call | solution.py:197
  23.4 0.5 collective-permute-start.1
  23.9 0.1 collective-permute-start.2
  24.0 0.4 collective-permute-start
  24.4 2.3 %collective-permute-done.2.got_b = f32[8,168,128]{2,1,0:T(8,128)S(1)} collective-permute-done((f32[8,168,128]{2,1,0:T(8,128)S(1)}, f32[8,168,128]{2,1,0:T(8,128)S(1)}, u32[]{:S(2)}, u32[]{:S(2)}) %collective-permute-start.2) | collective-permute-done | bytes 688160 | tf_op jit(solution)/shard_map/ppermute | solution.py:339
  26.7 0.7 first_step.1
  27.4 3.0 %collective-permute-start.3 = (f32[4,344,128]{2,1,0:T(8,128)S(1)}, f32[4,344,128]{2,1,0:T(8,128)S(1)}, u32[]{:S(2)}, u32[]{:S(2)}) collective-permute-start(f32[4,344,128]{2,1,0:T(8,128)S(1)} %get-tuple-element.30), channel_id=1, source_target_pairs={{0,2},{2,0},{4,6},{6,4},{8,10},{10,8},{12,14},{14,12},{1,3},{3,1},... | collective-permute-start | bytes 2113544 | tf_op jit(solution)/shard_map/ppermute | solution.py:342
  30.3 1.6 %collective-permute-start.4 = (f32[2,168,128]{2,1,0:T(8,128)S(1)}, f32[2,168,128]{2,1,0:T(8,128)S(1)}, u32[]{:S(2)}, u32[]{:S(2)}) collective-permute-start(f32[2,168,128]{2,1,0:T(8,128)S(1)} %get-tuple-element.32), channel_id=1, source_target_pairs={{0,4},{2,6},{4,0},{6,2},{8,12},{10,14},{12,8},{14,10},{1,5},{3,7},... | collective-permute-start | bytes 516104 | tf_op jit(solution)/shard_map/ppermute | solution.py:345
  31.9 2.6 %collective-permute-start.5 = (f32[2,168,128]{2,1,0:T(8,128)S(1)}, f32[2,168,128]{2,1,0:T(8,128)S(1)}, u32[]{:S(2)}, u32[]{:S(2)}) collective-permute-start(f32[2,168,128]{2,1,0:T(8,128)S(1)} %get-tuple-element.33), channel_id=1, source_target_pairs={{0,8},{2,10},{4,12},{6,14},{8,0},{10,2},{12,4},{14,6},{1,9},{3,11}... | collective-permute-start | bytes 516104 | tf_op jit(solution)/shard_map/ppermute | solution.py:345
  34.5 0.2 collective-permute-start.6
  34.7 4.5 %collective-permute-done.4.rest_0_ = f32[2,168,128]{2,1,0:T(8,128)S(1)} collective-permute-done((f32[2,168,128]{2,1,0:T(8,128)S(1)}, f32[2,168,128]{2,1,0:T(8,128)S(1)}, u32[]{:S(2)}, u32[]{:S(2)}) %collective-permute-start.4) | collective-permute-done | bytes 172064 | tf_op jit(solution)/shard_map/ppermute | solution.py:345
  39.2 8.2 %collective-permute-done.5.rest_1_ = f32[2,168,128]{2,1,0:T(8,128)S(1)} collective-permute-done((f32[2,168,128]{2,1,0:T(8,128)S(1)}, f32[2,168,128]{2,1,0:T(8,128)S(1)}, u32[]{:S(2)}, u32[]{:S(2)}) %collective-permute-start.5) | collective-permute-done | bytes 172064 | tf_op jit(solution)/shard_map/ppermute | solution.py:345
  47.5 0.7 %second_step.1 = (f32[344,128]{1,0:T(8,128)S(1)}, f32[168,128]{1,0:T(8,128)S(1)}, f32[168,128]{1,0:T(8,128)S(1)}, f32[344,128]{1,0:T(8,128)S(1)}, f32[344,128]{1,0:T(8,128)S(1)}, /*index=5*/f32[344,128]{1,0:T(8,128)S(1)}) custom-call(s32[3]{0:T(128)S(1)} %pad_add_fusion.place, f32[4,344,128]{2,1,0:T(8,128)S(1)} %get-tuple-element.24.kept_stay, ...), custom_call_target="tpu_custom_call" | custom-call | tf_op jit(solution)/shard_map/second_step/pallas_call | solution.py:232
  48.2 2.9 %collective-permute-start.8 = (f32[344,128]{1,0:T(8,128)S(1)}, f32[344,128]{1,0:T(8,128)S(1)}, u32[]{:S(2)}, u32[]{:S(2)}) collective-permute-start(f32[344,128]{1,0:T(8,128)S(1)} %get-tuple-element.38), channel_id=1, source_target_pairs={{0,4},{2,6},{4,0},{6,2},{8,12},{10,14},{12,8},{14,10},{1,5},{3,7},... | collective-permute-start | bytes 528392 | tf_op jit(solution)/shard_map/ppermute | solution.py:345
  51.1 1.1 %collective-permute-start.9 = (f32[344,128]{1,0:T(8,128)S(1)}, f32[344,128]{1,0:T(8,128)S(1)}, u32[]{:S(2)}, u32[]{:S(2)}) collective-permute-start(f32[344,128]{1,0:T(8,128)S(1)} %get-tuple-element.39), channel_id=1, source_target_pairs={{0,8},{2,10},{4,12},{6,14},{8,0},{10,2},{12,4},{14,6},{1,9},{3,11}... | collective-permute-start | bytes 528392 | tf_op jit(solution)/shard_map/ppermute | solution.py:345
  52.2 1.4 %collective-permute-start.10 = (f32[344,128]{1,0:T(8,128)S(1)}, f32[344,128]{1,0:T(8,128)S(1)}, u32[]{:S(2)}, u32[]{:S(2)}) collective-permute-start(f32[344,128]{1,0:T(8,128)S(1)} %get-tuple-element.40), channel_id=1, source_target_pairs={{0,12},{2,14},{4,8},{6,10},{8,4},{10,6},{12,0},{14,2},{1,13},{3,15... | collective-permute-start | bytes 528392 | tf_op jit(solution)/shard_map/ppermute | solution.py:345
  53.6 0.5 collective-permute-start.7
  54.1 4.0 %collective-permute-done.7.got_b = f32[168,128]{1,0:T(8,128)S(1)} collective-permute-done((f32[168,128]{1,0:T(8,128)S(1)}, f32[168,128]{1,0:T(8,128)S(1)}, u32[]{:S(2)}, u32[]{:S(2)}) %collective-permute-start.7) | collective-permute-done | bytes 86048 | tf_op jit(solution)/shard_map/ppermute | solution.py:342
  58.1 8.2 %collective-permute-done.9.rest_1_ = f32[344,128]{1,0:T(8,128)S(1)} collective-permute-done((f32[344,128]{1,0:T(8,128)S(1)}, f32[344,128]{1,0:T(8,128)S(1)}, u32[]{:S(2)}, u32[]{:S(2)}) %collective-permute-start.9) | collective-permute-done | bytes 176160 | tf_op jit(solution)/shard_map/ppermute | solution.py:345
  66.3 0.6 last_step.1
  67.0 0.5 collective-permute-start.11
  67.5 2.2 %bank_of_own_half.1.rest_0_ = f32[8,32,1024]{2,1,0:T(8,128)} custom-call(s32[3]{0:T(128)S(1)} %pad_add_fusion.place, f32[168,128]{1,0:T(8,128)S(1)} %get-tuple-element.41.rows_b, f32[344,128]{1,0:T(8,128)S(1)} %get-tuple-element.42.rows_a, f32[16,32,1024]{2,1,0:T(8,128)S(1)} %copy-done), custom_call_target="tpu_custom_call" | custom-call | tf_op jit(solution)/shard_map/bank_of_own_half/pallas_call | solution.py:310
  69.7 2.2 %bank_of_other_half.1 = f32[8,32,1024]{2,1,0:T(8,128)} custom-call(s32[3]{0:T(128)S(1)} %pad_add_fusion.place, f32[168,128]{1,0:T(8,128)S(1)} %collective-permute-done.11.rows_b, f32[344,128]{1,0:T(8,128)S(1)} %collective-permute-done.12.rows_a, f32[16,32,1024]{2,1,0:T(8,128)S(1)} %copy-done, ...), custom_call_target="tpu_custom_call", output_to_operand_aliasing={{}: (4, {})} | custom-call | tf_op jit(solution)/shard_map/bank_of_other_half/pallas_call | solution.py:310
  (11 shorter events, 0.1 us)
Async XLA Ops:
  23.4 3.3 %collective-permute-start.1 = (f32[4,344,128]{2,1,0:T(8,128)S(1)}, f32[4,344,128]{2,1,0:T(8,128)S(1)}, u32[]{:S(2)}, u32[]{:S(2)}) collective-permute-start(f32[4,344,128]{2,1,0:T(8,128)S(1)} %get-tuple-element.27), channel_id=1, source_target_pairs={{0,1},{1,0},{2,3},{3,2},{4,5},{5,4},{6,7},{7,6},{8,9},{9,8},{10,11... | collective-permute-start | bytes 2113544 | tf_op jit(solution)/shard_map/ppermute | solution.py:339
  23.9 2.8 %collective-permute-start.2 = (f32[8,168,128]{2,1,0:T(8,128)S(1)}, f32[8,168,128]{2,1,0:T(8,128)S(1)}, u32[]{:S(2)}, u32[]{:S(2)}) collective-permute-start(f32[8,168,128]{2,1,0:T(8,128)S(1)} %get-tuple-element.29), channel_id=1, source_target_pairs={{0,1},{1,0},{2,3},{3,2},{4,5},{5,4},{6,7},{7,6},{8,9},{9,8},{10,11... | collective-permute-start | bytes 2064392 | tf_op jit(solution)/shard_map/ppermute | solution.py:339
  24.0 10.8 %collective-permute-start = (f32[4,344,128]{2,1,0:T(8,128)S(1)}, f32[4,344,128]{2,1,0:T(8,128)S(1)}, u32[]{:S(2)}, u32[]{:S(2)}) collective-permute-start(f32[4,344,128]{2,1,0:T(8,128)S(1)} %get-tuple-element.25), channel_id=1, source_target_pairs={{0,1},{1,0},{2,3},{3,2},{4,5},{5,4},{6,7},{7,6},{8,9},{9,8},{10,11... | collective-permute-start | bytes 2113544 | tf_op jit(solution)/shard_map/ppermute | solution.py:339
  27.4 40.1 %copy-start = (f32[16,32,1024]{2,1,0:T(8,128)S(1)}, f32[16,32,1024]{2,1,0:T(8,128)}, u32[]{:S(2)}) copy-start(f32[16,32,1024]{2,1,0:T(8,128)} %bank.3) | copy-start | bytes 6291460
  27.4 20.1 %collective-permute-start.3 = (f32[4,344,128]{2,1,0:T(8,128)S(1)}, f32[4,344,128]{2,1,0:T(8,128)S(1)}, u32[]{:S(2)}, u32[]{:S(2)}) collective-permute-start(f32[4,344,128]{2,1,0:T(8,128)S(1)} %get-tuple-element.30), channel_id=1, source_target_pairs={{0,2},{2,0},{4,6},{6,4},{8,10},{10,8},{12,14},{14,12},{1,3},{3,1},... | collective-permute-start | bytes 2113544 | tf_op jit(solution)/shard_map/ppermute | solution.py:342
  30.3 8.9 %collective-permute-start.4 = (f32[2,168,128]{2,1,0:T(8,128)S(1)}, f32[2,168,128]{2,1,0:T(8,128)S(1)}, u32[]{:S(2)}, u32[]{:S(2)}) collective-permute-start(f32[2,168,128]{2,1,0:T(8,128)S(1)} %get-tuple-element.32), channel_id=1, source_target_pairs={{0,4},{2,6},{4,0},{6,2},{8,12},{10,14},{12,8},{14,10},{1,5},{3,7},... | collective-permute-start | bytes 516104 | tf_op jit(solution)/shard_map/ppermute | solution.py:345
  31.9 15.6 %collective-permute-start.5 = (f32[2,168,128]{2,1,0:T(8,128)S(1)}, f32[2,168,128]{2,1,0:T(8,128)S(1)}, u32[]{:S(2)}, u32[]{:S(2)}) collective-permute-start(f32[2,168,128]{2,1,0:T(8,128)S(1)} %get-tuple-element.33), channel_id=1, source_target_pairs={{0,8},{2,10},{4,12},{6,14},{8,0},{10,2},{12,4},{14,6},{1,9},{3,11}... | collective-permute-start | bytes 516104 | tf_op jit(solution)/shard_map/ppermute | solution.py:345
  34.5 13.0 %collective-permute-start.6 = (f32[2,168,128]{2,1,0:T(8,128)S(1)}, f32[2,168,128]{2,1,0:T(8,128)S(1)}, u32[]{:S(2)}, u32[]{:S(2)}) collective-permute-start(f32[2,168,128]{2,1,0:T(8,128)S(1)} %get-tuple-element.34), channel_id=1, source_target_pairs={{0,12},{2,14},{4,8},{6,10},{8,4},{10,6},{12,0},{14,2},{1,13},{3,15... | collective-permute-start | bytes 516104 | tf_op jit(solution)/shard_map/ppermute | solution.py:345
  48.2 9.9 %collective-permute-start.8 = (f32[344,128]{1,0:T(8,128)S(1)}, f32[344,128]{1,0:T(8,128)S(1)}, u32[]{:S(2)}, u32[]{:S(2)}) collective-permute-start(f32[344,128]{1,0:T(8,128)S(1)} %get-tuple-element.38), channel_id=1, source_target_pairs={{0,4},{2,6},{4,0},{6,2},{8,12},{10,14},{12,8},{14,10},{1,5},{3,7},... | collective-permute-start | bytes 528392 | tf_op jit(solution)/shard_map/ppermute | solution.py:345
  51.1 15.2 %collective-permute-start.9 = (f32[344,128]{1,0:T(8,128)S(1)}, f32[344,128]{1,0:T(8,128)S(1)}, u32[]{:S(2)}, u32[]{:S(2)}) collective-permute-start(f32[344,128]{1,0:T(8,128)S(1)} %get-tuple-element.39), channel_id=1, source_target_pairs={{0,8},{2,10},{4,12},{6,14},{8,0},{10,2},{12,4},{14,6},{1,9},{3,11}... | collective-permute-start | bytes 528392 | tf_op jit(solution)/shard_map/ppermute | solution.py:345
  52.2 14.1 %collective-permute-start.10 = (f32[344,128]{1,0:T(8,128)S(1)}, f32[344,128]{1,0:T(8,128)S(1)}, u32[]{:S(2)}, u32[]{:S(2)}) collective-permute-start(f32[344,128]{1,0:T(8,128)S(1)} %get-tuple-element.40), channel_id=1, source_target_pairs={{0,12},{2,14},{4,8},{6,10},{8,4},{10,6},{12,0},{14,2},{1,13},{3,15... | collective-permute-start | bytes 528392 | tf_op jit(solution)/shard_map/ppermute | solution.py:345
  53.6 4.5 %collective-permute-start.7 = (f32[168,128]{1,0:T(8,128)S(1)}, f32[168,128]{1,0:T(8,128)S(1)}, u32[]{:S(2)}, u32[]{:S(2)}) collective-permute-start(f32[168,128]{1,0:T(8,128)S(1)} %get-tuple-element.37), channel_id=1, source_target_pairs={{0,2},{2,0},{4,6},{6,4},{8,10},{10,8},{12,14},{14,12},{1,3},{3,1},... | collective-permute-start | bytes 258056 | tf_op jit(solution)/shard_map/ppermute | solution.py:342
  66.9 2.8 %collective-permute-start.12 = (f32[344,128]{1,0:T(8,128)S(1)}, f32[344,128]{1,0:T(8,128)S(1)}, u32[]{:S(2)}, u32[]{:S(2)}) collective-permute-start(f32[344,128]{1,0:T(8,128)S(1)} %get-tuple-element.42.rows_a), channel_id=1, source_target_pairs={{0,1},{1,0},{2,3},{3,2},{4,5},{5,4},{6,7},{7,6},{8,9},{9,8},{10,11... | collective-permute-start | bytes 528392 | tf_op jit(solution)/shard_map/ppermute | solution.py:339
  67.0 2.7 %collective-permute-start.11 = (f32[168,128]{1,0:T(8,128)S(1)}, f32[168,128]{1,0:T(8,128)S(1)}, u32[]{:S(2)}, u32[]{:S(2)}) collective-permute-start(f32[168,128]{1,0:T(8,128)S(1)} %get-tuple-element.41.rows_b), channel_id=1, source_target_pairs={{0,1},{1,0},{2,3},{3,2},{4,5},{5,4},{6,7},{7,6},{8,9},{9,8},{10,11... | collective-permute-start | bytes 258056 | tf_op jit(solution)/shard_map/ppermute | solution.py:339

commit v5 on v4

--- a/solution.py
+++ b/solution.py
@@ -18,7 +18,7 @@
     bank_size, n_owner, n_acc,
     place, proj_hbm, img_hbm, tra_hbm, w_hbm, pose_hbm, blocks_hbm, tiles_hbm,
     sent_away, kept_away, sent_b, kept_b, sent_stay, kept_stay,
-    proj, img, tra, w_smem, pose, blocks, tiles, idx_v, idx_s, square, cross,
+    proj, img, tra, weight, spread, pose, blocks, tiles, idx_v, idx_s, square, cross,
     *rest,
 ):
     accs = rest[:n_acc]
@@ -36,7 +36,7 @@
     small_copies = [
         pltpu.make_async_copy(img_hbm, img, small_sem.at[0]),
         pltpu.make_async_copy(tra_hbm, tra, small_sem.at[1]),
-        pltpu.make_async_copy(w_hbm, w_smem, small_sem.at[2]),
+        pltpu.make_async_copy(w_hbm, weight, small_sem.at[2]),
     ]
     for copy in table_copies + small_copies:
         copy.start()
@@ -47,6 +47,14 @@
 
     for p in range(n_part):
         proj_copy(p).start()
+
+    zero = jnp.zeros((8 * SUB, LANES), jnp.float32)
+
+    @pl.loop(0, n_row // (8 * SUB))
+    def _(i):
+        rows = pl.ds(pl.multiple_of(i * (8 * SUB), 8 * SUB), 8 * SUB)
+        for acc in accs:
+            acc[rows, :] = zero
 
     for copy in table_copies:
         copy.wait()
@@ -65,41 +73,44 @@
     idx_copy = pltpu.make_async_copy(idx_v, idx_s, idx_sem)
     idx_copy.start()
 
-    zero = jnp.zeros((8 * SUB, LANES), jnp.float32)
-
-    @pl.loop(0, n_row // (8 * SUB))
-    def _(i):
-        rows = pl.ds(pl.multiple_of(i * (8 * SUB), 8 * SUB), 8 * SUB)
-        for acc in accs:
-            acc[rows, :] = zero
-
-    def regroup(ref, first):
-        block = ref[pl.ds(pl.multiple_of(first, tile_rows), tile_rows), :].astype(jnp.float32)
-        return jnp.swapaxes(block.reshape(SUB, SUB, LANES), 0, 1)
-
     for copy in small_copies:
         copy.wait()
-
-    @pl.loop(0, n_tile)
-    def _(j):
-        for h in range(n_part // SUB):
-            first = (j * (n_part // SUB) + h) * tile_rows
-            t, i = regroup(tra, first), regroup(img, first)
-            for k in range(SUB):
-                rows = pl.ds(pl.multiple_of(((h * SUB + k) * n_tile + j) * SUB, SUB), SUB)
-                square[rows, :] = t[k] * t[k]
-                cross[rows, :] = t[k] * i[k]
-
-    def terms(unit):
-        x = regroup(proj, unit * tile_rows)
-        cell = pl.ds(pl.multiple_of(unit * SUB, SUB), SUB)
-        tt, ti = square[cell, :], cross[cell, :]
-        return [tt * x[k] - ti for k in range(n_pose)]
-
-    def add_rows(p, j, values, weights):
+    for p in range(n_part):
+        spread[p * n_pose : (p + 1) * n_pose, :] = jnp.broadcast_to(weight[:, p : p + 1], (n_pose, LANES))
+
+    @pl.loop(0, square.shape[0] // tile_rows)
+    def _(i):
+        rows = pl.ds(pl.multiple_of(i * tile_rows, tile_rows), tile_rows)
+        t = tra[rows, :].astype(jnp.float32)
+        square[rows, :] = t * t
+        cross[rows, :] = t * img[rows, :].astype(jnp.float32)
+
+    sublane = lax.broadcasted_iota(jnp.int32, (SUB, LANES), 0)
+    bits = [(sublane & (1 << t)) != 0 for t in range(3)]
+
+    def terms(p, j, unit, weights):
+        first = pl.multiple_of(unit * tile_rows, tile_rows)
+        cell = (j * (n_part // SUB) + p // SUB) * tile_rows + p % SUB
+        turned = []
+        for c in range(0, SUB, 2):
+            pair = proj[pl.ds(first + c * SUB, 2 * SUB), :].astype(jnp.float32)
+            for h in range(2):
+                x = pair[h * SUB : (h + 1) * SUB]
+                row = pl.ds(cell + (c + h) * SUB, 1)
+                value = (square[row, :] * x - cross[row, :]) * weights
+                turned.append(pltpu.roll(value, c + h, 0) if c + h else value)
+        for t, bit in enumerate(bits):
+            turned = [jnp.where(bit, turned[(i + (1 << t)) % SUB], turned[i]) for i in range(SUB)]
+        result = []
+        for k in range(n_pose):
+            back = (k % n_acc - k) % SUB
+            value = turned[-k % SUB]
+            result.append(pltpu.roll(value, back, 0) if back else value)
+        return result
+
+    def add_rows(p, j, values):
         at = [idx_s[p * n_pose + k, j] for k in range(n_pose)]
         rows = [pl.ds(pl.multiple_of(at[k], SUB), SUB) for k in range(n_pose)]
-        values = [values[k] * weights[k] for k in range(n_pose)]
         old = [accs[k % n_acc][rows[k], :] for k in range(n_pose)]
         new = []
         for k in range(n_pose):
@@ -110,27 +121,21 @@
         for k in range(n_pose):
             accs[k % n_acc][rows[k], :] = new[k]
 
-    proj_copy(0).wait()
     idx_copy.wait()
-    n_unit = n_part * n_tile
-
-    @pl.loop(0, n_part, init_carry=tuple(terms(0) + terms(1)))
-    def _(p, ready):
-        @pl.when(p + 1 < n_part)
-        def _():
-            proj_copy(p + 1).wait()
-
-        weights = [jnp.full((SUB, LANES), w_smem[k, p], jnp.float32) for k in range(n_pose)]
-
-        @pl.loop(0, n_tile, step=2, init_carry=ready)
-        def done(j, now):
-            unit = jnp.minimum(p * n_tile + j + 2, n_unit - 2)
-            later = terms(unit) + terms(unit + 1)
-            add_rows(p, j, now[:n_pose], weights)
-            add_rows(p, j + 1, now[n_pose:], weights)
+
+    @pl.loop(0, n_part)
+    def _(p):
+        proj_copy(p).wait()
+        weights = spread[pl.ds(pl.multiple_of(p * n_pose, n_pose), n_pose), :]
+        base = p * n_tile
+
+        @pl.loop(0, n_tile, step=2, init_carry=tuple(terms(p, 0, base, weights) + terms(p, 1, base + 1, weights)))
+        def _(j, now):
+            ahead = jnp.minimum(j + 2, n_tile - 2)
+            later = terms(p, ahead, base + ahead, weights) + terms(p, ahead + 1, base + ahead + 1, weights)
+            add_rows(p, j, now[:n_pose])
+            add_rows(p, j + 1, now[n_pose:])
             return tuple(later)
-
-        return done
 
     rep, near = place[0], place[1]
     half_rows = n_row // (n_owner * 2)
@@ -143,10 +148,10 @@
 
         def sum_rows(offset, count):
             rows = pl.ds(pl.multiple_of(first + offset, SUB), count)
-            total = accs[0][rows, :]
-            for acc in accs[1:]:
-                total += acc[rows, :]
-            out[o, pl.ds(pl.multiple_of(offset, SUB), count), :] = total
+            total = accs[0][rows, :].reshape(count // SUB, SUB, LANES)
+            for turn, acc in enumerate(accs[1:]):
+                total += pltpu.roll(acc[rows, :].reshape(count // SUB, SUB, LANES), SUB - 1 - turn, 1)
+            out[o, pl.ds(pl.multiple_of(offset, SUB), count), :] = total.reshape(count, LANES)
 
         @pl.loop(0, size // step)
         def _(i):
@@ -203,7 +208,8 @@
             pltpu.VMEM(projections.shape, jnp.bfloat16),
             pltpu.VMEM(images.shape, jnp.bfloat16),
             pltpu.VMEM(transfer.shape, jnp.bfloat16),
-            pltpu.SMEM((n_pose, n_part), jnp.float32),
+            pltpu.VMEM((n_pose, n_part), jnp.float32),
+            pltpu.VMEM((n_part * n_pose, LANES), jnp.float32),
             pltpu.VMEM((n_pose, n_part), jnp.int32),
             pltpu.VMEM(pose_blocks.shape[::-1], jnp.int32),
             pltpu.VMEM(pose_tiles.shape[::-1], jnp.int32),
@@ -227,45 +233,38 @@
     )
 
 
-def in_vmem(kernel, name, out_shape, place, *operands):
+def in_vmem(kernel, name, out_shape, *operands):
     vmem = pl.BlockSpec(memory_space=pltpu.VMEM)
+    smem = pl.BlockSpec(memory_space=pltpu.SMEM)
     return pl.pallas_call(
         kernel,
         out_shape=out_shape,
-        in_specs=[pl.BlockSpec(memory_space=pltpu.SMEM)] + [vmem] * len(operands),
+        in_specs=[smem if operand.dtype == jnp.int32 else vmem for operand in operands],
         out_specs=jax.tree.map(lambda _: vmem, out_shape),
         compiler_params=pltpu.CompilerParams(vmem_limit_bytes=32 * MIB),
         name=name,
-    )(place, *operands)
-
-
-def first_step_kernel(place, kept_away, got_away, kept_b, got_b, away, own_b, *far_b):
-    far = place[2]
+    )(*operands)
+
+
+def first_step_kernel(kept_away, got_away, kept_b, got_b, away, both_b):
     away[...] = kept_away[...] + got_away[...]
-    for d, out in enumerate((own_b,) + far_b):
-        line = jnp.bitwise_xor(far, d)
-        for y in range(2):
-            out[y] = kept_b[line * 2 + y] + got_b[line * 2 + y]
-
-
-def second_step_kernel(n_far, place, kept_stay, got_stay, got_near, own_b, *rest):
-    got_b, (own_a, stay_b, away_b, *far_a) = rest[: n_far - 1], rest[n_far - 1 :]
-    near, far = place[1], place[2]
-    for d, out in enumerate([own_a] + far_a):
-        line = jnp.bitwise_xor(far, d)
-        out[...] = kept_stay[line] + got_stay[line] + got_near[line]
+    both_b[...] = kept_b[...] + got_b[...]
+
+
+def second_step_kernel(place, kept_stay, got_stay, got_near, got_b, line_a, stay_b, away_b):
+    near = place[1]
+    line_a[...] = kept_stay[...] + got_stay[...] + got_near[...]
     for out, y in ((away_b, 1 - near), (stay_b, near)):
-        total = own_b[y]
-        for got in got_b:
-            total += got[y]
+        total = got_b[y]
+        for line in range(1, got_b.shape[0] // 2):
+            total += got_b[2 * line + y]
         out[...] = total
 
 
-def last_step_kernel(n_far, place, own_a, stay_b, got_b, *rest):
-    got_a, (all_a, all_b) = rest[: n_far - 1], rest[n_far - 1 :]
-    total = own_a[...]
-    for got in got_a:
-        total += got[...]
+def last_step_kernel(got_a, stay_b, got_b, all_a, all_b):
+    total = got_a[0]
+    for line in range(1, got_a.shape[0]):
+        total += got_a[line]
     all_a[...] = total
     all_b[...] = stay_b[...] + got_b[...]
 
@@ -341,31 +340,27 @@
     def over_near(array):
         return lax.ppermute(array, "blk", [(i, i ^ 1) for i in range(n_blk)])
 
-    def over_far(array, d):
-        return lax.ppermute(array, "blk", [(i, i ^ (2 * d)) for i in range(n_blk)])
+    def over_far(array):
+        lines = [list(range(i, n_blk, 2)) for i in range(2)]
+        return lax.all_to_all(array, "blk", 0, 0, axis_index_groups=lines, tiled=True)
 
     def like(*shape):
         return jax.ShapeDtypeStruct(shape, jnp.float32)
 
     a_rows, b_rows = sent_away.shape[1], sent_b.shape[1]
     got_away, got_b, got_stay = over_rep(sent_away), over_rep(sent_b), over_rep(sent_stay)
-    away, own_b, *far_b = in_vmem(
-        first_step_kernel, "first_step",
-        [like(n_far, a_rows, LANES)] + [like(2, b_rows, LANES)] * n_far,
-        place, kept_away, got_away, kept_b, got_b,
-    )
-    got_near = over_near(away)
-    got_far_b = [over_far(array, d + 1) for d, array in enumerate(far_b)]
-    own_a, stay_b, away_b, *far_a = in_vmem(
-        functools.partial(second_step_kernel, n_far), "second_step",
-        [like(a_rows, LANES)] + [like(b_rows, LANES)] * 2 + [like(a_rows, LANES)] * (n_far - 1),
-        place, kept_stay, got_stay, got_near, own_b, *got_far_b,
-    )
-    got_far_a = [over_far(array, d + 1) for d, array in enumerate(far_a)]
+    away, both_b = in_vmem(
+        first_step_kernel, "first_step", [like(n_far, a_rows, LANES), like(n_blk, b_rows, LANES)],
+        kept_away, got_away, kept_b, got_b,
+    )
+    line_a, stay_b, away_b = in_vmem(
+        second_step_kernel, "second_step",
+        [like(n_far, a_rows, LANES), like(b_rows, LANES), like(b_rows, LANES)],
+        place, kept_stay, got_stay, over_near(away), over_far(both_b),
+    )
     rows_a, rows_b = in_vmem(
-        functools.partial(last_step_kernel, n_far), "last_step",
-        [like(a_rows, LANES), like(b_rows, LANES)],
-        place, own_a, stay_b, over_near(away_b), *got_far_a,
+        last_step_kernel, "last_step", [like(a_rows, LANES), like(b_rows, LANES)],
+        over_far(line_a), stay_b, over_near(away_b),
     )
     out = apply_bank(place, rows_b, rows_a, weight_bank, None)
     return apply_bank(place, over_rep(rows_b), over_rep(rows_a), weight_bank, out)

time: 72 us -> 88.4 us (1.23)
  waiting for transfers between devices: 27.2 us -> 35.3 us
  local copies, waits for them, and re-layouts: 0.01 us -> 6.08 us
  Pallas kernels: 29.7 us -> 31 us
    ppermute x6 -> x0, waiting for transfers between devices: 21 us -> none  [over_far(): return lax.ppermute(array, 'blk', [(i, i ^ 2 * d) for i in range(n_blk)])]
    ppermute x2, waiting for transfers between devices: 3.99 us -> 18.4 us  [over_near(): return lax.ppermute(array, 'blk', [(i, i ^ 1) for i in range(n_blk)])]
    all_to_all x0 -> x2, waiting for transfers between devices: none -> 13.5 us  [over_far(): lax.all_to_all(array, 'blk', 0, 0, axis_index_groups=lines, tiled=True)]
    all_to_all x0 -> x2, starting transfers between devices: none -> 11.3 us  [over_far(): lax.all_to_all(array, 'blk', 0, 0, axis_index_groups=lines, tiled=True)]
    ppermute x6 -> x0, starting transfers between devices: 9.77 us -> none  [over_far(): return lax.ppermute(array, 'blk', [(i, i ^ 2 * d) for i in range(n_blk)])]
    unnamed x2 -> x16, local copies, waits for them, and re-layouts: 0.01 us -> 6.08 us
    ppermute x5, waiting for transfers between devices: 2.28 us -> 3.35 us  [over_rep(): return lax.ppermute(array, 'rep', [(0, 1), (1, 0)])]
  transfers between devices with their start and end apart: 13 -> 9, of which waited for: 5 -> 5; matrix products, arithmetic and copies ran while one was open for 0% -> 0% of each run, Pallas kernels for 4% -> 2%
where the time goes in v5:
time: 88.4 us; the launch traced here: 88 us
  waiting for transfers between devices  35.3 us (40%)
  Pallas kernels  31 us (35%)
  starting transfers between devices  15.5 us (18%)
  local copies, waits for them, and re-layouts  6.08 us (7%)
    pallas_call x1, Pallas kernels, accumulate(): pl.pallas_call(functools.partial(accumulate_kernel, bank_size, n_owner, n...  24 us
    ppermute x2, waiting for transfers between devices, over_near(): return lax.ppermute(array, 'blk', [(i, i ^ 1) for i in range(n_blk)])  18.4 us
    all_to_all x2, waiting for transfers between devices, over_far(): lax.all_to_all(array, 'blk', 0, 0, axis_index_groups=lines, tiled=True)  13.5 us
    all_to_all x2, starting transfers between devices, over_far(): lax.all_to_all(array, 'blk', 0, 0, axis_index_groups=lines, tiled=True)  11.3 us
    unnamed x16, local copies, waits for them, and re-layouts  6.08 us
    pallas_call x2, Pallas kernels, apply_bank(): pl.pallas_call(functools.partial(bank_kernel, mine), out_shape=jax.ShapeD...  4.41 us
    ppermute x5, waiting for transfers between devices, over_rep(): return lax.ppermute(array, 'rep', [(0, 1), (1, 0)])  3.35 us
    ppermute x2, starting transfers between devices, over_near(): return lax.ppermute(array, 'blk', [(i, i ^ 1) for i in range(n_blk)])  3.04 us
  transfers between devices with their start and end apart: 9, of which 5 were waited for; matrix products, arithmetic and copies ran while one was open for 0% of the time, Pallas kernels for 2%

profile of v5, /device:TPU:0, one launch (start us, length us, event | category | flops | bytes accessed | tf_op | source)
XLA Modules:
  0.0 88.0 jit_solution(8687881830985337272)
XLA Ops:
  0.1 24.0 %accumulate.1 = (f32[4,344,128]{2,1,0:T(8,128)S(1)}, f32[4,344,128]{2,1,0:T(8,128)S(1)}, f32[8,168,128]{2,1,0:T(8,128)S(1)}, f32[8,168,128]{2,1,0:T(8,128)S(1)},...) custom-call(s32[3]{0:T(128)S(1)} %pad_add_fusion.place, bf16[36864,128]{1,0:T(8,128)(2,1)} %bitcast.28, ...), custom_call_target="tpu_custom_call" | custom-call | tf_op jit(solution)/shard_map/accumulate/pallas_call | solution.py:202
  24.1 0.5 collective-permute-start.1
  24.6 0.1 collective-permute-start.2
  24.7 2.7 %collective-permute-done.2.got_b = f32[8,168,128]{2,1,0:T(8,128)S(1)} collective-permute-done((f32[8,168,128]{2,1,0:T(8,128)S(1)}, f32[8,168,128]{2,1,0:T(8,128)S(1)}, u32[]{:S(2)}, u32[]{:S(2)}) %collective-permute-start.2) | collective-permute-done | bytes 688160 | tf_op jit(solution)/shard_map/ppermute | solution.py:338
  27.4 1.0 %first_step.1 = (f32[4,344,128]{2,1,0:T(8,128)S(1)}, f32[8,168,128]{2,1,0:T(8,128)}) custom-call(f32[4,344,128]{2,1,0:T(8,128)S(1)} %get-tuple-element.20.kept_away, f32[4,344,128]{2,1,0:T(8,128)S(1)} %collective-permute-done.1.got_away, f32[8,168,128]{2,1,0:T(8,128)S(1)} %get-tuple-element.22.kept_b, f32[8,168,128]{2,1,0:T(8,128)S(1)} %collective-permute-done.2.got_b), custom_call_target="tpu_custom_call" | custom-call | tf_op jit(solution)/shard_map/first_step/pallas_call | solution.py:239
  28.4 6.2 %all-to-all-start = ((f32[8,168,128]{2,1,0:T(8,128)}), f32[8,168,128]{2,1,0:T(8,128)S(1)}, u32[]{:S(2)}, u32[]{:S(2)}) async-start(f32[8,168,128]{2,1,0:T(8,128)} %get-tuple-element.25), calls=%async_computation | async-start | bytes 1376256 | tf_op jit(solution)/shard_map/all_to_all | solution.py:345
  34.6 1.5 %collective-permute-start.3 = (f32[4,344,128]{2,1,0:T(8,128)S(1)}, f32[4,344,128]{2,1,0:T(8,128)S(1)}, u32[]{:S(2)}, u32[]{:S(2)}) collective-permute-start(f32[4,344,128]{2,1,0:T(8,128)S(1)} %get-tuple-element.24), channel_id=1, source_target_pairs={{0,2},{2,0},{4,6},{6,4},{8,10},{10,8},{12,14},{14,12},{1,3},{3,1},... | collective-permute-start | bytes 2113544 | tf_op jit(solution)/shard_map/ppermute | solution.py:341
  36.2 0.6 collective-permute-done.got_stay
  36.8 0.9 copy-done.1
  37.7 15.2 %collective-permute-done.3.got_near = f32[4,344,128]{2,1,0:T(8,128)S(1)} collective-permute-done((f32[4,344,128]{2,1,0:T(8,128)S(1)}, f32[4,344,128]{2,1,0:T(8,128)S(1)}, u32[]{:S(2)}, u32[]{:S(2)}) %collective-permute-start.3) | collective-permute-done | bytes 704544 | tf_op jit(solution)/shard_map/ppermute | solution.py:341
  52.8 0.9 copy-done.3
  53.7 1.1 %copy-done.2 = f32[4,344,128]{2,1,0:T(8,128)S(1)} copy-done((f32[4,344,128]{2,1,0:T(8,128)S(1)}, f32[4,344,128]{2,1,0:T(8,128)}, u32[]{:S(2)}) %copy-start.2) | copy-done | bytes 704536
  54.8 1.1 %copy-done.4 = f32[4,344,128]{2,1,0:T(8,128)S(1)} copy-done((f32[4,344,128]{2,1,0:T(8,128)S(1)}, f32[4,344,128]{2,1,0:T(8,128)}, u32[]{:S(2)}) %copy-start.4) | copy-done | bytes 704536
  55.9 1.6 %second_step.1 = (f32[4,344,128]{2,1,0:T(8,128)}, f32[168,128]{1,0:T(8,128)S(1)}, f32[168,128]{1,0:T(8,128)S(1)}) custom-call(s32[3]{0:T(128)S(1)} %pad_add_fusion.place, f32[4,344,128]{2,1,0:T(8,128)S(1)} %get-tuple-element.18.kept_stay, f32[4,344,128]{2,1,0:T(8,128)S(1)} %copy-done.2, f32[4,344,128]{2,1,0:T(8,128)S(1)} %copy-done.4, ...), custom_call_target="tpu_custom_call" | custom-call | tf_op jit(solution)/shard_map/second_step/pallas_call | solution.py:239
  57.5 0.6 copy-done.5
  58.1 0.6 copy-done.7
  58.7 5.1 %all-to-all-start.1 = ((f32[4,344,128]{2,1,0:T(8,128)}), f32[4,344,128]{2,1,0:T(8,128)S(1)}, u32[]{:S(2)}, u32[]{:S(2)}) async-start(f32[4,344,128]{2,1,0:T(8,128)} %get-tuple-element.26), calls=%async_computation.1 | async-start | bytes 1409024 | tf_op jit(solution)/shard_map/all_to_all | solution.py:345
  63.8 1.5 %collective-permute-start.4 = (f32[168,128]{1,0:T(8,128)}, f32[168,128]{1,0:T(8,128)S(1)}, u32[]{:S(2)}, u32[]{:S(2)}) collective-permute-start(f32[168,128]{1,0:T(8,128)} %copy-done.7), channel_id=1, source_target_pairs={{0,2},{2,0},{4,6},{6,4},{8,10},{10,8},{12,14},{14,12},{1,3},{3,1},... | collective-permute-start | bytes 258056 | tf_op jit(solution)/shard_map/ppermute | solution.py:341
  65.4 3.2 %collective-permute-done.4.got_b = f32[168,128]{1,0:T(8,128)S(1)} collective-permute-done((f32[168,128]{1,0:T(8,128)}, f32[168,128]{1,0:T(8,128)S(1)}, u32[]{:S(2)}, u32[]{:S(2)}) %collective-permute-start.4) | collective-permute-done | bytes 86048 | tf_op jit(solution)/shard_map/ppermute | solution.py:341
  68.5 13.5 %all-to-all-done.1.got_a = f32[4,344,128]{2,1,0:T(8,128)S(1)} async-done(((f32[4,344,128]{2,1,0:T(8,128)}), f32[4,344,128]{2,1,0:T(8,128)S(1)}, u32[]{:S(2)}, u32[]{:S(2)}) %all-to-all-start.1) | async-done | bytes 704544 | tf_op jit(solution)/shard_map/all_to_all | solution.py:345
  82.1 0.9 %copy-done.6 = f32[168,128]{1,0:T(8,128)S(1)} copy-done((f32[168,128]{1,0:T(8,128)S(1)}, f32[168,128]{1,0:T(8,128)}, u32[]{:S(2)}) %copy-start.6) | copy-done | bytes 86040
  83.1 0.5 collective-permute-start.5
  83.6 2.2 %bank_of_own_half.1.rest_0_ = f32[8,32,1024]{2,1,0:T(8,128)} custom-call(s32[3]{0:T(128)S(1)} %pad_add_fusion.place, f32[168,128]{1,0:T(8,128)S(1)} %get-tuple-element.29.rows_b, f32[344,128]{1,0:T(8,128)S(1)} %get-tuple-element.30.rows_a, f32[16,32,1024]{2,1,0:T(8,128)S(1)} %copy-done), custom_call_target="tpu_custom_call" | custom-call | tf_op jit(solution)/shard_map/bank_of_own_half/pallas_call | solution.py:309
  85.8 2.2 %bank_of_other_half.1 = f32[8,32,1024]{2,1,0:T(8,128)} custom-call(s32[3]{0:T(128)S(1)} %pad_add_fusion.place, f32[168,128]{1,0:T(8,128)S(1)} %collective-permute-done.5.rows_b, f32[344,128]{1,0:T(8,128)S(1)} %collective-permute-done.6.rows_a, f32[16,32,1024]{2,1,0:T(8,128)S(1)} %copy-done, ...), custom_call_target="tpu_custom_call", output_to_operand_aliasing={{}: (4, {})} | custom-call | tf_op jit(solution)/shard_map/bank_of_other_half/pallas_call | solution.py:309
  (17 shorter events, 0.2 us)
Async XLA Ops:
  24.1 3.3 %collective-permute-start.1 = (f32[4,344,128]{2,1,0:T(8,128)S(1)}, f32[4,344,128]{2,1,0:T(8,128)S(1)}, u32[]{:S(2)}, u32[]{:S(2)}) collective-permute-start(f32[4,344,128]{2,1,0:T(8,128)S(1)} %get-tuple-element.21), channel_id=1, source_target_pairs={{0,1},{1,0},{2,3},{3,2},{4,5},{5,4},{6,7},{7,6},{8,9},{9,8},{10,11... | collective-permute-start | bytes 2113544 | tf_op jit(solution)/shard_map/ppermute | solution.py:338
  24.6 2.8 %collective-permute-start.2 = (f32[8,168,128]{2,1,0:T(8,128)S(1)}, f32[8,168,128]{2,1,0:T(8,128)S(1)}, u32[]{:S(2)}, u32[]{:S(2)}) collective-permute-start(f32[8,168,128]{2,1,0:T(8,128)S(1)} %get-tuple-element.23), channel_id=1, source_target_pairs={{0,1},{1,0},{2,3},{3,2},{4,5},{5,4},{6,7},{7,6},{8,9},{9,8},{10,11... | collective-permute-start | bytes 2064392 | tf_op jit(solution)/shard_map/ppermute | solution.py:338
  28.4 25.3 %all-to-all-start = ((f32[8,168,128]{2,1,0:T(8,128)}), f32[8,168,128]{2,1,0:T(8,128)S(1)}, u32[]{:S(2)}, u32[]{:S(2)}) async-start(f32[8,168,128]{2,1,0:T(8,128)} %get-tuple-element.25), calls=%async_computation | async-start | bytes 1376256 | tf_op jit(solution)/shard_map/all_to_all | solution.py:345
  34.6 2.2 %collective-permute-start = (f32[4,344,128]{2,1,0:T(8,128)S(1)}, f32[4,344,128]{2,1,0:T(8,128)S(1)}, u32[]{:S(2)}, u32[]{:S(2)}) collective-permute-start(f32[4,344,128]{2,1,0:T(8,128)S(1)} %get-tuple-element.19), channel_id=1, source_target_pairs={{0,1},{1,0},{2,3},{3,2},{4,5},{5,4},{6,7},{7,6},{8,9},{9,8},{10,11... | collective-permute-start | bytes 2113544 | tf_op jit(solution)/shard_map/ppermute | solution.py:338
  34.6 18.2 %collective-permute-start.3 = (f32[4,344,128]{2,1,0:T(8,128)S(1)}, f32[4,344,128]{2,1,0:T(8,128)S(1)}, u32[]{:S(2)}, u32[]{:S(2)}) collective-permute-start(f32[4,344,128]{2,1,0:T(8,128)S(1)} %get-tuple-element.24), channel_id=1, source_target_pairs={{0,2},{2,0},{4,6},{6,4},{8,10},{10,8},{12,14},{14,12},{1,3},{3,1},... | collective-permute-start | bytes 2113544 | tf_op jit(solution)/shard_map/ppermute | solution.py:341
  36.8 0.9 copy-start.1
  52.8 0.9 copy-start.3
  53.7 1.1 %copy-start.2 = (f32[4,344,128]{2,1,0:T(8,128)S(1)}, f32[4,344,128]{2,1,0:T(8,128)}, u32[]{:S(2)}) copy-start(f32[4,344,128]{2,1,0:T(8,128)} %copy-done.1) | copy-start | bytes 2113540
  54.8 1.1 %copy-start.4 = (f32[4,344,128]{2,1,0:T(8,128)S(1)}, f32[4,344,128]{2,1,0:T(8,128)}, u32[]{:S(2)}) copy-start(f32[4,344,128]{2,1,0:T(8,128)} %copy-done.3) | copy-start | bytes 2113540
  55.9 27.7 %copy-start = (f32[16,32,1024]{2,1,0:T(8,128)S(1)}, f32[16,32,1024]{2,1,0:T(8,128)}, u32[]{:S(2)}) copy-start(f32[16,32,1024]{2,1,0:T(8,128)} %bank.3) | copy-start | bytes 6291460
  57.5 0.6 copy-start.5
  58.1 0.6 copy-start.7
  58.7 23.3 %all-to-all-start.1 = ((f32[4,344,128]{2,1,0:T(8,128)}), f32[4,344,128]{2,1,0:T(8,128)S(1)}, u32[]{:S(2)}, u32[]{:S(2)}) async-start(f32[4,344,128]{2,1,0:T(8,128)} %get-tuple-element.26), calls=%async_computation.1 | async-start | bytes 1409024 | tf_op jit(solution)/shard_map/all_to_all | solution.py:345
  63.8 4.7 %collective-permute-start.4 = (f32[168,128]{1,0:T(8,128)}, f32[168,128]{1,0:T(8,128)S(1)}, u32[]{:S(2)}, u32[]{:S(2)}) collective-permute-start(f32[168,128]{1,0:T(8,128)} %copy-done.7), channel_id=1, source_target_pairs={{0,2},{2,0},{4,6},{6,4},{8,10},{10,8},{12,14},{14,12},{1,3},{3,1},... | collective-permute-start | bytes 258056 | tf_op jit(solution)/shard_map/ppermute | solution.py:341
  82.1 0.9 %copy-start.6 = (f32[168,128]{1,0:T(8,128)S(1)}, f32[168,128]{1,0:T(8,128)}, u32[]{:S(2)}) copy-start(f32[168,128]{1,0:T(8,128)} %copy-done.5) | copy-start | bytes 258052
  83.0 2.8 %collective-permute-start.6 = (f32[344,128]{1,0:T(8,128)S(1)}, f32[344,128]{1,0:T(8,128)S(1)}, u32[]{:S(2)}, u32[]{:S(2)}) collective-permute-start(f32[344,128]{1,0:T(8,128)S(1)} %get-tuple-element.30.rows_a), channel_id=1, source_target_pairs={{0,1},{1,0},{2,3},{3,2},{4,5},{5,4},{6,7},{7,6},{8,9},{9,8},{10,11... | collective-permute-start | bytes 528392 | tf_op jit(solution)/shard_map/ppermute | solution.py:338
  83.1 2.7 %collective-permute-start.5 = (f32[168,128]{1,0:T(8,128)S(1)}, f32[168,128]{1,0:T(8,128)S(1)}, u32[]{:S(2)}, u32[]{:S(2)}) collective-permute-start(f32[168,128]{1,0:T(8,128)S(1)} %get-tuple-element.29.rows_b), channel_id=1, source_target_pairs={{0,1},{1,0},{2,3},{3,2},{4,5},{5,4},{6,7},{7,6},{8,9},{9,8},{10,11... | collective-permute-start | bytes 258056 | tf_op jit(solution)/shard_map/ppermute | solution.py:338

commit v6 on v5

v6 whole, which is shorter than its diff:
```python
import functools

import jax
import jax.numpy as jnp
from jax import lax
from jax.experimental import pallas as pl
from jax.experimental.pallas import tpu as pltpu
from jax.sharding import PartitionSpec as P

NB_DEV = 8
LANES = 128
SUB = 8
MIB = 1 << 20
UNROLL = 12


def accumulate_kernel(
    bank_size, n_owner, n_acc,
    place, proj_hbm, img_hbm, tra_hbm, w_hbm, pose_hbm, blocks_hbm, tiles_hbm,
    sent_away, kept_away, sent_stay, kept_stay,
    proj, img, tra, weight, spread, pose, blocks, tiles, idx_v, idx_s, square, cross,
    *rest,
):
    accs = rest[:n_acc]
    proj_sem, small_sem, table_sem, idx_sem = rest[n_acc:]
    n_pose, n_part = pose.shape
    n_tile, n_table = blocks.shape
    n_row = accs[0].shape[0]
    tile_rows = SUB * SUB
    part_rows = n_tile * tile_rows

    table_copies = [
        pltpu.make_async_copy(src, dst, table_sem.at[i])
        for i, (src, dst) in enumerate(((pose_hbm, pose), (blocks_hbm, blocks), (tiles_hbm, tiles)))
    ]
    small_copies = [
        pltpu.make_async_copy(img_hbm, img, small_sem.at[0]),
        pltpu.make_async_copy(tra_hbm, tra, small_sem.at[1]),
        pltpu.make_async_copy(w_hbm, weight, small_sem.at[2]),
    ]
    for copy in table_copies + small_copies:
        copy.start()

    def proj_copy(p):
        rows = pl.ds(pl.multiple_of(p * part_rows, part_rows), part_rows)
        return pltpu.make_async_copy(proj_hbm.at[rows, :], proj.at[rows, :], proj_sem.at[p])

    for p in range(n_part):
        proj_copy(p).start()

    zero = jnp.zeros((8 * SUB, LANES), jnp.float32)

    @pl.loop(0, n_row // (8 * SUB))
    def _(i):
        rows = pl.ds(pl.multiple_of(i * (8 * SUB), 8 * SUB), 8 * SUB)
        for acc in accs:
            acc[rows, :] = zero

    for copy in table_copies:
        copy.wait()
    lane = lax.broadcasted_iota(jnp.int32, (n_pose, n_table), 1)
    chosen = jnp.concatenate(
        [(pose[:, p : p + 1] == lane).astype(jnp.float32) for p in range(n_part)], axis=0
    ).astype(jnp.bfloat16)

    def look_up(table):
        return lax.dot_general(
            chosen, table[...].astype(jnp.float32).astype(jnp.bfloat16),
            (((1,), (1,)), ((), ())), preferred_element_type=jnp.float32,
        )

    idx_v[:, :n_tile] = ((look_up(blocks) * bank_size + look_up(tiles)) * SUB).astype(jnp.int32)
    idx_copy = pltpu.make_async_copy(idx_v, idx_s, idx_sem)
    idx_copy.start()

    for copy in small_copies:
        copy.wait()
    for p in range(n_part):
        spread[p * n_pose : (p + 1) * n_pose, :] = jnp.broadcast_to(weight[:, p : p + 1], (n_pose, LANES))

    @pl.loop(0, square.shape[0] // tile_rows)
    def _(i):
        rows = pl.ds(pl.multiple_of(i * tile_rows, tile_rows), tile_rows)
        t = tra[rows, :].astype(jnp.float32)
        square[rows, :] = t * t
        cross[rows, :] = t * img[rows, :].astype(jnp.float32)

    sublane = lax.broadcasted_iota(jnp.int32, (SUB, LANES), 0)
    bits = [(sublane & (1 << t)) != 0 for t in range(3)]

    def terms(p, j, unit, weights):
        first = pl.multiple_of(unit * tile_rows, tile_rows)
        cell = (j * (n_part // SUB) + p // SUB) * tile_rows + p % SUB
        turned = []
        for c in range(0, SUB, 2):
            pair = proj[pl.ds(first + c * SUB, 2 * SUB), :].astype(jnp.float32)
            for h in range(2):
                x = pair[h * SUB : (h + 1) * SUB]
                row = pl.ds(cell + (c + h) * SUB, 1)
                value = (square[row, :] * x - cross[row, :]) * weights
                turned.append(pltpu.roll(value, c + h, 0) if c + h else value)
        for t, bit in enumerate(bits):
            turned = [jnp.where(bit, turned[(i + (1 << t)) % SUB], turned[i]) for i in range(SUB)]
        result = []
        for k in range(n_pose):
            back = (k % n_acc - k) % SUB
            value = turned[-k % SUB]
            result.append(pltpu.roll(value, back, 0) if back else value)
        return result

    def add_rows(p, j, values):
        at = [idx_s[p * n_pose + k, j] for k in range(n_pose)]
        rows = [pl.ds(pl.multiple_of(at[k], SUB), SUB) for k in range(n_pose)]
        old = [accs[k % n_acc][rows[k], :] for k in range(n_pose)]
        new = []
        for k in range(n_pose):
            total = old[k] + values[k]
            for m in range(k % n_acc, k, n_acc):
                total += jnp.where(at[m] == at[k], 1.0, 0.0) * values[m]
            new.append(total)
        for k in range(n_pose):
            accs[k % n_acc][rows[k], :] = new[k]

    idx_copy.wait()

    @pl.loop(0, n_part)
    def _(p):
        proj_copy(p).wait()
        weights = spread[pl.ds(pl.multiple_of(p * n_pose, n_pose), n_pose), :]
        base = p * n_tile

        def ready(j):
            return terms(p, j, base + j, weights)

        @pl.loop(0, n_tile, step=UNROLL, init_carry=tuple(ready(0) + ready(1)))
        def _(j, carry):
            queue = [list(carry[:n_pose]), list(carry[n_pose:])]
            for u in range(UNROLL):
                ahead = j + u + 2
                queue.append(ready(ahead if u + 2 < UNROLL else jnp.minimum(ahead, n_tile - 1)))
                add_rows(p, j + u, queue.pop(0))
            return tuple(queue[0] + queue[1])

    rep, near, low, high = place[0], place[1], place[2], place[3]
    half_rows = n_row // (n_owner * 2)
    part_size = half_rows // 2
    step = 16 * SUB

    def finish(out, part, h, other, owner, half):
        first = (owner * 2 + half) * half_rows + part * part_size

        @pl.loop(0, part_size // step)
        def _(i):
            rows = pl.ds(pl.multiple_of(first + i * step, step), step)
            total = accs[0][rows, :].reshape(step // SUB, SUB, LANES)
            for turn, acc in enumerate(accs[1:]):
                total += pltpu.roll(acc[rows, :].reshape(step // SUB, SUB, LANES), SUB - 1 - turn, 1)
            out[part, other, h, pl.ds(pl.multiple_of(i * step, step), step), :] = total.reshape(step, LANES)

    for sent, kept, away in ((sent_away, kept_away, 1), (sent_stay, kept_stay, 0)):

        @pl.loop(0, n_owner // 4)
        def _(h):
            for part in range(2):
                for other in range(2):
                    y = near ^ (other if part else away)
                    l = low ^ (away if part else other)
                    owner = ((high ^ h) * 2 + l) * 2 + y
                    finish(sent, part, h, other, owner, 1 - rep)
                    finish(kept, part, h, other, owner, rep)


def tiles_in_order(array):
    lead = array.shape[:-2]
    rows, cells = array.shape[-2:]
    array = array.reshape(lead + (rows // SUB, SUB, cells // LANES, LANES))
    return jnp.swapaxes(array, -3, -2).reshape(-1, LANES)


def accumulate(
    projections, images, transfer, pose_weights, pose_of, pose_blocks, pose_tiles,
    bank_size, n_owner, place,
):
    n_part, n_pose, n_tile, n_cell = projections.shape
    assert n_cell == SUB * LANES and n_pose == SUB and n_part % SUB == 0 and n_tile % UNROLL == 0
    n_row = n_owner * NB_DEV * bank_size * SUB
    n_acc = 4 if n_row * LANES * 4 <= 4 * MIB else 2
    projections = tiles_in_order(jnp.transpose(projections, (0, 2, 1, 3)))
    images = tiles_in_order(jnp.transpose(images, (1, 0, 2)))
    transfer = tiles_in_order(jnp.transpose(transfer, (1, 0, 2)))
    stay = functools.partial(pltpu.with_memory_space_constraint, memory_space=pltpu.HBM)
    hbm = pl.BlockSpec(memory_space=pltpu.HBM)
    smem = pl.BlockSpec(memory_space=pltpu.SMEM)
    vmem = pl.BlockSpec(memory_space=pltpu.VMEM)
    out = jax.ShapeDtypeStruct((2, 2, n_owner // 4, n_row // (n_owner * 4), LANES), jnp.float32)
    return pl.pallas_call(
        functools.partial(accumulate_kernel, bank_size, n_owner, n_acc),
        out_shape=[out] * 4,
        in_specs=[smem] + [hbm] * 7,
        out_specs=[vmem] * 4,
        scratch_shapes=[
            pltpu.VMEM(projections.shape, jnp.bfloat16),
            pltpu.VMEM(images.shape, jnp.bfloat16),
            pltpu.VMEM(transfer.shape, jnp.bfloat16),
            pltpu.VMEM((n_pose, n_part), jnp.float32),
            pltpu.VMEM((n_part * n_pose, LANES), jnp.float32),
            pltpu.VMEM((n_pose, n_part), jnp.int32),
            pltpu.VMEM(pose_blocks.shape[::-1], jnp.int32),
            pltpu.VMEM(pose_tiles.shape[::-1], jnp.int32),
            pltpu.VMEM((n_part * n_pose, LANES), jnp.int32),
            pltpu.SMEM((n_part * n_pose, LANES), jnp.int32),
            pltpu.VMEM(transfer.shape, jnp.float32),
            pltpu.VMEM(transfer.shape, jnp.float32),
        ]
        + [pltpu.VMEM((n_row, LANES), jnp.float32)] * n_acc
        + [
            pltpu.SemaphoreType.DMA((n_part,)),
            pltpu.SemaphoreType.DMA((3,)),
            pltpu.SemaphoreType.DMA((3,)),
            pltpu.SemaphoreType.DMA,
        ],
        compiler_params=pltpu.CompilerParams(vmem_limit_bytes=(40 if n_acc == 4 else 56) * MIB),
        name="accumulate",
    )(
        place, stay(projections), stay(images), stay(transfer),
        stay(pose_weights.T), stay(pose_of.T), stay(pose_blocks.T), stay(pose_tiles.T),
    )


def bank_kernel(place, own, other, bank, out_hbm, block, sem):
    bank_size, n_z, n_cell = bank.shape
    n_half = block.shape[0] // 2
    group = 2 * SUB
    rep = place[0]

    def block_copy(b):
        half = rep if b < n_half else 1 - rep
        return pltpu.make_async_copy(block.at[b], out_hbm.at[half * n_half + b % n_half], sem.at[b])

    for first in range(0, 2 * n_half, 2):
        source = own if first < n_half else other
        rows_of = [(first + b) % n_half * bank_size for b in range(2)]
        for c in range(n_cell // LANES):
            cols = slice(c * LANES, (c + 1) * LANES)

            @pl.loop(0, n_z // group)
            def _(g):
                rows = pl.ds(pl.multiple_of(g * group, group), group)
                weights = [bank[t, rows, cols] for t in range(bank_size)]
                for b in range(2):
                    total = None
                    for t in range(bank_size):
                        at = (rows_of[b] + t) * SUB + c
                        value = weights[t] * source[at : at + 1, :]
                        total = value if total is None else total + value
                    block[first + b, rows, cols] = total

        for b in range(2):
            block_copy(first + b).start()

    for b in range(2 * n_half):
        block_copy(b).wait()


def apply_bank(place, own, other, weight_bank):
    bank_size, n_z, n_cell = weight_bank.shape
    vmem = pl.BlockSpec(memory_space=pltpu.VMEM)
    return pl.pallas_call(
        bank_kernel,
        out_shape=jax.ShapeDtypeStruct((NB_DEV, n_z, n_cell), jnp.float32),
        in_specs=[pl.BlockSpec(memory_space=pltpu.SMEM), vmem, vmem, vmem],
        out_specs=pl.BlockSpec(memory_space=pl.ANY),
        scratch_shapes=[
            pltpu.VMEM((NB_DEV, n_z, n_cell), jnp.float32),
            pltpu.SemaphoreType.DMA((NB_DEV,)),
        ],
        compiler_params=pltpu.CompilerParams(vmem_limit_bytes=32 * MIB),
        name="apply_bank",
    )(place, own, other, weight_bank)


def body(
    projections, images, transfer, pose_weights, pose_of, pose_blocks, pose_tiles, weight_bank
):
    bank_size = weight_bank.shape[0]
    n_blk = lax.axis_size("blk")
    here = lax.axis_index("blk")
    place = jnp.stack([lax.axis_index("rep"), here & 1, (here >> 1) & 1, here >> 2]).astype(jnp.int32)
    sent_away, kept_away, sent_stay, kept_stay = accumulate(
        projections, images, transfer, pose_weights, pose_of, pose_blocks, pose_tiles,
        bank_size, n_blk, place,
    )

    def over_rep(array):
        return lax.ppermute(array, "rep", [(0, 1), (1, 0)])

    def over_blk(array, bits):
        return lax.ppermute(array, "blk", [(i, i ^ bits) for i in range(n_blk)])

    got_away, got_stay = over_rep(sent_away), over_rep(sent_stay)
    first = [kept_away[part] + got_away[part] for part in range(2)]
    first = [over_blk(first[0], 1), over_blk(first[1], 2)]
    second = [kept_stay[part] + got_stay[part] + first[part] for part in range(2)]
    got_second = [over_blk(second[0][1], 2), over_blk(second[1][1], 1)]
    third = jnp.stack([second[part][0] + got_second[part] for part in range(2)], axis=1)
    own = third[0]
    for high in range(1, n_blk // 4):
        own = own + over_blk(third[high], 4 * high)
    own = own.reshape(-1, LANES)
    return apply_bank(place, own, over_rep(own), weight_bank)


def solution(mesh):
    placed = (
        P(("groups", "blk", "rep"), None, None, None),
        P(("groups", "blk", "rep"), None, None),
        P(("groups", "blk", "rep"), None, None),
        P(("groups", "blk", "rep"), None),
        P(("groups", "blk", "rep"), None),
        P("groups", None),
        P("groups", None),
        P(),
    )
    return jax.shard_map(
        body,
        mesh=mesh,
        in_specs=placed,
        out_specs=P(("groups", "blk"), None, None),
        check_vma=False,
    )
```

time: 88.4 us -> 67.7 us (0.77)
  local copies, waits for them, and re-layouts: 6.08 us -> 0.04 us
  Pallas kernels: 31 us -> 25.3 us
  starting transfers between devices: 15.5 us -> 10 us
  waiting for transfers between devices: 35.3 us -> 31.6 us
    all_to_all x2 -> x0, waiting for transfers between devices: 13.5 us -> none  [over_far(): lax.all_to_all(array, 'blk', 0, 0, axis_index_groups=lines, tiled=True)]
    all_to_all x2 -> x0, starting transfers between devices: 11.3 us -> none  [over_far(): lax.all_to_all(array, 'blk', 0, 0, axis_index_groups=lines, tiled=True)]
    ppermute x2 -> x5, waiting for transfers between devices: 18.4 us -> 27.9 us  [over_blk(): return lax.ppermute(array, 'blk', [(i, i ^ bits) for i in range(n_blk)])]
    ppermute x2 -> x5, starting transfers between devices: 3.04 us -> 9.33 us  [over_blk(): return lax.ppermute(array, 'blk', [(i, i ^ bits) for i in range(n_blk)])]
    unnamed x16 -> x2, local copies, waits for them, and re-layouts: 6.08 us -> 0.01 us
    pallas_call x5 -> x1, Pallas kernels: 7.03 us -> 3.35 us  [apply_bank(): pl.pallas_call(bank_kernel, out_shape=jax.ShapeDtypeStruct((NB_DEV, n_z,...]
    pallas_call x1, Pallas kernels: 24 us -> 22 us  [accumulate(): pl.pallas_call(functools.partial(accumulate_kernel, bank_size, n_owner, n...]
    ppermute x5 -> x3, waiting for transfers between devices: 3.35 us -> 3.73 us  [over_rep(): return lax.ppermute(array, 'rep', [(0, 1), (1, 0)])]
  transfers between devices with their start and end apart: 9 -> 8, of which waited for: 5 -> 7; matrix products, arithmetic and copies ran while one was open for 0% -> 0% of each run, Pallas kernels for 2% -> 0%
where the time goes in v6:
time: 67.7 us; the launch traced here: 67.6 us
  waiting for transfers between devices  31.6 us (47%)
  Pallas kernels  25.3 us (37%)
  starting transfers between devices  10 us (15%)
    ppermute x5, waiting for transfers between devices, over_blk(): return lax.ppermute(array, 'blk', [(i, i ^ bits) for i in range(n_blk)])  27.9 us
    pallas_call x1, Pallas kernels, accumulate(): pl.pallas_call(functools.partial(accumulate_kernel, bank_size, n_owner, n...  22 us
    ppermute x5, starting transfers between devices, over_blk(): return lax.ppermute(array, 'blk', [(i, i ^ bits) for i in range(n_blk)])  9.33 us
    ppermute x3, waiting for transfers between devices, over_rep(): return lax.ppermute(array, 'rep', [(0, 1), (1, 0)])  3.73 us
    pallas_call x1, Pallas kernels, apply_bank(): pl.pallas_call(bank_kernel, out_shape=jax.ShapeDtypeStruct((NB_DEV, n_z,...  3.35 us
  transfers between devices with their start and end apart: 8, of which 7 were waited for; matrix products, arithmetic and copies ran while one was open for 0% of the time, Pallas kernels for 0%

profile of v6, /device:TPU:0, one launch (start us, length us, event | category | flops | bytes accessed | tf_op | source)
XLA Modules:
  0.0 67.6 jit_solution(11344261459658799243)
XLA Ops:
  0.0 0.1 pad_add_fusion.place
  0.1 22.0 %accumulate.1 = (f32[2,2,2,256,128]{4,3,2,1,0:T(8,128)S(1)}, f32[2,2,2,256,128]{4,3,2,1,0:T(8,128)S(1)}, f32[2,2,2,256,128]{4,3,2,1,0:T(8,128)S(1)}, f32[2,2,2,256,128]{4,3,2,1,0:T(8,128)S(1)}) custom-call(s32[4]{0:T(128)S(1)} %pad_add_fusion.place, bf16[36864,128]{1,0:T(8,128)(2,1)} %bitcast.72, bf16[4608,128]{1,0:T(8,128)(2,1)} %bitcast.73, ...), custom_call_target="tpu_custom_call" | custom-call | tf_op jit(solution)/shard_map/accumulate/pallas_call | solution.py:196
  22.0 0.5 collective-permute-start.1
  22.6 0.1 collective-permute-start
  22.6 2.2 %collective-permute-done.1 = f32[2,2,2,256,128]{4,3,2,1,0:T(8,128)S(1)} collective-permute-done((f32[2,2,2,256,128]{4,3,2,1,0:T(8,128)S(1)}, f32[2,2,2,256,128]{4,3,2,1,0:T(8,128)S(1)}, u32[]{:S(2)}, u32[]{:S(2)}) %collective-permute-start.1) | collective-permute-done | bytes 1048608 | tf_op jit(solution)/shard_map/ppermute | solution.py:295
  24.8 0.1 fusion.3
  25.0 3.0 %collective-permute-start.2 = (f32[2,2,256,128]{3,2,1,0:T(8,128)S(1)}, f32[2,2,256,128]{3,2,1,0:T(8,128)S(1)}, u32[]{:S(2)}, u32[]{:S(2)}) collective-permute-start(f32[2,2,256,128]{3,2,1,0:T(8,128)S(1)} %get-tuple-element.15), channel_id=1, source_target_pairs={{0,2},{2,0},{4,6},{6,4},{8,10},{10,8},{12,14},{14,12},{1,3},{3,1},... | collective-permute-start | bytes 1572872 | tf_op jit(solution)/shard_map/ppermute | solution.py:298
  27.9 1.6 %collective-permute-start.4 = (f32[2,2,256,128]{3,2,1,0:T(8,128)S(1)}, f32[2,2,256,128]{3,2,1,0:T(8,128)S(1)}, u32[]{:S(2)}, u32[]{:S(2)}) collective-permute-start(f32[2,2,256,128]{3,2,1,0:T(8,128)S(1)} %get-tuple-element.16), channel_id=1, source_target_pairs={{0,4},{2,6},{4,0},{6,2},{8,12},{10,14},{12,8},{14,10},{1,5},{3,7},... | collective-permute-start | bytes 1572872 | tf_op jit(solution)/shard_map/ppermute | solution.py:298
  29.5 0.0 collective-permute-done
  29.5 10.6 %collective-permute-done.2 = f32[2,2,256,128]{3,2,1,0:T(8,128)S(1)} collective-permute-done((f32[2,2,256,128]{3,2,1,0:T(8,128)S(1)}, f32[2,2,256,128]{3,2,1,0:T(8,128)S(1)}, u32[]{:S(2)}, u32[]{:S(2)}) %collective-permute-start.2) | collective-permute-done | bytes 524320 | tf_op jit(solution)/shard_map/ppermute | solution.py:298
  40.2 1.5 %collective-permute-done.4 = f32[2,2,256,128]{3,2,1,0:T(8,128)S(1)} collective-permute-done((f32[2,2,256,128]{3,2,1,0:T(8,128)S(1)}, f32[2,2,256,128]{3,2,1,0:T(8,128)S(1)}, u32[]{:S(2)}, u32[]{:S(2)}) %collective-permute-start.4) | collective-permute-done | bytes 524320 | tf_op jit(solution)/shard_map/ppermute | solution.py:298
  41.6 0.2 fusion.5
  41.9 0.0 copy-start
  41.9 0.4 collective-permute-start.5
  42.3 1.8 %collective-permute-start.3 = (f32[2,256,128]{2,1,0:T(8,128)S(1)}, f32[2,256,128]{2,1,0:T(8,128)S(1)}, u32[]{:S(2)}, u32[]{:S(2)}) collective-permute-start(f32[2,256,128]{2,1,0:T(8,128)S(1)} %slice_bitcast_fusion.2), channel_id=1, source_target_pairs={{0,4},{2,6},{4,0},{6,2},{8,12},{10,14},{12,8},{14,10},{1,5},{3,7},... | collective-permute-start | bytes 786440 | tf_op jit(solution)/shard_map/ppermute | solution.py:298
  44.1 5.0 %collective-permute-done.5 = f32[2,256,128]{2,1,0:T(8,128)S(1)} collective-permute-done((f32[2,256,128]{2,1,0:T(8,128)S(1)}, f32[2,256,128]{2,1,0:T(8,128)S(1)}, u32[]{:S(2)}, u32[]{:S(2)}) %collective-permute-start.5) | collective-permute-done | bytes 262176 | tf_op jit(solution)/shard_map/ppermute | solution.py:298
  49.2 0.5 collective-permute-done.3
  49.7 2.6 %collective-permute-start.6 = (f32[2,256,128]{2,1,0:T(8,128)S(1)}, f32[2,256,128]{2,1,0:T(8,128)S(1)}, u32[]{:S(2)}, u32[]{:S(2)}) collective-permute-start(f32[2,256,128]{2,1,0:T(8,128)S(1)} %fusion.9), channel_id=1, source_target_pairs={{0,8},{2,10},{4,12},{6,14},{8,0},{10,2},{12,4},{14,6},{1,9},{3,11}... | collective-permute-start | bytes 786440 | tf_op jit(solution)/shard_map/ppermute | solution.py:298
  52.3 10.3 %collective-permute-done.6 = f32[2,256,128]{2,1,0:T(8,128)S(1)} collective-permute-done((f32[2,256,128]{2,1,0:T(8,128)S(1)}, f32[2,256,128]{2,1,0:T(8,128)S(1)}, u32[]{:S(2)}, u32[]{:S(2)}) %collective-permute-start.6) | collective-permute-done | bytes 262176 | tf_op jit(solution)/shard_map/ppermute | solution.py:298
  62.6 0.1 collective-permute-start.7
  62.7 1.5 %collective-permute-done.7.other = f32[512,128]{1,0:T(8,128)S(1)} collective-permute-done((f32[512,128]{1,0:T(8,128)S(1)}, f32[512,128]{1,0:T(8,128)S(1)}, u32[]{:S(2)}, u32[]{:S(2)}) %collective-permute-start.7) | collective-permute-done | bytes 262176 | tf_op jit(solution)/shard_map/ppermute | solution.py:295
  64.2 0.0 copy-done
  64.2 3.4 %apply_bank.1 = f32[8,32,1024]{2,1,0:T(8,128)} custom-call(s32[4]{0:T(128)S(1)} %pad_add_fusion.place, f32[512,128]{1,0:T(8,128)S(1)} %bitcast.71, f32[512,128]{1,0:T(8,128)S(1)} %collective-permute-done.7.other, f32[16,32,1024]{2,1,0:T(8,128)S(1)} %copy-done), custom_call_target="tpu_custom_call" | custom-call | tf_op jit(solution)/shard_map/apply_bank/pallas_call | solution.py:268
  (6 shorter events, 0.1 us)
Async XLA Ops:
  22.0 2.8 %collective-permute-start.1 = (f32[2,2,2,256,128]{4,3,2,1,0:T(8,128)S(1)}, f32[2,2,2,256,128]{4,3,2,1,0:T(8,128)S(1)}, u32[]{:S(2)}, u32[]{:S(2)}) collective-permute-start(f32[2,2,2,256,128]{4,3,2,1,0:T(8,128)S(1)} %get-tuple-element.12), channel_id=1, source_target_pairs={{0,1},{1,0},{2,3},{3,2},{4,5},{5,4},{6,7},{7,6},{8,9},{9,8},{10,11... | collective-permute-start | bytes 3145736 | tf_op jit(solution)/shard_map/ppermute | solution.py:295
  22.6 7.0 %collective-permute-start = (f32[2,2,2,256,128]{4,3,2,1,0:T(8,128)S(1)}, f32[2,2,2,256,128]{4,3,2,1,0:T(8,128)S(1)}, u32[]{:S(2)}, u32[]{:S(2)}) collective-permute-start(f32[2,2,2,256,128]{4,3,2,1,0:T(8,128)S(1)} %get-tuple-element.10), channel_id=1, source_target_pairs={{0,1},{1,0},{2,3},{3,2},{4,5},{5,4},{6,7},{7,6},{8,9},{9,8},{10,11... | collective-permute-start | bytes 3145736 | tf_op jit(solution)/shard_map/ppermute | solution.py:295
  25.0 15.2 %collective-permute-start.2 = (f32[2,2,256,128]{3,2,1,0:T(8,128)S(1)}, f32[2,2,256,128]{3,2,1,0:T(8,128)S(1)}, u32[]{:S(2)}, u32[]{:S(2)}) collective-permute-start(f32[2,2,256,128]{3,2,1,0:T(8,128)S(1)} %get-tuple-element.15), channel_id=1, source_target_pairs={{0,2},{2,0},{4,6},{6,4},{8,10},{10,8},{12,14},{14,12},{1,3},{3,1},... | collective-permute-start | bytes 1572872 | tf_op jit(solution)/shard_map/ppermute | solution.py:298
  27.9 13.7 %collective-permute-start.4 = (f32[2,2,256,128]{3,2,1,0:T(8,128)S(1)}, f32[2,2,256,128]{3,2,1,0:T(8,128)S(1)}, u32[]{:S(2)}, u32[]{:S(2)}) collective-permute-start(f32[2,2,256,128]{3,2,1,0:T(8,128)S(1)} %get-tuple-element.16), channel_id=1, source_target_pairs={{0,4},{2,6},{4,0},{6,2},{8,12},{10,14},{12,8},{14,10},{1,5},{3,7},... | collective-permute-start | bytes 1572872 | tf_op jit(solution)/shard_map/ppermute | solution.py:298
  41.9 22.4 %copy-start = (f32[16,32,1024]{2,1,0:T(8,128)S(1)}, f32[16,32,1024]{2,1,0:T(8,128)}, u32[]{:S(2)}) copy-start(f32[16,32,1024]{2,1,0:T(8,128)} %bank.1) | copy-start | bytes 6291460
  41.9 7.3 %collective-permute-start.5 = (f32[2,256,128]{2,1,0:T(8,128)S(1)}, f32[2,256,128]{2,1,0:T(8,128)S(1)}, u32[]{:S(2)}, u32[]{:S(2)}) collective-permute-start(f32[2,256,128]{2,1,0:T(8,128)S(1)} %slice_bitcast_fusion), channel_id=1, source_target_pairs={{0,2},{2,0},{4,6},{6,4},{8,10},{10,8},{12,14},{14,12},{1,3},{3,1},... | collective-permute-start | bytes 786440 | tf_op jit(solution)/shard_map/ppermute | solution.py:298
  42.3 7.3 %collective-permute-start.3 = (f32[2,256,128]{2,1,0:T(8,128)S(1)}, f32[2,256,128]{2,1,0:T(8,128)S(1)}, u32[]{:S(2)}, u32[]{:S(2)}) collective-permute-start(f32[2,256,128]{2,1,0:T(8,128)S(1)} %slice_bitcast_fusion.2), channel_id=1, source_target_pairs={{0,4},{2,6},{4,0},{6,2},{8,12},{10,14},{12,8},{14,10},{1,5},{3,7},... | collective-permute-start | bytes 786440 | tf_op jit(solution)/shard_map/ppermute | solution.py:298
  49.7 12.9 %collective-permute-start.6 = (f32[2,256,128]{2,1,0:T(8,128)S(1)}, f32[2,256,128]{2,1,0:T(8,128)S(1)}, u32[]{:S(2)}, u32[]{:S(2)}) collective-permute-start(f32[2,256,128]{2,1,0:T(8,128)S(1)} %fusion.9), channel_id=1, source_target_pairs={{0,8},{2,10},{4,12},{6,14},{8,0},{10,2},{12,4},{14,6},{1,9},{3,11}... | collective-permute-start | bytes 786440 | tf_op jit(solution)/shard_map/ppermute | solution.py:298
  62.6 1.6 %collective-permute-start.7 = (f32[512,128]{1,0:T(8,128)S(1)}, f32[512,128]{1,0:T(8,128)S(1)}, u32[]{:S(2)}, u32[]{:S(2)}) collective-permute-start(f32[512,128]{1,0:T(8,128)S(1)} %bitcast.70), channel_id=1, source_target_pairs={{0,1},{1,0},{2,3},{3,2},{4,5},{5,4},{6,7},{7,6},{8,9},{9,8},{10,11... | collective-permute-start | bytes 786440 | tf_op jit(solution)/shard_map/ppermute | solution.py:295

commit v7 on v6

--- a/solution.py
+++ b/solution.py
@@ -12,17 +12,18 @@
 SUB = 8
 MIB = 1 << 20
 UNROLL = 12
+N_BUF = 4
 
 
 def accumulate_kernel(
     bank_size, n_owner, n_acc,
     place, proj_hbm, img_hbm, tra_hbm, w_hbm, pose_hbm, blocks_hbm, tiles_hbm,
     sent_away, kept_away, sent_stay, kept_stay,
-    proj, img, tra, weight, spread, pose, blocks, tiles, idx_v, idx_s, square, cross,
+    proj, img, tra, weight, pose, blocks, tiles, idx_v, idx_s, square, cross,
     *rest,
 ):
-    accs = rest[:n_acc]
-    proj_sem, small_sem, table_sem, idx_sem = rest[n_acc:]
+    parts, accs = rest[:N_BUF], rest[N_BUF : N_BUF + n_acc]
+    proj_sem, small_sem, table_sem, idx_sem = rest[N_BUF + n_acc :]
     n_pose, n_part = pose.shape
     n_tile, n_table = blocks.shape
     n_row = accs[0].shape[0]
@@ -65,19 +66,16 @@
 
     def look_up(table):
         return lax.dot_general(
-            chosen, table[...].astype(jnp.float32).astype(jnp.bfloat16),
+            table[...].astype(jnp.float32).astype(jnp.bfloat16), chosen,
             (((1,), (1,)), ((), ())), preferred_element_type=jnp.float32,
         )
 
-    idx_v[:, :n_tile] = ((look_up(blocks) * bank_size + look_up(tiles)) * SUB).astype(jnp.int32)
+    idx_v[...] = ((look_up(blocks) * bank_size + look_up(tiles)) * SUB).astype(jnp.int32)
     idx_copy = pltpu.make_async_copy(idx_v, idx_s, idx_sem)
     idx_copy.start()
 
     for copy in small_copies:
         copy.wait()
-    for p in range(n_part):
-        spread[p * n_pose : (p + 1) * n_pose, :] = jnp.broadcast_to(weight[:, p : p + 1], (n_pose, LANES))
-
     @pl.loop(0, square.shape[0] // tile_rows)
     def _(i):
         rows = pl.ds(pl.multiple_of(i * tile_rows, tile_rows), tile_rows)
@@ -85,61 +83,47 @@
         square[rows, :] = t * t
         cross[rows, :] = t * img[rows, :].astype(jnp.float32)
 
-    sublane = lax.broadcasted_iota(jnp.int32, (SUB, LANES), 0)
-    bits = [(sublane & (1 << t)) != 0 for t in range(3)]
-
-    def terms(p, j, unit, weights):
+    def stage(unit, part):
         first = pl.multiple_of(unit * tile_rows, tile_rows)
-        cell = (j * (n_part // SUB) + p // SUB) * tile_rows + p % SUB
-        turned = []
-        for c in range(0, SUB, 2):
-            pair = proj[pl.ds(first + c * SUB, 2 * SUB), :].astype(jnp.float32)
-            for h in range(2):
-                x = pair[h * SUB : (h + 1) * SUB]
-                row = pl.ds(cell + (c + h) * SUB, 1)
-                value = (square[row, :] * x - cross[row, :]) * weights
-                turned.append(pltpu.roll(value, c + h, 0) if c + h else value)
-        for t, bit in enumerate(bits):
-            turned = [jnp.where(bit, turned[(i + (1 << t)) % SUB], turned[i]) for i in range(SUB)]
-        result = []
-        for k in range(n_pose):
-            back = (k % n_acc - k) % SUB
-            value = turned[-k % SUB]
-            result.append(pltpu.roll(value, back, 0) if back else value)
-        return result
+        part[...] = proj[pl.ds(first, tile_rows), :].astype(jnp.float32)
+
+    def terms(p, j, part, weights):
+        cell = pl.ds((j * (n_part // SUB) + p // SUB) * tile_rows + p % SUB, SUB, stride=SUB)
+        tt, ti = square[cell, :], cross[cell, :]
+        return [(tt * part[pl.ds(k, SUB, stride=SUB), :] - ti) * weights[k] for k in range(n_pose)]
 
     def add_rows(p, j, values):
-        at = [idx_s[p * n_pose + k, j] for k in range(n_pose)]
-        rows = [pl.ds(pl.multiple_of(at[k], SUB), SUB) for k in range(n_pose)]
-        old = [accs[k % n_acc][rows[k], :] for k in range(n_pose)]
-        new = []
-        for k in range(n_pose):
-            total = old[k] + values[k]
-            for m in range(k % n_acc, k, n_acc):
-                total += jnp.where(at[m] == at[k], 1.0, 0.0) * values[m]
-            new.append(total)
-        for k in range(n_pose):
-            accs[k % n_acc][rows[k], :] = new[k]
+        for first in range(0, n_pose, n_acc):
+            group = range(first, first + n_acc)
+            rows = [pl.ds(pl.multiple_of(idx_s[j, p * n_pose + k], SUB), SUB) for k in group]
+            old = [accs[i][rows[i], :] for i in range(n_acc)]
+            for i, k in enumerate(group):
+                accs[i][rows[i], :] = old[i] + values[k]
 
     idx_copy.wait()
+    n_buf = len(parts)
 
     @pl.loop(0, n_part)
     def _(p):
         proj_copy(p).wait()
-        weights = spread[pl.ds(pl.multiple_of(p * n_pose, n_pose), n_pose), :]
+        weights = [jnp.full((SUB, LANES), weight[k, p], jnp.float32) for k in range(n_pose)]
         base = p * n_tile
-
-        def ready(j):
-            return terms(p, j, base + j, weights)
-
-        @pl.loop(0, n_tile, step=UNROLL, init_carry=tuple(ready(0) + ready(1)))
-        def _(j, carry):
-            queue = [list(carry[:n_pose]), list(carry[n_pose:])]
+        stage(base, parts[0])
+        stage(base + 1, parts[1])
+
+        @pl.loop(0, n_tile, step=UNROLL, init_carry=tuple(terms(p, 0, parts[0], weights)))
+        def _(j, values):
             for u in range(UNROLL):
                 ahead = j + u + 2
-                queue.append(ready(ahead if u + 2 < UNROLL else jnp.minimum(ahead, n_tile - 1)))
-                add_rows(p, j + u, queue.pop(0))
-            return tuple(queue[0] + queue[1])
+                stage(base + (ahead if u + 2 < UNROLL else jnp.minimum(ahead, n_tile - 1)), parts[(u + 2) % n_buf])
+                following = j + u + 1
+                later = terms(
+                    p, following if u + 1 < UNROLL else jnp.minimum(following, n_tile - 1),
+                    parts[(u + 1) % n_buf], weights,
+                )
+                add_rows(p, j + u, values)
+                values = later
+            return tuple(values)
 
     rep, near, low, high = place[0], place[1], place[2], place[3]
     half_rows = n_row // (n_owner * 2)
@@ -152,10 +136,10 @@
         @pl.loop(0, part_size // step)
         def _(i):
             rows = pl.ds(pl.multiple_of(first + i * step, step), step)
-            total = accs[0][rows, :].reshape(step // SUB, SUB, LANES)
-            for turn, acc in enumerate(accs[1:]):
-                total += pltpu.roll(acc[rows, :].reshape(step // SUB, SUB, LANES), SUB - 1 - turn, 1)
-            out[part, other, h, pl.ds(pl.multiple_of(i * step, step), step), :] = total.reshape(step, LANES)
+            total = accs[0][rows, :]
+            for acc in accs[1:]:
+                total += acc[rows, :]
+            out[part, other, h, pl.ds(pl.multiple_of(i * step, step), step), :] = total
 
     for sent, kept, away in ((sent_away, kept_away, 1), (sent_stay, kept_stay, 0)):
 
@@ -182,7 +166,7 @@
     bank_size, n_owner, place,
 ):
     n_part, n_pose, n_tile, n_cell = projections.shape
-    assert n_cell == SUB * LANES and n_pose == SUB and n_part % SUB == 0 and n_tile % UNROLL == 0
+    assert n_cell == SUB * LANES and n_pose == SUB and n_part % SUB == 0 and n_tile % UNROLL == 0 and UNROLL % N_BUF == 0
     n_row = n_owner * NB_DEV * bank_size * SUB
     n_acc = 4 if n_row * LANES * 4 <= 4 * MIB else 2
     projections = tiles_in_order(jnp.transpose(projections, (0, 2, 1, 3)))
@@ -202,16 +186,16 @@
             pltpu.VMEM(projections.shape, jnp.bfloat16),
             pltpu.VMEM(images.shape, jnp.bfloat16),
             pltpu.VMEM(transfer.shape, jnp.bfloat16),
-            pltpu.VMEM((n_pose, n_part), jnp.float32),
-            pltpu.VMEM((n_part * n_pose, LANES), jnp.float32),
+            pltpu.SMEM((n_pose, n_part), jnp.float32),
             pltpu.VMEM((n_pose, n_part), jnp.int32),
             pltpu.VMEM(pose_blocks.shape[::-1], jnp.int32),
             pltpu.VMEM(pose_tiles.shape[::-1], jnp.int32),
-            pltpu.VMEM((n_part * n_pose, LANES), jnp.int32),
-            pltpu.SMEM((n_part * n_pose, LANES), jnp.int32),
+            pltpu.VMEM((n_tile, n_part * n_pose), jnp.int32),
+            pltpu.SMEM((n_tile, n_part * n_pose), jnp.int32),
             pltpu.VMEM(transfer.shape, jnp.float32),
             pltpu.VMEM(transfer.shape, jnp.float32),
         ]
+        + [pltpu.VMEM((n_pose * SUB, LANES), jnp.float32)] * N_BUF
         + [pltpu.VMEM((n_row, LANES), jnp.float32)] * n_acc
         + [
             pltpu.SemaphoreType.DMA((n_part,)),
@@ -227,39 +211,27 @@
     )
 
 
-def bank_kernel(place, own, other, bank, out_hbm, block, sem):
+def bank_kernel(place, own, other, bank, out):
     bank_size, n_z, n_cell = bank.shape
-    n_half = block.shape[0] // 2
+    n_half = out.shape[0] // 2
     group = 2 * SUB
     rep = place[0]
 
-    def block_copy(b):
-        half = rep if b < n_half else 1 - rep
-        return pltpu.make_async_copy(block.at[b], out_hbm.at[half * n_half + b % n_half], sem.at[b])
-
-    for first in range(0, 2 * n_half, 2):
-        source = own if first < n_half else other
-        rows_of = [(first + b) % n_half * bank_size for b in range(2)]
-        for c in range(n_cell // LANES):
-            cols = slice(c * LANES, (c + 1) * LANES)
-
-            @pl.loop(0, n_z // group)
-            def _(g):
-                rows = pl.ds(pl.multiple_of(g * group, group), group)
-                weights = [bank[t, rows, cols] for t in range(bank_size)]
-                for b in range(2):
+    for c in range(n_cell // LANES):
+        cols = slice(c * LANES, (c + 1) * LANES)
+
+        @pl.loop(0, n_z // group)
+        def _(g):
+            rows = pl.ds(pl.multiple_of(g * group, group), group)
+            weights = [bank[t, rows, cols] for t in range(bank_size)]
+            for source, half in ((own, rep), (other, 1 - rep)):
+                for b in range(n_half):
                     total = None
                     for t in range(bank_size):
-                        at = (rows_of[b] + t) * SUB + c
+                        at = (b * bank_size + t) * SUB + c
                         value = weights[t] * source[at : at + 1, :]
                         total = value if total is None else total + value
-                    block[first + b, rows, cols] = total
-
-        for b in range(2):
-            block_copy(first + b).start()
-
-    for b in range(2 * n_half):
-        block_copy(b).wait()
+                    out[half * n_half + b, rows, cols] = total
 
 
 def apply_bank(place, own, other, weight_bank):
@@ -269,11 +241,7 @@
         bank_kernel,
         out_shape=jax.ShapeDtypeStruct((NB_DEV, n_z, n_cell), jnp.float32),
         in_specs=[pl.BlockSpec(memory_space=pltpu.SMEM), vmem, vmem, vmem],
-        out_specs=pl.BlockSpec(memory_space=pl.ANY),
-        scratch_shapes=[
-            pltpu.VMEM((NB_DEV, n_z, n_cell), jnp.float32),
-            pltpu.SemaphoreType.DMA((NB_DEV,)),
-        ],
+        out_specs=vmem,
         compiler_params=pltpu.CompilerParams(vmem_limit_bytes=32 * MIB),
         name="apply_bank",
     )(place, own, other, weight_bank)

time: 67.7 us -> 62.4 us (0.922)
  Pallas kernels: 25.3 us -> 20 us
    pallas_call x1, Pallas kernels: 22 us -> 17 us  [accumulate(): pl.pallas_call(functools.partial(accumulate_kernel, bank_size, n_owner, n...]
where the time goes in v7:
time: 62.4 us; the launch traced here: 62.3 us
  waiting for transfers between devices  31.6 us (51%)
  Pallas kernels  20 us (32%)
  starting transfers between devices  10.1 us (16%)
    ppermute x5, waiting for transfers between devices, over_blk(): return lax.ppermute(array, 'blk', [(i, i ^ bits) for i in range(n_blk)])  27.8 us
    pallas_call x1, Pallas kernels, accumulate(): pl.pallas_call(functools.partial(accumulate_kernel, bank_size, n_owner, n...  17 us
    ppermute x5, starting transfers between devices, over_blk(): return lax.ppermute(array, 'blk', [(i, i ^ bits) for i in range(n_blk)])  9.38 us
    ppermute x3, waiting for transfers between devices, over_rep(): return lax.ppermute(array, 'rep', [(0, 1), (1, 0)])  3.73 us
    pallas_call x1, Pallas kernels, apply_bank(): pl.pallas_call(bank_kernel, out_shape=jax.ShapeDtypeStruct((NB_DEV, n_z,...  2.97 us
  transfers between devices with their start and end apart: 8, of which 7 were waited for; matrix products, arithmetic and copies ran while one was open for 0% of the time, Pallas kernels for 0%

profile of v7, /device:TPU:0, one launch (start us, length us, event | category | flops | bytes accessed | tf_op | source)
XLA Modules:
  0.0 62.3 jit_solution(13985922052794191289)
XLA Ops:
  0.0 0.1 pad_add_fusion.place
  0.1 17.0 %accumulate.1 = (f32[2,2,2,256,128]{4,3,2,1,0:T(8,128)S(1)}, f32[2,2,2,256,128]{4,3,2,1,0:T(8,128)S(1)}, f32[2,2,2,256,128]{4,3,2,1,0:T(8,128)S(1)}, f32[2,2,2,256,128]{4,3,2,1,0:T(8,128)S(1)}) custom-call(s32[4]{0:T(128)S(1)} %pad_add_fusion.place, bf16[36864,128]{1,0:T(8,128)(2,1)} %bitcast.72, bf16[4608,128]{1,0:T(8,128)(2,1)} %bitcast.73, ...), custom_call_target="tpu_custom_call" | custom-call | tf_op jit(solution)/shard_map/accumulate/pallas_call | solution.py:180
  17.1 0.5 collective-permute-start.1
  17.6 0.1 collective-permute-start
  17.7 2.2 %collective-permute-done.1 = f32[2,2,2,256,128]{4,3,2,1,0:T(8,128)S(1)} collective-permute-done((f32[2,2,2,256,128]{4,3,2,1,0:T(8,128)S(1)}, f32[2,2,2,256,128]{4,3,2,1,0:T(8,128)S(1)}, u32[]{:S(2)}, u32[]{:S(2)}) %collective-permute-start.1) | collective-permute-done | bytes 1048608 | tf_op jit(solution)/shard_map/ppermute | solution.py:263
  19.9 0.1 fusion.3
  20.1 3.0 %collective-permute-start.2 = (f32[2,2,256,128]{3,2,1,0:T(8,128)S(1)}, f32[2,2,256,128]{3,2,1,0:T(8,128)S(1)}, u32[]{:S(2)}, u32[]{:S(2)}) collective-permute-start(f32[2,2,256,128]{3,2,1,0:T(8,128)S(1)} %get-tuple-element.15), channel_id=1, source_target_pairs={{0,2},{2,0},{4,6},{6,4},{8,10},{10,8},{12,14},{14,12},{1,3},{3,1},... | collective-permute-start | bytes 1572872 | tf_op jit(solution)/shard_map/ppermute | solution.py:266
  23.0 1.6 %collective-permute-start.4 = (f32[2,2,256,128]{3,2,1,0:T(8,128)S(1)}, f32[2,2,256,128]{3,2,1,0:T(8,128)S(1)}, u32[]{:S(2)}, u32[]{:S(2)}) collective-permute-start(f32[2,2,256,128]{3,2,1,0:T(8,128)S(1)} %get-tuple-element.16), channel_id=1, source_target_pairs={{0,4},{2,6},{4,0},{6,2},{8,12},{10,14},{12,8},{14,10},{1,5},{3,7},... | collective-permute-start | bytes 1572872 | tf_op jit(solution)/shard_map/ppermute | solution.py:266
  24.6 0.0 collective-permute-done
  24.6 10.7 %collective-permute-done.2 = f32[2,2,256,128]{3,2,1,0:T(8,128)S(1)} collective-permute-done((f32[2,2,256,128]{3,2,1,0:T(8,128)S(1)}, f32[2,2,256,128]{3,2,1,0:T(8,128)S(1)}, u32[]{:S(2)}, u32[]{:S(2)}) %collective-permute-start.2) | collective-permute-done | bytes 524320 | tf_op jit(solution)/shard_map/ppermute | solution.py:266
  35.3 1.5 %collective-permute-done.4 = f32[2,2,256,128]{3,2,1,0:T(8,128)S(1)} collective-permute-done((f32[2,2,256,128]{3,2,1,0:T(8,128)S(1)}, f32[2,2,256,128]{3,2,1,0:T(8,128)S(1)}, u32[]{:S(2)}, u32[]{:S(2)}) %collective-permute-start.4) | collective-permute-done | bytes 524320 | tf_op jit(solution)/shard_map/ppermute | solution.py:266
  36.7 0.2 fusion.5
  36.9 0.0 copy-start
  37.0 0.4 collective-permute-start.5
  37.4 1.8 %collective-permute-start.3 = (f32[2,256,128]{2,1,0:T(8,128)S(1)}, f32[2,256,128]{2,1,0:T(8,128)S(1)}, u32[]{:S(2)}, u32[]{:S(2)}) collective-permute-start(f32[2,256,128]{2,1,0:T(8,128)S(1)} %slice_bitcast_fusion.2), channel_id=1, source_target_pairs={{0,4},{2,6},{4,0},{6,2},{8,12},{10,14},{12,8},{14,10},{1,5},{3,7},... | collective-permute-start | bytes 786440 | tf_op jit(solution)/shard_map/ppermute | solution.py:266
  39.2 5.0 %collective-permute-done.5 = f32[2,256,128]{2,1,0:T(8,128)S(1)} collective-permute-done((f32[2,256,128]{2,1,0:T(8,128)S(1)}, f32[2,256,128]{2,1,0:T(8,128)S(1)}, u32[]{:S(2)}, u32[]{:S(2)}) %collective-permute-start.5) | collective-permute-done | bytes 262176 | tf_op jit(solution)/shard_map/ppermute | solution.py:266
  44.3 0.5 collective-permute-done.3
  44.8 2.7 %collective-permute-start.6 = (f32[2,256,128]{2,1,0:T(8,128)S(1)}, f32[2,256,128]{2,1,0:T(8,128)S(1)}, u32[]{:S(2)}, u32[]{:S(2)}) collective-permute-start(f32[2,256,128]{2,1,0:T(8,128)S(1)} %fusion.9), channel_id=1, source_target_pairs={{0,8},{2,10},{4,12},{6,14},{8,0},{10,2},{12,4},{14,6},{1,9},{3,11}... | collective-permute-start | bytes 786440 | tf_op jit(solution)/shard_map/ppermute | solution.py:266
  47.4 10.2 %collective-permute-done.6 = f32[2,256,128]{2,1,0:T(8,128)S(1)} collective-permute-done((f32[2,256,128]{2,1,0:T(8,128)S(1)}, f32[2,256,128]{2,1,0:T(8,128)S(1)}, u32[]{:S(2)}, u32[]{:S(2)}) %collective-permute-start.6) | collective-permute-done | bytes 262176 | tf_op jit(solution)/shard_map/ppermute | solution.py:266
  57.7 0.1 collective-permute-start.7
  57.8 1.5 %collective-permute-done.7.other = f32[512,128]{1,0:T(8,128)S(1)} collective-permute-done((f32[512,128]{1,0:T(8,128)S(1)}, f32[512,128]{1,0:T(8,128)S(1)}, u32[]{:S(2)}, u32[]{:S(2)}) %collective-permute-start.7) | collective-permute-done | bytes 262176 | tf_op jit(solution)/shard_map/ppermute | solution.py:263
  59.3 0.0 copy-done
  59.3 3.0 %apply_bank.1 = f32[8,32,1024]{2,1,0:T(8,128)} custom-call(s32[4]{0:T(128)S(1)} %pad_add_fusion.place, f32[512,128]{1,0:T(8,128)S(1)} %bitcast.71, f32[512,128]{1,0:T(8,128)S(1)} %collective-permute-done.7.other, f32[16,32,1024]{2,1,0:T(8,128)S(1)} %copy-done), custom_call_target="tpu_custom_call" | custom-call | tf_op jit(solution)/shard_map/apply_bank/pallas_call | solution.py:240
  (6 shorter events, 0.1 us)
Async XLA Ops:
  17.1 2.8 %collective-permute-start.1 = (f32[2,2,2,256,128]{4,3,2,1,0:T(8,128)S(1)}, f32[2,2,2,256,128]{4,3,2,1,0:T(8,128)S(1)}, u32[]{:S(2)}, u32[]{:S(2)}) collective-permute-start(f32[2,2,2,256,128]{4,3,2,1,0:T(8,128)S(1)} %get-tuple-element.12), channel_id=1, source_target_pairs={{0,1},{1,0},{2,3},{3,2},{4,5},{5,4},{6,7},{7,6},{8,9},{9,8},{10,11... | collective-permute-start | bytes 3145736 | tf_op jit(solution)/shard_map/ppermute | solution.py:263
  17.6 7.0 %collective-permute-start = (f32[2,2,2,256,128]{4,3,2,1,0:T(8,128)S(1)}, f32[2,2,2,256,128]{4,3,2,1,0:T(8,128)S(1)}, u32[]{:S(2)}, u32[]{:S(2)}) collective-permute-start(f32[2,2,2,256,128]{4,3,2,1,0:T(8,128)S(1)} %get-tuple-element.10), channel_id=1, source_target_pairs={{0,1},{1,0},{2,3},{3,2},{4,5},{5,4},{6,7},{7,6},{8,9},{9,8},{10,11... | collective-permute-start | bytes 3145736 | tf_op jit(solution)/shard_map/ppermute | solution.py:263
  20.1 15.2 %collective-permute-start.2 = (f32[2,2,256,128]{3,2,1,0:T(8,128)S(1)}, f32[2,2,256,128]{3,2,1,0:T(8,128)S(1)}, u32[]{:S(2)}, u32[]{:S(2)}) collective-permute-start(f32[2,2,256,128]{3,2,1,0:T(8,128)S(1)} %get-tuple-element.15), channel_id=1, source_target_pairs={{0,2},{2,0},{4,6},{6,4},{8,10},{10,8},{12,14},{14,12},{1,3},{3,1},... | collective-permute-start | bytes 1572872 | tf_op jit(solution)/shard_map/ppermute | solution.py:266
  23.0 13.7 %collective-permute-start.4 = (f32[2,2,256,128]{3,2,1,0:T(8,128)S(1)}, f32[2,2,256,128]{3,2,1,0:T(8,128)S(1)}, u32[]{:S(2)}, u32[]{:S(2)}) collective-permute-start(f32[2,2,256,128]{3,2,1,0:T(8,128)S(1)} %get-tuple-element.16), channel_id=1, source_target_pairs={{0,4},{2,6},{4,0},{6,2},{8,12},{10,14},{12,8},{14,10},{1,5},{3,7},... | collective-permute-start | bytes 1572872 | tf_op jit(solution)/shard_map/ppermute | solution.py:266
  36.9 22.4 %copy-start = (f32[16,32,1024]{2,1,0:T(8,128)S(1)}, f32[16,32,1024]{2,1,0:T(8,128)}, u32[]{:S(2)}) copy-start(f32[16,32,1024]{2,1,0:T(8,128)} %bank.1) | copy-start | bytes 6291460
  37.0 7.3 %collective-permute-start.5 = (f32[2,256,128]{2,1,0:T(8,128)S(1)}, f32[2,256,128]{2,1,0:T(8,128)S(1)}, u32[]{:S(2)}, u32[]{:S(2)}) collective-permute-start(f32[2,256,128]{2,1,0:T(8,128)S(1)} %slice_bitcast_fusion), channel_id=1, source_target_pairs={{0,2},{2,0},{4,6},{6,4},{8,10},{10,8},{12,14},{14,12},{1,3},{3,1},... | collective-permute-start | bytes 786440 | tf_op jit(solution)/shard_map/ppermute | solution.py:266
  37.4 7.3 %collective-permute-start.3 = (f32[2,256,128]{2,1,0:T(8,128)S(1)}, f32[2,256,128]{2,1,0:T(8,128)S(1)}, u32[]{:S(2)}, u32[]{:S(2)}) collective-permute-start(f32[2,256,128]{2,1,0:T(8,128)S(1)} %slice_bitcast_fusion.2), channel_id=1, source_target_pairs={{0,4},{2,6},{4,0},{6,2},{8,12},{10,14},{12,8},{14,10},{1,5},{3,7},... | collective-permute-start | bytes 786440 | tf_op jit(solution)/shard_map/ppermute | solution.py:266
  44.8 12.9 %collective-permute-start.6 = (f32[2,256,128]{2,1,0:T(8,128)S(1)}, f32[2,256,128]{2,1,0:T(8,128)S(1)}, u32[]{:S(2)}, u32[]{:S(2)}) collective-permute-start(f32[2,256,128]{2,1,0:T(8,128)S(1)} %fusion.9), channel_id=1, source_target_pairs={{0,8},{2,10},{4,12},{6,14},{8,0},{10,2},{12,4},{14,6},{1,9},{3,11}... | collective-permute-start | bytes 786440 | tf_op jit(solution)/shard_map/ppermute | solution.py:266
  57.7 1.6 %collective-permute-start.7 = (f32[512,128]{1,0:T(8,128)S(1)}, f32[512,128]{1,0:T(8,128)S(1)}, u32[]{:S(2)}, u32[]{:S(2)}) collective-permute-start(f32[512,128]{1,0:T(8,128)S(1)} %bitcast.70), channel_id=1, source_target_pairs={{0,1},{1,0},{2,3},{3,2},{4,5},{5,4},{6,7},{7,6},{8,9},{9,8},{10,11... | collective-permute-start | bytes 786440 | tf_op jit(solution)/shard_map/ppermute | solution.py:263

commit v8 on v7

--- a/solution.py
+++ b/solution.py
@@ -18,7 +18,7 @@
 def accumulate_kernel(
     bank_size, n_owner, n_acc,
     place, proj_hbm, img_hbm, tra_hbm, w_hbm, pose_hbm, blocks_hbm, tiles_hbm,
-    sent_away, kept_away, sent_stay, kept_stay,
+    sent_away_1, kept_away_1, sent_stay_1, kept_stay_1, sent_away_2, kept_away_2, sent_stay_2, kept_stay_2,
     proj, img, tra, weight, pose, blocks, tiles, idx_v, idx_s, square, cross,
     *rest,
 ):
@@ -49,14 +49,16 @@
     for p in range(n_part):
         proj_copy(p).start()
 
-    zero = jnp.zeros((8 * SUB, LANES), jnp.float32)
-
-    @pl.loop(0, n_row // (8 * SUB))
-    def _(i):
-        rows = pl.ds(pl.multiple_of(i * (8 * SUB), 8 * SUB), 8 * SUB)
-        for acc in accs:
-            acc[rows, :] = zero
-
+    zero = jnp.zeros((16 * SUB, LANES), jnp.float32)
+
+    def clear(half):
+        @pl.loop(0, n_row // (32 * SUB))
+        def _(i):
+            rows = pl.ds(pl.multiple_of(half * (n_row // 2) + i * (16 * SUB), 16 * SUB), 16 * SUB)
+            for acc in accs:
+                acc[rows, :] = zero
+
+    clear(0)
     for copy in table_copies:
         copy.wait()
     lane = lax.broadcasted_iota(jnp.int32, (n_pose, n_table), 1)
@@ -73,6 +75,7 @@
     idx_v[...] = ((look_up(blocks) * bank_size + look_up(tiles)) * SUB).astype(jnp.int32)
     idx_copy = pltpu.make_async_copy(idx_v, idx_s, idx_sem)
     idx_copy.start()
+    clear(1)
 
     for copy in small_copies:
         copy.wait()
@@ -93,12 +96,17 @@
         return [(tt * part[pl.ds(k, SUB, stride=SUB), :] - ti) * weights[k] for k in range(n_pose)]
 
     def add_rows(p, j, values):
-        for first in range(0, n_pose, n_acc):
-            group = range(first, first + n_acc)
-            rows = [pl.ds(pl.multiple_of(idx_s[j, p * n_pose + k], SUB), SUB) for k in group]
-            old = [accs[i][rows[i], :] for i in range(n_acc)]
-            for i, k in enumerate(group):
-                accs[i][rows[i], :] = old[i] + values[k]
+        at = [idx_s[j, p * n_pose + k] for k in range(n_pose)]
+        rows = [pl.ds(pl.multiple_of(at[k], SUB), SUB) for k in range(n_pose)]
+        old = [accs[k % n_acc][rows[k], :] for k in range(n_pose)]
+        new = []
+        for k in range(n_pose):
+            total = old[k]
+            for m in range(k % n_acc, k, n_acc):
+                total = jnp.where(at[m] == at[k], new[m], total)
+            new.append(total + values[k])
+        for k in range(n_pose):
+            accs[k % n_acc][rows[k], :] = new[k]
 
     idx_copy.wait()
     n_buf = len(parts)
@@ -127,13 +135,13 @@
 
     rep, near, low, high = place[0], place[1], place[2], place[3]
     half_rows = n_row // (n_owner * 2)
-    part_size = half_rows // 2
-    step = 16 * SUB
-
-    def finish(out, part, h, other, owner, half):
-        first = (owner * 2 + half) * half_rows + part * part_size
-
-        @pl.loop(0, part_size // step)
+    size = half_rows // 4
+    step = min(size, 16 * SUB)
+
+    def finish(out, block, part, other, h, owner, half):
+        first = (owner * 2 + half) * half_rows + block * size
+
+        @pl.loop(0, size // step)
         def _(i):
             rows = pl.ds(pl.multiple_of(first + i * step, step), step)
             total = accs[0][rows, :]
@@ -141,7 +149,10 @@
                 total += acc[rows, :]
             out[part, other, h, pl.ds(pl.multiple_of(i * step, step), step), :] = total
 
-    for sent, kept, away in ((sent_away, kept_away, 1), (sent_stay, kept_stay, 0)):
+    for group, sent, kept, away in (
+        (0, sent_away_1, kept_away_1, 1), (0, sent_stay_1, kept_stay_1, 0),
+        (1, sent_away_2, kept_away_2, 1), (1, sent_stay_2, kept_stay_2, 0),
+    ):
 
         @pl.loop(0, n_owner // 4)
         def _(h):
@@ -150,8 +161,8 @@
                     y = near ^ (other if part else away)
                     l = low ^ (away if part else other)
                     owner = ((high ^ h) * 2 + l) * 2 + y
-                    finish(sent, part, h, other, owner, 1 - rep)
-                    finish(kept, part, h, other, owner, rep)
+                    finish(sent, part * 2 + group, part, other, h, owner, 1 - rep)
+                    finish(kept, part * 2 + group, part, other, h, owner, rep)
 
 
 def tiles_in_order(array):
@@ -176,12 +187,12 @@
     hbm = pl.BlockSpec(memory_space=pltpu.HBM)
     smem = pl.BlockSpec(memory_space=pltpu.SMEM)
     vmem = pl.BlockSpec(memory_space=pltpu.VMEM)
-    out = jax.ShapeDtypeStruct((2, 2, n_owner // 4, n_row // (n_owner * 4), LANES), jnp.float32)
+    out = jax.ShapeDtypeStruct((2, 2, n_owner // 4, n_row // (n_owner * 8), LANES), jnp.float32)
     return pl.pallas_call(
         functools.partial(accumulate_kernel, bank_size, n_owner, n_acc),
-        out_shape=[out] * 4,
+        out_shape=[out] * 8,
         in_specs=[smem] + [hbm] * 7,
-        out_specs=[vmem] * 4,
+        out_specs=[vmem] * 8,
         scratch_shapes=[
             pltpu.VMEM(projections.shape, jnp.bfloat16),
             pltpu.VMEM(images.shape, jnp.bfloat16),
@@ -211,7 +222,31 @@
     )
 
 
-def bank_kernel(place, own, other, bank, out):
+def middle_kernel(kept_stay, got_stay, near_a, near_b, kept_away, got_away, away_a, away_b, own, next_a, next_b):
+    for part, got, away, following in ((0, near_a, away_a, next_a), (1, near_b, away_b, next_b)):
+        own[part] = kept_stay[part, 0] + got_stay[part, 0] + got[0]
+        away[...] = kept_stay[part, 1] + got_stay[part, 1] + got[1]
+        following[...] = kept_away[part] + got_away[part]
+
+
+def middle(*operands):
+    shape = operands[0].shape
+    vmem = pl.BlockSpec(memory_space=pltpu.VMEM)
+
+    def like(*lead):
+        return jax.ShapeDtypeStruct(lead + shape[2:], jnp.float32)
+
+    return pl.pallas_call(
+        middle_kernel,
+        out_shape=[like(), like(), like(2), like(2), like(2)],
+        in_specs=[vmem] * len(operands),
+        out_specs=[vmem] * 5,
+        compiler_params=pltpu.CompilerParams(vmem_limit_bytes=32 * MIB),
+        name="middle",
+    )(*operands)
+
+
+def bank_kernel(place, own_1, own_2, other_1, other_2, bank, out):
     bank_size, n_z, n_cell = bank.shape
     n_half = out.shape[0] // 2
     group = 2 * SUB
@@ -224,27 +259,27 @@
         def _(g):
             rows = pl.ds(pl.multiple_of(g * group, group), group)
             weights = [bank[t, rows, cols] for t in range(bank_size)]
-            for source, half in ((own, rep), (other, 1 - rep)):
+            for sources, half in (((own_1, own_2), rep), ((other_1, other_2), 1 - rep)):
                 for b in range(n_half):
                     total = None
                     for t in range(bank_size):
-                        at = (b * bank_size + t) * SUB + c
-                        value = weights[t] * source[at : at + 1, :]
+                        value = weights[t] * sources[b % 2][b // 2, t, c : c + 1, :]
                         total = value if total is None else total + value
                     out[half * n_half + b, rows, cols] = total
 
 
-def apply_bank(place, own, other, weight_bank):
+def apply_bank(place, sums, weight_bank):
     bank_size, n_z, n_cell = weight_bank.shape
     vmem = pl.BlockSpec(memory_space=pltpu.VMEM)
+    sums = [array.reshape(2, bank_size, SUB, LANES) for array in sums]
     return pl.pallas_call(
         bank_kernel,
         out_shape=jax.ShapeDtypeStruct((NB_DEV, n_z, n_cell), jnp.float32),
-        in_specs=[pl.BlockSpec(memory_space=pltpu.SMEM), vmem, vmem, vmem],
+        in_specs=[pl.BlockSpec(memory_space=pltpu.SMEM)] + [vmem] * 5,
         out_specs=vmem,
         compiler_params=pltpu.CompilerParams(vmem_limit_bytes=32 * MIB),
         name="apply_bank",
-    )(place, own, other, weight_bank)
+    )(place, *sums, weight_bank)
 
 
 def body(
@@ -254,7 +289,7 @@
     n_blk = lax.axis_size("blk")
     here = lax.axis_index("blk")
     place = jnp.stack([lax.axis_index("rep"), here & 1, (here >> 1) & 1, here >> 2]).astype(jnp.int32)
-    sent_away, kept_away, sent_stay, kept_stay = accumulate(
+    outs = accumulate(
         projections, images, transfer, pose_weights, pose_of, pose_blocks, pose_tiles,
         bank_size, n_blk, place,
     )
@@ -265,17 +300,30 @@
     def over_blk(array, bits):
         return lax.ppermute(array, "blk", [(i, i ^ bits) for i in range(n_blk)])
 
-    got_away, got_stay = over_rep(sent_away), over_rep(sent_stay)
-    first = [kept_away[part] + got_away[part] for part in range(2)]
-    first = [over_blk(first[0], 1), over_blk(first[1], 2)]
-    second = [kept_stay[part] + got_stay[part] + first[part] for part in range(2)]
-    got_second = [over_blk(second[0][1], 2), over_blk(second[1][1], 1)]
-    third = jnp.stack([second[part][0] + got_second[part] for part in range(2)], axis=1)
-    own = third[0]
-    for high in range(1, n_blk // 4):
-        own = own + over_blk(third[high], 4 * high)
-    own = own.reshape(-1, LANES)
-    return apply_bank(place, own, over_rep(own), weight_bank)
+    def last_step(own, got):
+        third = jnp.stack([own[part] + got[part] for part in range(2)], axis=1)
+        total = third[0]
+        for high in range(1, n_blk // 4):
+            total = total + over_blk(third[high], 4 * high)
+        return total
+
+    (sent_away_1, kept_away_1, sent_stay_1, kept_stay_1), (sent_away_2, kept_away_2, sent_stay_2, kept_stay_2) = (
+        outs[:4], outs[4:]
+    )
+    got_away_1, got_stay_1 = over_rep(sent_away_1), over_rep(sent_stay_1)
+    got_away_2, got_stay_2 = over_rep(sent_away_2), over_rep(sent_stay_2)
+    first_1 = [kept_away_1[part] + got_away_1[part] for part in range(2)]
+    near_1 = [over_blk(first_1[0], 1), over_blk(first_1[1], 2)]
+    away_a, away_b, own_1, first_2a, first_2b = middle(
+        kept_stay_1, got_stay_1, *near_1, kept_away_2, got_away_2
+    )
+    far_1 = [over_blk(away_a, 2), over_blk(away_b, 1)]
+    near_2 = [over_blk(first_2a, 1), over_blk(first_2b, 2)]
+    own_1 = last_step(own_1, far_1)
+    second_2 = [kept_stay_2[part] + got_stay_2[part] + near_2[part] for part in range(2)]
+    far_2 = [over_blk(second_2[0][1], 2), over_blk(second_2[1][1], 1)]
+    own_2 = last_step([second_2[0][0], second_2[1][0]], far_2)
+    return apply_bank(place, (own_1, own_2, over_rep(own_1), over_rep(own_2)), weight_bank)
 
 
 def solution(mesh):

time: 62.4 us -> 63.6 us (1.019)
  waiting for transfers between devices: 31.6 us -> 22.6 us
  starting transfers between devices: 10.1 us -> 17.7 us
  Pallas kernels: 20 us -> 22.6 us
    ppermute x5 -> x10, waiting for transfers between devices: 27.8 us -> 20.2 us  [over_blk(): return lax.ppermute(array, 'blk', [(i, i ^ bits) for i in range(n_blk)])]
    ppermute x5 -> x10, starting transfers between devices: 9.38 us -> 16.6 us  [over_blk(): return lax.ppermute(array, 'blk', [(i, i ^ bits) for i in range(n_blk)])]
    pallas_call x1, Pallas kernels: 17 us -> 19.5 us  [accumulate(): pl.pallas_call(functools.partial(accumulate_kernel, bank_size, n_owner, n...]
    ppermute x3 -> x6, waiting for transfers between devices: 3.73 us -> 2.36 us  [over_rep(): return lax.ppermute(array, 'rep', [(0, 1), (1, 0)])]
  transfers between devices with their start and end apart: 8 -> 16, of which waited for: 7 -> 11; matrix products, arithmetic and copies ran while one was open for 0% -> 1% of each run, Pallas kernels for 0% -> 0%
where the time goes in v8:
time: 63.6 us; the launch traced here: 63.4 us
  Pallas kernels  22.6 us (36%)
  waiting for transfers between devices  22.6 us (36%)
  starting transfers between devices  17.7 us (28%)
    ppermute x10, waiting for transfers between devices, over_blk(): return lax.ppermute(array, 'blk', [(i, i ^ bits) for i in range(n_blk)])  20.2 us
    pallas_call x1, Pallas kernels, accumulate(): pl.pallas_call(functools.partial(accumulate_kernel, bank_size, n_owner, n...  19.5 us
    ppermute x10, starting transfers between devices, over_blk(): return lax.ppermute(array, 'blk', [(i, i ^ bits) for i in range(n_blk)])  16.6 us
    pallas_call x1, Pallas kernels, apply_bank(): pl.pallas_call(bank_kernel, out_shape=jax.ShapeDtypeStruct((NB_DEV, n_z,...  2.97 us
    ppermute x6, waiting for transfers between devices, over_rep(): return lax.ppermute(array, 'rep', [(0, 1), (1, 0)])  2.36 us
  transfers between devices with their start and end apart: 16, of which 11 were waited for; matrix products, arithmetic and copies ran while one was open for 1% of the time, Pallas kernels for 0%

profile of v8, /device:TPU:0, one launch (start us, length us, event | category | flops | bytes accessed | tf_op | source)
XLA Modules:
  0.0 63.4 jit_solution(12288337901022022396)
XLA Ops:
  0.1 19.5 %accumulate.1 = (f32[2,2,2,128,128]{4,3,2,1,0:T(8,128)S(1)}, f32[2,2,2,128,128]{4,3,2,1,0:T(8,128)S(1)}, f32[2,2,2,128,128]{4,3,2,1,0:T(8,128)S(1)}, f32[2,2,2,1...) custom-call(s32[4]{0:T(128)S(1)} %pad_add_fusion.place, ...), custom_call_target="tpu_custom_call" | custom-call | tf_op jit(solution)/shard_map/accumulate/pallas_call | solution.py:191
  19.6 0.5 collective-permute-start.1
  20.2 0.4 collective-permute-start.4
  20.6 1.0 %collective-permute-done.1 = f32[2,2,2,128,128]{4,3,2,1,0:T(8,128)S(1)} collective-permute-done((f32[2,2,2,128,128]{4,3,2,1,0:T(8,128)S(1)}, f32[2,2,2,128,128]{4,3,2,1,0:T(8,128)S(1)}, u32[]{:S(2)}, u32[]{:S(2)}) %collective-permute-start.1) | collective-permute-done | bytes 524320 | tf_op jit(solution)/shard_map/ppermute | solution.py:298
  21.7 3.0 %collective-permute-start.3 = (f32[2,2,128,128]{3,2,1,0:T(8,128)S(1)}, f32[2,2,128,128]{3,2,1,0:T(8,128)S(1)}, u32[]{:S(2)}, u32[]{:S(2)}) collective-permute-start(f32[2,2,128,128]{3,2,1,0:T(8,128)S(1)} %get-tuple-element.33), channel_id=1, source_target_pairs={{0,4},{2,6},{4,0},{6,2},{8,12},{10,14},{12,8},{14,10},{1,5},{3,7},... | collective-permute-start | bytes 786440 | tf_op jit(solution)/shard_map/ppermute | solution.py:301
  24.7 1.5 %collective-permute-start.2 = (f32[2,2,128,128]{3,2,1,0:T(8,128)S(1)}, f32[2,2,128,128]{3,2,1,0:T(8,128)S(1)}, u32[]{:S(2)}, u32[]{:S(2)}) collective-permute-start(f32[2,2,128,128]{3,2,1,0:T(8,128)S(1)} %get-tuple-element.34), channel_id=1, source_target_pairs={{0,2},{2,0},{4,6},{6,4},{8,10},{10,8},{12,14},{14,12},{1,3},{3,1},... | collective-permute-start | bytes 786440 | tf_op jit(solution)/shard_map/ppermute | solution.py:301
  26.3 5.1 %collective-permute-done.3.near_b = f32[2,2,128,128]{3,2,1,0:T(8,128)S(1)} collective-permute-done((f32[2,2,128,128]{3,2,1,0:T(8,128)S(1)}, f32[2,2,128,128]{3,2,1,0:T(8,128)S(1)}, u32[]{:S(2)}, u32[]{:S(2)}) %collective-permute-start.3) | collective-permute-done | bytes 262176 | tf_op jit(solution)/shard_map/ppermute | solution.py:301
  31.3 1.5 %collective-permute-done.2.near_a = f32[2,2,128,128]{3,2,1,0:T(8,128)S(1)} collective-permute-done((f32[2,2,128,128]{3,2,1,0:T(8,128)S(1)}, f32[2,2,128,128]{3,2,1,0:T(8,128)S(1)}, u32[]{:S(2)}, u32[]{:S(2)}) %collective-permute-start.2) | collective-permute-done | bytes 262176 | tf_op jit(solution)/shard_map/ppermute | solution.py:301
  32.9 0.4 collective-permute-start.5
  33.4 1.6 %collective-permute-start.6 = (f32[2,128,128]{2,1,0:T(8,128)S(1)}, f32[2,128,128]{2,1,0:T(8,128)S(1)}, u32[]{:S(2)}, u32[]{:S(2)}) collective-permute-start(f32[2,128,128]{2,1,0:T(8,128)S(1)} %get-tuple-element.26), channel_id=1, source_target_pairs={{0,2},{2,0},{4,6},{6,4},{8,10},{10,8},{12,14},{14,12},{1,3},{3,1},... | collective-permute-start | bytes 393224 | tf_op jit(solution)/shard_map/ppermute | solution.py:301
  35.0 0.4 collective-permute-start.9
  35.4 1.7 %collective-permute-start.11 = (f32[2,2,128,128]{3,2,1,0:T(8,128)S(1)}, f32[2,2,128,128]{3,2,1,0:T(8,128)S(1)}, u32[]{:S(2)}, u32[]{:S(2)}) collective-permute-start(f32[2,2,128,128]{3,2,1,0:T(8,128)S(1)} %get-tuple-element.30), channel_id=1, source_target_pairs={{0,4},{2,6},{4,0},{6,2},{8,12},{10,14},{12,8},{14,10},{1,5},{3,7},... | collective-permute-start | bytes 786440 | tf_op jit(solution)/shard_map/ppermute | solution.py:301
  37.0 2.3 %collective-permute-done.5 = f32[2,128,128]{2,1,0:T(8,128)S(1)} collective-permute-done((f32[2,128,128]{2,1,0:T(8,128)S(1)}, f32[2,128,128]{2,1,0:T(8,128)S(1)}, u32[]{:S(2)}, u32[]{:S(2)}) %collective-permute-start.5) | collective-permute-done | bytes 131104 | tf_op jit(solution)/shard_map/ppermute | solution.py:301
  39.4 0.4 collective-permute-done.6
  39.9 2.7 %collective-permute-start.7 = (f32[2,128,128]{2,1,0:T(8,128)S(1)}, f32[2,128,128]{2,1,0:T(8,128)S(1)}, u32[]{:S(2)}, u32[]{:S(2)}) collective-permute-start(f32[2,128,128]{2,1,0:T(8,128)S(1)} %fusion.17), channel_id=1, source_target_pairs={{0,8},{2,10},{4,12},{6,14},{8,0},{10,2},{12,4},{14,6},{1,9},{3,11}... | collective-permute-start | bytes 393224 | tf_op jit(solution)/shard_map/ppermute | solution.py:301
  42.6 0.8 %collective-permute-done.9 = f32[2,2,128,128]{3,2,1,0:T(8,128)S(1)} collective-permute-done((f32[2,2,128,128]{3,2,1,0:T(8,128)S(1)}, f32[2,2,128,128]{3,2,1,0:T(8,128)S(1)}, u32[]{:S(2)}, u32[]{:S(2)}) %collective-permute-start.9) | collective-permute-done | bytes 262176 | tf_op jit(solution)/shard_map/ppermute | solution.py:301
  43.4 2.0 %collective-permute-done.11 = f32[2,2,128,128]{3,2,1,0:T(8,128)S(1)} collective-permute-done((f32[2,2,128,128]{3,2,1,0:T(8,128)S(1)}, f32[2,2,128,128]{3,2,1,0:T(8,128)S(1)}, u32[]{:S(2)}, u32[]{:S(2)}) %collective-permute-start.11) | collective-permute-done | bytes 262176 | tf_op jit(solution)/shard_map/ppermute | solution.py:301
  45.5 1.3 %collective-permute-start.12 = (f32[2,128,128]{2,1,0:T(8,128)S(1)}, f32[2,128,128]{2,1,0:T(8,128)S(1)}, u32[]{:S(2)}, u32[]{:S(2)}) collective-permute-start(f32[2,128,128]{2,1,0:T(8,128)S(1)} %slice_bitcast_fusion), channel_id=1, source_target_pairs={{0,2},{2,0},{4,6},{6,4},{8,10},{10,8},{12,14},{14,12},{1,3},{3,1},... | collective-permute-start | bytes 393224 | tf_op jit(solution)/shard_map/ppermute | solution.py:301
  47.2 3.3 %collective-permute-done.12 = f32[2,128,128]{2,1,0:T(8,128)S(1)} collective-permute-done((f32[2,128,128]{2,1,0:T(8,128)S(1)}, f32[2,128,128]{2,1,0:T(8,128)S(1)}, u32[]{:S(2)}, u32[]{:S(2)}) %collective-permute-start.12) | collective-permute-done | bytes 131104 | tf_op jit(solution)/shard_map/ppermute | solution.py:301
  50.5 1.3 %collective-permute-done.10 = f32[2,128,128]{2,1,0:T(8,128)S(1)} collective-permute-done((f32[2,128,128]{2,1,0:T(8,128)S(1)}, f32[2,128,128]{2,1,0:T(8,128)S(1)}, u32[]{:S(2)}, u32[]{:S(2)}) %collective-permute-start.10) | collective-permute-done | bytes 131104 | tf_op jit(solution)/shard_map/ppermute | solution.py:301
  51.9 3.4 %collective-permute-start.13 = (f32[2,128,128]{2,1,0:T(8,128)S(1)}, f32[2,128,128]{2,1,0:T(8,128)S(1)}, u32[]{:S(2)}, u32[]{:S(2)}) collective-permute-start(f32[2,128,128]{2,1,0:T(8,128)S(1)} %fusion.12), channel_id=1, source_target_pairs={{0,8},{2,10},{4,12},{6,14},{8,0},{10,2},{12,4},{14,6},{1,9},{3,11}... | collective-permute-start | bytes 393224 | tf_op jit(solution)/shard_map/ppermute | solution.py:301
  55.4 3.6 %collective-permute-done.13 = f32[2,128,128]{2,1,0:T(8,128)S(1)} collective-permute-done((f32[2,128,128]{2,1,0:T(8,128)S(1)}, f32[2,128,128]{2,1,0:T(8,128)S(1)}, u32[]{:S(2)}, u32[]{:S(2)}) %collective-permute-start.13) | collective-permute-done | bytes 131104 | tf_op jit(solution)/shard_map/ppermute | solution.py:301
  59.1 1.3 %collective-permute-done.15 = f32[2,128,128]{2,1,0:T(8,128)S(1)} collective-permute-done((f32[2,128,128]{2,1,0:T(8,128)S(1)}, f32[2,128,128]{2,1,0:T(8,128)S(1)}, u32[]{:S(2)}, u32[]{:S(2)}) %collective-permute-start.15) | collective-permute-done | bytes 131104 | tf_op jit(solution)/shard_map/ppermute | solution.py:298
  60.4 3.0 %apply_bank.1 = f32[8,32,1024]{2,1,0:T(8,128)} custom-call(s32[4]{0:T(128)S(1)} %pad_add_fusion.place, f32[2,16,8,128]{3,2,1,0:T(8,128)S(1)} %bitcast.93, f32[2,16,8,128]{3,2,1,0:T(8,128)S(1)} %bitcast.94, f32[2,16,8,128]{3,2,1,0:T(8,128)S(1)} %bitcast.95, f32[2,16,8,128]{3,2,1,0:T(8,128)S(1)} %bitcast.96, f32[16,32,1024]{2,1,0:T(8,128)S(1)} %copy-done), custom_call_target="tpu_custom_call" | custom-call | tf_op jit(solution)/shard_map/apply_bank/pallas_call | solution.py:275
  (25 shorter events, 1.2 us)
Async XLA Ops:
  19.6 2.1 %collective-permute-start.1 = (f32[2,2,2,128,128]{4,3,2,1,0:T(8,128)S(1)}, f32[2,2,2,128,128]{4,3,2,1,0:T(8,128)S(1)}, u32[]{:S(2)}, u32[]{:S(2)}) collective-permute-start(f32[2,2,2,128,128]{4,3,2,1,0:T(8,128)S(1)} %get-tuple-element.21), channel_id=1, source_target_pairs={{0,1},{1,0},{2,3},{3,2},{4,5},{5,4},{6,7},{7,6},{8,9},{9,8},{10,11... | collective-permute-start | bytes 1572872 | tf_op jit(solution)/shard_map/ppermute | solution.py:298
  20.1 6.2 %collective-permute-start = (f32[2,2,2,128,128]{4,3,2,1,0:T(8,128)S(1)}, f32[2,2,2,128,128]{4,3,2,1,0:T(8,128)S(1)}, u32[]{:S(2)}, u32[]{:S(2)}) collective-permute-start(f32[2,2,2,128,128]{4,3,2,1,0:T(8,128)S(1)} %get-tuple-element.19), channel_id=1, source_target_pairs={{0,1},{1,0},{2,3},{3,2},{4,5},{5,4},{6,7},{7,6},{8,9},{9,8},{10,11... | collective-permute-start | bytes 1572872 | tf_op jit(solution)/shard_map/ppermute | solution.py:298
  20.2 6.1 %collective-permute-start.4 = (f32[2,2,2,128,128]{4,3,2,1,0:T(8,128)S(1)}, f32[2,2,2,128,128]{4,3,2,1,0:T(8,128)S(1)}, u32[]{:S(2)}, u32[]{:S(2)}) collective-permute-start(f32[2,2,2,128,128]{4,3,2,1,0:T(8,128)S(1)} %get-tuple-element.23), channel_id=1, source_target_pairs={{0,1},{1,0},{2,3},{3,2},{4,5},{5,4},{6,7},{7,6},{8,9},{9,8},{10,11... | collective-permute-start | bytes 1572872 | tf_op jit(solution)/shard_map/ppermute | solution.py:298
  21.7 9.6 %collective-permute-start.3 = (f32[2,2,128,128]{3,2,1,0:T(8,128)S(1)}, f32[2,2,128,128]{3,2,1,0:T(8,128)S(1)}, u32[]{:S(2)}, u32[]{:S(2)}) collective-permute-start(f32[2,2,128,128]{3,2,1,0:T(8,128)S(1)} %get-tuple-element.33), channel_id=1, source_target_pairs={{0,4},{2,6},{4,0},{6,2},{8,12},{10,14},{12,8},{14,10},{1,5},{3,7},... | collective-permute-start | bytes 786440 | tf_op jit(solution)/shard_map/ppermute | solution.py:301
  24.7 8.1 %collective-permute-start.2 = (f32[2,2,128,128]{3,2,1,0:T(8,128)S(1)}, f32[2,2,128,128]{3,2,1,0:T(8,128)S(1)}, u32[]{:S(2)}, u32[]{:S(2)}) collective-permute-start(f32[2,2,128,128]{3,2,1,0:T(8,128)S(1)} %get-tuple-element.34), channel_id=1, source_target_pairs={{0,2},{2,0},{4,6},{6,4},{8,10},{10,8},{12,14},{14,12},{1,3},{3,1},... | collective-permute-start | bytes 786440 | tf_op jit(solution)/shard_map/ppermute | solution.py:301
  26.3 16.4 %collective-permute-start.8 = (f32[2,2,2,128,128]{4,3,2,1,0:T(8,128)S(1)}, f32[2,2,2,128,128]{4,3,2,1,0:T(8,128)S(1)}, u32[]{:S(2)}, u32[]{:S(2)}) collective-permute-start(f32[2,2,2,128,128]{4,3,2,1,0:T(8,128)S(1)} %get-tuple-element.28), channel_id=1, source_target_pairs={{0,1},{1,0},{2,3},{3,2},{4,5},{5,4},{6,7},{7,6},{8,9},{9,8},{10,11... | collective-permute-start | bytes 1572872 | tf_op jit(solution)/shard_map/ppermute | solution.py:298
  32.9 6.4 %collective-permute-start.5 = (f32[2,128,128]{2,1,0:T(8,128)S(1)}, f32[2,128,128]{2,1,0:T(8,128)S(1)}, u32[]{:S(2)}, u32[]{:S(2)}) collective-permute-start(f32[2,128,128]{2,1,0:T(8,128)S(1)} %get-tuple-element.25), channel_id=1, source_target_pairs={{0,4},{2,6},{4,0},{6,2},{8,12},{10,14},{12,8},{14,10},{1,5},{3,7},... | collective-permute-start | bytes 393224 | tf_op jit(solution)/shard_map/ppermute | solution.py:301
  33.4 6.4 %collective-permute-start.6 = (f32[2,128,128]{2,1,0:T(8,128)S(1)}, f32[2,128,128]{2,1,0:T(8,128)S(1)}, u32[]{:S(2)}, u32[]{:S(2)}) collective-permute-start(f32[2,128,128]{2,1,0:T(8,128)S(1)} %get-tuple-element.26), channel_id=1, source_target_pairs={{0,2},{2,0},{4,6},{6,4},{8,10},{10,8},{12,14},{14,12},{1,3},{3,1},... | collective-permute-start | bytes 393224 | tf_op jit(solution)/shard_map/ppermute | solution.py:301
  35.0 8.4 %collective-permute-start.9 = (f32[2,2,128,128]{3,2,1,0:T(8,128)S(1)}, f32[2,2,128,128]{3,2,1,0:T(8,128)S(1)}, u32[]{:S(2)}, u32[]{:S(2)}) collective-permute-start(f32[2,2,128,128]{3,2,1,0:T(8,128)S(1)} %get-tuple-element.29), channel_id=1, source_target_pairs={{0,2},{2,0},{4,6},{6,4},{8,10},{10,8},{12,14},{14,12},{1,3},{3,1},... | collective-permute-start | bytes 786440 | tf_op jit(solution)/shard_map/ppermute | solution.py:301
  35.4 10.0 %collective-permute-start.11 = (f32[2,2,128,128]{3,2,1,0:T(8,128)S(1)}, f32[2,2,128,128]{3,2,1,0:T(8,128)S(1)}, u32[]{:S(2)}, u32[]{:S(2)}) collective-permute-start(f32[2,2,128,128]{3,2,1,0:T(8,128)S(1)} %get-tuple-element.30), channel_id=1, source_target_pairs={{0,4},{2,6},{4,0},{6,2},{8,12},{10,14},{12,8},{14,10},{1,5},{3,7},... | collective-permute-start | bytes 786440 | tf_op jit(solution)/shard_map/ppermute | solution.py:301
  39.9 15.5 %collective-permute-start.7 = (f32[2,128,128]{2,1,0:T(8,128)S(1)}, f32[2,128,128]{2,1,0:T(8,128)S(1)}, u32[]{:S(2)}, u32[]{:S(2)}) collective-permute-start(f32[2,128,128]{2,1,0:T(8,128)S(1)} %fusion.17), channel_id=1, source_target_pairs={{0,8},{2,10},{4,12},{6,14},{8,0},{10,2},{12,4},{14,6},{1,9},{3,11}... | collective-permute-start | bytes 393224 | tf_op jit(solution)/shard_map/ppermute | solution.py:301
  45.4 15.1 %copy-start = (f32[16,32,1024]{2,1,0:T(8,128)S(1)}, f32[16,32,1024]{2,1,0:T(8,128)}, u32[]{:S(2)}) copy-start(f32[16,32,1024]{2,1,0:T(8,128)} %bank.1) | copy-start | bytes 6291460
  45.5 5.0 %collective-permute-start.12 = (f32[2,128,128]{2,1,0:T(8,128)S(1)}, f32[2,128,128]{2,1,0:T(8,128)S(1)}, u32[]{:S(2)}, u32[]{:S(2)}) collective-permute-start(f32[2,128,128]{2,1,0:T(8,128)S(1)} %slice_bitcast_fusion), channel_id=1, source_target_pairs={{0,2},{2,0},{4,6},{6,4},{8,10},{10,8},{12,14},{14,12},{1,3},{3,1},... | collective-permute-start | bytes 393224 | tf_op jit(solution)/shard_map/ppermute | solution.py:301
  46.8 5.0 %collective-permute-start.10 = (f32[2,128,128]{2,1,0:T(8,128)S(1)}, f32[2,128,128]{2,1,0:T(8,128)S(1)}, u32[]{:S(2)}, u32[]{:S(2)}) collective-permute-start(f32[2,128,128]{2,1,0:T(8,128)S(1)} %slice_bitcast_fusion.2), channel_id=1, source_target_pairs={{0,4},{2,6},{4,0},{6,2},{8,12},{10,14},{12,8},{14,10},{1,5},{3,7},... | collective-permute-start | bytes 393224 | tf_op jit(solution)/shard_map/ppermute | solution.py:301
  51.9 7.1 %collective-permute-start.13 = (f32[2,128,128]{2,1,0:T(8,128)S(1)}, f32[2,128,128]{2,1,0:T(8,128)S(1)}, u32[]{:S(2)}, u32[]{:S(2)}) collective-permute-start(f32[2,128,128]{2,1,0:T(8,128)S(1)} %fusion.12), channel_id=1, source_target_pairs={{0,8},{2,10},{4,12},{6,14},{8,0},{10,2},{12,4},{14,6},{1,9},{3,11}... | collective-permute-start | bytes 393224 | tf_op jit(solution)/shard_map/ppermute | solution.py:301
  55.4 3.8 %collective-permute-start.14 = (f32[2,128,128]{2,1,0:T(8,128)S(1)}, f32[2,128,128]{2,1,0:T(8,128)S(1)}, u32[]{:S(2)}, u32[]{:S(2)}) collective-permute-start(f32[2,128,128]{2,1,0:T(8,128)S(1)} %fusion.11), channel_id=1, source_target_pairs={{0,1},{1,0},{2,3},{3,2},{4,5},{5,4},{6,7},{7,6},{8,9},{9,8},{10,11... | collective-permute-start | bytes 393224 | tf_op jit(solution)/shard_map/ppermute | solution.py:298
  59.0 1.4 %collective-permute-start.15 = (f32[2,128,128]{2,1,0:T(8,128)S(1)}, f32[2,128,128]{2,1,0:T(8,128)S(1)}, u32[]{:S(2)}, u32[]{:S(2)}) collective-permute-start(f32[2,128,128]{2,1,0:T(8,128)S(1)} %fusion.8), channel_id=1, source_target_pairs={{0,1},{1,0},{2,3},{3,2},{4,5},{5,4},{6,7},{7,6},{8,9},{9,8},{10,11... | collective-permute-start | bytes 393224 | tf_op jit(solution)/shard_map/ppermute | solution.py:298

commit v9 on v7

--- a/solution.py
+++ b/solution.py
@@ -12,6 +12,7 @@
 SUB = 8
 MIB = 1 << 20
 UNROLL = 12
+ORDERS = ("ylh", "yhl", "lyh", "hyl")
 N_BUF = 4
 
 
@@ -19,7 +20,7 @@
     bank_size, n_owner, n_acc,
     place, proj_hbm, img_hbm, tra_hbm, w_hbm, pose_hbm, blocks_hbm, tiles_hbm,
     sent_away, kept_away, sent_stay, kept_stay,
-    proj, img, tra, weight, pose, blocks, tiles, idx_v, idx_s, square, cross,
+    proj, img, tra, weight, pose, blocks, tiles, idx_v, idx_s, same_v, same_s, square, cross,
     *rest,
 ):
     parts, accs = rest[:N_BUF], rest[N_BUF : N_BUF + n_acc]
@@ -49,14 +50,16 @@
     for p in range(n_part):
         proj_copy(p).start()
 
-    zero = jnp.zeros((8 * SUB, LANES), jnp.float32)
-
-    @pl.loop(0, n_row // (8 * SUB))
-    def _(i):
-        rows = pl.ds(pl.multiple_of(i * (8 * SUB), 8 * SUB), 8 * SUB)
-        for acc in accs:
-            acc[rows, :] = zero
-
+    zero = jnp.zeros((16 * SUB, LANES), jnp.float32)
+
+    def clear(half):
+        @pl.loop(0, n_row // (32 * SUB))
+        def _(i):
+            rows = pl.ds(pl.multiple_of(half * (n_row // 2) + i * (16 * SUB), 16 * SUB), 16 * SUB)
+            for acc in accs:
+                acc[rows, :] = zero
+
+    clear(0)
     for copy in table_copies:
         copy.wait()
     lane = lax.broadcasted_iota(jnp.int32, (n_pose, n_table), 1)
@@ -71,8 +74,17 @@
         )
 
     idx_v[...] = ((look_up(blocks) * bank_size + look_up(tiles)) * SUB).astype(jnp.int32)
-    idx_copy = pltpu.make_async_copy(idx_v, idx_s, idx_sem)
-    idx_copy.start()
+    for d in range(n_acc, n_pose, n_acc):
+        shifted = pltpu.roll(idx_v[...], idx_v.shape[1] - d, 1)
+        at = (d // n_acc - 1) * n_tile
+        same_v[at : at + n_tile, :] = jnp.where(idx_v[...] == shifted, 1.0, 0.0)
+    idx_copies = [
+        pltpu.make_async_copy(idx_v, idx_s, idx_sem.at[0]),
+        pltpu.make_async_copy(same_v, same_s, idx_sem.at[1]),
+    ]
+    for copy in idx_copies:
+        copy.start()
+    clear(1)
 
     for copy in small_copies:
         copy.wait()
@@ -93,14 +105,20 @@
         return [(tt * part[pl.ds(k, SUB, stride=SUB), :] - ti) * weights[k] for k in range(n_pose)]
 
     def add_rows(p, j, values):
-        for first in range(0, n_pose, n_acc):
-            group = range(first, first + n_acc)
-            rows = [pl.ds(pl.multiple_of(idx_s[j, p * n_pose + k], SUB), SUB) for k in group]
-            old = [accs[i][rows[i], :] for i in range(n_acc)]
-            for i, k in enumerate(group):
-                accs[i][rows[i], :] = old[i] + values[k]
-
-    idx_copy.wait()
+        at = [idx_s[j, p * n_pose + k] for k in range(n_pose)]
+        rows = [pl.ds(pl.multiple_of(at[k], SUB), SUB) for k in range(n_pose)]
+        old = [accs[k % n_acc][rows[k], :] for k in range(n_pose)]
+        new = []
+        for k in range(n_pose):
+            total = old[k] + values[k]
+            for m in range(k % n_acc, k, n_acc):
+                total += same_s[((k - m) // n_acc - 1) * n_tile + j, p * n_pose + m] * values[m]
+            new.append(total)
+        for k in range(n_pose):
+            accs[k % n_acc][rows[k], :] = new[k]
+
+    for copy in idx_copies:
+        copy.wait()
     n_buf = len(parts)
 
     @pl.loop(0, n_part)
@@ -127,31 +145,36 @@
 
     rep, near, low, high = place[0], place[1], place[2], place[3]
     half_rows = n_row // (n_owner * 2)
-    part_size = half_rows // 2
-    step = 16 * SUB
-
-    def finish(out, part, h, other, owner, half):
-        first = (owner * 2 + half) * half_rows + part * part_size
-
-        @pl.loop(0, part_size // step)
+    size = half_rows // len(ORDERS)
+    sizes = {"y": 2, "l": 2, "h": n_owner // 4}
+
+    def finish(out, place_of, part, owner, half):
+        first = pl.multiple_of((owner * 2 + half) * half_rows + part * size, size)
+        rows = pl.ds(first, size)
+        total = accs[0][rows, :]
+        for acc in accs[1:]:
+            total += acc[rows, :]
+        out[place_of] = total
+
+    def pieces(sent, kept, begin, part, firsts):
+        order = ORDERS[part]
+        inner = sizes[order[1]] * sizes[order[2]]
+
+        @pl.loop(0, len(firsts) * inner)
         def _(i):
-            rows = pl.ds(pl.multiple_of(first + i * step, step), step)
-            total = accs[0][rows, :]
-            for acc in accs[1:]:
-                total += acc[rows, :]
-            out[part, other, h, pl.ds(pl.multiple_of(i * step, step), step), :] = total
-
-    for sent, kept, away in ((sent_away, kept_away, 1), (sent_stay, kept_stay, 0)):
-
-        @pl.loop(0, n_owner // 4)
-        def _(h):
-            for part in range(2):
-                for other in range(2):
-                    y = near ^ (other if part else away)
-                    l = low ^ (away if part else other)
-                    owner = ((high ^ h) * 2 + l) * 2 + y
-                    finish(sent, part, h, other, owner, 1 - rep)
-                    finish(kept, part, h, other, owner, rep)
+            off = {order[0]: firsts[0] + i // inner}
+            off[order[1]] = i % inner // sizes[order[2]]
+            off[order[2]] = i % sizes[order[2]]
+            owner = ((high ^ off["h"]) * 2 + (low ^ off["l"])) * 2 + (near ^ off["y"])
+            finish(sent, begin + i, part, owner, 1 - rep)
+            finish(kept, begin + i, part, owner, rep)
+
+        return begin + len(firsts) * inner
+
+    for sent, kept, away in ((sent_away, kept_away, True), (sent_stay, kept_stay, False)):
+        begin = 0
+        for part, order in enumerate(ORDERS):
+            begin = pieces(sent, kept, begin, part, range(1, sizes[order[0]]) if away else range(1))
 
 
 def tiles_in_order(array):
@@ -176,10 +199,15 @@
     hbm = pl.BlockSpec(memory_space=pltpu.HBM)
     smem = pl.BlockSpec(memory_space=pltpu.SMEM)
     vmem = pl.BlockSpec(memory_space=pltpu.VMEM)
-    out = jax.ShapeDtypeStruct((2, 2, n_owner // 4, n_row // (n_owner * 4), LANES), jnp.float32)
+    n_high = n_owner // 4
+    size = n_row // (n_owner * 2 * len(ORDERS))
+
+    def out(pieces):
+        return jax.ShapeDtypeStruct((pieces, size, LANES), jnp.float32)
+
     return pl.pallas_call(
         functools.partial(accumulate_kernel, bank_size, n_owner, n_acc),
-        out_shape=[out] * 4,
+        out_shape=[out(6 * n_high + 4 * (n_high - 1))] * 2 + [out(6 * n_high + 4)] * 2,
         in_specs=[smem] + [hbm] * 7,
         out_specs=[vmem] * 4,
         scratch_shapes=[
@@ -192,6 +220,8 @@
             pltpu.VMEM(pose_tiles.shape[::-1], jnp.int32),
             pltpu.VMEM((n_tile, n_part * n_pose), jnp.int32),
             pltpu.SMEM((n_tile, n_part * n_pose), jnp.int32),
+            pltpu.VMEM((n_tile * (n_pose // n_acc - 1), n_part * n_pose), jnp.float32),
+            pltpu.SMEM((n_tile * (n_pose // n_acc - 1), n_part * n_pose), jnp.float32),
             pltpu.VMEM(transfer.shape, jnp.float32),
             pltpu.VMEM(transfer.shape, jnp.float32),
         ]
@@ -201,7 +231,7 @@
             pltpu.SemaphoreType.DMA((n_part,)),
             pltpu.SemaphoreType.DMA((3,)),
             pltpu.SemaphoreType.DMA((3,)),
-            pltpu.SemaphoreType.DMA,
+            pltpu.SemaphoreType.DMA((2,)),
         ],
         compiler_params=pltpu.CompilerParams(vmem_limit_bytes=(40 if n_acc == 4 else 56) * MIB),
         name="accumulate",
@@ -211,36 +241,115 @@
     )
 
 
+def in_vmem(kernel, name, pieces, *operands):
+    vmem = pl.BlockSpec(memory_space=pltpu.VMEM)
+    size = operands[0].shape[1:]
+    return pl.pallas_call(
+        kernel,
+        out_shape=[jax.ShapeDtypeStruct((n,) + size, jnp.float32) for n in pieces],
+        in_specs=[vmem] * len(operands),
+        out_specs=[vmem] * len(pieces),
+        compiler_params=pltpu.CompilerParams(vmem_limit_bytes=32 * MIB),
+        name=name,
+    )(*operands)
+
+
+def first_kernel(n_high, kept, got, to_y, to_l, *to_h):
+    begin = 0
+    for out in (to_y, to_l) + to_h:
+        rows = slice(begin, begin + out.shape[0])
+        out[...] = kept[rows] + got[rows]
+        begin += out.shape[0]
+
+
+def second_kernel(n_high, kept, got, got_y, got_l, *rest):
+    got_h, (own, to_y, to_l, *to_h) = rest[: n_high - 1], rest[n_high - 1 :]
+    n = 2 * n_high
+
+    def part_sum(begin, count, *arrivals):
+        total = kept[begin : begin + count] + got[begin : begin + count]
+        for array, at in arrivals:
+            total += array[at : at + count]
+        return total
+
+    ylh = part_sum(0, n, (got_y, 0))
+    yhl = part_sum(n, n, (got_y, n))
+    lyh = part_sum(2 * n, n, (got_l, 0))
+    hyl = part_sum(3 * n, 4, *[(array, 0) for array in got_h])
+    to_l[...] = ylh[n_high:]
+    for i, out in enumerate(to_h):
+        out[...] = yhl[2 * (i + 1) : 2 * (i + 2)]
+    to_y[:n_high] = lyh[n_high:]
+    to_y[n_high:] = hyl[2:]
+    own[:n_high] = ylh[:n_high]
+    own[n_high : n_high + 2] = yhl[:2]
+    own[n_high + 2 : 2 * n_high + 2] = lyh[:n_high]
+    own[2 * n_high + 2 :] = hyl[:2]
+
+
+def third_kernel(n_high, before, got_y, got_l, *rest):
+    got_h, (own, to_l, *to_h) = rest[: n_high - 1], rest[n_high - 1 :]
+    ylh = before[:n_high] + got_l[...]
+    yhl = before[n_high : n_high + 2]
+    for array in got_h:
+        yhl += array[...]
+    lyh = before[n_high + 2 : 2 * n_high + 2] + got_y[:n_high]
+    hyl = before[2 * n_high + 2 :] + got_y[n_high:]
+    for part, value in enumerate((ylh, yhl, lyh, hyl)):
+        own[part] = value[0]
+    to_l[0] = yhl[1]
+    to_l[1] = hyl[1]
+    for i, out in enumerate(to_h):
+        out[0] = ylh[i + 1]
+        out[1] = lyh[i + 1]
+
+
+def last_kernel(n_high, before, got_l, *rest):
+    got_h, (own,) = rest[: n_high - 1], rest[n_high - 1 :]
+    for part, (arrivals, at) in enumerate(((got_h, 0), ((got_l,), 0), (got_h, 1), ((got_l,), 1))):
+        total = before[part]
+        for array in arrivals:
+            total += array[at]
+        own[part] = total
+
+
 def bank_kernel(place, own, other, bank, out):
     bank_size, n_z, n_cell = bank.shape
     n_half = out.shape[0] // 2
     group = 2 * SUB
-    rep = place[0]
-
-    for c in range(n_cell // LANES):
-        cols = slice(c * LANES, (c + 1) * LANES)
-
-        @pl.loop(0, n_z // group)
-        def _(g):
-            rows = pl.ds(pl.multiple_of(g * group, group), group)
-            weights = [bank[t, rows, cols] for t in range(bank_size)]
-            for source, half in ((own, rep), (other, 1 - rep)):
-                for b in range(n_half):
+
+    def apply(halves):
+        for c in range(n_cell // LANES):
+            cols = slice(c * LANES, (c + 1) * LANES)
+
+            @pl.loop(0, n_z // group)
+            def _(g):
+                rows = pl.ds(pl.multiple_of(g * group, group), group)
+                weights = [bank[t, rows, cols] for t in range(bank_size)]
+                for b in range(2 * n_half):
                     total = None
                     for t in range(bank_size):
-                        at = (b * bank_size + t) * SUB + c
-                        value = weights[t] * source[at : at + 1, :]
+                        value = weights[t] * halves[b // n_half][b % n_half, t, c : c + 1, :]
                         total = value if total is None else total + value
-                    out[half * n_half + b, rows, cols] = total
+                    out[b, rows, cols] = total
+
+    @pl.when(place[0] == 0)
+    def _():
+        apply((own, other))
+
+    @pl.when(place[0] == 1)
+    def _():
+        apply((other, own))
 
 
 def apply_bank(place, own, other, weight_bank):
     bank_size, n_z, n_cell = weight_bank.shape
     vmem = pl.BlockSpec(memory_space=pltpu.VMEM)
+    own, other = [array.reshape(NB_DEV // 2, bank_size, SUB, LANES) for array in (own, other)]
     return pl.pallas_call(
         bank_kernel,
         out_shape=jax.ShapeDtypeStruct((NB_DEV, n_z, n_cell), jnp.float32),
-        in_specs=[pl.BlockSpec(memory_space=pltpu.SMEM), vmem, vmem, vmem],
+        in_specs=[pl.BlockSpec(memory_space=pltpu.SMEM)] + [vmem] * 3,
         out_specs=vmem,
         compiler_params=pltpu.CompilerParams(vmem_limit_bytes=32 * MIB),
         name="apply_bank",
@@ -252,6 +361,7 @@
 ):
     bank_size = weight_bank.shape[0]
     n_blk = lax.axis_size("blk")
+    n_high = n_blk // 4
     here = lax.axis_index("blk")
     place = jnp.stack([lax.axis_index("rep"), here & 1, (here >> 1) & 1, here >> 2]).astype(jnp.int32)
     sent_away, kept_away, sent_stay, kept_stay = accumulate(
@@ -265,16 +375,24 @@
     def over_blk(array, bits):
         return lax.ppermute(array, "blk", [(i, i ^ bits) for i in range(n_blk)])
 
+    def over_h(arrays):
+        return [over_blk(array, 4 * (i + 1)) for i, array in enumerate(arrays)]
+
+    def step(kernel, name, pieces, *operands):
+        return in_vmem(functools.partial(kernel, n_high), name, pieces, *operands)
+
+    n_h = n_high - 1
     got_away, got_stay = over_rep(sent_away), over_rep(sent_stay)
-    first = [kept_away[part] + got_away[part] for part in range(2)]
-    first = [over_blk(first[0], 1), over_blk(first[1], 2)]
-    second = [kept_stay[part] + got_stay[part] + first[part] for part in range(2)]
-    got_second = [over_blk(second[0][1], 2), over_blk(second[1][1], 1)]
-    third = jnp.stack([second[part][0] + got_second[part] for part in range(2)], axis=1)
-    own = third[0]
-    for high in range(1, n_blk // 4):
-        own = own + over_blk(third[high], 4 * high)
-    own = own.reshape(-1, LANES)
+    to_y, to_l, *to_h = step(first_kernel, "first", [4 * n_high, 2 * n_high] + [4] * n_h, kept_away, got_away)
+    got_h, got_y, got_l = over_h(to_h), over_blk(to_y, 1), over_blk(to_l, 2)
+    own, to_y, to_l, *to_h = step(
+        second_kernel, "second", [2 * n_high + 4, n_high + 2, n_high] + [2] * n_h,
+        kept_stay, got_stay, got_y, got_l, *got_h,
+    )
+    got_h, got_y, got_l = over_h(to_h), over_blk(to_y, 1), over_blk(to_l, 2)
+    own, to_l, *to_h = step(third_kernel, "third", [4, 2] + [2] * n_h, own, got_y, got_l, *got_h)
+    got_h, got_l = over_h(to_h), over_blk(to_l, 2)
+    (own,) = step(last_kernel, "last", [4], own, got_l, *got_h)
     return apply_bank(place, own, over_rep(own), weight_bank)
 
 

time: 62.4 us -> 62.2 us (level)
  waiting for transfers between devices: 31.6 us -> 25.3 us
  Pallas kernels: 20 us -> 23.5 us
  starting transfers between devices: 10.1 us -> 13.2 us
    ppermute x5 -> x8, waiting for transfers between devices: 27.8 us -> 21.6 us  [over_blk(): return lax.ppermute(array, 'blk', [(i, i ^ bits) for i in range(n_blk)])]
    ppermute x5 -> x8, starting transfers between devices: 9.38 us -> 12.5 us  [over_blk(): return lax.ppermute(array, 'blk', [(i, i ^ bits) for i in range(n_blk)])]
    pallas_call x1, Pallas kernels: 17 us -> 20 us  [accumulate(): pl.pallas_call(functools.partial(accumulate_kernel, bank_size, n_owner, n...]
  transfers between devices with their start and end apart: 8 -> 11, of which waited for: 7 -> 7; matrix products, arithmetic and copies ran while one was open for 0% -> 0% of each run, Pallas kernels for 0% -> 0%
where the time goes in v9:
time: 62.2 us; the launch traced here: 62.1 us
  waiting for transfers between devices  25.3 us (41%)
  Pallas kernels  23.5 us (38%)
  starting transfers between devices  13.2 us (21%)
    ppermute x8, waiting for transfers between devices, over_blk(): return lax.ppermute(array, 'blk', [(i, i ^ bits) for i in range(n_blk)])  21.6 us
    pallas_call x1, Pallas kernels, accumulate(): pl.pallas_call(functools.partial(accumulate_kernel, bank_size, n_owner, n...  20 us
    ppermute x8, starting transfers between devices, over_blk(): return lax.ppermute(array, 'blk', [(i, i ^ bits) for i in range(n_blk)])  12.5 us
    ppermute x3, waiting for transfers between devices, over_rep(): return lax.ppermute(array, 'rep', [(0, 1), (1, 0)])  3.73 us
    pallas_call x1, Pallas kernels, apply_bank(): pl.pallas_call(bank_kernel, out_shape=jax.ShapeDtypeStruct((NB_DEV, n_z,...  3.07 us
  transfers between devices with their start and end apart: 11, of which 7 were waited for; matrix products, arithmetic and copies ran while one was open for 0% of the time, Pallas kernels for 0%

profile of v9, /device:TPU:0, one launch (start us, length us, event | category | flops | bytes accessed | tf_op | source)
XLA Modules:
  0.0 62.1 jit_solution(14147456110572920897)
XLA Ops:
  0.0 0.1 pad_add_fusion.place
  0.1 20.0 %accumulate.1 = (f32[16,128,128]{2,1,0:T(8,128)S(1)}, f32[16,128,128]{2,1,0:T(8,128)S(1)}, f32[16,128,128]{2,1,0:T(8,128)S(1)}, f32[16,128,128]{2,1,0:T(8,128)S(1)}) custom-call(s32[4]{0:T(128)S(1)} %pad_add_fusion.place, bf16[36864,128]{1,0:T(8,128)(2,1)} %bitcast.33, bf16[4608,128]{1,0:T(8,128)(2,1)} %bitcast.34, bf16[4608,128]{1,0:T(8,128)(2,1)} %bitcast.35, ...), custom_call_target="tpu_custom_call" | custom-call | tf_op jit(solution)/shard_map/accumulate/pallas_call | solution.py:208
  20.1 0.5 collective-permute-start.1
  20.6 0.1 collective-permute-start
  20.7 2.2 %collective-permute-done.1.got = f32[16,128,128]{2,1,0:T(8,128)S(1)} collective-permute-done((f32[16,128,128]{2,1,0:T(8,128)S(1)}, f32[16,128,128]{2,1,0:T(8,128)S(1)}, u32[]{:S(2)}, u32[]{:S(2)}) %collective-permute-start.1) | collective-permute-done | bytes 1048608 | tf_op jit(solution)/shard_map/ppermute | solution.py:373
  22.9 0.1 first.1
  23.0 3.0 %collective-permute-start.2 = (f32[8,128,128]{2,1,0:T(8,128)S(1)}, f32[8,128,128]{2,1,0:T(8,128)S(1)}, u32[]{:S(2)}, u32[]{:S(2)}) collective-permute-start(f32[8,128,128]{2,1,0:T(8,128)S(1)} %get-tuple-element.23), channel_id=1, source_target_pairs={{0,2},{2,0},{4,6},{6,4},{8,10},{10,8},{12,14},{14,12},{1,3},{3,1},... | collective-permute-start | bytes 1572872 | tf_op jit(solution)/shard_map/ppermute | solution.py:376
  26.0 1.6 %collective-permute-start.3 = (f32[4,128,128]{2,1,0:T(8,128)S(1)}, f32[4,128,128]{2,1,0:T(8,128)S(1)}, u32[]{:S(2)}, u32[]{:S(2)}) collective-permute-start(f32[4,128,128]{2,1,0:T(8,128)S(1)} %get-tuple-element.24), channel_id=1, source_target_pairs={{0,4},{2,6},{4,0},{6,2},{8,12},{10,14},{12,8},{14,10},{1,5},{3,7},... | collective-permute-start | bytes 786440 | tf_op jit(solution)/shard_map/ppermute | solution.py:376
  27.6 2.6 %collective-permute-start.4 = (f32[4,128,128]{2,1,0:T(8,128)S(1)}, f32[4,128,128]{2,1,0:T(8,128)S(1)}, u32[]{:S(2)}, u32[]{:S(2)}) collective-permute-start(f32[4,128,128]{2,1,0:T(8,128)S(1)} %get-tuple-element.25), channel_id=1, source_target_pairs={{0,8},{2,10},{4,12},{6,14},{8,0},{10,2},{12,4},{14,6},{1,9},{3,11}... | collective-permute-start | bytes 786440 | tf_op jit(solution)/shard_map/ppermute | solution.py:376
  30.2 9.4 %collective-permute-done.3.got_l = f32[4,128,128]{2,1,0:T(8,128)S(1)} collective-permute-done((f32[4,128,128]{2,1,0:T(8,128)S(1)}, f32[4,128,128]{2,1,0:T(8,128)S(1)}, u32[]{:S(2)}, u32[]{:S(2)}) %collective-permute-start.3) | collective-permute-done | bytes 262176 | tf_op jit(solution)/shard_map/ppermute | solution.py:376
  39.6 2.4 %collective-permute-done.4.rest_0_ = f32[4,128,128]{2,1,0:T(8,128)S(1)} collective-permute-done((f32[4,128,128]{2,1,0:T(8,128)S(1)}, f32[4,128,128]{2,1,0:T(8,128)S(1)}, u32[]{:S(2)}, u32[]{:S(2)}) %collective-permute-start.4) | collective-permute-done | bytes 262176 | tf_op jit(solution)/shard_map/ppermute | solution.py:376
  41.9 0.2 second.1
  42.1 0.6 collective-permute-start.5
  42.7 0.4 collective-permute-start.6
  43.1 2.6 %collective-permute-start.7 = (f32[2,128,128]{2,1,0:T(8,128)S(1)}, f32[2,128,128]{2,1,0:T(8,128)S(1)}, u32[]{:S(2)}, u32[]{:S(2)}) collective-permute-start(f32[2,128,128]{2,1,0:T(8,128)S(1)} %get-tuple-element.29), channel_id=1, source_target_pairs={{0,8},{2,10},{4,12},{6,14},{8,0},{10,2},{12,4},{14,6},{1,9},{3,11}... | collective-permute-start | bytes 393224 | tf_op jit(solution)/shard_map/ppermute | solution.py:376
  45.7 3.8 %collective-permute-done.6.got_l = f32[2,128,128]{2,1,0:T(8,128)S(1)} collective-permute-done((f32[2,128,128]{2,1,0:T(8,128)S(1)}, f32[2,128,128]{2,1,0:T(8,128)S(1)}, u32[]{:S(2)}, u32[]{:S(2)}) %collective-permute-start.6) | collective-permute-done | bytes 131104 | tf_op jit(solution)/shard_map/ppermute | solution.py:376
  49.5 1.1 %collective-permute-done.7.rest_0_ = f32[2,128,128]{2,1,0:T(8,128)S(1)} collective-permute-done((f32[2,128,128]{2,1,0:T(8,128)S(1)}, f32[2,128,128]{2,1,0:T(8,128)S(1)}, u32[]{:S(2)}, u32[]{:S(2)}) %collective-permute-start.7) | collective-permute-done | bytes 131104 | tf_op jit(solution)/shard_map/ppermute | solution.py:376
  50.6 0.1 third.1
  50.7 0.1 collective-permute-start.8
  50.8 1.7 %collective-permute-start.9 = (f32[2,128,128]{2,1,0:T(8,128)S(1)}, f32[2,128,128]{2,1,0:T(8,128)S(1)}, u32[]{:S(2)}, u32[]{:S(2)}) collective-permute-start(f32[2,128,128]{2,1,0:T(8,128)S(1)} %get-tuple-element.32), channel_id=1, source_target_pairs={{0,8},{2,10},{4,12},{6,14},{8,0},{10,2},{12,4},{14,6},{1,9},{3,11}... | collective-permute-start | bytes 393224 | tf_op jit(solution)/shard_map/ppermute | solution.py:376
  52.5 4.9 %collective-permute-done.8.got_l = f32[2,128,128]{2,1,0:T(8,128)S(1)} collective-permute-done((f32[2,128,128]{2,1,0:T(8,128)S(1)}, f32[2,128,128]{2,1,0:T(8,128)S(1)}, u32[]{:S(2)}, u32[]{:S(2)}) %collective-permute-start.8) | collective-permute-done | bytes 131104 | tf_op jit(solution)/shard_map/ppermute | solution.py:376
  57.4 0.1 collective-permute-start.10
  57.5 1.5 %collective-permute-done.10 = f32[4,128,128]{2,1,0:T(8,128)S(1)} collective-permute-done((f32[4,128,128]{2,1,0:T(8,128)S(1)}, f32[4,128,128]{2,1,0:T(8,128)S(1)}, u32[]{:S(2)}, u32[]{:S(2)}) %collective-permute-start.10) | collective-permute-done | bytes 262176 | tf_op jit(solution)/shard_map/ppermute | solution.py:373
  59.0 3.1 %apply_bank.1 = f32[8,32,1024]{2,1,0:T(8,128)} custom-call(s32[4]{0:T(128)S(1)} %pad_add_fusion.place, f32[4,16,8,128]{3,2,1,0:T(8,128)S(1)} %bitcast.31, f32[4,16,8,128]{3,2,1,0:T(8,128)S(1)} %bitcast.32, f32[16,32,1024]{2,1,0:T(8,128)S(1)} %copy-done), custom_call_target="tpu_custom_call" | custom-call | tf_op jit(solution)/shard_map/apply_bank/pallas_call | solution.py:349
  (7 shorter events, 0.0 us)
Async XLA Ops:
  20.1 2.8 %collective-permute-start.1 = (f32[16,128,128]{2,1,0:T(8,128)S(1)}, f32[16,128,128]{2,1,0:T(8,128)S(1)}, u32[]{:S(2)}, u32[]{:S(2)}) collective-permute-start(f32[16,128,128]{2,1,0:T(8,128)S(1)} %get-tuple-element.22), channel_id=1, source_target_pairs={{0,1},{1,0},{2,3},{3,2},{4,5},{5,4},{6,7},{7,6},{8,9},{9,8},{10,11... | collective-permute-start | bytes 3145736 | tf_op jit(solution)/shard_map/ppermute | solution.py:373
  20.6 9.5 %collective-permute-start = (f32[16,128,128]{2,1,0:T(8,128)S(1)}, f32[16,128,128]{2,1,0:T(8,128)S(1)}, u32[]{:S(2)}, u32[]{:S(2)}) collective-permute-start(f32[16,128,128]{2,1,0:T(8,128)S(1)} %get-tuple-element.20), channel_id=1, source_target_pairs={{0,1},{1,0},{2,3},{3,2},{4,5},{5,4},{6,7},{7,6},{8,9},{9,8},{10,11... | collective-permute-start | bytes 3145736 | tf_op jit(solution)/shard_map/ppermute | solution.py:373
  23.0 18.9 %collective-permute-start.2 = (f32[8,128,128]{2,1,0:T(8,128)S(1)}, f32[8,128,128]{2,1,0:T(8,128)S(1)}, u32[]{:S(2)}, u32[]{:S(2)}) collective-permute-start(f32[8,128,128]{2,1,0:T(8,128)S(1)} %get-tuple-element.23), channel_id=1, source_target_pairs={{0,2},{2,0},{4,6},{6,4},{8,10},{10,8},{12,14},{14,12},{1,3},{3,1},... | collective-permute-start | bytes 1572872 | tf_op jit(solution)/shard_map/ppermute | solution.py:376
  26.0 13.6 %collective-permute-start.3 = (f32[4,128,128]{2,1,0:T(8,128)S(1)}, f32[4,128,128]{2,1,0:T(8,128)S(1)}, u32[]{:S(2)}, u32[]{:S(2)}) collective-permute-start(f32[4,128,128]{2,1,0:T(8,128)S(1)} %get-tuple-element.24), channel_id=1, source_target_pairs={{0,4},{2,6},{4,0},{6,2},{8,12},{10,14},{12,8},{14,10},{1,5},{3,7},... | collective-permute-start | bytes 786440 | tf_op jit(solution)/shard_map/ppermute | solution.py:376
  27.6 14.4 %collective-permute-start.4 = (f32[4,128,128]{2,1,0:T(8,128)S(1)}, f32[4,128,128]{2,1,0:T(8,128)S(1)}, u32[]{:S(2)}, u32[]{:S(2)}) collective-permute-start(f32[4,128,128]{2,1,0:T(8,128)S(1)} %get-tuple-element.25), channel_id=1, source_target_pairs={{0,8},{2,10},{4,12},{6,14},{8,0},{10,2},{12,4},{14,6},{1,9},{3,11}... | collective-permute-start | bytes 786440 | tf_op jit(solution)/shard_map/ppermute | solution.py:376
  41.9 17.1 %copy-start = (f32[16,32,1024]{2,1,0:T(8,128)S(1)}, f32[16,32,1024]{2,1,0:T(8,128)}, u32[]{:S(2)}) copy-start(f32[16,32,1024]{2,1,0:T(8,128)} %bank.1) | copy-start | bytes 6291460
  42.1 8.5 %collective-permute-start.5 = (f32[4,128,128]{2,1,0:T(8,128)S(1)}, f32[4,128,128]{2,1,0:T(8,128)S(1)}, u32[]{:S(2)}, u32[]{:S(2)}) collective-permute-start(f32[4,128,128]{2,1,0:T(8,128)S(1)} %get-tuple-element.27), channel_id=1, source_target_pairs={{0,2},{2,0},{4,6},{6,4},{8,10},{10,8},{12,14},{14,12},{1,3},{3,1},... | collective-permute-start | bytes 786440 | tf_op jit(solution)/shard_map/ppermute | solution.py:376
  42.7 6.9 %collective-permute-start.6 = (f32[2,128,128]{2,1,0:T(8,128)S(1)}, f32[2,128,128]{2,1,0:T(8,128)S(1)}, u32[]{:S(2)}, u32[]{:S(2)}) collective-permute-start(f32[2,128,128]{2,1,0:T(8,128)S(1)} %get-tuple-element.28), channel_id=1, source_target_pairs={{0,4},{2,6},{4,0},{6,2},{8,12},{10,14},{12,8},{14,10},{1,5},{3,7},... | collective-permute-start | bytes 393224 | tf_op jit(solution)/shard_map/ppermute | solution.py:376
  43.1 7.5 %collective-permute-start.7 = (f32[2,128,128]{2,1,0:T(8,128)S(1)}, f32[2,128,128]{2,1,0:T(8,128)S(1)}, u32[]{:S(2)}, u32[]{:S(2)}) collective-permute-start(f32[2,128,128]{2,1,0:T(8,128)S(1)} %get-tuple-element.29), channel_id=1, source_target_pairs={{0,8},{2,10},{4,12},{6,14},{8,0},{10,2},{12,4},{14,6},{1,9},{3,11}... | collective-permute-start | bytes 393224 | tf_op jit(solution)/shard_map/ppermute | solution.py:376
  50.7 6.7 %collective-permute-start.8 = (f32[2,128,128]{2,1,0:T(8,128)S(1)}, f32[2,128,128]{2,1,0:T(8,128)S(1)}, u32[]{:S(2)}, u32[]{:S(2)}) collective-permute-start(f32[2,128,128]{2,1,0:T(8,128)S(1)} %get-tuple-element.31), channel_id=1, source_target_pairs={{0,4},{2,6},{4,0},{6,2},{8,12},{10,14},{12,8},{14,10},{1,5},{3,7},... | collective-permute-start | bytes 393224 | tf_op jit(solution)/shard_map/ppermute | solution.py:376
  50.8 6.6 %collective-permute-start.9 = (f32[2,128,128]{2,1,0:T(8,128)S(1)}, f32[2,128,128]{2,1,0:T(8,128)S(1)}, u32[]{:S(2)}, u32[]{:S(2)}) collective-permute-start(f32[2,128,128]{2,1,0:T(8,128)S(1)} %get-tuple-element.32), channel_id=1, source_target_pairs={{0,8},{2,10},{4,12},{6,14},{8,0},{10,2},{12,4},{14,6},{1,9},{3,11}... | collective-permute-start | bytes 393224 | tf_op jit(solution)/shard_map/ppermute | solution.py:376
  57.4 1.6 %collective-permute-start.10 = (f32[4,128,128]{2,1,0:T(8,128)S(1)}, f32[4,128,128]{2,1,0:T(8,128)S(1)}, u32[]{:S(2)}, u32[]{:S(2)}) collective-permute-start(f32[4,128,128]{2,1,0:T(8,128)S(1)} %last.1), channel_id=1, source_target_pairs={{0,1},{1,0},{2,3},{3,2},{4,5},{5,4},{6,7},{7,6},{8,9},{9,8},{10,11... | collective-permute-start | bytes 786440 | tf_op jit(solution)/shard_map/ppermute | solution.py:373

commit v10 on v9

--- a/solution.py
+++ b/solution.py
@@ -16,11 +16,16 @@
 N_BUF = 4
 
 
+def position():
+    here = lax.axis_index("blk")
+    return lax.axis_index("rep"), here & 1, (here >> 1) & 1, here >> 2
+
+
 def accumulate_kernel(
     bank_size, n_owner, n_acc,
-    place, proj_hbm, img_hbm, tra_hbm, w_hbm, pose_hbm, blocks_hbm, tiles_hbm,
+    proj_hbm, img_hbm, tra_hbm, w_hbm, pose_hbm, blocks_hbm, tiles_hbm,
     sent_away, kept_away, sent_stay, kept_stay,
-    proj, img, tra, weight, pose, blocks, tiles, idx_v, idx_s, same_v, same_s, square, cross,
+    proj, weight, pose, blocks, tiles, idx_v, idx_s, square, cross,
     *rest,
 ):
     parts, accs = rest[:N_BUF], rest[N_BUF : N_BUF + n_acc]
@@ -35,6 +40,10 @@
         pltpu.make_async_copy(src, dst, table_sem.at[i])
         for i, (src, dst) in enumerate(((pose_hbm, pose), (blocks_hbm, blocks), (tiles_hbm, tiles)))
     ]
+    n_late = n_part // 4
+    n_small = img_hbm.shape[0]
+    img_first, tra_first = proj.shape[0] - n_small, proj.shape[0] - 2 * n_small
+    img, tra = proj.at[pl.ds(img_first, n_small), :], proj.at[pl.ds(tra_first, n_small), :]
     small_copies = [
         pltpu.make_async_copy(img_hbm, img, small_sem.at[0]),
         pltpu.make_async_copy(tra_hbm, tra, small_sem.at[1]),
@@ -47,7 +56,7 @@
         rows = pl.ds(pl.multiple_of(p * part_rows, part_rows), part_rows)
         return pltpu.make_async_copy(proj_hbm.at[rows, :], proj.at[rows, :], proj_sem.at[p])
 
-    for p in range(n_part):
+    for p in range(n_part - n_late):
         proj_copy(p).start()
 
     zero = jnp.zeros((16 * SUB, LANES), jnp.float32)
@@ -74,16 +83,8 @@
         )
 
     idx_v[...] = ((look_up(blocks) * bank_size + look_up(tiles)) * SUB).astype(jnp.int32)
-    for d in range(n_acc, n_pose, n_acc):
-        shifted = pltpu.roll(idx_v[...], idx_v.shape[1] - d, 1)
-        at = (d // n_acc - 1) * n_tile
-        same_v[at : at + n_tile, :] = jnp.where(idx_v[...] == shifted, 1.0, 0.0)
-    idx_copies = [
-        pltpu.make_async_copy(idx_v, idx_s, idx_sem.at[0]),
-        pltpu.make_async_copy(same_v, same_s, idx_sem.at[1]),
-    ]
-    for copy in idx_copies:
-        copy.start()
+    idx_copy = pltpu.make_async_copy(idx_v, idx_s, idx_sem)
+    idx_copy.start()
     clear(1)
 
     for copy in small_copies:
@@ -91,9 +92,13 @@
     @pl.loop(0, square.shape[0] // tile_rows)
     def _(i):
         rows = pl.ds(pl.multiple_of(i * tile_rows, tile_rows), tile_rows)
-        t = tra[rows, :].astype(jnp.float32)
+        t = proj[pl.ds(pl.multiple_of(tra_first + i * tile_rows, tile_rows), tile_rows), :].astype(jnp.float32)
+        x = proj[pl.ds(pl.multiple_of(img_first + i * tile_rows, tile_rows), tile_rows), :].astype(jnp.float32)
         square[rows, :] = t * t
-        cross[rows, :] = t * img[rows, :].astype(jnp.float32)
+        cross[rows, :] = t * x
+
+    for p in range(n_part - n_late, n_part):
+        proj_copy(p).start()
 
     def stage(unit, part):
         first = pl.multiple_of(unit * tile_rows, tile_rows)
@@ -105,20 +110,14 @@
         return [(tt * part[pl.ds(k, SUB, stride=SUB), :] - ti) * weights[k] for k in range(n_pose)]
 
     def add_rows(p, j, values):
-        at = [idx_s[j, p * n_pose + k] for k in range(n_pose)]
-        rows = [pl.ds(pl.multiple_of(at[k], SUB), SUB) for k in range(n_pose)]
-        old = [accs[k % n_acc][rows[k], :] for k in range(n_pose)]
-        new = []
-        for k in range(n_pose):
-            total = old[k] + values[k]
-            for m in range(k % n_acc, k, n_acc):
-                total += same_s[((k - m) // n_acc - 1) * n_tile + j, p * n_pose + m] * values[m]
-            new.append(total)
-        for k in range(n_pose):
-            accs[k % n_acc][rows[k], :] = new[k]
-
-    for copy in idx_copies:
-        copy.wait()
+        for first in range(0, n_pose, n_acc):
+            group = range(first, first + n_acc)
+            rows = [pl.ds(pl.multiple_of(idx_s[j, p * n_pose + k], SUB), SUB) for k in group]
+            old = [accs[i][rows[i], :] for i in range(n_acc)]
+            for i, k in enumerate(group):
+                accs[i][rows[i], :] = old[i] + values[k]
+
+    idx_copy.wait()
     n_buf = len(parts)
 
     @pl.loop(0, n_part)
@@ -143,7 +142,7 @@
                 values = later
             return tuple(values)
 
-    rep, near, low, high = place[0], place[1], place[2], place[3]
+    rep, near, low, high = position()
     half_rows = n_row // (n_owner * 2)
     size = half_rows // len(ORDERS)
     sizes = {"y": 2, "l": 2, "h": n_owner // 4}
@@ -186,18 +185,17 @@
 
 def accumulate(
     projections, images, transfer, pose_weights, pose_of, pose_blocks, pose_tiles,
-    bank_size, n_owner, place,
+    bank_size, n_owner,
 ):
     n_part, n_pose, n_tile, n_cell = projections.shape
     assert n_cell == SUB * LANES and n_pose == SUB and n_part % SUB == 0 and n_tile % UNROLL == 0 and UNROLL % N_BUF == 0
     n_row = n_owner * NB_DEV * bank_size * SUB
-    n_acc = 4 if n_row * LANES * 4 <= 4 * MIB else 2
+    n_acc = 8 if n_row * LANES * 4 <= 4 * MIB else 2
     projections = tiles_in_order(jnp.transpose(projections, (0, 2, 1, 3)))
     images = tiles_in_order(jnp.transpose(images, (1, 0, 2)))
     transfer = tiles_in_order(jnp.transpose(transfer, (1, 0, 2)))
     stay = functools.partial(pltpu.with_memory_space_constraint, memory_space=pltpu.HBM)
     hbm = pl.BlockSpec(memory_space=pltpu.HBM)
-    smem = pl.BlockSpec(memory_space=pltpu.SMEM)
     vmem = pl.BlockSpec(memory_space=pltpu.VMEM)
     n_high = n_owner // 4
     size = n_row // (n_owner * 2 * len(ORDERS))
@@ -208,20 +206,16 @@
     return pl.pallas_call(
         functools.partial(accumulate_kernel, bank_size, n_owner, n_acc),
         out_shape=[out(6 * n_high + 4 * (n_high - 1))] * 2 + [out(6 * n_high + 4)] * 2,
-        in_specs=[smem] + [hbm] * 7,
+        in_specs=[hbm] * 7,
         out_specs=[vmem] * 4,
         scratch_shapes=[
             pltpu.VMEM(projections.shape, jnp.bfloat16),
-            pltpu.VMEM(images.shape, jnp.bfloat16),
-            pltpu.VMEM(transfer.shape, jnp.bfloat16),
             pltpu.SMEM((n_pose, n_part), jnp.float32),
             pltpu.VMEM((n_pose, n_part), jnp.int32),
             pltpu.VMEM(pose_blocks.shape[::-1], jnp.int32),
             pltpu.VMEM(pose_tiles.shape[::-1], jnp.int32),
             pltpu.VMEM((n_tile, n_part * n_pose), jnp.int32),
             pltpu.SMEM((n_tile, n_part * n_pose), jnp.int32),
-            pltpu.VMEM((n_tile * (n_pose // n_acc - 1), n_part * n_pose), jnp.float32),
-            pltpu.SMEM((n_tile * (n_pose // n_acc - 1), n_part * n_pose), jnp.float32),
             pltpu.VMEM(transfer.shape, jnp.float32),
             pltpu.VMEM(transfer.shape, jnp.float32),
         ]
@@ -231,12 +225,12 @@
             pltpu.SemaphoreType.DMA((n_part,)),
             pltpu.SemaphoreType.DMA((3,)),
             pltpu.SemaphoreType.DMA((3,)),
-            pltpu.SemaphoreType.DMA((2,)),
+            pltpu.SemaphoreType.DMA,
         ],
-        compiler_params=pltpu.CompilerParams(vmem_limit_bytes=(40 if n_acc == 4 else 56) * MIB),
+        compiler_params=pltpu.CompilerParams(vmem_limit_bytes=(47 if n_acc == 8 else 56) * MIB),
         name="accumulate",
     )(
-        place, stay(projections), stay(images), stay(transfer),
+        stay(projections), stay(images), stay(transfer),
         stay(pose_weights.T), stay(pose_of.T), stay(pose_blocks.T), stay(pose_tiles.T),
     )
 
@@ -313,7 +307,7 @@
         own[part] = total
 
 
-def bank_kernel(place, own, other, bank, out):
+def bank_kernel(own, other, bank, out):
     bank_size, n_z, n_cell = bank.shape
     n_half = out.shape[0] // 2
     group = 2 * SUB
@@ -333,27 +327,29 @@
                         total = value if total is None else total + value
                     out[b, rows, cols] = total
 
-    @pl.when(place[0] == 0)
+    rep = position()[0]
+
+    @pl.when(rep == 0)
     def _():
         apply((own, other))
 
-    @pl.when(place[0] == 1)
+    @pl.when(rep == 1)
     def _():
         apply((other, own))
 
 
-def apply_bank(place, own, other, weight_bank):
+def apply_bank(own, other, weight_bank):
     bank_size, n_z, n_cell = weight_bank.shape
     vmem = pl.BlockSpec(memory_space=pltpu.VMEM)
     own, other = [array.reshape(NB_DEV // 2, bank_size, SUB, LANES) for array in (own, other)]
     return pl.pallas_call(
         bank_kernel,
         out_shape=jax.ShapeDtypeStruct((NB_DEV, n_z, n_cell), jnp.float32),
-        in_specs=[pl.BlockSpec(memory_space=pltpu.SMEM)] + [vmem] * 3,
+        in_specs=[vmem] * 3,
         out_specs=vmem,
         compiler_params=pltpu.CompilerParams(vmem_limit_bytes=32 * MIB),
         name="apply_bank",
-    )(place, own, other, weight_bank)
+    )(own, other, weight_bank)
 
 
 def body(
@@ -362,11 +358,9 @@
     bank_size = weight_bank.shape[0]
     n_blk = lax.axis_size("blk")
     n_high = n_blk // 4
-    here = lax.axis_index("blk")
-    place = jnp.stack([lax.axis_index("rep"), here & 1, (here >> 1) & 1, here >> 2]).astype(jnp.int32)
     sent_away, kept_away, sent_stay, kept_stay = accumulate(
         projections, images, transfer, pose_weights, pose_of, pose_blocks, pose_tiles,
-        bank_size, n_blk, place,
+        bank_size, n_blk,
     )
 
     def over_rep(array):
@@ -393,7 +387,7 @@
     own, to_l, *to_h = step(third_kernel, "third", [4, 2] + [2] * n_h, own, got_y, got_l, *got_h)
     got_h, got_l = over_h(to_h), over_blk(to_l, 2)
     (own,) = step(last_kernel, "last", [4], own, got_l, *got_h)
-    return apply_bank(place, own, over_rep(own), weight_bank)
+    return apply_bank(own, over_rep(own), weight_bank)
 
 
 def solution(mesh):

time: 62.2 us -> 59.9 us (0.963)
  Pallas kernels: 23.5 us -> 21.2 us
    pallas_call x1, Pallas kernels: 20 us -> 18.5 us  [accumulate(): pl.pallas_call(functools.partial(accumulate_kernel, bank_size, n_owner, n...]
    pallas_call x1, Pallas kernels: 3.07 us -> 2.36 us  [apply_bank(): pl.pallas_call(bank_kernel, out_shape=jax.ShapeDtypeStruct((NB_DEV, n_z,...]
where the time goes in v10:
time: 59.9 us; the launch traced here: 59.8 us
  waiting for transfers between devices  25.3 us (42%)
  Pallas kernels  21.2 us (35%)
  starting transfers between devices  13.2 us (22%)
    ppermute x8, waiting for transfers between devices, over_blk(): return lax.ppermute(array, 'blk', [(i, i ^ bits) for i in range(n_blk)])  21.6 us
    pallas_call x1, Pallas kernels, accumulate(): pl.pallas_call(functools.partial(accumulate_kernel, bank_size, n_owner, n...  18.5 us
    ppermute x8, starting transfers between devices, over_blk(): return lax.ppermute(array, 'blk', [(i, i ^ bits) for i in range(n_blk)])  12.5 us
    ppermute x3, waiting for transfers between devices, over_rep(): return lax.ppermute(array, 'rep', [(0, 1), (1, 0)])  3.73 us
    pallas_call x1, Pallas kernels, apply_bank(): pl.pallas_call(bank_kernel, out_shape=jax.ShapeDtypeStruct((NB_DEV, n_z,...  2.36 us
  transfers between devices with their start and end apart: 11, of which 7 were waited for; matrix products, arithmetic and copies ran while one was open for 0% of the time, Pallas kernels for 0%

profile of v10, /device:TPU:0, one launch (start us, length us, event | category | flops | bytes accessed | tf_op | source)
XLA Modules:
  0.0 59.8 jit_solution(18204919222220355121)
XLA Ops:
  0.0 18.5 %accumulate.1 = (f32[16,128,128]{2,1,0:T(8,128)S(1)}, f32[16,128,128]{2,1,0:T(8,128)S(1)}, f32[16,128,128]{2,1,0:T(8,128)S(1)}, f32[16,128,128]{2,1,0:T(8,128)S(1)}) custom-call(bf16[36864,128]{1,0:T(8,128)(2,1)} %bitcast.29, bf16[4608,128]{1,0:T(8,128)(2,1)} %bitcast.30, bf16[4608,128]{1,0:T(8,128)(2,1)} %bitcast.31, f32[8,16]{1,0:T(8,128)} %bitcast.34, ...), custom_call_target="tpu_custom_call" | custom-call | tf_op jit(solution)/shard_map/accumulate/pallas_call | solution.py:206
  18.5 0.5 collective-permute-start.1
  19.0 0.1 collective-permute-start
  19.1 2.2 %collective-permute-done.1.got = f32[16,128,128]{2,1,0:T(8,128)S(1)} collective-permute-done((f32[16,128,128]{2,1,0:T(8,128)S(1)}, f32[16,128,128]{2,1,0:T(8,128)S(1)}, u32[]{:S(2)}, u32[]{:S(2)}) %collective-permute-start.1) | collective-permute-done | bytes 1048608 | tf_op jit(solution)/shard_map/ppermute | solution.py:367
  21.3 0.1 first.1
  21.4 3.0 %collective-permute-start.2 = (f32[8,128,128]{2,1,0:T(8,128)S(1)}, f32[8,128,128]{2,1,0:T(8,128)S(1)}, u32[]{:S(2)}, u32[]{:S(2)}) collective-permute-start(f32[8,128,128]{2,1,0:T(8,128)S(1)} %get-tuple-element.23), channel_id=1, source_target_pairs={{0,2},{2,0},{4,6},{6,4},{8,10},{10,8},{12,14},{14,12},{1,3},{3,1},... | collective-permute-start | bytes 1572872 | tf_op jit(solution)/shard_map/ppermute | solution.py:370
  24.4 1.6 %collective-permute-start.3 = (f32[4,128,128]{2,1,0:T(8,128)S(1)}, f32[4,128,128]{2,1,0:T(8,128)S(1)}, u32[]{:S(2)}, u32[]{:S(2)}) collective-permute-start(f32[4,128,128]{2,1,0:T(8,128)S(1)} %get-tuple-element.24), channel_id=1, source_target_pairs={{0,4},{2,6},{4,0},{6,2},{8,12},{10,14},{12,8},{14,10},{1,5},{3,7},... | collective-permute-start | bytes 786440 | tf_op jit(solution)/shard_map/ppermute | solution.py:370
  26.0 2.6 %collective-permute-start.4 = (f32[4,128,128]{2,1,0:T(8,128)S(1)}, f32[4,128,128]{2,1,0:T(8,128)S(1)}, u32[]{:S(2)}, u32[]{:S(2)}) collective-permute-start(f32[4,128,128]{2,1,0:T(8,128)S(1)} %get-tuple-element.25), channel_id=1, source_target_pairs={{0,8},{2,10},{4,12},{6,14},{8,0},{10,2},{12,4},{14,6},{1,9},{3,11}... | collective-permute-start | bytes 786440 | tf_op jit(solution)/shard_map/ppermute | solution.py:370
  28.5 0.0 collective-permute-done.got
  28.5 9.4 %collective-permute-done.3.got_l = f32[4,128,128]{2,1,0:T(8,128)S(1)} collective-permute-done((f32[4,128,128]{2,1,0:T(8,128)S(1)}, f32[4,128,128]{2,1,0:T(8,128)S(1)}, u32[]{:S(2)}, u32[]{:S(2)}) %collective-permute-start.3) | collective-permute-done | bytes 262176 | tf_op jit(solution)/shard_map/ppermute | solution.py:370
  37.9 2.4 %collective-permute-done.4.rest_0_ = f32[4,128,128]{2,1,0:T(8,128)S(1)} collective-permute-done((f32[4,128,128]{2,1,0:T(8,128)S(1)}, f32[4,128,128]{2,1,0:T(8,128)S(1)}, u32[]{:S(2)}, u32[]{:S(2)}) %collective-permute-start.4) | collective-permute-done | bytes 262176 | tf_op jit(solution)/shard_map/ppermute | solution.py:370
  40.3 0.2 second.1
  40.5 0.6 collective-permute-start.5
  41.0 0.4 collective-permute-start.6
  41.5 2.6 %collective-permute-start.7 = (f32[2,128,128]{2,1,0:T(8,128)S(1)}, f32[2,128,128]{2,1,0:T(8,128)S(1)}, u32[]{:S(2)}, u32[]{:S(2)}) collective-permute-start(f32[2,128,128]{2,1,0:T(8,128)S(1)} %get-tuple-element.29), channel_id=1, source_target_pairs={{0,8},{2,10},{4,12},{6,14},{8,0},{10,2},{12,4},{14,6},{1,9},{3,11}... | collective-permute-start | bytes 393224 | tf_op jit(solution)/shard_map/ppermute | solution.py:370
  44.1 3.8 %collective-permute-done.6.got_l = f32[2,128,128]{2,1,0:T(8,128)S(1)} collective-permute-done((f32[2,128,128]{2,1,0:T(8,128)S(1)}, f32[2,128,128]{2,1,0:T(8,128)S(1)}, u32[]{:S(2)}, u32[]{:S(2)}) %collective-permute-start.6) | collective-permute-done | bytes 131104 | tf_op jit(solution)/shard_map/ppermute | solution.py:370
  47.9 1.1 %collective-permute-done.7.rest_0_ = f32[2,128,128]{2,1,0:T(8,128)S(1)} collective-permute-done((f32[2,128,128]{2,1,0:T(8,128)S(1)}, f32[2,128,128]{2,1,0:T(8,128)S(1)}, u32[]{:S(2)}, u32[]{:S(2)}) %collective-permute-start.7) | collective-permute-done | bytes 131104 | tf_op jit(solution)/shard_map/ppermute | solution.py:370
  49.0 0.1 third.1
  49.1 0.1 collective-permute-start.8
  49.2 1.7 %collective-permute-start.9 = (f32[2,128,128]{2,1,0:T(8,128)S(1)}, f32[2,128,128]{2,1,0:T(8,128)S(1)}, u32[]{:S(2)}, u32[]{:S(2)}) collective-permute-start(f32[2,128,128]{2,1,0:T(8,128)S(1)} %get-tuple-element.32), channel_id=1, source_target_pairs={{0,8},{2,10},{4,12},{6,14},{8,0},{10,2},{12,4},{14,6},{1,9},{3,11}... | collective-permute-start | bytes 393224 | tf_op jit(solution)/shard_map/ppermute | solution.py:370
  50.8 4.9 %collective-permute-done.8.got_l = f32[2,128,128]{2,1,0:T(8,128)S(1)} collective-permute-done((f32[2,128,128]{2,1,0:T(8,128)S(1)}, f32[2,128,128]{2,1,0:T(8,128)S(1)}, u32[]{:S(2)}, u32[]{:S(2)}) %collective-permute-start.8) | collective-permute-done | bytes 131104 | tf_op jit(solution)/shard_map/ppermute | solution.py:370
  55.8 0.1 collective-permute-start.10
  55.9 1.5 %collective-permute-done.10 = f32[4,128,128]{2,1,0:T(8,128)S(1)} collective-permute-done((f32[4,128,128]{2,1,0:T(8,128)S(1)}, f32[4,128,128]{2,1,0:T(8,128)S(1)}, u32[]{:S(2)}, u32[]{:S(2)}) %collective-permute-start.10) | collective-permute-done | bytes 262176 | tf_op jit(solution)/shard_map/ppermute | solution.py:367
  57.4 2.4 %apply_bank.1 = f32[8,32,1024]{2,1,0:T(8,128)} custom-call(f32[4,16,8,128]{3,2,1,0:T(8,128)S(1)} %bitcast.27, f32[4,16,8,128]{3,2,1,0:T(8,128)S(1)} %bitcast.28, f32[16,32,1024]{2,1,0:T(8,128)S(1)} %copy-done), custom_call_target="tpu_custom_call" | custom-call | tf_op jit(solution)/shard_map/apply_bank/pallas_call | solution.py:345
  (6 shorter events, 0.0 us)
Async XLA Ops:
  18.5 2.8 %collective-permute-start.1 = (f32[16,128,128]{2,1,0:T(8,128)S(1)}, f32[16,128,128]{2,1,0:T(8,128)S(1)}, u32[]{:S(2)}, u32[]{:S(2)}) collective-permute-start(f32[16,128,128]{2,1,0:T(8,128)S(1)} %get-tuple-element.22), channel_id=1, source_target_pairs={{0,1},{1,0},{2,3},{3,2},{4,5},{5,4},{6,7},{7,6},{8,9},{9,8},{10,11... | collective-permute-start | bytes 3145736 | tf_op jit(solution)/shard_map/ppermute | solution.py:367
  19.0 9.5 %collective-permute-start = (f32[16,128,128]{2,1,0:T(8,128)S(1)}, f32[16,128,128]{2,1,0:T(8,128)S(1)}, u32[]{:S(2)}, u32[]{:S(2)}) collective-permute-start(f32[16,128,128]{2,1,0:T(8,128)S(1)} %get-tuple-element.20), channel_id=1, source_target_pairs={{0,1},{1,0},{2,3},{3,2},{4,5},{5,4},{6,7},{7,6},{8,9},{9,8},{10,11... | collective-permute-start | bytes 3145736 | tf_op jit(solution)/shard_map/ppermute | solution.py:367
  21.4 18.9 %collective-permute-start.2 = (f32[8,128,128]{2,1,0:T(8,128)S(1)}, f32[8,128,128]{2,1,0:T(8,128)S(1)}, u32[]{:S(2)}, u32[]{:S(2)}) collective-permute-start(f32[8,128,128]{2,1,0:T(8,128)S(1)} %get-tuple-element.23), channel_id=1, source_target_pairs={{0,2},{2,0},{4,6},{6,4},{8,10},{10,8},{12,14},{14,12},{1,3},{3,1},... | collective-permute-start | bytes 1572872 | tf_op jit(solution)/shard_map/ppermute | solution.py:370
  24.4 13.6 %collective-permute-start.3 = (f32[4,128,128]{2,1,0:T(8,128)S(1)}, f32[4,128,128]{2,1,0:T(8,128)S(1)}, u32[]{:S(2)}, u32[]{:S(2)}) collective-permute-start(f32[4,128,128]{2,1,0:T(8,128)S(1)} %get-tuple-element.24), channel_id=1, source_target_pairs={{0,4},{2,6},{4,0},{6,2},{8,12},{10,14},{12,8},{14,10},{1,5},{3,7},... | collective-permute-start | bytes 786440 | tf_op jit(solution)/shard_map/ppermute | solution.py:370
  26.0 14.4 %collective-permute-start.4 = (f32[4,128,128]{2,1,0:T(8,128)S(1)}, f32[4,128,128]{2,1,0:T(8,128)S(1)}, u32[]{:S(2)}, u32[]{:S(2)}) collective-permute-start(f32[4,128,128]{2,1,0:T(8,128)S(1)} %get-tuple-element.25), channel_id=1, source_target_pairs={{0,8},{2,10},{4,12},{6,14},{8,0},{10,2},{12,4},{14,6},{1,9},{3,11}... | collective-permute-start | bytes 786440 | tf_op jit(solution)/shard_map/ppermute | solution.py:370
  40.3 17.1 %copy-start = (f32[16,32,1024]{2,1,0:T(8,128)S(1)}, f32[16,32,1024]{2,1,0:T(8,128)}, u32[]{:S(2)}) copy-start(f32[16,32,1024]{2,1,0:T(8,128)} %bank.1) | copy-start | bytes 6291460
  40.5 8.5 %collective-permute-start.5 = (f32[4,128,128]{2,1,0:T(8,128)S(1)}, f32[4,128,128]{2,1,0:T(8,128)S(1)}, u32[]{:S(2)}, u32[]{:S(2)}) collective-permute-start(f32[4,128,128]{2,1,0:T(8,128)S(1)} %get-tuple-element.27), channel_id=1, source_target_pairs={{0,2},{2,0},{4,6},{6,4},{8,10},{10,8},{12,14},{14,12},{1,3},{3,1},... | collective-permute-start | bytes 786440 | tf_op jit(solution)/shard_map/ppermute | solution.py:370
  41.0 6.9 %collective-permute-start.6 = (f32[2,128,128]{2,1,0:T(8,128)S(1)}, f32[2,128,128]{2,1,0:T(8,128)S(1)}, u32[]{:S(2)}, u32[]{:S(2)}) collective-permute-start(f32[2,128,128]{2,1,0:T(8,128)S(1)} %get-tuple-element.28), channel_id=1, source_target_pairs={{0,4},{2,6},{4,0},{6,2},{8,12},{10,14},{12,8},{14,10},{1,5},{3,7},... | collective-permute-start | bytes 393224 | tf_op jit(solution)/shard_map/ppermute | solution.py:370
  41.5 7.5 %collective-permute-start.7 = (f32[2,128,128]{2,1,0:T(8,128)S(1)}, f32[2,128,128]{2,1,0:T(8,128)S(1)}, u32[]{:S(2)}, u32[]{:S(2)}) collective-permute-start(f32[2,128,128]{2,1,0:T(8,128)S(1)} %get-tuple-element.29), channel_id=1, source_target_pairs={{0,8},{2,10},{4,12},{6,14},{8,0},{10,2},{12,4},{14,6},{1,9},{3,11}... | collective-permute-start | bytes 393224 | tf_op jit(solution)/shard_map/ppermute | solution.py:370
  49.1 6.7 %collective-permute-start.8 = (f32[2,128,128]{2,1,0:T(8,128)S(1)}, f32[2,128,128]{2,1,0:T(8,128)S(1)}, u32[]{:S(2)}, u32[]{:S(2)}) collective-permute-start(f32[2,128,128]{2,1,0:T(8,128)S(1)} %get-tuple-element.31), channel_id=1, source_target_pairs={{0,4},{2,6},{4,0},{6,2},{8,12},{10,14},{12,8},{14,10},{1,5},{3,7},... | collective-permute-start | bytes 393224 | tf_op jit(solution)/shard_map/ppermute | solution.py:370
  49.2 6.6 %collective-permute-start.9 = (f32[2,128,128]{2,1,0:T(8,128)S(1)}, f32[2,128,128]{2,1,0:T(8,128)S(1)}, u32[]{:S(2)}, u32[]{:S(2)}) collective-permute-start(f32[2,128,128]{2,1,0:T(8,128)S(1)} %get-tuple-element.32), channel_id=1, source_target_pairs={{0,8},{2,10},{4,12},{6,14},{8,0},{10,2},{12,4},{14,6},{1,9},{3,11}... | collective-permute-start | bytes 393224 | tf_op jit(solution)/shard_map/ppermute | solution.py:370
  55.8 1.6 %collective-permute-start.10 = (f32[4,128,128]{2,1,0:T(8,128)S(1)}, f32[4,128,128]{2,1,0:T(8,128)S(1)}, u32[]{:S(2)}, u32[]{:S(2)}) collective-permute-start(f32[4,128,128]{2,1,0:T(8,128)S(1)} %last.1), channel_id=1, source_target_pairs={{0,1},{1,0},{2,3},{3,2},{4,5},{5,4},{6,7},{7,6},{8,9},{9,8},{10,11... | collective-permute-start | bytes 786440 | tf_op jit(solution)/shard_map/ppermute | solution.py:367

commit v11 on v10

--- a/solution.py
+++ b/solution.py
@@ -13,7 +13,7 @@
 MIB = 1 << 20
 UNROLL = 12
 ORDERS = ("ylh", "yhl", "lyh", "hyl")
-N_BUF = 4
+PART_ROWS = (24, 10, 18, 12)
 
 
 def position():
@@ -24,12 +24,12 @@
 def accumulate_kernel(
     bank_size, n_owner, n_acc,
     proj_hbm, img_hbm, tra_hbm, w_hbm, pose_hbm, blocks_hbm, tiles_hbm,
-    sent_away, kept_away, sent_stay, kept_stay,
+    sent_y, kept_y, sent_z, kept_z, sent_stay, kept_stay,
     proj, weight, pose, blocks, tiles, idx_v, idx_s, square, cross,
     *rest,
 ):
-    parts, accs = rest[:N_BUF], rest[N_BUF : N_BUF + n_acc]
-    proj_sem, small_sem, table_sem, idx_sem = rest[N_BUF + n_acc :]
+    accs = rest[:n_acc]
+    proj_sem, small_sem, table_sem, idx_sem = rest[n_acc:]
     n_pose, n_part = pose.shape
     n_tile, n_table = blocks.shape
     n_row = accs[0].shape[0]
@@ -100,14 +100,22 @@
     for p in range(n_part - n_late, n_part):
         proj_copy(p).start()
 
-    def stage(unit, part):
-        first = pl.multiple_of(unit * tile_rows, tile_rows)
-        part[...] = proj[pl.ds(first, tile_rows), :].astype(jnp.float32)
-
-    def terms(p, j, part, weights):
+    sublane = lax.broadcasted_iota(jnp.int32, (SUB, LANES), 0)
+    bits = [(sublane & (1 << t)) != 0 for t in range(3)]
+
+    def terms(p, j, weights):
+        first = (p * n_tile + j) * tile_rows
+        cells = []
+        for c in range(0, SUB, 2):
+            pair = proj[pl.ds(pl.multiple_of(first + c * SUB, 2 * SUB), 2 * SUB), :].astype(jnp.float32)
+            cells += [pair[:SUB], pair[SUB:]]
+        cells = [pltpu.roll(x, c, 0) if c else x for c, x in enumerate(cells)]
+        for t, bit in enumerate(bits):
+            cells = [jnp.where(bit, cells[(i + (1 << t)) % SUB], cells[i]) for i in range(SUB)]
+        cells = [pltpu.roll(cells[-k % SUB], SUB - k, 0) if k else cells[0] for k in range(n_pose)]
         cell = pl.ds((j * (n_part // SUB) + p // SUB) * tile_rows + p % SUB, SUB, stride=SUB)
         tt, ti = square[cell, :], cross[cell, :]
-        return [(tt * part[pl.ds(k, SUB, stride=SUB), :] - ti) * weights[k] for k in range(n_pose)]
+        return [(tt * cells[k] - ti) * weights[k] for k in range(n_pose)]
 
     def add_rows(p, j, values):
         for first in range(0, n_pose, n_acc):
@@ -118,46 +126,37 @@
                 accs[i][rows[i], :] = old[i] + values[k]
 
     idx_copy.wait()
-    n_buf = len(parts)
 
     @pl.loop(0, n_part)
     def _(p):
         proj_copy(p).wait()
         weights = [jnp.full((SUB, LANES), weight[k, p], jnp.float32) for k in range(n_pose)]
-        base = p * n_tile
-        stage(base, parts[0])
-        stage(base + 1, parts[1])
-
-        @pl.loop(0, n_tile, step=UNROLL, init_carry=tuple(terms(p, 0, parts[0], weights)))
+
+        @pl.loop(0, n_tile, step=UNROLL, init_carry=tuple(terms(p, 0, weights)))
         def _(j, values):
             for u in range(UNROLL):
-                ahead = j + u + 2
-                stage(base + (ahead if u + 2 < UNROLL else jnp.minimum(ahead, n_tile - 1)), parts[(u + 2) % n_buf])
                 following = j + u + 1
-                later = terms(
-                    p, following if u + 1 < UNROLL else jnp.minimum(following, n_tile - 1),
-                    parts[(u + 1) % n_buf], weights,
-                )
+                later = terms(p, following if u + 1 < UNROLL else jnp.minimum(following, n_tile - 1), weights)
                 add_rows(p, j + u, values)
                 values = later
             return tuple(values)
 
     rep, near, low, high = position()
     half_rows = n_row // (n_owner * 2)
-    size = half_rows // len(ORDERS)
     sizes = {"y": 2, "l": 2, "h": n_owner // 4}
 
-    def finish(out, place_of, part, owner, half):
-        first = pl.multiple_of((owner * 2 + half) * half_rows + part * size, size)
-        rows = pl.ds(first, size)
-        total = accs[0][rows, :]
+    def finish(out, at, first, size):
+        first = pl.multiple_of(first, SUB)
+        total = accs[0][pl.ds(first, size), :]
         for acc in accs[1:]:
-            total += acc[rows, :]
-        out[place_of] = total
+            total += acc[pl.ds(first, size), :]
+        out[pl.ds(pl.multiple_of(at, SUB), size), :] = total
 
     def pieces(sent, kept, begin, part, firsts):
         order = ORDERS[part]
         inner = sizes[order[1]] * sizes[order[2]]
+        size = PART_ROWS[part] * SUB
+        within = sum(PART_ROWS[:part]) * SUB
 
         @pl.loop(0, len(firsts) * inner)
         def _(i):
@@ -165,15 +164,18 @@
             off[order[1]] = i % inner // sizes[order[2]]
             off[order[2]] = i % sizes[order[2]]
             owner = ((high ^ off["h"]) * 2 + (low ^ off["l"])) * 2 + (near ^ off["y"])
-            finish(sent, begin + i, part, owner, 1 - rep)
-            finish(kept, begin + i, part, owner, rep)
-
-        return begin + len(firsts) * inner
-
-    for sent, kept, away in ((sent_away, kept_away, True), (sent_stay, kept_stay, False)):
-        begin = 0
-        for part, order in enumerate(ORDERS):
-            begin = pieces(sent, kept, begin, part, range(1, sizes[order[0]]) if away else range(1))
+            finish(sent, begin + i * size, (owner * 2 + 1 - rep) * half_rows + within, size)
+            finish(kept, begin + i * size, (owner * 2 + rep) * half_rows + within, size)
+
+        return begin + len(firsts) * inner * size
+
+    away_y = pieces(sent_y, kept_y, 0, 0, range(1, 2))
+    pieces(sent_y, kept_y, away_y, 1, range(1, 2))
+    away_z = pieces(sent_z, kept_z, 0, 2, range(1, 2))
+    pieces(sent_z, kept_z, away_z, 3, range(1, sizes["h"]))
+    begin = 0
+    for part in range(len(ORDERS)):
+        begin = pieces(sent_stay, kept_stay, begin, part, range(1))
 
 
 def tiles_in_order(array):
@@ -188,9 +190,9 @@
     bank_size, n_owner,
 ):
     n_part, n_pose, n_tile, n_cell = projections.shape
-    assert n_cell == SUB * LANES and n_pose == SUB and n_part % SUB == 0 and n_tile % UNROLL == 0 and UNROLL % N_BUF == 0
+    assert n_cell == SUB * LANES and n_pose == SUB and n_part % SUB == 0 and n_tile % UNROLL == 0
     n_row = n_owner * NB_DEV * bank_size * SUB
-    n_acc = 8 if n_row * LANES * 4 <= 4 * MIB else 2
+    n_acc = 4 if n_row * LANES * 4 <= 4 * MIB else 2
     projections = tiles_in_order(jnp.transpose(projections, (0, 2, 1, 3)))
     images = tiles_in_order(jnp.transpose(images, (1, 0, 2)))
     transfer = tiles_in_order(jnp.transpose(transfer, (1, 0, 2)))
@@ -198,16 +200,19 @@
     hbm = pl.BlockSpec(memory_space=pltpu.HBM)
     vmem = pl.BlockSpec(memory_space=pltpu.VMEM)
     n_high = n_owner // 4
-    size = n_row // (n_owner * 2 * len(ORDERS))
-
-    def out(pieces):
-        return jax.ShapeDtypeStruct((pieces, size, LANES), jnp.float32)
+    a, d, b, e = (rows * SUB for rows in PART_ROWS)
+    assert sum(PART_ROWS) == NB_DEV // 2 * bank_size
+
+    def out(rows):
+        return [jax.ShapeDtypeStruct((rows, LANES), jnp.float32)] * 2
 
     return pl.pallas_call(
         functools.partial(accumulate_kernel, bank_size, n_owner, n_acc),
-        out_shape=[out(6 * n_high + 4 * (n_high - 1))] * 2 + [out(6 * n_high + 4)] * 2,
+        out_shape=out(2 * n_high * (a + d))
+        + out(2 * n_high * b + 4 * (n_high - 1) * e)
+        + out(2 * n_high * (a + d + b) + 4 * e),
         in_specs=[hbm] * 7,
-        out_specs=[vmem] * 4,
+        out_specs=[vmem] * 6,
         scratch_shapes=[
             pltpu.VMEM(projections.shape, jnp.bfloat16),
             pltpu.SMEM((n_pose, n_part), jnp.float32),
@@ -219,7 +224,6 @@
             pltpu.VMEM(transfer.shape, jnp.float32),
             pltpu.VMEM(transfer.shape, jnp.float32),
         ]
-        + [pltpu.VMEM((n_pose * SUB, LANES), jnp.float32)] * N_BUF
         + [pltpu.VMEM((n_row, LANES), jnp.float32)] * n_acc
         + [
             pltpu.SemaphoreType.DMA((n_part,)),
@@ -227,7 +231,7 @@
             pltpu.SemaphoreType.DMA((3,)),
             pltpu.SemaphoreType.DMA,
         ],
-        compiler_params=pltpu.CompilerParams(vmem_limit_bytes=(47 if n_acc == 8 else 56) * MIB),
+        compiler_params=pltpu.CompilerParams(vmem_limit_bytes=(40 if n_acc == 4 else 56) * MIB),
         name="accumulate",
     )(
         stay(projections), stay(images), stay(transfer),
@@ -235,76 +239,85 @@
     )
 
 
-def in_vmem(kernel, name, pieces, *operands):
+def in_vmem(kernel, name, rows, *operands):
     vmem = pl.BlockSpec(memory_space=pltpu.VMEM)
-    size = operands[0].shape[1:]
     return pl.pallas_call(
         kernel,
-        out_shape=[jax.ShapeDtypeStruct((n,) + size, jnp.float32) for n in pieces],
+        out_shape=[jax.ShapeDtypeStruct((n, LANES), jnp.float32) for n in rows],
         in_specs=[vmem] * len(operands),
-        out_specs=[vmem] * len(pieces),
+        out_specs=[vmem] * len(rows),
         compiler_params=pltpu.CompilerParams(vmem_limit_bytes=32 * MIB),
         name=name,
     )(*operands)
 
 
-def first_kernel(n_high, kept, got, to_y, to_l, *to_h):
+def first_kernel(kept, got, *to):
     begin = 0
-    for out in (to_y, to_l) + to_h:
+    for out in to:
         rows = slice(begin, begin + out.shape[0])
-        out[...] = kept[rows] + got[rows]
+        out[...] = kept[rows, :] + got[rows, :]
         begin += out.shape[0]
 
 
 def second_kernel(n_high, kept, got, got_y, got_l, *rest):
-    got_h, (own, to_y, to_l, *to_h) = rest[: n_high - 1], rest[n_high - 1 :]
-    n = 2 * n_high
-
-    def part_sum(begin, count, *arrivals):
-        total = kept[begin : begin + count] + got[begin : begin + count]
-        for array, at in arrivals:
-            total += array[at : at + count]
-        return total
-
-    ylh = part_sum(0, n, (got_y, 0))
-    yhl = part_sum(n, n, (got_y, n))
-    lyh = part_sum(2 * n, n, (got_l, 0))
-    hyl = part_sum(3 * n, 4, *[(array, 0) for array in got_h])
-    to_l[...] = ylh[n_high:]
+    got_h, (own_a, own_d, own_b, own_e, to_y, to_l, *to_h) = rest[: n_high - 1], rest[n_high - 1 :]
+    a, d, b, e = (rows * SUB for rows in PART_ROWS)
+
+    def put(out, at, begin, size, *arrivals):
+        total = kept[begin : begin + size, :] + got[begin : begin + size, :]
+        for array, first in arrivals:
+            total += array[first : first + size, :]
+        out[at : at + size, :] = total
+
+    n = n_high * a
+    put(own_a, 0, 0, n, (got_y, 0))
+    put(to_l, 0, n, n, (got_y, n))
+    begin, y_begin = 2 * n, 2 * n
+    put(own_d, 0, begin, 2 * d, (got_y, y_begin))
     for i, out in enumerate(to_h):
-        out[...] = yhl[2 * (i + 1) : 2 * (i + 2)]
-    to_y[:n_high] = lyh[n_high:]
-    to_y[n_high:] = hyl[2:]
-    own[:n_high] = ylh[:n_high]
-    own[n_high : n_high + 2] = yhl[:2]
-    own[n_high + 2 : 2 * n_high + 2] = lyh[:n_high]
-    own[2 * n_high + 2 :] = hyl[:2]
-
-
-def third_kernel(n_high, before, got_y, got_l, *rest):
+        put(out, 0, begin + 2 * d * (i + 1), 2 * d, (got_y, y_begin + 2 * d * (i + 1)))
+    begin, n = begin + 2 * n_high * d, n_high * b
+    put(own_b, 0, begin, n, (got_l, 0))
+    put(to_y, 0, begin + n, n, (got_l, n))
+    begin += 2 * n
+    put(own_e, 0, begin, 2 * e, *[(array, 0) for array in got_h])
+    put(to_y, n, begin + 2 * e, 2 * e, *[(array, 2 * e) for array in got_h])
+
+
+def third_kernel(n_high, own_a, own_d, own_b, own_e, got_y, got_l, *rest):
     got_h, (own, to_l, *to_h) = rest[: n_high - 1], rest[n_high - 1 :]
-    ylh = before[:n_high] + got_l[...]
-    yhl = before[n_high : n_high + 2]
-    for array in got_h:
-        yhl += array[...]
-    lyh = before[n_high + 2 : 2 * n_high + 2] + got_y[:n_high]
-    hyl = before[2 * n_high + 2 :] + got_y[n_high:]
-    for part, value in enumerate((ylh, yhl, lyh, hyl)):
-        own[part] = value[0]
-    to_l[0] = yhl[1]
-    to_l[1] = hyl[1]
+    a, d, b, e = (rows * SUB for rows in PART_ROWS)
+
+    def put(out, at, source, begin, size, *arrivals):
+        total = source[begin : begin + size, :]
+        for array, first in arrivals:
+            total += array[first : first + size, :]
+        out[at : at + size, :] = total
+
+    put(own, 0, own_a, 0, a, (got_l, 0))
+    put(own, a, own_d, 0, d, *[(array, 0) for array in got_h])
+    put(own, a + d, own_b, 0, b, (got_y, 0))
+    put(own, a + d + b, own_e, 0, e, (got_y, n_high * b))
+    put(to_l, 0, own_d, d, d, *[(array, d) for array in got_h])
+    put(to_l, d, own_e, e, e, (got_y, n_high * b + e))
     for i, out in enumerate(to_h):
-        out[0] = ylh[i + 1]
-        out[1] = lyh[i + 1]
-
-
-def last_kernel(n_high, before, got_l, *rest):
-    got_h, (own,) = rest[: n_high - 1], rest[n_high - 1 :]
-    for part, (arrivals, at) in enumerate(((got_h, 0), ((got_l,), 0), (got_h, 1), ((got_l,), 1))):
-        total = before[part]
-        for array in arrivals:
-            total += array[at]
-        own[part] = total
+        put(out, 0, own_a, (i + 1) * a, a, (got_l, (i + 1) * a))
+        put(out, a, own_b, (i + 1) * b, b, (got_y, (i + 1) * b))
+
+
+def last_kernel(before, got_l, *rest):
+    got_h, (own,) = rest[:-1], rest[-1:]
+    a, d, b, e = (rows * SUB for rows in PART_ROWS)
+    for at, size, arrivals in (
+        (0, a, [(array, 0) for array in got_h]),
+        (a, d, [(got_l, 0)]),
+        (a + d, b, [(array, a) for array in got_h]),
+        (a + d + b, e, [(got_l, d)]),
+    ):
+        total = before[at : at + size, :]
+        for array, first in arrivals:
+            total += array[first : first + size, :]
+        own[at : at + size, :] = total
 
 
 def bank_kernel(own, other, bank, out):
@@ -358,10 +371,11 @@
     bank_size = weight_bank.shape[0]
     n_blk = lax.axis_size("blk")
     n_high = n_blk // 4
-    sent_away, kept_away, sent_stay, kept_stay = accumulate(
+    sent_y, kept_y, sent_z, kept_z, sent_stay, kept_stay = accumulate(
         projections, images, transfer, pose_weights, pose_of, pose_blocks, pose_tiles,
         bank_size, n_blk,
     )
+    a, d, b, e = (rows * SUB for rows in PART_ROWS)
 
     def over_rep(array):
         return lax.ppermute(array, "rep", [(0, 1), (1, 0)])
@@ -372,21 +386,24 @@
     def over_h(arrays):
         return [over_blk(array, 4 * (i + 1)) for i, array in enumerate(arrays)]
 
-    def step(kernel, name, pieces, *operands):
-        return in_vmem(functools.partial(kernel, n_high), name, pieces, *operands)
-
     n_h = n_high - 1
-    got_away, got_stay = over_rep(sent_away), over_rep(sent_stay)
-    to_y, to_l, *to_h = step(first_kernel, "first", [4 * n_high, 2 * n_high] + [4] * n_h, kept_away, got_away)
-    got_h, got_y, got_l = over_h(to_h), over_blk(to_y, 1), over_blk(to_l, 2)
-    own, to_y, to_l, *to_h = step(
-        second_kernel, "second", [2 * n_high + 4, n_high + 2, n_high] + [2] * n_h,
+    got_y, got_z, got_stay = over_rep(sent_y), over_rep(sent_z), over_rep(sent_stay)
+    (to_y,) = in_vmem(first_kernel, "first_y", [kept_y.shape[0]], kept_y, got_y)
+    got_y = over_blk(to_y, 1)
+    to_l, *to_h = in_vmem(first_kernel, "first_z", [2 * n_high * b] + [4 * e] * n_h, kept_z, got_z)
+    got_l, got_h = over_blk(to_l, 2), over_h(to_h)
+    own_a, own_d, own_b, own_e, to_y, to_l, *to_h = in_vmem(
+        functools.partial(second_kernel, n_high), "second",
+        [n_high * a, 2 * d, n_high * b, 2 * e, n_high * b + 2 * e, n_high * a] + [2 * d] * n_h,
         kept_stay, got_stay, got_y, got_l, *got_h,
     )
-    got_h, got_y, got_l = over_h(to_h), over_blk(to_y, 1), over_blk(to_l, 2)
-    own, to_l, *to_h = step(third_kernel, "third", [4, 2] + [2] * n_h, own, got_y, got_l, *got_h)
-    got_h, got_l = over_h(to_h), over_blk(to_l, 2)
-    (own,) = step(last_kernel, "last", [4], own, got_l, *got_h)
+    got_y, got_l, got_h = over_blk(to_y, 1), over_blk(to_l, 2), over_h(to_h)
+    own, to_l, *to_h = in_vmem(
+        functools.partial(third_kernel, n_high), "third", [a + d + b + e, d + e] + [a + b] * n_h,
+        own_a, own_d, own_b, own_e, got_y, got_l, *got_h,
+    )
+    got_l, got_h = over_blk(to_l, 2), over_h(to_h)
+    (own,) = in_vmem(last_kernel, "last", [a + d + b + e], own, got_l, *got_h)
     return apply_bank(own, over_rep(own), weight_bank)
 
 

time: 59.9 us -> 61.3 us (1.023)
  starting transfers between devices: 13.2 us -> 18.1 us
  waiting for transfers between devices: 25.3 us -> 21.2 us
    ppermute x8, starting transfers between devices: 12.5 us -> 17 us  [over_blk(): return lax.ppermute(array, 'blk', [(i, i ^ bits) for i in range(n_blk)])]
    ppermute x8, waiting for transfers between devices: 21.6 us -> 18.6 us  [over_blk(): return lax.ppermute(array, 'blk', [(i, i ^ bits) for i in range(n_blk)])]
    ppermute x3 -> x4, waiting for transfers between devices: 3.73 us -> 2.6 us  [over_rep(): return lax.ppermute(array, 'rep', [(0, 1), (1, 0)])]
  transfers between devices with their start and end apart: 11 -> 12, of which waited for: 7 -> 8; matrix products, arithmetic and copies ran while one was open for 0% -> 0% of each run, Pallas kernels for 0% -> 0%
where the time goes in v11:
time: 61.3 us; the launch traced here: 61.2 us
  Pallas kernels  21.8 us (36%)
  waiting for transfers between devices  21.2 us (35%)
  starting transfers between devices  18.1 us (30%)
    pallas_call x1, Pallas kernels, accumulate(): pl.pallas_call(functools.partial(accumulate_kernel, bank_size, n_owner, n...  19.1 us
    ppermute x8, waiting for transfers between devices, over_blk(): return lax.ppermute(array, 'blk', [(i, i ^ bits) for i in range(n_blk)])  18.6 us
    ppermute x8, starting transfers between devices, over_blk(): return lax.ppermute(array, 'blk', [(i, i ^ bits) for i in range(n_blk)])  17 us
    ppermute x4, waiting for transfers between devices, over_rep(): return lax.ppermute(array, 'rep', [(0, 1), (1, 0)])  2.6 us
    pallas_call x1, Pallas kernels, apply_bank(): pl.pallas_call(bank_kernel, out_shape=jax.ShapeDtypeStruct((NB_DEV, n_z,...  2.36 us
  transfers between devices with their start and end apart: 12, of which 8 were waited for; matrix products, arithmetic and copies ran while one was open for 0% of the time, Pallas kernels for 0%

profile of v11, /device:TPU:0, one launch (start us, length us, event | category | flops | bytes accessed | tf_op | source)
XLA Modules:
  0.0 61.2 jit_solution(68338086162550329)
XLA Ops:
  0.0 19.1 %accumulate.1 = (f32[1088,128]{1,0:T(8,128)S(1)}, f32[1088,128]{1,0:T(8,128)S(1)}, f32[960,128]{1,0:T(8,128)S(1)}, f32[960,128]{1,0:T(8,128)S(1)}, f32[2048,128]{1,0:T(8,128)S(1)}, /*index=5*/f32[2048,128]{1,0:T(8,128)S(1)}) custom-call(bf16[36864,128]{1,0:T(8,128)(2,1)} %bitcast.29, bf16[4608,128]{1,0:T(8,128)(2,1)} %bitcast.30, ...), custom_call_target="tpu_custom_call" | custom-call | tf_op jit(solution)/shard_map/accumulate/pallas_call | solution.py:209
  19.1 0.5 collective-permute-start.1
  19.6 0.1 collective-permute-start
  19.7 0.4 collective-permute-start.3
  20.1 1.1 %collective-permute-done.1.got = f32[1088,128]{1,0:T(8,128)S(1)} collective-permute-done((f32[1088,128]{1,0:T(8,128)S(1)}, f32[1088,128]{1,0:T(8,128)S(1)}, u32[]{:S(2)}, u32[]{:S(2)}) %collective-permute-start.1) | collective-permute-done | bytes 557088 | tf_op jit(solution)/shard_map/ppermute | solution.py:381
  21.2 0.1 first_y.1
  21.2 3.0 %collective-permute-start.2 = (f32[1088,128]{1,0:T(8,128)S(1)}, f32[1088,128]{1,0:T(8,128)S(1)}, u32[]{:S(2)}, u32[]{:S(2)}) collective-permute-start(f32[1088,128]{1,0:T(8,128)S(1)} %first_y.1), channel_id=1, source_target_pairs={{0,2},{2,0},{4,6},{6,4},{8,10},{10,8},{12,14},{14,12},{1,3},{3,1},... | collective-permute-start | bytes 1671176 | tf_op jit(solution)/shard_map/ppermute | solution.py:384
  24.3 2.2 %collective-permute-start.4 = (f32[576,128]{1,0:T(8,128)S(1)}, f32[576,128]{1,0:T(8,128)S(1)}, u32[]{:S(2)}, u32[]{:S(2)}) collective-permute-start(f32[576,128]{1,0:T(8,128)S(1)} %get-tuple-element.29), channel_id=1, source_target_pairs={{0,4},{2,6},{4,0},{6,2},{8,12},{10,14},{12,8},{14,10},{1,5},{3,7},... | collective-permute-start | bytes 884744 | tf_op jit(solution)/shard_map/ppermute | solution.py:384
  26.4 2.6 %collective-permute-start.5 = (f32[384,128]{1,0:T(8,128)S(1)}, f32[384,128]{1,0:T(8,128)S(1)}, u32[]{:S(2)}, u32[]{:S(2)}) collective-permute-start(f32[384,128]{1,0:T(8,128)S(1)} %get-tuple-element.30), channel_id=1, source_target_pairs={{0,8},{2,10},{4,12},{6,14},{8,0},{10,2},{12,4},{14,6},{1,9},{3,11}... | collective-permute-start | bytes 589832 | tf_op jit(solution)/shard_map/ppermute | solution.py:384
  29.0 8.2 %collective-permute-done.5.rest_0_ = f32[384,128]{1,0:T(8,128)S(1)} collective-permute-done((f32[384,128]{1,0:T(8,128)S(1)}, f32[384,128]{1,0:T(8,128)S(1)}, u32[]{:S(2)}, u32[]{:S(2)}) %collective-permute-start.5) | collective-permute-done | bytes 196640 | tf_op jit(solution)/shard_map/ppermute | solution.py:384
  37.2 0.7 %collective-permute-done.4.got_l = f32[576,128]{1,0:T(8,128)S(1)} collective-permute-done((f32[576,128]{1,0:T(8,128)S(1)}, f32[576,128]{1,0:T(8,128)S(1)}, u32[]{:S(2)}, u32[]{:S(2)}) %collective-permute-start.4) | collective-permute-done | bytes 294944 | tf_op jit(solution)/shard_map/ppermute | solution.py:384
  38.0 0.2 second.1
  38.1 1.7 %collective-permute-start.6 = (f32[480,128]{1,0:T(8,128)S(1)}, f32[480,128]{1,0:T(8,128)S(1)}, u32[]{:S(2)}, u32[]{:S(2)}) collective-permute-start(f32[480,128]{1,0:T(8,128)S(1)} %get-tuple-element.35), channel_id=1, source_target_pairs={{0,2},{2,0},{4,6},{6,4},{8,10},{10,8},{12,14},{14,12},{1,3},{3,1},... | collective-permute-start | bytes 737288 | tf_op jit(solution)/shard_map/ppermute | solution.py:384
  39.9 2.6 %collective-permute-start.7 = (f32[384,128]{1,0:T(8,128)S(1)}, f32[384,128]{1,0:T(8,128)S(1)}, u32[]{:S(2)}, u32[]{:S(2)}) collective-permute-start(f32[384,128]{1,0:T(8,128)S(1)} %get-tuple-element.36), channel_id=1, source_target_pairs={{0,4},{2,6},{4,0},{6,2},{8,12},{10,14},{12,8},{14,10},{1,5},{3,7},... | collective-permute-start | bytes 589832 | tf_op jit(solution)/shard_map/ppermute | solution.py:384
  42.5 1.6 %collective-permute-start.8 = (f32[160,128]{1,0:T(8,128)S(1)}, f32[160,128]{1,0:T(8,128)S(1)}, u32[]{:S(2)}, u32[]{:S(2)}) collective-permute-start(f32[160,128]{1,0:T(8,128)S(1)} %get-tuple-element.37), channel_id=1, source_target_pairs={{0,8},{2,10},{4,12},{6,14},{8,0},{10,2},{12,4},{14,6},{1,9},{3,11}... | collective-permute-start | bytes 245768 | tf_op jit(solution)/shard_map/ppermute | solution.py:384
  44.1 4.1 %collective-permute-done.8.rest_0_ = f32[160,128]{1,0:T(8,128)S(1)} collective-permute-done((f32[160,128]{1,0:T(8,128)S(1)}, f32[160,128]{1,0:T(8,128)S(1)}, u32[]{:S(2)}, u32[]{:S(2)}) %collective-permute-start.8) | collective-permute-done | bytes 81952 | tf_op jit(solution)/shard_map/ppermute | solution.py:384
  48.2 0.2 collective-permute-done.7.got_l
  48.4 2.7 %collective-permute-start.10 = (f32[336,128]{1,0:T(8,128)S(1)}, f32[336,128]{1,0:T(8,128)S(1)}, u32[]{:S(2)}, u32[]{:S(2)}) collective-permute-start(f32[336,128]{1,0:T(8,128)S(1)} %get-tuple-element.40), channel_id=1, source_target_pairs={{0,8},{2,10},{4,12},{6,14},{8,0},{10,2},{12,4},{14,6},{1,9},{3,11}... | collective-permute-start | bytes 516104 | tf_op jit(solution)/shard_map/ppermute | solution.py:384
  51.1 0.7 %collective-permute-start.9 = (f32[176,128]{1,0:T(8,128)S(1)}, f32[176,128]{1,0:T(8,128)S(1)}, u32[]{:S(2)}, u32[]{:S(2)}) collective-permute-start(f32[176,128]{1,0:T(8,128)S(1)} %get-tuple-element.39), channel_id=1, source_target_pairs={{0,4},{2,6},{4,0},{6,2},{8,12},{10,14},{12,8},{14,10},{1,5},{3,7},... | collective-permute-start | bytes 270344 | tf_op jit(solution)/shard_map/ppermute | solution.py:384
  51.8 3.9 %collective-permute-done.9.got_l = f32[176,128]{1,0:T(8,128)S(1)} collective-permute-done((f32[176,128]{1,0:T(8,128)S(1)}, f32[176,128]{1,0:T(8,128)S(1)}, u32[]{:S(2)}, u32[]{:S(2)}) %collective-permute-start.9) | collective-permute-done | bytes 90144 | tf_op jit(solution)/shard_map/ppermute | solution.py:384
  55.7 1.5 %collective-permute-done.10.rest_0_ = f32[336,128]{1,0:T(8,128)S(1)} collective-permute-done((f32[336,128]{1,0:T(8,128)S(1)}, f32[336,128]{1,0:T(8,128)S(1)}, u32[]{:S(2)}, u32[]{:S(2)}) %collective-permute-start.10) | collective-permute-done | bytes 172064 | tf_op jit(solution)/shard_map/ppermute | solution.py:384
  57.2 0.1 collective-permute-start.11
  57.3 1.5 %collective-permute-done.11 = f32[512,128]{1,0:T(8,128)S(1)} collective-permute-done((f32[512,128]{1,0:T(8,128)S(1)}, f32[512,128]{1,0:T(8,128)S(1)}, u32[]{:S(2)}, u32[]{:S(2)}) %collective-permute-start.11) | collective-permute-done | bytes 262176 | tf_op jit(solution)/shard_map/ppermute | solution.py:381
  58.8 2.4 %apply_bank.1 = f32[8,32,1024]{2,1,0:T(8,128)} custom-call(f32[4,16,8,128]{3,2,1,0:T(8,128)S(1)} %bitcast.27, f32[4,16,8,128]{3,2,1,0:T(8,128)S(1)} %bitcast.28, f32[16,32,1024]{2,1,0:T(8,128)S(1)} %copy-done), custom_call_target="tpu_custom_call" | custom-call | tf_op jit(solution)/shard_map/apply_bank/pallas_call | solution.py:358
  (9 shorter events, 0.2 us)
Async XLA Ops:
  19.1 2.1 %collective-permute-start.1 = (f32[1088,128]{1,0:T(8,128)S(1)}, f32[1088,128]{1,0:T(8,128)S(1)}, u32[]{:S(2)}, u32[]{:S(2)}) collective-permute-start(f32[1088,128]{1,0:T(8,128)S(1)} %get-tuple-element.26), channel_id=1, source_target_pairs={{0,1},{1,0},{2,3},{3,2},{4,5},{5,4},{6,7},{7,6},{8,9},{9,8},{10,11... | collective-permute-start | bytes 1671176 | tf_op jit(solution)/shard_map/ppermute | solution.py:381
  19.6 18.4 %collective-permute-start = (f32[2048,128]{1,0:T(8,128)S(1)}, f32[2048,128]{1,0:T(8,128)S(1)}, u32[]{:S(2)}, u32[]{:S(2)}) collective-permute-start(f32[2048,128]{1,0:T(8,128)S(1)} %get-tuple-element.24), channel_id=1, source_target_pairs={{0,1},{1,0},{2,3},{3,2},{4,5},{5,4},{6,7},{7,6},{8,9},{9,8},{10,11... | collective-permute-start | bytes 3145736 | tf_op jit(solution)/shard_map/ppermute | solution.py:381
  19.7 4.5 %collective-permute-start.3 = (f32[960,128]{1,0:T(8,128)S(1)}, f32[960,128]{1,0:T(8,128)S(1)}, u32[]{:S(2)}, u32[]{:S(2)}) collective-permute-start(f32[960,128]{1,0:T(8,128)S(1)} %get-tuple-element.28), channel_id=1, source_target_pairs={{0,1},{1,0},{2,3},{3,2},{4,5},{5,4},{6,7},{7,6},{8,9},{9,8},{10,11... | collective-permute-start | bytes 1474568 | tf_op jit(solution)/shard_map/ppermute | solution.py:381
  21.2 16.7 %collective-permute-start.2 = (f32[1088,128]{1,0:T(8,128)S(1)}, f32[1088,128]{1,0:T(8,128)S(1)}, u32[]{:S(2)}, u32[]{:S(2)}) collective-permute-start(f32[1088,128]{1,0:T(8,128)S(1)} %first_y.1), channel_id=1, source_target_pairs={{0,2},{2,0},{4,6},{6,4},{8,10},{10,8},{12,14},{14,12},{1,3},{3,1},... | collective-permute-start | bytes 1671176 | tf_op jit(solution)/shard_map/ppermute | solution.py:384
  24.3 13.7 %collective-permute-start.4 = (f32[576,128]{1,0:T(8,128)S(1)}, f32[576,128]{1,0:T(8,128)S(1)}, u32[]{:S(2)}, u32[]{:S(2)}) collective-permute-start(f32[576,128]{1,0:T(8,128)S(1)} %get-tuple-element.29), channel_id=1, source_target_pairs={{0,4},{2,6},{4,0},{6,2},{8,12},{10,14},{12,8},{14,10},{1,5},{3,7},... | collective-permute-start | bytes 884744 | tf_op jit(solution)/shard_map/ppermute | solution.py:384
  26.4 10.8 %collective-permute-start.5 = (f32[384,128]{1,0:T(8,128)S(1)}, f32[384,128]{1,0:T(8,128)S(1)}, u32[]{:S(2)}, u32[]{:S(2)}) collective-permute-start(f32[384,128]{1,0:T(8,128)S(1)} %get-tuple-element.30), channel_id=1, source_target_pairs={{0,8},{2,10},{4,12},{6,14},{8,0},{10,2},{12,4},{14,6},{1,9},{3,11}... | collective-permute-start | bytes 589832 | tf_op jit(solution)/shard_map/ppermute | solution.py:384
  38.0 20.8 %copy-start = (f32[16,32,1024]{2,1,0:T(8,128)S(1)}, f32[16,32,1024]{2,1,0:T(8,128)}, u32[]{:S(2)}) copy-start(f32[16,32,1024]{2,1,0:T(8,128)} %bank.1) | copy-start | bytes 6291460
  38.1 10.2 %collective-permute-start.6 = (f32[480,128]{1,0:T(8,128)S(1)}, f32[480,128]{1,0:T(8,128)S(1)}, u32[]{:S(2)}, u32[]{:S(2)}) collective-permute-start(f32[480,128]{1,0:T(8,128)S(1)} %get-tuple-element.35), channel_id=1, source_target_pairs={{0,2},{2,0},{4,6},{6,4},{8,10},{10,8},{12,14},{14,12},{1,3},{3,1},... | collective-permute-start | bytes 737288 | tf_op jit(solution)/shard_map/ppermute | solution.py:384
  39.9 8.4 %collective-permute-start.7 = (f32[384,128]{1,0:T(8,128)S(1)}, f32[384,128]{1,0:T(8,128)S(1)}, u32[]{:S(2)}, u32[]{:S(2)}) collective-permute-start(f32[384,128]{1,0:T(8,128)S(1)} %get-tuple-element.36), channel_id=1, source_target_pairs={{0,4},{2,6},{4,0},{6,2},{8,12},{10,14},{12,8},{14,10},{1,5},{3,7},... | collective-permute-start | bytes 589832 | tf_op jit(solution)/shard_map/ppermute | solution.py:384
  42.5 5.7 %collective-permute-start.8 = (f32[160,128]{1,0:T(8,128)S(1)}, f32[160,128]{1,0:T(8,128)S(1)}, u32[]{:S(2)}, u32[]{:S(2)}) collective-permute-start(f32[160,128]{1,0:T(8,128)S(1)} %get-tuple-element.37), channel_id=1, source_target_pairs={{0,8},{2,10},{4,12},{6,14},{8,0},{10,2},{12,4},{14,6},{1,9},{3,11}... | collective-permute-start | bytes 245768 | tf_op jit(solution)/shard_map/ppermute | solution.py:384
  48.4 8.8 %collective-permute-start.10 = (f32[336,128]{1,0:T(8,128)S(1)}, f32[336,128]{1,0:T(8,128)S(1)}, u32[]{:S(2)}, u32[]{:S(2)}) collective-permute-start(f32[336,128]{1,0:T(8,128)S(1)} %get-tuple-element.40), channel_id=1, source_target_pairs={{0,8},{2,10},{4,12},{6,14},{8,0},{10,2},{12,4},{14,6},{1,9},{3,11}... | collective-permute-start | bytes 516104 | tf_op jit(solution)/shard_map/ppermute | solution.py:384
  51.1 4.5 %collective-permute-start.9 = (f32[176,128]{1,0:T(8,128)S(1)}, f32[176,128]{1,0:T(8,128)S(1)}, u32[]{:S(2)}, u32[]{:S(2)}) collective-permute-start(f32[176,128]{1,0:T(8,128)S(1)} %get-tuple-element.39), channel_id=1, source_target_pairs={{0,4},{2,6},{4,0},{6,2},{8,12},{10,14},{12,8},{14,10},{1,5},{3,7},... | collective-permute-start | bytes 270344 | tf_op jit(solution)/shard_map/ppermute | solution.py:384
  57.2 1.6 %collective-permute-start.11 = (f32[512,128]{1,0:T(8,128)S(1)}, f32[512,128]{1,0:T(8,128)S(1)}, u32[]{:S(2)}, u32[]{:S(2)}) collective-permute-start(f32[512,128]{1,0:T(8,128)S(1)} %last.1), channel_id=1, source_target_pairs={{0,1},{1,0},{2,3},{3,2},{4,5},{5,4},{6,7},{7,6},{8,9},{9,8},{10,11... | collective-permute-start | bytes 786440 | tf_op jit(solution)/shard_map/ppermute | solution.py:381

commit v12 on v11

--- a/solution.py
+++ b/solution.py
@@ -12,8 +12,9 @@
 SUB = 8
 MIB = 1 << 20
 UNROLL = 12
+N_BUF = 2
 ORDERS = ("ylh", "yhl", "lyh", "hyl")
-PART_ROWS = (24, 10, 18, 12)
+PART_ROWS = (16, 16, 18, 14)
 
 
 def position():
@@ -24,12 +25,12 @@
 def accumulate_kernel(
     bank_size, n_owner, n_acc,
     proj_hbm, img_hbm, tra_hbm, w_hbm, pose_hbm, blocks_hbm, tiles_hbm,
-    sent_y, kept_y, sent_z, kept_z, sent_stay, kept_stay,
-    proj, weight, pose, blocks, tiles, idx_v, idx_s, square, cross,
-    *rest,
+    sent_y, sent_z, *rest,
 ):
-    accs = rest[:n_acc]
-    proj_sem, small_sem, table_sem, idx_sem = rest[n_acc:]
+    accs, rest = rest[:n_acc], rest[n_acc:]
+    proj, weight, pose, blocks, tiles, idx_v, idx_s, square, cross = rest[:9]
+    parts = rest[9 : 9 + N_BUF]
+    proj_sem, small_sem, table_sem, idx_sem = rest[9 + N_BUF :]
     n_pose, n_part = pose.shape
     n_tile, n_table = blocks.shape
     n_row = accs[0].shape[0]
@@ -103,7 +104,14 @@
     sublane = lax.broadcasted_iota(jnp.int32, (SUB, LANES), 0)
     bits = [(sublane & (1 << t)) != 0 for t in range(3)]
 
-    def terms(p, j, weights):
+    def stage(p, j, part):
+        first = pl.multiple_of((p * n_tile + j) * tile_rows, tile_rows)
+        part[...] = proj[pl.ds(first, tile_rows), :].astype(jnp.float32)
+
+    def staged(part):
+        return [part[pl.ds(k, SUB, stride=SUB), :] for k in range(n_pose)]
+
+    def rolled(p, j):
         first = (p * n_tile + j) * tile_rows
         cells = []
         for c in range(0, SUB, 2):
@@ -112,7 +120,9 @@
         cells = [pltpu.roll(x, c, 0) if c else x for c, x in enumerate(cells)]
         for t, bit in enumerate(bits):
             cells = [jnp.where(bit, cells[(i + (1 << t)) % SUB], cells[i]) for i in range(SUB)]
-        cells = [pltpu.roll(cells[-k % SUB], SUB - k, 0) if k else cells[0] for k in range(n_pose)]
+        return [pltpu.roll(cells[-k % SUB], SUB - k, 0) if k else cells[0] for k in range(n_pose)]
+
+    def terms(p, j, cells, weights):
         cell = pl.ds((j * (n_part // SUB) + p // SUB) * tile_rows + p % SUB, SUB, stride=SUB)
         tt, ti = square[cell, :], cross[cell, :]
         return [(tt * cells[k] - ti) * weights[k] for k in range(n_pose)]
@@ -132,50 +142,72 @@
         proj_copy(p).wait()
         weights = [jnp.full((SUB, LANES), weight[k, p], jnp.float32) for k in range(n_pose)]
 
-        @pl.loop(0, n_tile, step=UNROLL, init_carry=tuple(terms(p, 0, weights)))
+        stage(p, 0, parts[0])
+
+        @pl.loop(0, n_tile, step=UNROLL, init_carry=tuple(terms(p, 0, staged(parts[0]), weights)))
         def _(j, values):
             for u in range(UNROLL):
-                following = j + u + 1
-                later = terms(p, following if u + 1 < UNROLL else jnp.minimum(following, n_tile - 1), weights)
+                part = parts[(u // 2 + 1) % len(parts)]
+                if u % 2 == 0:
+                    stage(p, jnp.minimum(j + u + 2, n_tile - 1) if u + 2 == UNROLL else j + u + 2, part)
+                    following = j + u + 1
+                    later = terms(p, following, rolled(p, following), weights)
+                else:
+                    following = jnp.minimum(j + u + 1, n_tile - 1) if u + 1 == UNROLL else j + u + 1
+                    later = terms(p, following, staged(part), weights)
                 add_rows(p, j + u, values)
                 values = later
             return tuple(values)
 
-    rep, near, low, high = position()
-    half_rows = n_row // (n_owner * 2)
-    sizes = {"y": 2, "l": 2, "h": n_owner // 4}
-
-    def finish(out, at, first, size):
-        first = pl.multiple_of(first, SUB)
-        total = accs[0][pl.ds(first, size), :]
-        for acc in accs[1:]:
-            total += acc[pl.ds(first, size), :]
-        out[pl.ds(pl.multiple_of(at, SUB), size), :] = total
-
-    def pieces(sent, kept, begin, part, firsts):
+    Sums(n_owner, accs).pieces_away(sent_y, sent_z, sent=True)
+
+
+class Sums:
+    def __init__(self, n_owner, accs):
+        self.accs = accs
+        self.half_rows = accs[0].shape[0] // (n_owner * 2)
+        self.sizes = {"y": 2, "l": 2, "h": n_owner // 4}
+
+    def pieces(self, out, begin, part, firsts, sent):
+        rep, near, low, high = position()
         order = ORDERS[part]
-        inner = sizes[order[1]] * sizes[order[2]]
+        inner = self.sizes[order[1]] * self.sizes[order[2]]
         size = PART_ROWS[part] * SUB
         within = sum(PART_ROWS[:part]) * SUB
+        half = 1 - rep if sent else rep
 
         @pl.loop(0, len(firsts) * inner)
         def _(i):
             off = {order[0]: firsts[0] + i // inner}
-            off[order[1]] = i % inner // sizes[order[2]]
-            off[order[2]] = i % sizes[order[2]]
+            off[order[1]] = i % inner // self.sizes[order[2]]
+            off[order[2]] = i % self.sizes[order[2]]
             owner = ((high ^ off["h"]) * 2 + (low ^ off["l"])) * 2 + (near ^ off["y"])
-            finish(sent, begin + i * size, (owner * 2 + 1 - rep) * half_rows + within, size)
-            finish(kept, begin + i * size, (owner * 2 + rep) * half_rows + within, size)
+            first = pl.multiple_of((owner * 2 + half) * self.half_rows + within, SUB)
+            total = self.accs[0][pl.ds(first, size), :]
+            for acc in self.accs[1:]:
+                total += acc[pl.ds(first, size), :]
+            out[pl.ds(pl.multiple_of(begin + i * size, SUB), size), :] = total
 
         return begin + len(firsts) * inner * size
 
-    away_y = pieces(sent_y, kept_y, 0, 0, range(1, 2))
-    pieces(sent_y, kept_y, away_y, 1, range(1, 2))
-    away_z = pieces(sent_z, kept_z, 0, 2, range(1, 2))
-    pieces(sent_z, kept_z, away_z, 3, range(1, sizes["h"]))
-    begin = 0
-    for part in range(len(ORDERS)):
-        begin = pieces(sent_stay, kept_stay, begin, part, range(1))
+    def pieces_away(self, out_y, out_z, sent):
+        begin = self.pieces(out_y, 0, 0, range(1, 2), sent)
+        self.pieces(out_y, begin, 1, range(1, 2), sent)
+        begin = self.pieces(out_z, 0, 2, range(1, 2), sent)
+        self.pieces(out_z, begin, 3, range(1, self.sizes["h"]), sent)
+
+    def pieces_stay(self, out, sent):
+        begin = 0
+        for part in range(len(ORDERS)):
+            begin = self.pieces(out, begin, part, range(1), sent)
+
+
+def rest_kernel(n_owner, *refs):
+    accs, (kept_y, kept_z, sent_stay, kept_stay) = refs[:-4], refs[-4:]
+    sums = Sums(n_owner, accs)
+    sums.pieces_away(kept_y, kept_z, sent=False)
+    sums.pieces_stay(sent_stay, sent=True)
+    sums.pieces_stay(kept_stay, sent=False)
 
 
 def tiles_in_order(array):
@@ -203,16 +235,16 @@
     a, d, b, e = (rows * SUB for rows in PART_ROWS)
     assert sum(PART_ROWS) == NB_DEV // 2 * bank_size
 
+    away_y, away_z = 2 * n_high * (a + d), 2 * n_high * b + 4 * (n_high - 1) * e
+
     def out(rows):
-        return [jax.ShapeDtypeStruct((rows, LANES), jnp.float32)] * 2
-
-    return pl.pallas_call(
+        return jax.ShapeDtypeStruct((rows, LANES), jnp.float32)
+
+    sent_y, sent_z, *accs = pl.pallas_call(
         functools.partial(accumulate_kernel, bank_size, n_owner, n_acc),
-        out_shape=out(2 * n_high * (a + d))
-        + out(2 * n_high * b + 4 * (n_high - 1) * e)
-        + out(2 * n_high * (a + d + b) + 4 * e),
+        out_shape=[out(away_y), out(away_z)] + [out(n_row)] * n_acc,
         in_specs=[hbm] * 7,
-        out_specs=[vmem] * 6,
+        out_specs=[vmem] * (2 + n_acc),
         scratch_shapes=[
             pltpu.VMEM(projections.shape, jnp.bfloat16),
             pltpu.SMEM((n_pose, n_part), jnp.float32),
@@ -224,19 +256,24 @@
             pltpu.VMEM(transfer.shape, jnp.float32),
             pltpu.VMEM(transfer.shape, jnp.float32),
         ]
-        + [pltpu.VMEM((n_row, LANES), jnp.float32)] * n_acc
+        + [pltpu.VMEM((n_pose * SUB, LANES), jnp.float32)] * N_BUF
         + [
             pltpu.SemaphoreType.DMA((n_part,)),
             pltpu.SemaphoreType.DMA((3,)),
             pltpu.SemaphoreType.DMA((3,)),
             pltpu.SemaphoreType.DMA,
         ],
-        compiler_params=pltpu.CompilerParams(vmem_limit_bytes=(40 if n_acc == 4 else 56) * MIB),
+        compiler_params=pltpu.CompilerParams(vmem_limit_bytes=24 * MIB),
         name="accumulate",
     )(
         stay(projections), stay(images), stay(transfer),
         stay(pose_weights.T), stay(pose_of.T), stay(pose_blocks.T), stay(pose_tiles.T),
     )
+    rows = 2 * n_high * (a + d + b) + 4 * e
+    kept_y, kept_z, sent_stay, kept_stay = in_vmem(
+        functools.partial(rest_kernel, n_owner), "rest", [away_y, away_z, rows, rows], *accs
+    )
+    return sent_y, kept_y, sent_z, kept_z, sent_stay, kept_stay
 
 
 def in_vmem(kernel, name, rows, *operands):

time: 61.3 us -> 62.5 us (1.020)
  waiting for transfers between devices: 21.2 us -> 23.7 us
  starting transfers between devices: 18.1 us -> 17.1 us
    ppermute x8, waiting for transfers between devices: 18.6 us -> 22 us  [over_blk(): return lax.ppermute(array, 'blk', [(i, i ^ bits) for i in range(n_blk)])]
    pallas_call x1, Pallas kernels: 19.1 us -> 17.2 us  [accumulate(): pl.pallas_call(functools.partial(accumulate_kernel, bank_size, n_owner, n...]
    pallas_call x5 -> x6, Pallas kernels: 0.35 us -> 1.83 us  [in_vmem(): pl.pallas_call(kernel, out_shape=[jax.ShapeDtypeStruct((n, LANES), jnp.fl...]
    ppermute x8, starting transfers between devices: 17 us -> 16 us  [over_blk(): return lax.ppermute(array, 'blk', [(i, i ^ bits) for i in range(n_blk)])]
    ppermute x4, waiting for transfers between devices: 2.6 us -> 1.71 us  [over_rep(): return lax.ppermute(array, 'rep', [(0, 1), (1, 0)])]
  transfers between devices with their start and end apart: 12 -> 12, of which waited for: 8 -> 7; matrix products, arithmetic and copies ran while one was open for 0% -> 0% of each run, Pallas kernels for 0% -> 3%
where the time goes in v12:
time: 62.5 us; the launch traced here: 62.3 us
  waiting for transfers between devices  23.7 us (38%)
  Pallas kernels  21.4 us (34%)
  starting transfers between devices  17.1 us (27%)
    ppermute x8, waiting for transfers between devices, over_blk(): return lax.ppermute(array, 'blk', [(i, i ^ bits) for i in range(n_blk)])  22 us
    pallas_call x1, Pallas kernels, accumulate(): pl.pallas_call(functools.partial(accumulate_kernel, bank_size, n_owner, n...  17.2 us
    ppermute x8, starting transfers between devices, over_blk(): return lax.ppermute(array, 'blk', [(i, i ^ bits) for i in range(n_blk)])  16 us
    pallas_call x1, Pallas kernels, apply_bank(): pl.pallas_call(bank_kernel, out_shape=jax.ShapeDtypeStruct((NB_DEV, n_z,...  2.36 us
    pallas_call x6, Pallas kernels, in_vmem(): pl.pallas_call(kernel, out_shape=[jax.ShapeDtypeStruct((n, LANES), jnp.fl...  1.83 us
    ppermute x4, waiting for transfers between devices, over_rep(): return lax.ppermute(array, 'rep', [(0, 1), (1, 0)])  1.71 us
  transfers between devices with their start and end apart: 12, of which 7 were waited for; matrix products, arithmetic and copies ran while one was open for 0% of the time, Pallas kernels for 3%

profile of v12, /device:TPU:0, one launch (start us, length us, event | category | flops | bytes accessed | tf_op | source)
XLA Modules:
  0.0 62.3 jit_solution(16278156860349647680)
XLA Ops:
  0.0 17.2 %accumulate.1 = (f32[1024,128]{1,0:T(8,128)S(1)}, f32[1024,128]{1,0:T(8,128)S(1)}, f32[8192,128]{1,0:T(8,128)S(1)}, f32[8192,128]{1,0:T(8,128)S(1)}, f32[8192,128]{1,0:T(8,128)S(1)}, /*index=5*/f32[8192,128]{1,0:T(8,128)S(1)}) custom-call(bf16[36864,128]{1,0:T(8,128)(2,1)} %bitcast.29, bf16[4608,128]{1,0:T(8,128)(2,1)} %bitcast.30, ...), custom_call_target="tpu_custom_call" | custom-call | tf_op jit(solution)/shard_map/accumulate/pallas_call | solution.py:243
  17.2 0.5 collective-permute-start.1
  17.7 1.5 %rest.1 = (f32[1024,128]{1,0:T(8,128)S(1)}, f32[1024,128]{1,0:T(8,128)S(1)}, f32[2048,128]{1,0:T(8,128)S(1)}, f32[2048,128]{1,0:T(8,128)S(1)}) custom-call(f32[8192,128]{1,0:T(8,128)S(1)} %get-tuple-element.27.refs_0_, f32[8192,128]{1,0:T(8,128)S(1)} %get-tuple-element.28.refs_1_, f32[8192,128]{1,0:T(8,128)S(1)} %get-tuple-element.29.refs_2_, ...), custom_call_target="tpu_custom_call" | custom-call | tf_op jit(solution)/shard_map/rest/pallas_call | solution.py:281
  19.2 0.1 collective-permute-start
  19.4 0.5 collective-permute-start.3
  19.8 0.1 first_y.1
  19.9 2.7 %collective-permute-start.2 = (f32[1024,128]{1,0:T(8,128)S(1)}, f32[1024,128]{1,0:T(8,128)S(1)}, u32[]{:S(2)}, u32[]{:S(2)}) collective-permute-start(f32[1024,128]{1,0:T(8,128)S(1)} %first_y.1), channel_id=1, source_target_pairs={{0,2},{2,0},{4,6},{6,4},{8,10},{10,8},{12,14},{14,12},{1,3},{3,1},... | collective-permute-start | bytes 1572872 | tf_op jit(solution)/shard_map/ppermute | solution.py:421
  22.5 0.2 collective-permute-done.3.got
  22.8 2.8 %collective-permute-start.4 = (f32[576,128]{1,0:T(8,128)S(1)}, f32[576,128]{1,0:T(8,128)S(1)}, u32[]{:S(2)}, u32[]{:S(2)}) collective-permute-start(f32[576,128]{1,0:T(8,128)S(1)} %get-tuple-element.37), channel_id=1, source_target_pairs={{0,4},{2,6},{4,0},{6,2},{8,12},{10,14},{12,8},{14,10},{1,5},{3,7},... | collective-permute-start | bytes 884744 | tf_op jit(solution)/shard_map/ppermute | solution.py:421
  25.6 2.6 %collective-permute-start.5 = (f32[448,128]{1,0:T(8,128)S(1)}, f32[448,128]{1,0:T(8,128)S(1)}, u32[]{:S(2)}, u32[]{:S(2)}) collective-permute-start(f32[448,128]{1,0:T(8,128)S(1)} %get-tuple-element.38), channel_id=1, source_target_pairs={{0,8},{2,10},{4,12},{6,14},{8,0},{10,2},{12,4},{14,6},{1,9},{3,11}... | collective-permute-start | bytes 688136 | tf_op jit(solution)/shard_map/ppermute | solution.py:421
  28.1 9.1 %collective-permute-done.5.rest_0_ = f32[448,128]{1,0:T(8,128)S(1)} collective-permute-done((f32[448,128]{1,0:T(8,128)S(1)}, f32[448,128]{1,0:T(8,128)S(1)}, u32[]{:S(2)}, u32[]{:S(2)}) %collective-permute-start.5) | collective-permute-done | bytes 229408 | tf_op jit(solution)/shard_map/ppermute | solution.py:421
  37.3 0.7 %collective-permute-done.4.got_l = f32[576,128]{1,0:T(8,128)S(1)} collective-permute-done((f32[576,128]{1,0:T(8,128)S(1)}, f32[576,128]{1,0:T(8,128)S(1)}, u32[]{:S(2)}, u32[]{:S(2)}) %collective-permute-start.4) | collective-permute-done | bytes 294944 | tf_op jit(solution)/shard_map/ppermute | solution.py:421
  38.0 0.2 second.1
  38.2 1.7 %collective-permute-start.6 = (f32[512,128]{1,0:T(8,128)S(1)}, f32[512,128]{1,0:T(8,128)S(1)}, u32[]{:S(2)}, u32[]{:S(2)}) collective-permute-start(f32[512,128]{1,0:T(8,128)S(1)} %get-tuple-element.43), channel_id=1, source_target_pairs={{0,2},{2,0},{4,6},{6,4},{8,10},{10,8},{12,14},{14,12},{1,3},{3,1},... | collective-permute-start | bytes 786440 | tf_op jit(solution)/shard_map/ppermute | solution.py:421
  39.9 2.6 %collective-permute-start.7 = (f32[256,128]{1,0:T(8,128)S(1)}, f32[256,128]{1,0:T(8,128)S(1)}, u32[]{:S(2)}, u32[]{:S(2)}) collective-permute-start(f32[256,128]{1,0:T(8,128)S(1)} %get-tuple-element.44), channel_id=1, source_target_pairs={{0,4},{2,6},{4,0},{6,2},{8,12},{10,14},{12,8},{14,10},{1,5},{3,7},... | collective-permute-start | bytes 393224 | tf_op jit(solution)/shard_map/ppermute | solution.py:421
  42.5 1.6 %collective-permute-start.8 = (f32[256,128]{1,0:T(8,128)S(1)}, f32[256,128]{1,0:T(8,128)S(1)}, u32[]{:S(2)}, u32[]{:S(2)}) collective-permute-start(f32[256,128]{1,0:T(8,128)S(1)} %get-tuple-element.45), channel_id=1, source_target_pairs={{0,8},{2,10},{4,12},{6,14},{8,0},{10,2},{12,4},{14,6},{1,9},{3,11}... | collective-permute-start | bytes 393224 | tf_op jit(solution)/shard_map/ppermute | solution.py:421
  44.1 2.0 %collective-permute-done.7.got_l = f32[256,128]{1,0:T(8,128)S(1)} collective-permute-done((f32[256,128]{1,0:T(8,128)S(1)}, f32[256,128]{1,0:T(8,128)S(1)}, u32[]{:S(2)}, u32[]{:S(2)}) %collective-permute-start.7) | collective-permute-done | bytes 131104 | tf_op jit(solution)/shard_map/ppermute | solution.py:421
  46.1 4.5 %collective-permute-done.8.rest_0_ = f32[256,128]{1,0:T(8,128)S(1)} collective-permute-done((f32[256,128]{1,0:T(8,128)S(1)}, f32[256,128]{1,0:T(8,128)S(1)}, u32[]{:S(2)}, u32[]{:S(2)}) %collective-permute-start.8) | collective-permute-done | bytes 131104 | tf_op jit(solution)/shard_map/ppermute | solution.py:421
  50.7 0.3 collective-permute-start.10
  51.0 1.7 %collective-permute-start.9 = (f32[240,128]{1,0:T(8,128)S(1)}, f32[240,128]{1,0:T(8,128)S(1)}, u32[]{:S(2)}, u32[]{:S(2)}) collective-permute-start(f32[240,128]{1,0:T(8,128)S(1)} %get-tuple-element.47), channel_id=1, source_target_pairs={{0,4},{2,6},{4,0},{6,2},{8,12},{10,14},{12,8},{14,10},{1,5},{3,7},... | collective-permute-start | bytes 368648 | tf_op jit(solution)/shard_map/ppermute | solution.py:421
  52.7 5.6 %collective-permute-done.9.got_l = f32[240,128]{1,0:T(8,128)S(1)} collective-permute-done((f32[240,128]{1,0:T(8,128)S(1)}, f32[240,128]{1,0:T(8,128)S(1)}, u32[]{:S(2)}, u32[]{:S(2)}) %collective-permute-start.9) | collective-permute-done | bytes 122912 | tf_op jit(solution)/shard_map/ppermute | solution.py:421
  58.3 0.1 collective-permute-start.11
  58.4 1.5 %collective-permute-done.11 = f32[512,128]{1,0:T(8,128)S(1)} collective-permute-done((f32[512,128]{1,0:T(8,128)S(1)}, f32[512,128]{1,0:T(8,128)S(1)}, u32[]{:S(2)}, u32[]{:S(2)}) %collective-permute-start.11) | collective-permute-done | bytes 262176 | tf_op jit(solution)/shard_map/ppermute | solution.py:418
  59.9 2.4 %apply_bank.1 = f32[8,32,1024]{2,1,0:T(8,128)} custom-call(f32[4,16,8,128]{3,2,1,0:T(8,128)S(1)} %bitcast.27, f32[4,16,8,128]{3,2,1,0:T(8,128)S(1)} %bitcast.28, f32[16,32,1024]{2,1,0:T(8,128)S(1)} %copy-done), custom_call_target="tpu_custom_call" | custom-call | tf_op jit(solution)/shard_map/apply_bank/pallas_call | solution.py:395
  (10 shorter events, 0.2 us)
Async XLA Ops:
  17.2 2.6 %collective-permute-start.1 = (f32[1024,128]{1,0:T(8,128)S(1)}, f32[1024,128]{1,0:T(8,128)S(1)}, u32[]{:S(2)}, u32[]{:S(2)}) collective-permute-start(f32[1024,128]{1,0:T(8,128)S(1)} %get-tuple-element.34), channel_id=1, source_target_pairs={{0,1},{1,0},{2,3},{3,2},{4,5},{5,4},{6,7},{7,6},{8,9},{9,8},{10,11... | collective-permute-start | bytes 1572872 | tf_op jit(solution)/shard_map/ppermute | solution.py:418
  19.2 40.7 %copy-start = (f32[16,32,1024]{2,1,0:T(8,128)S(1)}, f32[16,32,1024]{2,1,0:T(8,128)}, u32[]{:S(2)}) copy-start(f32[16,32,1024]{2,1,0:T(8,128)} %bank.1) | copy-start | bytes 6291460
  19.2 18.8 %collective-permute-start = (f32[2048,128]{1,0:T(8,128)S(1)}, f32[2048,128]{1,0:T(8,128)S(1)}, u32[]{:S(2)}, u32[]{:S(2)}) collective-permute-start(f32[2048,128]{1,0:T(8,128)S(1)} %get-tuple-element.32), channel_id=1, source_target_pairs={{0,1},{1,0},{2,3},{3,2},{4,5},{5,4},{6,7},{7,6},{8,9},{9,8},{10,11... | collective-permute-start | bytes 3145736 | tf_op jit(solution)/shard_map/ppermute | solution.py:418
  19.4 3.4 %collective-permute-start.3 = (f32[1024,128]{1,0:T(8,128)S(1)}, f32[1024,128]{1,0:T(8,128)S(1)}, u32[]{:S(2)}, u32[]{:S(2)}) collective-permute-start(f32[1024,128]{1,0:T(8,128)S(1)} %get-tuple-element.36), channel_id=1, source_target_pairs={{0,1},{1,0},{2,3},{3,2},{4,5},{5,4},{6,7},{7,6},{8,9},{9,8},{10,11... | collective-permute-start | bytes 1572872 | tf_op jit(solution)/shard_map/ppermute | solution.py:418
  19.9 18.1 %collective-permute-start.2 = (f32[1024,128]{1,0:T(8,128)S(1)}, f32[1024,128]{1,0:T(8,128)S(1)}, u32[]{:S(2)}, u32[]{:S(2)}) collective-permute-start(f32[1024,128]{1,0:T(8,128)S(1)} %first_y.1), channel_id=1, source_target_pairs={{0,2},{2,0},{4,6},{6,4},{8,10},{10,8},{12,14},{14,12},{1,3},{3,1},... | collective-permute-start | bytes 1572872 | tf_op jit(solution)/shard_map/ppermute | solution.py:421
  22.8 15.2 %collective-permute-start.4 = (f32[576,128]{1,0:T(8,128)S(1)}, f32[576,128]{1,0:T(8,128)S(1)}, u32[]{:S(2)}, u32[]{:S(2)}) collective-permute-start(f32[576,128]{1,0:T(8,128)S(1)} %get-tuple-element.37), channel_id=1, source_target_pairs={{0,4},{2,6},{4,0},{6,2},{8,12},{10,14},{12,8},{14,10},{1,5},{3,7},... | collective-permute-start | bytes 884744 | tf_op jit(solution)/shard_map/ppermute | solution.py:421
  25.6 11.7 %collective-permute-start.5 = (f32[448,128]{1,0:T(8,128)S(1)}, f32[448,128]{1,0:T(8,128)S(1)}, u32[]{:S(2)}, u32[]{:S(2)}) collective-permute-start(f32[448,128]{1,0:T(8,128)S(1)} %get-tuple-element.38), channel_id=1, source_target_pairs={{0,8},{2,10},{4,12},{6,14},{8,0},{10,2},{12,4},{14,6},{1,9},{3,11}... | collective-permute-start | bytes 688136 | tf_op jit(solution)/shard_map/ppermute | solution.py:421
  38.2 12.5 %collective-permute-start.6 = (f32[512,128]{1,0:T(8,128)S(1)}, f32[512,128]{1,0:T(8,128)S(1)}, u32[]{:S(2)}, u32[]{:S(2)}) collective-permute-start(f32[512,128]{1,0:T(8,128)S(1)} %get-tuple-element.43), channel_id=1, source_target_pairs={{0,2},{2,0},{4,6},{6,4},{8,10},{10,8},{12,14},{14,12},{1,3},{3,1},... | collective-permute-start | bytes 786440 | tf_op jit(solution)/shard_map/ppermute | solution.py:421
  39.9 6.2 %collective-permute-start.7 = (f32[256,128]{1,0:T(8,128)S(1)}, f32[256,128]{1,0:T(8,128)S(1)}, u32[]{:S(2)}, u32[]{:S(2)}) collective-permute-start(f32[256,128]{1,0:T(8,128)S(1)} %get-tuple-element.44), channel_id=1, source_target_pairs={{0,4},{2,6},{4,0},{6,2},{8,12},{10,14},{12,8},{14,10},{1,5},{3,7},... | collective-permute-start | bytes 393224 | tf_op jit(solution)/shard_map/ppermute | solution.py:421
  42.5 8.1 %collective-permute-start.8 = (f32[256,128]{1,0:T(8,128)S(1)}, f32[256,128]{1,0:T(8,128)S(1)}, u32[]{:S(2)}, u32[]{:S(2)}) collective-permute-start(f32[256,128]{1,0:T(8,128)S(1)} %get-tuple-element.45), channel_id=1, source_target_pairs={{0,8},{2,10},{4,12},{6,14},{8,0},{10,2},{12,4},{14,6},{1,9},{3,11}... | collective-permute-start | bytes 393224 | tf_op jit(solution)/shard_map/ppermute | solution.py:421
  50.7 7.6 %collective-permute-start.10 = (f32[272,128]{1,0:T(8,128)S(1)}, f32[272,128]{1,0:T(8,128)S(1)}, u32[]{:S(2)}, u32[]{:S(2)}) collective-permute-start(f32[272,128]{1,0:T(8,128)S(1)} %get-tuple-element.48), channel_id=1, source_target_pairs={{0,8},{2,10},{4,12},{6,14},{8,0},{10,2},{12,4},{14,6},{1,9},{3,11}... | collective-permute-start | bytes 417800 | tf_op jit(solution)/shard_map/ppermute | solution.py:421
  51.0 7.3 %collective-permute-start.9 = (f32[240,128]{1,0:T(8,128)S(1)}, f32[240,128]{1,0:T(8,128)S(1)}, u32[]{:S(2)}, u32[]{:S(2)}) collective-permute-start(f32[240,128]{1,0:T(8,128)S(1)} %get-tuple-element.47), channel_id=1, source_target_pairs={{0,4},{2,6},{4,0},{6,2},{8,12},{10,14},{12,8},{14,10},{1,5},{3,7},... | collective-permute-start | bytes 368648 | tf_op jit(solution)/shard_map/ppermute | solution.py:421
  58.3 1.6 %collective-permute-start.11 = (f32[512,128]{1,0:T(8,128)S(1)}, f32[512,128]{1,0:T(8,128)S(1)}, u32[]{:S(2)}, u32[]{:S(2)}) collective-permute-start(f32[512,128]{1,0:T(8,128)S(1)} %last.1), channel_id=1, source_target_pairs={{0,1},{1,0},{2,3},{3,2},{4,5},{5,4},{6,7},{7,6},{8,9},{9,8},{10,11... | collective-permute-start | bytes 786440 | tf_op jit(solution)/shard_map/ppermute | solution.py:418

commit v13 on v12

--- a/solution.py
+++ b/solution.py
@@ -12,9 +12,9 @@
 SUB = 8
 MIB = 1 << 20
 UNROLL = 12
-N_BUF = 2
+N_BUF = 4
 ORDERS = ("ylh", "yhl", "lyh", "hyl")
-PART_ROWS = (16, 16, 18, 14)
+PART_ROWS = (16, 16, 16, 16)
 
 
 def position():
@@ -25,7 +25,7 @@
 def accumulate_kernel(
     bank_size, n_owner, n_acc,
     proj_hbm, img_hbm, tra_hbm, w_hbm, pose_hbm, blocks_hbm, tiles_hbm,
-    sent_y, sent_z, *rest,
+    sent_away, *rest,
 ):
     accs, rest = rest[:n_acc], rest[n_acc:]
     proj, weight, pose, blocks, tiles, idx_v, idx_s, square, cross = rest[:9]
@@ -143,23 +143,23 @@
         weights = [jnp.full((SUB, LANES), weight[k, p], jnp.float32) for k in range(n_pose)]
 
         stage(p, 0, parts[0])
+        stage(p, 1, parts[1])
 
         @pl.loop(0, n_tile, step=UNROLL, init_carry=tuple(terms(p, 0, staged(parts[0]), weights)))
         def _(j, values):
+            def tile(u):
+                return jnp.minimum(j + u, n_tile - 1) if u >= UNROLL else j + u
+
             for u in range(UNROLL):
-                part = parts[(u // 2 + 1) % len(parts)]
-                if u % 2 == 0:
-                    stage(p, jnp.minimum(j + u + 2, n_tile - 1) if u + 2 == UNROLL else j + u + 2, part)
-                    following = j + u + 1
-                    later = terms(p, following, rolled(p, following), weights)
-                else:
-                    following = jnp.minimum(j + u + 1, n_tile - 1) if u + 1 == UNROLL else j + u + 1
-                    later = terms(p, following, staged(part), weights)
+                if (u + 2) % 3 != 2:
+                    stage(p, tile(u + 2), parts[(u + 2) % N_BUF])
+                cells = staged(parts[(u + 1) % N_BUF]) if (u + 1) % 3 != 2 else rolled(p, tile(u + 1))
+                later = terms(p, tile(u + 1), cells, weights)
                 add_rows(p, j + u, values)
                 values = later
             return tuple(values)
 
-    Sums(n_owner, accs).pieces_away(sent_y, sent_z, sent=True)
+    Sums(n_owner, accs).pieces_away(sent_away, sent=True)
 
 
 class Sums:
@@ -190,11 +190,10 @@
 
         return begin + len(firsts) * inner * size
 
-    def pieces_away(self, out_y, out_z, sent):
-        begin = self.pieces(out_y, 0, 0, range(1, 2), sent)
-        self.pieces(out_y, begin, 1, range(1, 2), sent)
-        begin = self.pieces(out_z, 0, 2, range(1, 2), sent)
-        self.pieces(out_z, begin, 3, range(1, self.sizes["h"]), sent)
+    def pieces_away(self, out, sent):
+        begin = 0
+        for part, order in enumerate(ORDERS):
+            begin = self.pieces(out, begin, part, range(1, self.sizes[order[0]]), sent)
 
     def pieces_stay(self, out, sent):
         begin = 0
@@ -203,9 +202,9 @@
 
 
 def rest_kernel(n_owner, *refs):
-    accs, (kept_y, kept_z, sent_stay, kept_stay) = refs[:-4], refs[-4:]
+    accs, (kept_away, sent_stay, kept_stay) = refs[:-3], refs[-3:]
     sums = Sums(n_owner, accs)
-    sums.pieces_away(kept_y, kept_z, sent=False)
+    sums.pieces_away(kept_away, sent=False)
     sums.pieces_stay(sent_stay, sent=True)
     sums.pieces_stay(kept_stay, sent=False)
 
@@ -222,7 +221,7 @@
     bank_size, n_owner,
 ):
     n_part, n_pose, n_tile, n_cell = projections.shape
-    assert n_cell == SUB * LANES and n_pose == SUB and n_part % SUB == 0 and n_tile % UNROLL == 0
+    assert n_cell == SUB * LANES and n_pose == SUB and n_part % SUB == 0 and n_tile % UNROLL == 0 and UNROLL % (3 * N_BUF) == 0
     n_row = n_owner * NB_DEV * bank_size * SUB
     n_acc = 4 if n_row * LANES * 4 <= 4 * MIB else 2
     projections = tiles_in_order(jnp.transpose(projections, (0, 2, 1, 3)))
@@ -235,16 +234,16 @@
     a, d, b, e = (rows * SUB for rows in PART_ROWS)
     assert sum(PART_ROWS) == NB_DEV // 2 * bank_size
 
-    away_y, away_z = 2 * n_high * (a + d), 2 * n_high * b + 4 * (n_high - 1) * e
+    away = 2 * n_high * (a + d + b) + 4 * (n_high - 1) * e
 
     def out(rows):
         return jax.ShapeDtypeStruct((rows, LANES), jnp.float32)
 
-    sent_y, sent_z, *accs = pl.pallas_call(
+    sent_away, *accs = pl.pallas_call(
         functools.partial(accumulate_kernel, bank_size, n_owner, n_acc),
-        out_shape=[out(away_y), out(away_z)] + [out(n_row)] * n_acc,
+        out_shape=[out(away)] + [out(n_row)] * n_acc,
         in_specs=[hbm] * 7,
-        out_specs=[vmem] * (2 + n_acc),
+        out_specs=[vmem] * (1 + n_acc),
         scratch_shapes=[
             pltpu.VMEM(projections.shape, jnp.bfloat16),
             pltpu.SMEM((n_pose, n_part), jnp.float32),
@@ -270,10 +269,7 @@
         stay(pose_weights.T), stay(pose_of.T), stay(pose_blocks.T), stay(pose_tiles.T),
     )
     rows = 2 * n_high * (a + d + b) + 4 * e
-    kept_y, kept_z, sent_stay, kept_stay = in_vmem(
-        functools.partial(rest_kernel, n_owner), "rest", [away_y, away_z, rows, rows], *accs
-    )
-    return sent_y, kept_y, sent_z, kept_z, sent_stay, kept_stay
+    return sent_away, *in_vmem(functools.partial(rest_kernel, n_owner), "rest", [away, rows, rows], *accs)
 
 
 def in_vmem(kernel, name, rows, *operands):
@@ -408,7 +404,7 @@
     bank_size = weight_bank.shape[0]
     n_blk = lax.axis_size("blk")
     n_high = n_blk // 4
-    sent_y, kept_y, sent_z, kept_z, sent_stay, kept_stay = accumulate(
+    sent_away, kept_away, sent_stay, kept_stay = accumulate(
         projections, images, transfer, pose_weights, pose_of, pose_blocks, pose_tiles,
         bank_size, n_blk,
     )
@@ -424,11 +420,11 @@
         return [over_blk(array, 4 * (i + 1)) for i, array in enumerate(arrays)]
 
     n_h = n_high - 1
-    got_y, got_z, got_stay = over_rep(sent_y), over_rep(sent_z), over_rep(sent_stay)
-    (to_y,) = in_vmem(first_kernel, "first_y", [kept_y.shape[0]], kept_y, got_y)
-    got_y = over_blk(to_y, 1)
-    to_l, *to_h = in_vmem(first_kernel, "first_z", [2 * n_high * b] + [4 * e] * n_h, kept_z, got_z)
-    got_l, got_h = over_blk(to_l, 2), over_h(to_h)
+    got_away, got_stay = over_rep(sent_away), over_rep(sent_stay)
+    to_y, to_l, *to_h = in_vmem(
+        first_kernel, "first", [2 * n_high * (a + d), 2 * n_high * b] + [4 * e] * n_h, kept_away, got_away
+    )
+    got_y, got_l, got_h = over_blk(to_y, 1), over_blk(to_l, 2), over_h(to_h)
     own_a, own_d, own_b, own_e, to_y, to_l, *to_h = in_vmem(
         functools.partial(second_kernel, n_high), "second",
         [n_high * a, 2 * d, n_high * b, 2 * e, n_high * b + 2 * e, n_high * a] + [2 * d] * n_h,

time: 62.5 us -> 58.4 us (0.934)
  starting transfers between devices: 17.1 us -> 13.2 us
    ppermute x8, starting transfers between devices: 16 us -> 12.5 us  [over_blk(): return lax.ppermute(array, 'blk', [(i, i ^ bits) for i in range(n_blk)])]
    ppermute x4 -> x3, waiting for transfers between devices: 1.71 us -> 2.2 us  [over_rep(): return lax.ppermute(array, 'rep', [(0, 1), (1, 0)])]
    pallas_call x6 -> x5, Pallas kernels: 1.83 us -> 1.81 us  [in_vmem(): pl.pallas_call(kernel, out_shape=[jax.ShapeDtypeStruct((n, LANES), jnp.fl...]
  transfers between devices with their start and end apart: 12 -> 11, of which waited for: 7 -> 7; matrix products, arithmetic and copies ran while one was open for 0% -> 0% of each run, Pallas kernels for 3% -> 3%
where the time goes in v13:
time: 58.4 us; the launch traced here: 58.3 us
  waiting for transfers between devices  23.8 us (41%)
  Pallas kernels  21.2 us (36%)
  starting transfers between devices  13.2 us (23%)
    ppermute x8, waiting for transfers between devices, over_blk(): return lax.ppermute(array, 'blk', [(i, i ^ bits) for i in range(n_blk)])  21.6 us
    pallas_call x1, Pallas kernels, accumulate(): pl.pallas_call(functools.partial(accumulate_kernel, bank_size, n_owner, n...  17 us
    ppermute x8, starting transfers between devices, over_blk(): return lax.ppermute(array, 'blk', [(i, i ^ bits) for i in range(n_blk)])  12.5 us
    pallas_call x1, Pallas kernels, apply_bank(): pl.pallas_call(bank_kernel, out_shape=jax.ShapeDtypeStruct((NB_DEV, n_z,...  2.36 us
    ppermute x3, waiting for transfers between devices, over_rep(): return lax.ppermute(array, 'rep', [(0, 1), (1, 0)])  2.2 us
    pallas_call x5, Pallas kernels, in_vmem(): pl.pallas_call(kernel, out_shape=[jax.ShapeDtypeStruct((n, LANES), jnp.fl...  1.81 us
  transfers between devices with their start and end apart: 11, of which 7 were waited for; matrix products, arithmetic and copies ran while one was open for 0% of the time, Pallas kernels for 3%

profile of v13, /device:TPU:0, one launch (start us, length us, event | category | flops | bytes accessed | tf_op | source)
XLA Modules:
  0.0 58.3 jit_solution(10904156138409723174)
XLA Ops:
  0.0 17.0 %accumulate.1 = (f32[2048,128]{1,0:T(8,128)S(1)}, f32[8192,128]{1,0:T(8,128)S(1)}, f32[8192,128]{1,0:T(8,128)S(1)}, f32[8192,128]{1,0:T(8,128)S(1)}, f32[8192,128]{1,0:T(8,128)S(1)}) custom-call(bf16[36864,128]{1,0:T(8,128)(2,1)} %bitcast.29, bf16[4608,128]{1,0:T(8,128)(2,1)} %bitcast.30, bf16[4608,128]{1,0:T(8,128)(2,1)} %bitcast.31, f32[8,16]{1,0:T(8,128)} %bitcast.34, ...), custom_call_target="tpu_custom_call" | custom-call | tf_op jit(solution)/shard_map/accumulate/pallas_call | solution.py:242
  17.0 0.5 collective-permute-start.1
  17.5 1.5 %rest.1 = (f32[2048,128]{1,0:T(8,128)S(1)}, f32[2048,128]{1,0:T(8,128)S(1)}, f32[2048,128]{1,0:T(8,128)S(1)}) custom-call(f32[8192,128]{1,0:T(8,128)S(1)} %get-tuple-element.26.refs_0_, f32[8192,128]{1,0:T(8,128)S(1)} %get-tuple-element.27.refs_1_, f32[8192,128]{1,0:T(8,128)S(1)} %get-tuple-element.28.refs_2_, f32[8192,128]{1,0:T(8,128)S(1)} %get-tuple-element.29.refs_3_), custom_call_target="tpu_custom_call" | custom-call | tf_op jit(solution)/shard_map/rest/pallas_call | solution.py:277
  19.0 0.1 collective-permute-start
  19.2 0.7 %collective-permute-done.1.got = f32[2048,128]{1,0:T(8,128)S(1)} collective-permute-done((f32[2048,128]{1,0:T(8,128)S(1)}, f32[2048,128]{1,0:T(8,128)S(1)}, u32[]{:S(2)}, u32[]{:S(2)}) %collective-permute-start.1) | collective-permute-done | bytes 1048608 | tf_op jit(solution)/shard_map/ppermute | solution.py:414
  19.8 0.1 first.1
  19.9 3.0 %collective-permute-start.2 = (f32[1024,128]{1,0:T(8,128)S(1)}, f32[1024,128]{1,0:T(8,128)S(1)}, u32[]{:S(2)}, u32[]{:S(2)}) collective-permute-start(f32[1024,128]{1,0:T(8,128)S(1)} %get-tuple-element.34), channel_id=1, source_target_pairs={{0,2},{2,0},{4,6},{6,4},{8,10},{10,8},{12,14},{14,12},{1,3},{3,1},... | collective-permute-start | bytes 1572872 | tf_op jit(solution)/shard_map/ppermute | solution.py:417
  22.9 1.6 %collective-permute-start.3 = (f32[512,128]{1,0:T(8,128)S(1)}, f32[512,128]{1,0:T(8,128)S(1)}, u32[]{:S(2)}, u32[]{:S(2)}) collective-permute-start(f32[512,128]{1,0:T(8,128)S(1)} %get-tuple-element.35), channel_id=1, source_target_pairs={{0,4},{2,6},{4,0},{6,2},{8,12},{10,14},{12,8},{14,10},{1,5},{3,7},... | collective-permute-start | bytes 786440 | tf_op jit(solution)/shard_map/ppermute | solution.py:417
  24.5 2.6 %collective-permute-start.4 = (f32[512,128]{1,0:T(8,128)S(1)}, f32[512,128]{1,0:T(8,128)S(1)}, u32[]{:S(2)}, u32[]{:S(2)}) collective-permute-start(f32[512,128]{1,0:T(8,128)S(1)} %get-tuple-element.36), channel_id=1, source_target_pairs={{0,8},{2,10},{4,12},{6,14},{8,0},{10,2},{12,4},{14,6},{1,9},{3,11}... | collective-permute-start | bytes 786440 | tf_op jit(solution)/shard_map/ppermute | solution.py:417
  27.1 9.4 %collective-permute-done.3.got_l = f32[512,128]{1,0:T(8,128)S(1)} collective-permute-done((f32[512,128]{1,0:T(8,128)S(1)}, f32[512,128]{1,0:T(8,128)S(1)}, u32[]{:S(2)}, u32[]{:S(2)}) %collective-permute-start.3) | collective-permute-done | bytes 262176 | tf_op jit(solution)/shard_map/ppermute | solution.py:417
  36.5 2.4 %collective-permute-done.4.rest_0_ = f32[512,128]{1,0:T(8,128)S(1)} collective-permute-done((f32[512,128]{1,0:T(8,128)S(1)}, f32[512,128]{1,0:T(8,128)S(1)}, u32[]{:S(2)}, u32[]{:S(2)}) %collective-permute-start.4) | collective-permute-done | bytes 262176 | tf_op jit(solution)/shard_map/ppermute | solution.py:417
  38.8 0.2 second.1
  39.0 0.6 collective-permute-start.5
  39.6 0.5 collective-permute-start.6
  40.0 2.6 %collective-permute-start.7 = (f32[256,128]{1,0:T(8,128)S(1)}, f32[256,128]{1,0:T(8,128)S(1)}, u32[]{:S(2)}, u32[]{:S(2)}) collective-permute-start(f32[256,128]{1,0:T(8,128)S(1)} %get-tuple-element.43), channel_id=1, source_target_pairs={{0,8},{2,10},{4,12},{6,14},{8,0},{10,2},{12,4},{14,6},{1,9},{3,11}... | collective-permute-start | bytes 393224 | tf_op jit(solution)/shard_map/ppermute | solution.py:417
  42.6 3.8 %collective-permute-done.6.got_l = f32[256,128]{1,0:T(8,128)S(1)} collective-permute-done((f32[256,128]{1,0:T(8,128)S(1)}, f32[256,128]{1,0:T(8,128)S(1)}, u32[]{:S(2)}, u32[]{:S(2)}) %collective-permute-start.6) | collective-permute-done | bytes 131104 | tf_op jit(solution)/shard_map/ppermute | solution.py:417
  46.4 1.1 %collective-permute-done.7.rest_0_ = f32[256,128]{1,0:T(8,128)S(1)} collective-permute-done((f32[256,128]{1,0:T(8,128)S(1)}, f32[256,128]{1,0:T(8,128)S(1)}, u32[]{:S(2)}, u32[]{:S(2)}) %collective-permute-start.7) | collective-permute-done | bytes 131104 | tf_op jit(solution)/shard_map/ppermute | solution.py:417
  47.5 0.1 third.1
  47.6 0.1 collective-permute-start.8
  47.7 1.7 %collective-permute-start.9 = (f32[256,128]{1,0:T(8,128)S(1)}, f32[256,128]{1,0:T(8,128)S(1)}, u32[]{:S(2)}, u32[]{:S(2)}) collective-permute-start(f32[256,128]{1,0:T(8,128)S(1)} %get-tuple-element.46), channel_id=1, source_target_pairs={{0,8},{2,10},{4,12},{6,14},{8,0},{10,2},{12,4},{14,6},{1,9},{3,11}... | collective-permute-start | bytes 393224 | tf_op jit(solution)/shard_map/ppermute | solution.py:417
  49.4 4.9 %collective-permute-done.8.got_l = f32[256,128]{1,0:T(8,128)S(1)} collective-permute-done((f32[256,128]{1,0:T(8,128)S(1)}, f32[256,128]{1,0:T(8,128)S(1)}, u32[]{:S(2)}, u32[]{:S(2)}) %collective-permute-start.8) | collective-permute-done | bytes 131104 | tf_op jit(solution)/shard_map/ppermute | solution.py:417
  54.3 0.1 collective-permute-start.10
  54.4 1.5 %collective-permute-done.10 = f32[512,128]{1,0:T(8,128)S(1)} collective-permute-done((f32[512,128]{1,0:T(8,128)S(1)}, f32[512,128]{1,0:T(8,128)S(1)}, u32[]{:S(2)}, u32[]{:S(2)}) %collective-permute-start.10) | collective-permute-done | bytes 262176 | tf_op jit(solution)/shard_map/ppermute | solution.py:414
  55.9 2.4 %apply_bank.1 = f32[8,32,1024]{2,1,0:T(8,128)} custom-call(f32[4,16,8,128]{3,2,1,0:T(8,128)S(1)} %bitcast.27, f32[4,16,8,128]{3,2,1,0:T(8,128)S(1)} %bitcast.28, f32[16,32,1024]{2,1,0:T(8,128)S(1)} %copy-done), custom_call_target="tpu_custom_call" | custom-call | tf_op jit(solution)/shard_map/apply_bank/pallas_call | solution.py:391
  (7 shorter events, 0.0 us)
Async XLA Ops:
  17.0 2.8 %collective-permute-start.1 = (f32[2048,128]{1,0:T(8,128)S(1)}, f32[2048,128]{1,0:T(8,128)S(1)}, u32[]{:S(2)}, u32[]{:S(2)}) collective-permute-start(f32[2048,128]{1,0:T(8,128)S(1)} %get-tuple-element.33), channel_id=1, source_target_pairs={{0,1},{1,0},{2,3},{3,2},{4,5},{5,4},{6,7},{7,6},{8,9},{9,8},{10,11... | collective-permute-start | bytes 3145736 | tf_op jit(solution)/shard_map/ppermute | solution.py:414
  19.0 36.9 %copy-start = (f32[16,32,1024]{2,1,0:T(8,128)S(1)}, f32[16,32,1024]{2,1,0:T(8,128)}, u32[]{:S(2)}) copy-start(f32[16,32,1024]{2,1,0:T(8,128)} %bank.1) | copy-start | bytes 6291460
  19.0 8.0 %collective-permute-start = (f32[2048,128]{1,0:T(8,128)S(1)}, f32[2048,128]{1,0:T(8,128)S(1)}, u32[]{:S(2)}, u32[]{:S(2)}) collective-permute-start(f32[2048,128]{1,0:T(8,128)S(1)} %get-tuple-element.31), channel_id=1, source_target_pairs={{0,1},{1,0},{2,3},{3,2},{4,5},{5,4},{6,7},{7,6},{8,9},{9,8},{10,11... | collective-permute-start | bytes 3145736 | tf_op jit(solution)/shard_map/ppermute | solution.py:414
  19.9 18.9 %collective-permute-start.2 = (f32[1024,128]{1,0:T(8,128)S(1)}, f32[1024,128]{1,0:T(8,128)S(1)}, u32[]{:S(2)}, u32[]{:S(2)}) collective-permute-start(f32[1024,128]{1,0:T(8,128)S(1)} %get-tuple-element.34), channel_id=1, source_target_pairs={{0,2},{2,0},{4,6},{6,4},{8,10},{10,8},{12,14},{14,12},{1,3},{3,1},... | collective-permute-start | bytes 1572872 | tf_op jit(solution)/shard_map/ppermute | solution.py:417
  22.9 13.6 %collective-permute-start.3 = (f32[512,128]{1,0:T(8,128)S(1)}, f32[512,128]{1,0:T(8,128)S(1)}, u32[]{:S(2)}, u32[]{:S(2)}) collective-permute-start(f32[512,128]{1,0:T(8,128)S(1)} %get-tuple-element.35), channel_id=1, source_target_pairs={{0,4},{2,6},{4,0},{6,2},{8,12},{10,14},{12,8},{14,10},{1,5},{3,7},... | collective-permute-start | bytes 786440 | tf_op jit(solution)/shard_map/ppermute | solution.py:417
  24.5 14.4 %collective-permute-start.4 = (f32[512,128]{1,0:T(8,128)S(1)}, f32[512,128]{1,0:T(8,128)S(1)}, u32[]{:S(2)}, u32[]{:S(2)}) collective-permute-start(f32[512,128]{1,0:T(8,128)S(1)} %get-tuple-element.36), channel_id=1, source_target_pairs={{0,8},{2,10},{4,12},{6,14},{8,0},{10,2},{12,4},{14,6},{1,9},{3,11}... | collective-permute-start | bytes 786440 | tf_op jit(solution)/shard_map/ppermute | solution.py:417
  39.0 8.6 %collective-permute-start.5 = (f32[512,128]{1,0:T(8,128)S(1)}, f32[512,128]{1,0:T(8,128)S(1)}, u32[]{:S(2)}, u32[]{:S(2)}) collective-permute-start(f32[512,128]{1,0:T(8,128)S(1)} %get-tuple-element.41), channel_id=1, source_target_pairs={{0,2},{2,0},{4,6},{6,4},{8,10},{10,8},{12,14},{14,12},{1,3},{3,1},... | collective-permute-start | bytes 786440 | tf_op jit(solution)/shard_map/ppermute | solution.py:417
  39.6 6.9 %collective-permute-start.6 = (f32[256,128]{1,0:T(8,128)S(1)}, f32[256,128]{1,0:T(8,128)S(1)}, u32[]{:S(2)}, u32[]{:S(2)}) collective-permute-start(f32[256,128]{1,0:T(8,128)S(1)} %get-tuple-element.42), channel_id=1, source_target_pairs={{0,4},{2,6},{4,0},{6,2},{8,12},{10,14},{12,8},{14,10},{1,5},{3,7},... | collective-permute-start | bytes 393224 | tf_op jit(solution)/shard_map/ppermute | solution.py:417
  40.0 7.5 %collective-permute-start.7 = (f32[256,128]{1,0:T(8,128)S(1)}, f32[256,128]{1,0:T(8,128)S(1)}, u32[]{:S(2)}, u32[]{:S(2)}) collective-permute-start(f32[256,128]{1,0:T(8,128)S(1)} %get-tuple-element.43), channel_id=1, source_target_pairs={{0,8},{2,10},{4,12},{6,14},{8,0},{10,2},{12,4},{14,6},{1,9},{3,11}... | collective-permute-start | bytes 393224 | tf_op jit(solution)/shard_map/ppermute | solution.py:417
  47.6 6.7 %collective-permute-start.8 = (f32[256,128]{1,0:T(8,128)S(1)}, f32[256,128]{1,0:T(8,128)S(1)}, u32[]{:S(2)}, u32[]{:S(2)}) collective-permute-start(f32[256,128]{1,0:T(8,128)S(1)} %get-tuple-element.45), channel_id=1, source_target_pairs={{0,4},{2,6},{4,0},{6,2},{8,12},{10,14},{12,8},{14,10},{1,5},{3,7},... | collective-permute-start | bytes 393224 | tf_op jit(solution)/shard_map/ppermute | solution.py:417
  47.7 6.6 %collective-permute-start.9 = (f32[256,128]{1,0:T(8,128)S(1)}, f32[256,128]{1,0:T(8,128)S(1)}, u32[]{:S(2)}, u32[]{:S(2)}) collective-permute-start(f32[256,128]{1,0:T(8,128)S(1)} %get-tuple-element.46), channel_id=1, source_target_pairs={{0,8},{2,10},{4,12},{6,14},{8,0},{10,2},{12,4},{14,6},{1,9},{3,11}... | collective-permute-start | bytes 393224 | tf_op jit(solution)/shard_map/ppermute | solution.py:417
  54.3 1.6 %collective-permute-start.10 = (f32[512,128]{1,0:T(8,128)S(1)}, f32[512,128]{1,0:T(8,128)S(1)}, u32[]{:S(2)}, u32[]{:S(2)}) collective-permute-start(f32[512,128]{1,0:T(8,128)S(1)} %last.1), channel_id=1, source_target_pairs={{0,1},{1,0},{2,3},{3,2},{4,5},{5,4},{6,7},{7,6},{8,9},{9,8},{10,11... | collective-permute-start | bytes 786440 | tf_op jit(solution)/shard_map/ppermute | solution.py:414

commit v14 on v13

--- a/solution.py
+++ b/solution.py
@@ -28,9 +28,9 @@
     sent_away, *rest,
 ):
     accs, rest = rest[:n_acc], rest[n_acc:]
-    proj, weight, pose, blocks, tiles, idx_v, idx_s, square, cross = rest[:9]
-    parts = rest[9 : 9 + N_BUF]
-    proj_sem, small_sem, table_sem, idx_sem = rest[9 + N_BUF :]
+    proj, img, tra, weight, pose, blocks, tiles, idx_v, idx_s, square, cross = rest[:11]
+    parts = rest[11 : 11 + N_BUF]
+    proj_sem, small_sem, table_sem, idx_sem = rest[11 + N_BUF :]
     n_pose, n_part = pose.shape
     n_tile, n_table = blocks.shape
     n_row = accs[0].shape[0]
@@ -41,10 +41,6 @@
         pltpu.make_async_copy(src, dst, table_sem.at[i])
         for i, (src, dst) in enumerate(((pose_hbm, pose), (blocks_hbm, blocks), (tiles_hbm, tiles)))
     ]
-    n_late = n_part // 4
-    n_small = img_hbm.shape[0]
-    img_first, tra_first = proj.shape[0] - n_small, proj.shape[0] - 2 * n_small
-    img, tra = proj.at[pl.ds(img_first, n_small), :], proj.at[pl.ds(tra_first, n_small), :]
     small_copies = [
         pltpu.make_async_copy(img_hbm, img, small_sem.at[0]),
         pltpu.make_async_copy(tra_hbm, tra, small_sem.at[1]),
@@ -57,19 +53,17 @@
         rows = pl.ds(pl.multiple_of(p * part_rows, part_rows), part_rows)
         return pltpu.make_async_copy(proj_hbm.at[rows, :], proj.at[rows, :], proj_sem.at[p])
 
-    for p in range(n_part - n_late):
+    for p in range(n_part):
         proj_copy(p).start()
 
-    zero = jnp.zeros((16 * SUB, LANES), jnp.float32)
-
-    def clear(half):
-        @pl.loop(0, n_row // (32 * SUB))
-        def _(i):
-            rows = pl.ds(pl.multiple_of(half * (n_row // 2) + i * (16 * SUB), 16 * SUB), 16 * SUB)
-            for acc in accs:
-                acc[rows, :] = zero
-
-    clear(0)
+    zero = jnp.zeros((8 * SUB, LANES), jnp.float32)
+
+    @pl.loop(0, n_row // (8 * SUB))
+    def _(i):
+        rows = pl.ds(pl.multiple_of(i * (8 * SUB), 8 * SUB), 8 * SUB)
+        for acc in accs:
+            acc[rows, :] = zero
+
     for copy in table_copies:
         copy.wait()
     lane = lax.broadcasted_iota(jnp.int32, (n_pose, n_table), 1)
@@ -86,23 +80,16 @@
     idx_v[...] = ((look_up(blocks) * bank_size + look_up(tiles)) * SUB).astype(jnp.int32)
     idx_copy = pltpu.make_async_copy(idx_v, idx_s, idx_sem)
     idx_copy.start()
-    clear(1)
 
     for copy in small_copies:
         copy.wait()
+
     @pl.loop(0, square.shape[0] // tile_rows)
     def _(i):
         rows = pl.ds(pl.multiple_of(i * tile_rows, tile_rows), tile_rows)
-        t = proj[pl.ds(pl.multiple_of(tra_first + i * tile_rows, tile_rows), tile_rows), :].astype(jnp.float32)
-        x = proj[pl.ds(pl.multiple_of(img_first + i * tile_rows, tile_rows), tile_rows), :].astype(jnp.float32)
+        t = tra[rows, :].astype(jnp.float32)
         square[rows, :] = t * t
-        cross[rows, :] = t * x
-
-    for p in range(n_part - n_late, n_part):
-        proj_copy(p).start()
-
-    sublane = lax.broadcasted_iota(jnp.int32, (SUB, LANES), 0)
-    bits = [(sublane & (1 << t)) != 0 for t in range(3)]
+        cross[rows, :] = t * img[rows, :].astype(jnp.float32)
 
     def stage(p, j, part):
         first = pl.multiple_of((p * n_tile + j) * tile_rows, tile_rows)
@@ -110,17 +97,6 @@
 
     def staged(part):
         return [part[pl.ds(k, SUB, stride=SUB), :] for k in range(n_pose)]
-
-    def rolled(p, j):
-        first = (p * n_tile + j) * tile_rows
-        cells = []
-        for c in range(0, SUB, 2):
-            pair = proj[pl.ds(pl.multiple_of(first + c * SUB, 2 * SUB), 2 * SUB), :].astype(jnp.float32)
-            cells += [pair[:SUB], pair[SUB:]]
-        cells = [pltpu.roll(x, c, 0) if c else x for c, x in enumerate(cells)]
-        for t, bit in enumerate(bits):
-            cells = [jnp.where(bit, cells[(i + (1 << t)) % SUB], cells[i]) for i in range(SUB)]
-        return [pltpu.roll(cells[-k % SUB], SUB - k, 0) if k else cells[0] for k in range(n_pose)]
 
     def terms(p, j, cells, weights):
         cell = pl.ds((j * (n_part // SUB) + p // SUB) * tile_rows + p % SUB, SUB, stride=SUB)
@@ -151,10 +127,8 @@
                 return jnp.minimum(j + u, n_tile - 1) if u >= UNROLL else j + u
 
             for u in range(UNROLL):
-                if (u + 2) % 3 != 2:
-                    stage(p, tile(u + 2), parts[(u + 2) % N_BUF])
-                cells = staged(parts[(u + 1) % N_BUF]) if (u + 1) % 3 != 2 else rolled(p, tile(u + 1))
-                later = terms(p, tile(u + 1), cells, weights)
+                stage(p, tile(u + 2), parts[(u + 2) % N_BUF])
+                later = terms(p, tile(u + 1), staged(parts[(u + 1) % N_BUF]), weights)
                 add_rows(p, j + u, values)
                 values = later
             return tuple(values)
@@ -221,7 +195,7 @@
     bank_size, n_owner,
 ):
     n_part, n_pose, n_tile, n_cell = projections.shape
-    assert n_cell == SUB * LANES and n_pose == SUB and n_part % SUB == 0 and n_tile % UNROLL == 0 and UNROLL % (3 * N_BUF) == 0
+    assert n_cell == SUB * LANES and n_pose == SUB and n_part % SUB == 0 and n_tile % UNROLL == 0 and UNROLL % N_BUF == 0
     n_row = n_owner * NB_DEV * bank_size * SUB
     n_acc = 4 if n_row * LANES * 4 <= 4 * MIB else 2
     projections = tiles_in_order(jnp.transpose(projections, (0, 2, 1, 3)))
@@ -246,6 +220,8 @@
         out_specs=[vmem] * (1 + n_acc),
         scratch_shapes=[
             pltpu.VMEM(projections.shape, jnp.bfloat16),
+            pltpu.VMEM(images.shape, jnp.bfloat16),
+            pltpu.VMEM(transfer.shape, jnp.bfloat16),
             pltpu.SMEM((n_pose, n_part), jnp.float32),
             pltpu.VMEM((n_pose, n_part), jnp.int32),
             pltpu.VMEM(pose_blocks.shape[::-1], jnp.int32),

time: 58.4 us -> 58.3 us (level)
  no operation moved by 1% of the time
where the time goes in v14:
time: 58.3 us; the launch traced here: 58.2 us
  waiting for transfers between devices  23.8 us (41%)
  Pallas kernels  21.1 us (36%)
  starting transfers between devices  13.2 us (23%)
    ppermute x8, waiting for transfers between devices, over_blk(): return lax.ppermute(array, 'blk', [(i, i ^ bits) for i in range(n_blk)])  21.6 us
    pallas_call x1, Pallas kernels, accumulate(): pl.pallas_call(functools.partial(accumulate_kernel, bank_size, n_owner, n...  16.9 us
    ppermute x8, starting transfers between devices, over_blk(): return lax.ppermute(array, 'blk', [(i, i ^ bits) for i in range(n_blk)])  12.5 us
    pallas_call x1, Pallas kernels, apply_bank(): pl.pallas_call(bank_kernel, out_shape=jax.ShapeDtypeStruct((NB_DEV, n_z,...  2.36 us
    ppermute x3, waiting for transfers between devices, over_rep(): return lax.ppermute(array, 'rep', [(0, 1), (1, 0)])  2.2 us
    pallas_call x5, Pallas kernels, in_vmem(): pl.pallas_call(kernel, out_shape=[jax.ShapeDtypeStruct((n, LANES), jnp.fl...  1.81 us
  transfers between devices with their start and end apart: 11, of which 7 were waited for; matrix products, arithmetic and copies ran while one was open for 0% of the time, Pallas kernels for 3%

profile of v14, /device:TPU:0, one launch (start us, length us, event | category | flops | bytes accessed | tf_op | source)
XLA Modules:
  0.0 58.2 jit_solution(3332052053853946688)
XLA Ops:
  0.0 16.9 %accumulate.1 = (f32[2048,128]{1,0:T(8,128)S(1)}, f32[8192,128]{1,0:T(8,128)S(1)}, f32[8192,128]{1,0:T(8,128)S(1)}, f32[8192,128]{1,0:T(8,128)S(1)}, f32[8192,128]{1,0:T(8,128)S(1)}) custom-call(bf16[36864,128]{1,0:T(8,128)(2,1)} %bitcast.29, bf16[4608,128]{1,0:T(8,128)(2,1)} %bitcast.30, bf16[4608,128]{1,0:T(8,128)(2,1)} %bitcast.31, f32[8,16]{1,0:T(8,128)} %bitcast.34, ...), custom_call_target="tpu_custom_call" | custom-call | tf_op jit(solution)/shard_map/accumulate/pallas_call | solution.py:216
  16.9 0.5 collective-permute-start.1
  17.4 1.5 %rest.1 = (f32[2048,128]{1,0:T(8,128)S(1)}, f32[2048,128]{1,0:T(8,128)S(1)}, f32[2048,128]{1,0:T(8,128)S(1)}) custom-call(f32[8192,128]{1,0:T(8,128)S(1)} %get-tuple-element.26.refs_0_, f32[8192,128]{1,0:T(8,128)S(1)} %get-tuple-element.27.refs_1_, f32[8192,128]{1,0:T(8,128)S(1)} %get-tuple-element.28.refs_2_, f32[8192,128]{1,0:T(8,128)S(1)} %get-tuple-element.29.refs_3_), custom_call_target="tpu_custom_call" | custom-call | tf_op jit(solution)/shard_map/rest/pallas_call | solution.py:253
  18.9 0.1 collective-permute-start
  19.1 0.7 %collective-permute-done.1.got = f32[2048,128]{1,0:T(8,128)S(1)} collective-permute-done((f32[2048,128]{1,0:T(8,128)S(1)}, f32[2048,128]{1,0:T(8,128)S(1)}, u32[]{:S(2)}, u32[]{:S(2)}) %collective-permute-start.1) | collective-permute-done | bytes 1048608 | tf_op jit(solution)/shard_map/ppermute | solution.py:390
  19.7 0.1 first.1
  19.8 2.9 %collective-permute-start.2 = (f32[1024,128]{1,0:T(8,128)S(1)}, f32[1024,128]{1,0:T(8,128)S(1)}, u32[]{:S(2)}, u32[]{:S(2)}) collective-permute-start(f32[1024,128]{1,0:T(8,128)S(1)} %get-tuple-element.34), channel_id=1, source_target_pairs={{0,2},{2,0},{4,6},{6,4},{8,10},{10,8},{12,14},{14,12},{1,3},{3,1},... | collective-permute-start | bytes 1572872 | tf_op jit(solution)/shard_map/ppermute | solution.py:393
  22.8 1.6 %collective-permute-start.3 = (f32[512,128]{1,0:T(8,128)S(1)}, f32[512,128]{1,0:T(8,128)S(1)}, u32[]{:S(2)}, u32[]{:S(2)}) collective-permute-start(f32[512,128]{1,0:T(8,128)S(1)} %get-tuple-element.35), channel_id=1, source_target_pairs={{0,4},{2,6},{4,0},{6,2},{8,12},{10,14},{12,8},{14,10},{1,5},{3,7},... | collective-permute-start | bytes 786440 | tf_op jit(solution)/shard_map/ppermute | solution.py:393
  24.4 2.6 %collective-permute-start.4 = (f32[512,128]{1,0:T(8,128)S(1)}, f32[512,128]{1,0:T(8,128)S(1)}, u32[]{:S(2)}, u32[]{:S(2)}) collective-permute-start(f32[512,128]{1,0:T(8,128)S(1)} %get-tuple-element.36), channel_id=1, source_target_pairs={{0,8},{2,10},{4,12},{6,14},{8,0},{10,2},{12,4},{14,6},{1,9},{3,11}... | collective-permute-start | bytes 786440 | tf_op jit(solution)/shard_map/ppermute | solution.py:393
  27.0 9.4 %collective-permute-done.3.got_l = f32[512,128]{1,0:T(8,128)S(1)} collective-permute-done((f32[512,128]{1,0:T(8,128)S(1)}, f32[512,128]{1,0:T(8,128)S(1)}, u32[]{:S(2)}, u32[]{:S(2)}) %collective-permute-start.3) | collective-permute-done | bytes 262176 | tf_op jit(solution)/shard_map/ppermute | solution.py:393
  36.4 2.4 %collective-permute-done.4.rest_0_ = f32[512,128]{1,0:T(8,128)S(1)} collective-permute-done((f32[512,128]{1,0:T(8,128)S(1)}, f32[512,128]{1,0:T(8,128)S(1)}, u32[]{:S(2)}, u32[]{:S(2)}) %collective-permute-start.4) | collective-permute-done | bytes 262176 | tf_op jit(solution)/shard_map/ppermute | solution.py:393
  38.7 0.2 second.1
  38.9 0.6 collective-permute-start.5
  39.5 0.4 collective-permute-start.6
  39.9 2.6 %collective-permute-start.7 = (f32[256,128]{1,0:T(8,128)S(1)}, f32[256,128]{1,0:T(8,128)S(1)}, u32[]{:S(2)}, u32[]{:S(2)}) collective-permute-start(f32[256,128]{1,0:T(8,128)S(1)} %get-tuple-element.43), channel_id=1, source_target_pairs={{0,8},{2,10},{4,12},{6,14},{8,0},{10,2},{12,4},{14,6},{1,9},{3,11}... | collective-permute-start | bytes 393224 | tf_op jit(solution)/shard_map/ppermute | solution.py:393
  42.5 3.8 %collective-permute-done.6.got_l = f32[256,128]{1,0:T(8,128)S(1)} collective-permute-done((f32[256,128]{1,0:T(8,128)S(1)}, f32[256,128]{1,0:T(8,128)S(1)}, u32[]{:S(2)}, u32[]{:S(2)}) %collective-permute-start.6) | collective-permute-done | bytes 131104 | tf_op jit(solution)/shard_map/ppermute | solution.py:393
  46.3 1.1 %collective-permute-done.7.rest_0_ = f32[256,128]{1,0:T(8,128)S(1)} collective-permute-done((f32[256,128]{1,0:T(8,128)S(1)}, f32[256,128]{1,0:T(8,128)S(1)}, u32[]{:S(2)}, u32[]{:S(2)}) %collective-permute-start.7) | collective-permute-done | bytes 131104 | tf_op jit(solution)/shard_map/ppermute | solution.py:393
  47.4 0.1 third.1
  47.5 0.1 collective-permute-start.8
  47.6 1.7 %collective-permute-start.9 = (f32[256,128]{1,0:T(8,128)S(1)}, f32[256,128]{1,0:T(8,128)S(1)}, u32[]{:S(2)}, u32[]{:S(2)}) collective-permute-start(f32[256,128]{1,0:T(8,128)S(1)} %get-tuple-element.46), channel_id=1, source_target_pairs={{0,8},{2,10},{4,12},{6,14},{8,0},{10,2},{12,4},{14,6},{1,9},{3,11}... | collective-permute-start | bytes 393224 | tf_op jit(solution)/shard_map/ppermute | solution.py:393
  49.3 4.9 %collective-permute-done.8.got_l = f32[256,128]{1,0:T(8,128)S(1)} collective-permute-done((f32[256,128]{1,0:T(8,128)S(1)}, f32[256,128]{1,0:T(8,128)S(1)}, u32[]{:S(2)}, u32[]{:S(2)}) %collective-permute-start.8) | collective-permute-done | bytes 131104 | tf_op jit(solution)/shard_map/ppermute | solution.py:393
  54.2 0.1 collective-permute-start.10
  54.3 1.5 %collective-permute-done.10 = f32[512,128]{1,0:T(8,128)S(1)} collective-permute-done((f32[512,128]{1,0:T(8,128)S(1)}, f32[512,128]{1,0:T(8,128)S(1)}, u32[]{:S(2)}, u32[]{:S(2)}) %collective-permute-start.10) | collective-permute-done | bytes 262176 | tf_op jit(solution)/shard_map/ppermute | solution.py:390
  55.8 2.4 %apply_bank.1 = f32[8,32,1024]{2,1,0:T(8,128)} custom-call(f32[4,16,8,128]{3,2,1,0:T(8,128)S(1)} %bitcast.27, f32[4,16,8,128]{3,2,1,0:T(8,128)S(1)} %bitcast.28, f32[16,32,1024]{2,1,0:T(8,128)S(1)} %copy-done), custom_call_target="tpu_custom_call" | custom-call | tf_op jit(solution)/shard_map/apply_bank/pallas_call | solution.py:367
  (7 shorter events, 0.0 us)
Async XLA Ops:
  16.9 2.8 %collective-permute-start.1 = (f32[2048,128]{1,0:T(8,128)S(1)}, f32[2048,128]{1,0:T(8,128)S(1)}, u32[]{:S(2)}, u32[]{:S(2)}) collective-permute-start(f32[2048,128]{1,0:T(8,128)S(1)} %get-tuple-element.33), channel_id=1, source_target_pairs={{0,1},{1,0},{2,3},{3,2},{4,5},{5,4},{6,7},{7,6},{8,9},{9,8},{10,11... | collective-permute-start | bytes 3145736 | tf_op jit(solution)/shard_map/ppermute | solution.py:390
  18.9 36.9 %copy-start = (f32[16,32,1024]{2,1,0:T(8,128)S(1)}, f32[16,32,1024]{2,1,0:T(8,128)}, u32[]{:S(2)}) copy-start(f32[16,32,1024]{2,1,0:T(8,128)} %bank.1) | copy-start | bytes 6291460
  18.9 8.0 %collective-permute-start = (f32[2048,128]{1,0:T(8,128)S(1)}, f32[2048,128]{1,0:T(8,128)S(1)}, u32[]{:S(2)}, u32[]{:S(2)}) collective-permute-start(f32[2048,128]{1,0:T(8,128)S(1)} %get-tuple-element.31), channel_id=1, source_target_pairs={{0,1},{1,0},{2,3},{3,2},{4,5},{5,4},{6,7},{7,6},{8,9},{9,8},{10,11... | collective-permute-start | bytes 3145736 | tf_op jit(solution)/shard_map/ppermute | solution.py:390
  19.8 18.9 %collective-permute-start.2 = (f32[1024,128]{1,0:T(8,128)S(1)}, f32[1024,128]{1,0:T(8,128)S(1)}, u32[]{:S(2)}, u32[]{:S(2)}) collective-permute-start(f32[1024,128]{1,0:T(8,128)S(1)} %get-tuple-element.34), channel_id=1, source_target_pairs={{0,2},{2,0},{4,6},{6,4},{8,10},{10,8},{12,14},{14,12},{1,3},{3,1},... | collective-permute-start | bytes 1572872 | tf_op jit(solution)/shard_map/ppermute | solution.py:393
  22.8 13.6 %collective-permute-start.3 = (f32[512,128]{1,0:T(8,128)S(1)}, f32[512,128]{1,0:T(8,128)S(1)}, u32[]{:S(2)}, u32[]{:S(2)}) collective-permute-start(f32[512,128]{1,0:T(8,128)S(1)} %get-tuple-element.35), channel_id=1, source_target_pairs={{0,4},{2,6},{4,0},{6,2},{8,12},{10,14},{12,8},{14,10},{1,5},{3,7},... | collective-permute-start | bytes 786440 | tf_op jit(solution)/shard_map/ppermute | solution.py:393
  24.4 14.4 %collective-permute-start.4 = (f32[512,128]{1,0:T(8,128)S(1)}, f32[512,128]{1,0:T(8,128)S(1)}, u32[]{:S(2)}, u32[]{:S(2)}) collective-permute-start(f32[512,128]{1,0:T(8,128)S(1)} %get-tuple-element.36), channel_id=1, source_target_pairs={{0,8},{2,10},{4,12},{6,14},{8,0},{10,2},{12,4},{14,6},{1,9},{3,11}... | collective-permute-start | bytes 786440 | tf_op jit(solution)/shard_map/ppermute | solution.py:393
  38.9 8.5 %collective-permute-start.5 = (f32[512,128]{1,0:T(8,128)S(1)}, f32[512,128]{1,0:T(8,128)S(1)}, u32[]{:S(2)}, u32[]{:S(2)}) collective-permute-start(f32[512,128]{1,0:T(8,128)S(1)} %get-tuple-element.41), channel_id=1, source_target_pairs={{0,2},{2,0},{4,6},{6,4},{8,10},{10,8},{12,14},{14,12},{1,3},{3,1},... | collective-permute-start | bytes 786440 | tf_op jit(solution)/shard_map/ppermute | solution.py:393
  39.5 6.9 %collective-permute-start.6 = (f32[256,128]{1,0:T(8,128)S(1)}, f32[256,128]{1,0:T(8,128)S(1)}, u32[]{:S(2)}, u32[]{:S(2)}) collective-permute-start(f32[256,128]{1,0:T(8,128)S(1)} %get-tuple-element.42), channel_id=1, source_target_pairs={{0,4},{2,6},{4,0},{6,2},{8,12},{10,14},{12,8},{14,10},{1,5},{3,7},... | collective-permute-start | bytes 393224 | tf_op jit(solution)/shard_map/ppermute | solution.py:393
  39.9 7.5 %collective-permute-start.7 = (f32[256,128]{1,0:T(8,128)S(1)}, f32[256,128]{1,0:T(8,128)S(1)}, u32[]{:S(2)}, u32[]{:S(2)}) collective-permute-start(f32[256,128]{1,0:T(8,128)S(1)} %get-tuple-element.43), channel_id=1, source_target_pairs={{0,8},{2,10},{4,12},{6,14},{8,0},{10,2},{12,4},{14,6},{1,9},{3,11}... | collective-permute-start | bytes 393224 | tf_op jit(solution)/shard_map/ppermute | solution.py:393
  47.5 6.7 %collective-permute-start.8 = (f32[256,128]{1,0:T(8,128)S(1)}, f32[256,128]{1,0:T(8,128)S(1)}, u32[]{:S(2)}, u32[]{:S(2)}) collective-permute-start(f32[256,128]{1,0:T(8,128)S(1)} %get-tuple-element.45), channel_id=1, source_target_pairs={{0,4},{2,6},{4,0},{6,2},{8,12},{10,14},{12,8},{14,10},{1,5},{3,7},... | collective-permute-start | bytes 393224 | tf_op jit(solution)/shard_map/ppermute | solution.py:393
  47.6 6.6 %collective-permute-start.9 = (f32[256,128]{1,0:T(8,128)S(1)}, f32[256,128]{1,0:T(8,128)S(1)}, u32[]{:S(2)}, u32[]{:S(2)}) collective-permute-start(f32[256,128]{1,0:T(8,128)S(1)} %get-tuple-element.46), channel_id=1, source_target_pairs={{0,8},{2,10},{4,12},{6,14},{8,0},{10,2},{12,4},{14,6},{1,9},{3,11}... | collective-permute-start | bytes 393224 | tf_op jit(solution)/shard_map/ppermute | solution.py:393
  54.2 1.6 %collective-permute-start.10 = (f32[512,128]{1,0:T(8,128)S(1)}, f32[512,128]{1,0:T(8,128)S(1)}, u32[]{:S(2)}, u32[]{:S(2)}) collective-permute-start(f32[512,128]{1,0:T(8,128)S(1)} %last.1), channel_id=1, source_target_pairs={{0,1},{1,0},{2,3},{3,2},{4,5},{5,4},{6,7},{7,6},{8,9},{9,8},{10,11... | collective-permute-start | bytes 786440 | tf_op jit(solution)/shard_map/ppermute | solution.py:390

commit v15 on v14

--- a/solution.py
+++ b/solution.py
@@ -25,12 +25,11 @@
 def accumulate_kernel(
     bank_size, n_owner, n_acc,
     proj_hbm, img_hbm, tra_hbm, w_hbm, pose_hbm, blocks_hbm, tiles_hbm,
-    sent_away, *rest,
+    sent_away, kept_away, sent_stay, kept_stay, *rest,
 ):
-    accs, rest = rest[:n_acc], rest[n_acc:]
     proj, img, tra, weight, pose, blocks, tiles, idx_v, idx_s, square, cross = rest[:11]
-    parts = rest[11 : 11 + N_BUF]
-    proj_sem, small_sem, table_sem, idx_sem = rest[11 + N_BUF :]
+    parts, accs = rest[11 : 11 + N_BUF], rest[11 + N_BUF : 11 + N_BUF + n_acc]
+    proj_sem, small_sem, table_sem, idx_sem = rest[11 + N_BUF + n_acc :]
     n_pose, n_part = pose.shape
     n_tile, n_table = blocks.shape
     n_row = accs[0].shape[0]
@@ -91,12 +90,26 @@
         square[rows, :] = t * t
         cross[rows, :] = t * img[rows, :].astype(jnp.float32)
 
+    sublane = lax.broadcasted_iota(jnp.int32, (SUB, LANES), 0)
+    bits = [(sublane & (1 << t)) != 0 for t in range(3)]
+
     def stage(p, j, part):
         first = pl.multiple_of((p * n_tile + j) * tile_rows, tile_rows)
         part[...] = proj[pl.ds(first, tile_rows), :].astype(jnp.float32)
 
     def staged(part):
         return [part[pl.ds(k, SUB, stride=SUB), :] for k in range(n_pose)]
+
+    def rolled(p, j):
+        first = (p * n_tile + j) * tile_rows
+        cells = []
+        for c in range(0, SUB, 2):
+            pair = proj[pl.ds(pl.multiple_of(first + c * SUB, 2 * SUB), 2 * SUB), :].astype(jnp.float32)
+            cells += [pair[:SUB], pair[SUB:]]
+        cells = [pltpu.roll(x, c, 0) if c else x for c, x in enumerate(cells)]
+        for t, bit in enumerate(bits):
+            cells = [jnp.where(bit, cells[(i + (1 << t)) % SUB], cells[i]) for i in range(SUB)]
+        return [pltpu.roll(cells[-k % SUB], SUB - k, 0) if k else cells[0] for k in range(n_pose)]
 
     def terms(p, j, cells, weights):
         cell = pl.ds((j * (n_part // SUB) + p // SUB) * tile_rows + p % SUB, SUB, stride=SUB)
@@ -127,13 +140,19 @@
                 return jnp.minimum(j + u, n_tile - 1) if u >= UNROLL else j + u
 
             for u in range(UNROLL):
-                stage(p, tile(u + 2), parts[(u + 2) % N_BUF])
-                later = terms(p, tile(u + 1), staged(parts[(u + 1) % N_BUF]), weights)
+                if (u + 2) % 3 != 2:
+                    stage(p, tile(u + 2), parts[(u + 2) % N_BUF])
+                cells = staged(parts[(u + 1) % N_BUF]) if (u + 1) % 3 != 2 else rolled(p, tile(u + 1))
+                later = terms(p, tile(u + 1), cells, weights)
                 add_rows(p, j + u, values)
                 values = later
             return tuple(values)
 
-    Sums(n_owner, accs).pieces_away(sent_away, sent=True)
+    sums = Sums(n_owner, accs)
+    sums.pieces_away(sent_away, sent=True)
+    sums.pieces_away(kept_away, sent=False)
+    sums.pieces_stay(sent_stay, sent=True)
+    sums.pieces_stay(kept_stay, sent=False)
 
 
 class Sums:
@@ -175,14 +194,6 @@
             begin = self.pieces(out, begin, part, range(1), sent)
 
 
-def rest_kernel(n_owner, *refs):
-    accs, (kept_away, sent_stay, kept_stay) = refs[:-3], refs[-3:]
-    sums = Sums(n_owner, accs)
-    sums.pieces_away(kept_away, sent=False)
-    sums.pieces_stay(sent_stay, sent=True)
-    sums.pieces_stay(kept_stay, sent=False)
-
-
 def tiles_in_order(array):
     lead = array.shape[:-2]
     rows, cells = array.shape[-2:]
@@ -195,7 +206,7 @@
     bank_size, n_owner,
 ):
     n_part, n_pose, n_tile, n_cell = projections.shape
-    assert n_cell == SUB * LANES and n_pose == SUB and n_part % SUB == 0 and n_tile % UNROLL == 0 and UNROLL % N_BUF == 0
+    assert n_cell == SUB * LANES and n_pose == SUB and n_part % SUB == 0 and n_tile % UNROLL == 0 and UNROLL % (3 * N_BUF) == 0
     n_row = n_owner * NB_DEV * bank_size * SUB
     n_acc = 4 if n_row * LANES * 4 <= 4 * MIB else 2
     projections = tiles_in_order(jnp.transpose(projections, (0, 2, 1, 3)))
@@ -209,15 +220,16 @@
     assert sum(PART_ROWS) == NB_DEV // 2 * bank_size
 
     away = 2 * n_high * (a + d + b) + 4 * (n_high - 1) * e
+    stays = 2 * n_high * (a + d + b) + 4 * e
 
     def out(rows):
         return jax.ShapeDtypeStruct((rows, LANES), jnp.float32)
 
-    sent_away, *accs = pl.pallas_call(
+    return pl.pallas_call(
         functools.partial(accumulate_kernel, bank_size, n_owner, n_acc),
-        out_shape=[out(away)] + [out(n_row)] * n_acc,
+        out_shape=[out(away)] * 2 + [out(stays)] * 2,
         in_specs=[hbm] * 7,
-        out_specs=[vmem] * (1 + n_acc),
+        out_specs=[vmem] * 4,
         scratch_shapes=[
             pltpu.VMEM(projections.shape, jnp.bfloat16),
             pltpu.VMEM(images.shape, jnp.bfloat16),
@@ -232,20 +244,19 @@
             pltpu.VMEM(transfer.shape, jnp.float32),
         ]
         + [pltpu.VMEM((n_pose * SUB, LANES), jnp.float32)] * N_BUF
+        + [pltpu.VMEM((n_row, LANES), jnp.float32)] * n_acc
         + [
             pltpu.SemaphoreType.DMA((n_part,)),
             pltpu.SemaphoreType.DMA((3,)),
             pltpu.SemaphoreType.DMA((3,)),
             pltpu.SemaphoreType.DMA,
         ],
-        compiler_params=pltpu.CompilerParams(vmem_limit_bytes=24 * MIB),
+        compiler_params=pltpu.CompilerParams(vmem_limit_bytes=(40 if n_acc == 4 else 56) * MIB),
         name="accumulate",
     )(
         stay(projections), stay(images), stay(transfer),
         stay(pose_weights.T), stay(pose_of.T), stay(pose_blocks.T), stay(pose_tiles.T),
     )
-    rows = 2 * n_high * (a + d + b) + 4 * e
-    return sent_away, *in_vmem(functools.partial(rest_kernel, n_owner), "rest", [away, rows, rows], *accs)
 
 
 def in_vmem(kernel, name, rows, *operands):

time: 58.3 us -> 59.5 us (1.021)
  waiting for transfers between devices: 23.8 us -> 25.3 us
    ppermute x3, waiting for transfers between devices: 2.2 us -> 3.73 us  [over_rep(): return lax.ppermute(array, 'rep', [(0, 1), (1, 0)])]
    pallas_call x5 -> x4, Pallas kernels: 1.81 us -> 0.34 us  [in_vmem(): pl.pallas_call(kernel, out_shape=[jax.ShapeDtypeStruct((n, LANES), jnp.fl...]
    pallas_call x1, Pallas kernels: 16.9 us -> 18.1 us  [accumulate(): pl.pallas_call(functools.partial(accumulate_kernel, bank_size, n_owner, n...]
  transfers between devices with their start and end apart: 11 -> 11, of which waited for: 7 -> 7; matrix products, arithmetic and copies ran while one was open for 0% -> 0% of each run, Pallas kernels for 3% -> 0%
where the time goes in v15:
time: 59.5 us; the launch traced here: 59.4 us
  waiting for transfers between devices  25.3 us (43%)
  Pallas kernels  20.8 us (35%)
  starting transfers between devices  13.2 us (22%)
    ppermute x8, waiting for transfers between devices, over_blk(): return lax.ppermute(array, 'blk', [(i, i ^ bits) for i in range(n_blk)])  21.6 us
    pallas_call x1, Pallas kernels, accumulate(): pl.pallas_call(functools.partial(accumulate_kernel, bank_size, n_owner, n...  18.1 us
    ppermute x8, starting transfers between devices, over_blk(): return lax.ppermute(array, 'blk', [(i, i ^ bits) for i in range(n_blk)])  12.5 us
    ppermute x3, waiting for transfers between devices, over_rep(): return lax.ppermute(array, 'rep', [(0, 1), (1, 0)])  3.73 us
    pallas_call x1, Pallas kernels, apply_bank(): pl.pallas_call(bank_kernel, out_shape=jax.ShapeDtypeStruct((NB_DEV, n_z,...  2.36 us
  transfers between devices with their start and end apart: 11, of which 7 were waited for; matrix products, arithmetic and copies ran while one was open for 0% of the time, Pallas kernels for 0%

profile of v15, /device:TPU:0, one launch (start us, length us, event | category | flops | bytes accessed | tf_op | source)
XLA Modules:
  0.0 59.4 jit_solution(4336193809492220250)
XLA Ops:
  0.0 18.1 %accumulate.1 = (f32[2048,128]{1,0:T(8,128)S(1)}, f32[2048,128]{1,0:T(8,128)S(1)}, f32[2048,128]{1,0:T(8,128)S(1)}, f32[2048,128]{1,0:T(8,128)S(1)}) custom-call(bf16[36864,128]{1,0:T(8,128)(2,1)} %bitcast.29, bf16[4608,128]{1,0:T(8,128)(2,1)} %bitcast.30, bf16[4608,128]{1,0:T(8,128)(2,1)} %bitcast.31, f32[8,16]{1,0:T(8,128)} %bitcast.34, s32[8,16]{1,0:T(8,128)} %bitcast.35, ...), custom_call_target="tpu_custom_call" | custom-call | tf_op jit(solution)/shard_map/accumulate/pallas_call | solution.py:228
  18.1 0.5 collective-permute-start.1
  18.6 0.1 collective-permute-start
  18.7 2.2 %collective-permute-done.1.got = f32[2048,128]{1,0:T(8,128)S(1)} collective-permute-done((f32[2048,128]{1,0:T(8,128)S(1)}, f32[2048,128]{1,0:T(8,128)S(1)}, u32[]{:S(2)}, u32[]{:S(2)}) %collective-permute-start.1) | collective-permute-done | bytes 1048608 | tf_op jit(solution)/shard_map/ppermute | solution.py:401
  20.9 0.1 first.1
  21.0 3.0 %collective-permute-start.2 = (f32[1024,128]{1,0:T(8,128)S(1)}, f32[1024,128]{1,0:T(8,128)S(1)}, u32[]{:S(2)}, u32[]{:S(2)}) collective-permute-start(f32[1024,128]{1,0:T(8,128)S(1)} %get-tuple-element.26), channel_id=1, source_target_pairs={{0,2},{2,0},{4,6},{6,4},{8,10},{10,8},{12,14},{14,12},{1,3},{3,1},... | collective-permute-start | bytes 1572872 | tf_op jit(solution)/shard_map/ppermute | solution.py:404
  24.0 1.6 %collective-permute-start.3 = (f32[512,128]{1,0:T(8,128)S(1)}, f32[512,128]{1,0:T(8,128)S(1)}, u32[]{:S(2)}, u32[]{:S(2)}) collective-permute-start(f32[512,128]{1,0:T(8,128)S(1)} %get-tuple-element.27), channel_id=1, source_target_pairs={{0,4},{2,6},{4,0},{6,2},{8,12},{10,14},{12,8},{14,10},{1,5},{3,7},... | collective-permute-start | bytes 786440 | tf_op jit(solution)/shard_map/ppermute | solution.py:404
  25.6 2.6 %collective-permute-start.4 = (f32[512,128]{1,0:T(8,128)S(1)}, f32[512,128]{1,0:T(8,128)S(1)}, u32[]{:S(2)}, u32[]{:S(2)}) collective-permute-start(f32[512,128]{1,0:T(8,128)S(1)} %get-tuple-element.28), channel_id=1, source_target_pairs={{0,8},{2,10},{4,12},{6,14},{8,0},{10,2},{12,4},{14,6},{1,9},{3,11}... | collective-permute-start | bytes 786440 | tf_op jit(solution)/shard_map/ppermute | solution.py:404
  28.1 9.4 %collective-permute-done.3.got_l = f32[512,128]{1,0:T(8,128)S(1)} collective-permute-done((f32[512,128]{1,0:T(8,128)S(1)}, f32[512,128]{1,0:T(8,128)S(1)}, u32[]{:S(2)}, u32[]{:S(2)}) %collective-permute-start.3) | collective-permute-done | bytes 262176 | tf_op jit(solution)/shard_map/ppermute | solution.py:404
  37.5 2.4 %collective-permute-done.4.rest_0_ = f32[512,128]{1,0:T(8,128)S(1)} collective-permute-done((f32[512,128]{1,0:T(8,128)S(1)}, f32[512,128]{1,0:T(8,128)S(1)}, u32[]{:S(2)}, u32[]{:S(2)}) %collective-permute-start.4) | collective-permute-done | bytes 262176 | tf_op jit(solution)/shard_map/ppermute | solution.py:404
  39.9 0.2 second.1
  40.1 0.6 collective-permute-start.5
  40.6 0.4 collective-permute-start.6
  41.1 2.6 %collective-permute-start.7 = (f32[256,128]{1,0:T(8,128)S(1)}, f32[256,128]{1,0:T(8,128)S(1)}, u32[]{:S(2)}, u32[]{:S(2)}) collective-permute-start(f32[256,128]{1,0:T(8,128)S(1)} %get-tuple-element.35), channel_id=1, source_target_pairs={{0,8},{2,10},{4,12},{6,14},{8,0},{10,2},{12,4},{14,6},{1,9},{3,11}... | collective-permute-start | bytes 393224 | tf_op jit(solution)/shard_map/ppermute | solution.py:404
  43.7 3.8 %collective-permute-done.6.got_l = f32[256,128]{1,0:T(8,128)S(1)} collective-permute-done((f32[256,128]{1,0:T(8,128)S(1)}, f32[256,128]{1,0:T(8,128)S(1)}, u32[]{:S(2)}, u32[]{:S(2)}) %collective-permute-start.6) | collective-permute-done | bytes 131104 | tf_op jit(solution)/shard_map/ppermute | solution.py:404
  47.5 1.1 %collective-permute-done.7.rest_0_ = f32[256,128]{1,0:T(8,128)S(1)} collective-permute-done((f32[256,128]{1,0:T(8,128)S(1)}, f32[256,128]{1,0:T(8,128)S(1)}, u32[]{:S(2)}, u32[]{:S(2)}) %collective-permute-start.7) | collective-permute-done | bytes 131104 | tf_op jit(solution)/shard_map/ppermute | solution.py:404
  48.6 0.0 collective-permute-done.5.got_y
  48.6 0.1 third.1
  48.7 0.1 collective-permute-start.8
  48.8 1.7 %collective-permute-start.9 = (f32[256,128]{1,0:T(8,128)S(1)}, f32[256,128]{1,0:T(8,128)S(1)}, u32[]{:S(2)}, u32[]{:S(2)}) collective-permute-start(f32[256,128]{1,0:T(8,128)S(1)} %get-tuple-element.38), channel_id=1, source_target_pairs={{0,8},{2,10},{4,12},{6,14},{8,0},{10,2},{12,4},{14,6},{1,9},{3,11}... | collective-permute-start | bytes 393224 | tf_op jit(solution)/shard_map/ppermute | solution.py:404
  50.5 4.9 %collective-permute-done.8.got_l = f32[256,128]{1,0:T(8,128)S(1)} collective-permute-done((f32[256,128]{1,0:T(8,128)S(1)}, f32[256,128]{1,0:T(8,128)S(1)}, u32[]{:S(2)}, u32[]{:S(2)}) %collective-permute-start.8) | collective-permute-done | bytes 131104 | tf_op jit(solution)/shard_map/ppermute | solution.py:404
  55.4 0.1 collective-permute-start.10
  55.5 1.5 %collective-permute-done.10 = f32[512,128]{1,0:T(8,128)S(1)} collective-permute-done((f32[512,128]{1,0:T(8,128)S(1)}, f32[512,128]{1,0:T(8,128)S(1)}, u32[]{:S(2)}, u32[]{:S(2)}) %collective-permute-start.10) | collective-permute-done | bytes 262176 | tf_op jit(solution)/shard_map/ppermute | solution.py:401
  57.0 2.4 %apply_bank.1 = f32[8,32,1024]{2,1,0:T(8,128)} custom-call(f32[4,16,8,128]{3,2,1,0:T(8,128)S(1)} %bitcast.27, f32[4,16,8,128]{3,2,1,0:T(8,128)S(1)} %bitcast.28, f32[16,32,1024]{2,1,0:T(8,128)S(1)} %copy-done), custom_call_target="tpu_custom_call" | custom-call | tf_op jit(solution)/shard_map/apply_bank/pallas_call | solution.py:378
  (6 shorter events, 0.0 us)
Async XLA Ops:
  18.1 2.8 %collective-permute-start.1 = (f32[2048,128]{1,0:T(8,128)S(1)}, f32[2048,128]{1,0:T(8,128)S(1)}, u32[]{:S(2)}, u32[]{:S(2)}) collective-permute-start(f32[2048,128]{1,0:T(8,128)S(1)} %get-tuple-element.25), channel_id=1, source_target_pairs={{0,1},{1,0},{2,3},{3,2},{4,5},{5,4},{6,7},{7,6},{8,9},{9,8},{10,11... | collective-permute-start | bytes 3145736 | tf_op jit(solution)/shard_map/ppermute | solution.py:401
  18.6 9.5 %collective-permute-start = (f32[2048,128]{1,0:T(8,128)S(1)}, f32[2048,128]{1,0:T(8,128)S(1)}, u32[]{:S(2)}, u32[]{:S(2)}) collective-permute-start(f32[2048,128]{1,0:T(8,128)S(1)} %get-tuple-element.23), channel_id=1, source_target_pairs={{0,1},{1,0},{2,3},{3,2},{4,5},{5,4},{6,7},{7,6},{8,9},{9,8},{10,11... | collective-permute-start | bytes 3145736 | tf_op jit(solution)/shard_map/ppermute | solution.py:401
  21.0 18.9 %collective-permute-start.2 = (f32[1024,128]{1,0:T(8,128)S(1)}, f32[1024,128]{1,0:T(8,128)S(1)}, u32[]{:S(2)}, u32[]{:S(2)}) collective-permute-start(f32[1024,128]{1,0:T(8,128)S(1)} %get-tuple-element.26), channel_id=1, source_target_pairs={{0,2},{2,0},{4,6},{6,4},{8,10},{10,8},{12,14},{14,12},{1,3},{3,1},... | collective-permute-start | bytes 1572872 | tf_op jit(solution)/shard_map/ppermute | solution.py:404
  24.0 13.6 %collective-permute-start.3 = (f32[512,128]{1,0:T(8,128)S(1)}, f32[512,128]{1,0:T(8,128)S(1)}, u32[]{:S(2)}, u32[]{:S(2)}) collective-permute-start(f32[512,128]{1,0:T(8,128)S(1)} %get-tuple-element.27), channel_id=1, source_target_pairs={{0,4},{2,6},{4,0},{6,2},{8,12},{10,14},{12,8},{14,10},{1,5},{3,7},... | collective-permute-start | bytes 786440 | tf_op jit(solution)/shard_map/ppermute | solution.py:404
  25.6 14.4 %collective-permute-start.4 = (f32[512,128]{1,0:T(8,128)S(1)}, f32[512,128]{1,0:T(8,128)S(1)}, u32[]{:S(2)}, u32[]{:S(2)}) collective-permute-start(f32[512,128]{1,0:T(8,128)S(1)} %get-tuple-element.28), channel_id=1, source_target_pairs={{0,8},{2,10},{4,12},{6,14},{8,0},{10,2},{12,4},{14,6},{1,9},{3,11}... | collective-permute-start | bytes 786440 | tf_op jit(solution)/shard_map/ppermute | solution.py:404
  39.9 17.1 %copy-start = (f32[16,32,1024]{2,1,0:T(8,128)S(1)}, f32[16,32,1024]{2,1,0:T(8,128)}, u32[]{:S(2)}) copy-start(f32[16,32,1024]{2,1,0:T(8,128)} %bank.1) | copy-start | bytes 6291460
  40.1 8.5 %collective-permute-start.5 = (f32[512,128]{1,0:T(8,128)S(1)}, f32[512,128]{1,0:T(8,128)S(1)}, u32[]{:S(2)}, u32[]{:S(2)}) collective-permute-start(f32[512,128]{1,0:T(8,128)S(1)} %get-tuple-element.33), channel_id=1, source_target_pairs={{0,2},{2,0},{4,6},{6,4},{8,10},{10,8},{12,14},{14,12},{1,3},{3,1},... | collective-permute-start | bytes 786440 | tf_op jit(solution)/shard_map/ppermute | solution.py:404
  40.6 6.9 %collective-permute-start.6 = (f32[256,128]{1,0:T(8,128)S(1)}, f32[256,128]{1,0:T(8,128)S(1)}, u32[]{:S(2)}, u32[]{:S(2)}) collective-permute-start(f32[256,128]{1,0:T(8,128)S(1)} %get-tuple-element.34), channel_id=1, source_target_pairs={{0,4},{2,6},{4,0},{6,2},{8,12},{10,14},{12,8},{14,10},{1,5},{3,7},... | collective-permute-start | bytes 393224 | tf_op jit(solution)/shard_map/ppermute | solution.py:404
  41.1 7.5 %collective-permute-start.7 = (f32[256,128]{1,0:T(8,128)S(1)}, f32[256,128]{1,0:T(8,128)S(1)}, u32[]{:S(2)}, u32[]{:S(2)}) collective-permute-start(f32[256,128]{1,0:T(8,128)S(1)} %get-tuple-element.35), channel_id=1, source_target_pairs={{0,8},{2,10},{4,12},{6,14},{8,0},{10,2},{12,4},{14,6},{1,9},{3,11}... | collective-permute-start | bytes 393224 | tf_op jit(solution)/shard_map/ppermute | solution.py:404
  48.7 6.7 %collective-permute-start.8 = (f32[256,128]{1,0:T(8,128)S(1)}, f32[256,128]{1,0:T(8,128)S(1)}, u32[]{:S(2)}, u32[]{:S(2)}) collective-permute-start(f32[256,128]{1,0:T(8,128)S(1)} %get-tuple-element.37), channel_id=1, source_target_pairs={{0,4},{2,6},{4,0},{6,2},{8,12},{10,14},{12,8},{14,10},{1,5},{3,7},... | collective-permute-start | bytes 393224 | tf_op jit(solution)/shard_map/ppermute | solution.py:404
  48.8 6.6 %collective-permute-start.9 = (f32[256,128]{1,0:T(8,128)S(1)}, f32[256,128]{1,0:T(8,128)S(1)}, u32[]{:S(2)}, u32[]{:S(2)}) collective-permute-start(f32[256,128]{1,0:T(8,128)S(1)} %get-tuple-element.38), channel_id=1, source_target_pairs={{0,8},{2,10},{4,12},{6,14},{8,0},{10,2},{12,4},{14,6},{1,9},{3,11}... | collective-permute-start | bytes 393224 | tf_op jit(solution)/shard_map/ppermute | solution.py:404
  55.4 1.6 %collective-permute-start.10 = (f32[512,128]{1,0:T(8,128)S(1)}, f32[512,128]{1,0:T(8,128)S(1)}, u32[]{:S(2)}, u32[]{:S(2)}) collective-permute-start(f32[512,128]{1,0:T(8,128)S(1)} %last.1), channel_id=1, source_target_pairs={{0,1},{1,0},{2,3},{3,2},{4,5},{5,4},{6,7},{7,6},{8,9},{9,8},{10,11... | collective-permute-start | bytes 786440 | tf_op jit(solution)/shard_map/ppermute | solution.py:401

commit v16 on v14

--- a/solution.py
+++ b/solution.py
@@ -268,65 +268,51 @@
         begin += out.shape[0]
 
 
-def second_kernel(n_high, kept, got, got_y, got_l, *rest):
-    got_h, (own_a, own_d, own_b, own_e, to_y, to_l, *to_h) = rest[: n_high - 1], rest[n_high - 1 :]
+def add_up(out, at, begin, size, *sources):
+    total = None
+    for array, offset in sources:
+        value = array[offset + begin : offset + begin + size, :]
+        total = value if total is None else total + value
+    out[at : at + size, :] = total
+
+
+def second_y_kernel(n_high, kept, got, got_y, own_a, own_d, to_l, *to_h):
     a, d, b, e = (rows * SUB for rows in PART_ROWS)
-
-    def put(out, at, begin, size, *arrivals):
-        total = kept[begin : begin + size, :] + got[begin : begin + size, :]
-        for array, first in arrivals:
-            total += array[first : first + size, :]
-        out[at : at + size, :] = total
-
+    sources = ((kept, 0), (got, 0), (got_y, 0))
     n = n_high * a
-    put(own_a, 0, 0, n, (got_y, 0))
-    put(to_l, 0, n, n, (got_y, n))
-    begin, y_begin = 2 * n, 2 * n
-    put(own_d, 0, begin, 2 * d, (got_y, y_begin))
+    add_up(to_l, 0, n, n, *sources)
     for i, out in enumerate(to_h):
-        put(out, 0, begin + 2 * d * (i + 1), 2 * d, (got_y, y_begin + 2 * d * (i + 1)))
-    begin, n = begin + 2 * n_high * d, n_high * b
-    put(own_b, 0, begin, n, (got_l, 0))
-    put(to_y, 0, begin + n, n, (got_l, n))
+        add_up(out, 0, 2 * n + 2 * d * (i + 1), 2 * d, *sources)
+    add_up(own_a, 0, 0, n, *sources)
+    add_up(own_d, 0, 2 * n, 2 * d, *sources)
+
+
+def second_z_kernel(n_high, kept, got, got_l, *rest):
+    got_h, (before, own_b, own_e, to_y) = rest[: n_high - 1], rest[n_high - 1 :]
+    a, d, b, e = (rows * SUB for rows in PART_ROWS)
+    begin, n = 2 * n_high * (a + d), n_high * b
+    sources = ((kept, begin), (got, begin), (got_l, 0))
+    add_up(to_y, 0, n, n, *sources)
+    add_up(own_b, 0, 0, n, *sources)
     begin += 2 * n
-    put(own_e, 0, begin, 2 * e, *[(array, 0) for array in got_h])
-    put(to_y, n, begin + 2 * e, 2 * e, *[(array, 2 * e) for array in got_h])
-
-
-def third_kernel(n_high, own_a, own_d, own_b, own_e, got_y, got_l, *rest):
-    got_h, (own, to_l, *to_h) = rest[: n_high - 1], rest[n_high - 1 :]
-    a, d, b, e = (rows * SUB for rows in PART_ROWS)
-
-    def put(out, at, source, begin, size, *arrivals):
-        total = source[begin : begin + size, :]
-        for array, first in arrivals:
-            total += array[first : first + size, :]
-        out[at : at + size, :] = total
-
-    put(own, 0, own_a, 0, a, (got_l, 0))
-    put(own, a, own_d, 0, d, *[(array, 0) for array in got_h])
-    put(own, a + d, own_b, 0, b, (got_y, 0))
-    put(own, a + d + b, own_e, 0, e, (got_y, n_high * b))
-    put(to_l, 0, own_d, d, d, *[(array, d) for array in got_h])
-    put(to_l, d, own_e, e, e, (got_y, n_high * b + e))
-    for i, out in enumerate(to_h):
-        put(out, 0, own_a, (i + 1) * a, a, (got_l, (i + 1) * a))
-        put(out, a, own_b, (i + 1) * b, b, (got_y, (i + 1) * b))
-
-
-def last_kernel(before, got_l, *rest):
-    got_h, (own,) = rest[:-1], rest[-1:]
-    a, d, b, e = (rows * SUB for rows in PART_ROWS)
-    for at, size, arrivals in (
-        (0, a, [(array, 0) for array in got_h]),
-        (a, d, [(got_l, 0)]),
-        (a + d, b, [(array, a) for array in got_h]),
-        (a + d + b, e, [(got_l, d)]),
-    ):
-        total = before[at : at + size, :]
-        for array, first in arrivals:
-            total += array[first : first + size, :]
-        own[at : at + size, :] = total
+    sources = ((kept, begin), (got, begin)) + tuple((array, 0) for array in got_h)
+    add_up(to_y, n, 2 * e, 2 * e, *sources)
+    add_up(own_e, 0, 0, 2 * e, *sources)
+
+
+def third_kernel(size, sources, *refs):
+    operands, outs = refs[: len(sources)], refs[len(sources) :]
+    for i, out in enumerate(outs):
+        add_up(out, 0, i * size, size, *[(array, offset) for array, offset in zip(operands, sources)])
+
+
+def last_kernel(n_high, own_a, own_d, own_b, own_e, got_d, got_e, *rest):
+    got_a, got_b, own = rest[: n_high - 1], rest[n_high - 1 : -1], rest[-1]
+    at = 0
+    for mine, arrivals in ((own_a, got_a), (own_d, (got_d,)), (own_b, got_b), (own_e, (got_e,))):
+        size = mine.shape[0]
+        add_up(own, at, 0, size, (mine, 0), *[(array, 0) for array in arrivals])
+        at += size
 
 
 def bank_kernel(own, other, bank, out):
@@ -401,18 +387,34 @@
         first_kernel, "first", [2 * n_high * (a + d), 2 * n_high * b] + [4 * e] * n_h, kept_away, got_away
     )
     got_y, got_l, got_h = over_blk(to_y, 1), over_blk(to_l, 2), over_h(to_h)
-    own_a, own_d, own_b, own_e, to_y, to_l, *to_h = in_vmem(
-        functools.partial(second_kernel, n_high), "second",
-        [n_high * a, 2 * d, n_high * b, 2 * e, n_high * b + 2 * e, n_high * a] + [2 * d] * n_h,
-        kept_stay, got_stay, got_y, got_l, *got_h,
-    )
-    got_y, got_l, got_h = over_blk(to_y, 1), over_blk(to_l, 2), over_h(to_h)
-    own, to_l, *to_h = in_vmem(
-        functools.partial(third_kernel, n_high), "third", [a + d + b + e, d + e] + [a + b] * n_h,
-        own_a, own_d, own_b, own_e, got_y, got_l, *got_h,
-    )
-    got_l, got_h = over_blk(to_l, 2), over_h(to_h)
-    (own,) = in_vmem(last_kernel, "last", [a + d + b + e], own, got_l, *got_h)
+    own_a, own_d, to_l, *to_h = in_vmem(
+        functools.partial(second_y_kernel, n_high), "second_y",
+        [n_high * a, 2 * d, n_high * a] + [2 * d] * n_h, kept_stay, got_stay, got_y,
+    )
+    next_l, next_h = over_blk(to_l, 2), over_h(to_h)
+
+    def third(name, size, count, *sources):
+        kernel = functools.partial(third_kernel, size, [offset for _, offset in sources])
+        return in_vmem(kernel, name, [size] * count, *[array for array, _ in sources])
+
+    own_a, *to_h = third("third_a", a, n_high, (own_a, 0), (next_l, 0))
+    last_a = over_h(to_h)
+    own_b, own_e, to_y = in_vmem(
+        functools.partial(second_z_kernel, n_high), "second_z",
+        [n_high * b, 2 * e, n_high * b + 2 * e], kept_stay, got_stay, got_l, *got_h, own_a,
+    )
+    next_y = over_blk(to_y, 1)
+
+    own_d, to_l = third("third_d", d, 2, (own_d, 0), *[(array, 0) for array in next_h])
+    last_d = over_blk(to_l, 2)
+    own_b, *to_h = third("third_b", b, n_high, (own_b, 0), (next_y, 0))
+    last_b = over_h(to_h)
+    own_e, to_l = third("third_e", e, 2, (own_e, 0), (next_y, n_high * b))
+    last_e = over_blk(to_l, 2)
+    (own,) = in_vmem(
+        functools.partial(last_kernel, n_high), "last", [a + d + b + e],
+        own_a, own_d, own_b, own_e, last_d, last_e, *last_a, *last_b,
+    )
     return apply_bank(own, over_rep(own), weight_bank)
 
 

time: 58.3 us -> 63 us (1.081)
  starting transfers between devices: 13.2 us -> 18.3 us
    ppermute x8 -> x10, starting transfers between devices: 12.5 us -> 17.6 us  [over_blk(): return lax.ppermute(array, 'blk', [(i, i ^ bits) for i in range(n_blk)])]
    ppermute x8 -> x10, waiting for transfers between devices: 21.6 us -> 21.2 us  [over_blk(): return lax.ppermute(array, 'blk', [(i, i ^ bits) for i in range(n_blk)])]
    pallas_call x5 -> x9, Pallas kernels: 1.81 us -> 1.82 us  [in_vmem(): pl.pallas_call(kernel, out_shape=[jax.ShapeDtypeStruct((n, LANES), jnp.fl...]
  transfers between devices with their start and end apart: 11 -> 13, of which waited for: 7 -> 8; matrix products, arithmetic and copies ran while one was open for 0% -> 0% of each run, Pallas kernels for 3% -> 3%
where the time goes in v16:
time: 63 us; the launch traced here: 62.9 us
  waiting for transfers between devices  23.4 us (37%)
  Pallas kernels  21.1 us (33%)
  starting transfers between devices  18.3 us (29%)
    ppermute x10, waiting for transfers between devices, over_blk(): return lax.ppermute(array, 'blk', [(i, i ^ bits) for i in range(n_blk)])  21.2 us
    ppermute x10, starting transfers between devices, over_blk(): return lax.ppermute(array, 'blk', [(i, i ^ bits) for i in range(n_blk)])  17.6 us
    pallas_call x1, Pallas kernels, accumulate(): pl.pallas_call(functools.partial(accumulate_kernel, bank_size, n_owner, n...  16.9 us
    pallas_call x1, Pallas kernels, apply_bank(): pl.pallas_call(bank_kernel, out_shape=jax.ShapeDtypeStruct((NB_DEV, n_z,...  2.36 us
    ppermute x3, waiting for transfers between devices, over_rep(): return lax.ppermute(array, 'rep', [(0, 1), (1, 0)])  2.21 us
    pallas_call x9, Pallas kernels, in_vmem(): pl.pallas_call(kernel, out_shape=[jax.ShapeDtypeStruct((n, LANES), jnp.fl...  1.82 us
  transfers between devices with their start and end apart: 13, of which 8 were waited for; matrix products, arithmetic and copies ran while one was open for 0% of the time, Pallas kernels for 3%

profile of v16, /device:TPU:0, one launch (start us, length us, event | category | flops | bytes accessed | tf_op | source)
XLA Modules:
  0.0 62.9 jit_solution(1479018190951655033)
XLA Ops:
  0.0 16.9 %accumulate.1 = (f32[2048,128]{1,0:T(8,128)S(1)}, f32[8192,128]{1,0:T(8,128)S(1)}, f32[8192,128]{1,0:T(8,128)S(1)}, f32[8192,128]{1,0:T(8,128)S(1)}, f32[8192,128]{1,0:T(8,128)S(1)}) custom-call(bf16[36864,128]{1,0:T(8,128)(2,1)} %bitcast.29, bf16[4608,128]{1,0:T(8,128)(2,1)} %bitcast.30, bf16[4608,128]{1,0:T(8,128)(2,1)} %bitcast.31, f32[8,16]{1,0:T(8,128)} %bitcast.34, ...), custom_call_target="tpu_custom_call" | custom-call | tf_op jit(solution)/shard_map/accumulate/pallas_call | solution.py:216
  16.9 0.5 collective-permute-start.1
  17.4 1.5 %rest.1 = (f32[2048,128]{1,0:T(8,128)S(1)}, f32[2048,128]{1,0:T(8,128)S(1)}, f32[2048,128]{1,0:T(8,128)S(1)}) custom-call(f32[8192,128]{1,0:T(8,128)S(1)} %get-tuple-element.31.refs_0_, f32[8192,128]{1,0:T(8,128)S(1)} %get-tuple-element.32.refs_1_, f32[8192,128]{1,0:T(8,128)S(1)} %get-tuple-element.33.refs_2_, f32[8192,128]{1,0:T(8,128)S(1)} %get-tuple-element.34.refs_3_), custom_call_target="tpu_custom_call" | custom-call | tf_op jit(solution)/shard_map/rest/pallas_call | solution.py:253
  18.9 0.1 collective-permute-start
  19.0 0.7 %collective-permute-done.1.got = f32[2048,128]{1,0:T(8,128)S(1)} collective-permute-done((f32[2048,128]{1,0:T(8,128)S(1)}, f32[2048,128]{1,0:T(8,128)S(1)}, u32[]{:S(2)}, u32[]{:S(2)}) %collective-permute-start.1) | collective-permute-done | bytes 1048608 | tf_op jit(solution)/shard_map/ppermute | solution.py:376
  19.7 0.1 first.1
  19.9 3.0 %collective-permute-start.2 = (f32[1024,128]{1,0:T(8,128)S(1)}, f32[1024,128]{1,0:T(8,128)S(1)}, u32[]{:S(2)}, u32[]{:S(2)}) collective-permute-start(f32[1024,128]{1,0:T(8,128)S(1)} %get-tuple-element.39), channel_id=1, source_target_pairs={{0,2},{2,0},{4,6},{6,4},{8,10},{10,8},{12,14},{14,12},{1,3},{3,1},... | collective-permute-start | bytes 1572872 | tf_op jit(solution)/shard_map/ppermute | solution.py:379
  22.8 1.6 %collective-permute-start.5 = (f32[512,128]{1,0:T(8,128)S(1)}, f32[512,128]{1,0:T(8,128)S(1)}, u32[]{:S(2)}, u32[]{:S(2)}) collective-permute-start(f32[512,128]{1,0:T(8,128)S(1)} %get-tuple-element.46), channel_id=1, source_target_pairs={{0,4},{2,6},{4,0},{6,2},{8,12},{10,14},{12,8},{14,10},{1,5},{3,7},... | collective-permute-start | bytes 786440 | tf_op jit(solution)/shard_map/ppermute | solution.py:379
  24.4 2.6 %collective-permute-start.6 = (f32[512,128]{1,0:T(8,128)S(1)}, f32[512,128]{1,0:T(8,128)S(1)}, u32[]{:S(2)}, u32[]{:S(2)}) collective-permute-start(f32[512,128]{1,0:T(8,128)S(1)} %get-tuple-element.47), channel_id=1, source_target_pairs={{0,8},{2,10},{4,12},{6,14},{8,0},{10,2},{12,4},{14,6},{1,9},{3,11}... | collective-permute-start | bytes 786440 | tf_op jit(solution)/shard_map/ppermute | solution.py:379
  27.0 8.1 %collective-permute-done.2.got_y = f32[1024,128]{1,0:T(8,128)S(1)} collective-permute-done((f32[1024,128]{1,0:T(8,128)S(1)}, f32[1024,128]{1,0:T(8,128)S(1)}, u32[]{:S(2)}, u32[]{:S(2)}) %collective-permute-start.2) | collective-permute-done | bytes 524320 | tf_op jit(solution)/shard_map/ppermute | solution.py:379
  35.1 1.9 %collective-permute-start.3 = (f32[256,128]{1,0:T(8,128)S(1)}, f32[256,128]{1,0:T(8,128)S(1)}, u32[]{:S(2)}, u32[]{:S(2)}) collective-permute-start(f32[256,128]{1,0:T(8,128)S(1)} %get-tuple-element.41), channel_id=1, source_target_pairs={{0,4},{2,6},{4,0},{6,2},{8,12},{10,14},{12,8},{14,10},{1,5},{3,7},... | collective-permute-start | bytes 393224 | tf_op jit(solution)/shard_map/ppermute | solution.py:379
  37.0 3.3 %collective-permute-done.3.refs_1_ = f32[256,128]{1,0:T(8,128)S(1)} collective-permute-done((f32[256,128]{1,0:T(8,128)S(1)}, f32[256,128]{1,0:T(8,128)S(1)}, u32[]{:S(2)}, u32[]{:S(2)}) %collective-permute-start.3) | collective-permute-done | bytes 131104 | tf_op jit(solution)/shard_map/ppermute | solution.py:379
  40.5 1.6 %collective-permute-start.7 = (f32[512,128]{1,0:T(8,128)S(1)}, f32[512,128]{1,0:T(8,128)S(1)}, u32[]{:S(2)}, u32[]{:S(2)}) collective-permute-start(f32[512,128]{1,0:T(8,128)S(1)} %get-tuple-element.49), channel_id=1, source_target_pairs={{0,2},{2,0},{4,6},{6,4},{8,10},{10,8},{12,14},{14,12},{1,3},{3,1},... | collective-permute-start | bytes 786440 | tf_op jit(solution)/shard_map/ppermute | solution.py:379
  42.1 2.6 %collective-permute-start.4 = (f32[256,128]{1,0:T(8,128)S(1)}, f32[256,128]{1,0:T(8,128)S(1)}, u32[]{:S(2)}, u32[]{:S(2)}) collective-permute-start(f32[256,128]{1,0:T(8,128)S(1)} %get-tuple-element.44), channel_id=1, source_target_pairs={{0,8},{2,10},{4,12},{6,14},{8,0},{10,2},{12,4},{14,6},{1,9},{3,11}... | collective-permute-start | bytes 393224 | tf_op jit(solution)/shard_map/ppermute | solution.py:379
  44.7 0.3 collective-permute-start.10
  45.0 6.4 %collective-permute-done.4.refs_1_ = f32[256,128]{1,0:T(8,128)S(1)} collective-permute-done((f32[256,128]{1,0:T(8,128)S(1)}, f32[256,128]{1,0:T(8,128)S(1)}, u32[]{:S(2)}, u32[]{:S(2)}) %collective-permute-start.4) | collective-permute-done | bytes 131104 | tf_op jit(solution)/shard_map/ppermute | solution.py:379
  51.5 0.5 collective-permute-start.8
  52.0 1.7 %collective-permute-start.9 = (f32[128,128]{1,0:T(8,128)S(1)}, f32[128,128]{1,0:T(8,128)S(1)}, u32[]{:S(2)}, u32[]{:S(2)}) collective-permute-start(f32[128,128]{1,0:T(8,128)S(1)} %get-tuple-element.54), channel_id=1, source_target_pairs={{0,4},{2,6},{4,0},{6,2},{8,12},{10,14},{12,8},{14,10},{1,5},{3,7},... | collective-permute-start | bytes 196616 | tf_op jit(solution)/shard_map/ppermute | solution.py:379
  53.6 1.9 %collective-permute-start.11 = (f32[128,128]{1,0:T(8,128)S(1)}, f32[128,128]{1,0:T(8,128)S(1)}, u32[]{:S(2)}, u32[]{:S(2)}) collective-permute-start(f32[128,128]{1,0:T(8,128)S(1)} %get-tuple-element.56), channel_id=1, source_target_pairs={{0,8},{2,10},{4,12},{6,14},{8,0},{10,2},{12,4},{14,6},{1,9},{3,11}... | collective-permute-start | bytes 196616 | tf_op jit(solution)/shard_map/ppermute | solution.py:379
  55.5 0.3 collective-permute-done.8.got_d
  55.8 0.7 %collective-permute-done.9.got_e = f32[128,128]{1,0:T(8,128)S(1)} collective-permute-done((f32[128,128]{1,0:T(8,128)S(1)}, f32[128,128]{1,0:T(8,128)S(1)}, u32[]{:S(2)}, u32[]{:S(2)}) %collective-permute-start.9) | collective-permute-done | bytes 65568 | tf_op jit(solution)/shard_map/ppermute | solution.py:379
  56.5 2.4 %collective-permute-done.11.rest_1_ = f32[128,128]{1,0:T(8,128)S(1)} collective-permute-done((f32[128,128]{1,0:T(8,128)S(1)}, f32[128,128]{1,0:T(8,128)S(1)}, u32[]{:S(2)}, u32[]{:S(2)}) %collective-permute-start.11) | collective-permute-done | bytes 65568 | tf_op jit(solution)/shard_map/ppermute | solution.py:379
  59.0 1.5 %collective-permute-done.12 = f32[512,128]{1,0:T(8,128)S(1)} collective-permute-done((f32[512,128]{1,0:T(8,128)S(1)}, f32[512,128]{1,0:T(8,128)S(1)}, u32[]{:S(2)}, u32[]{:S(2)}) %collective-permute-start.12) | collective-permute-done | bytes 262176 | tf_op jit(solution)/shard_map/ppermute | solution.py:376
  60.5 2.4 %apply_bank.1 = f32[8,32,1024]{2,1,0:T(8,128)} custom-call(f32[4,16,8,128]{3,2,1,0:T(8,128)S(1)} %bitcast.27, f32[4,16,8,128]{3,2,1,0:T(8,128)S(1)} %bitcast.28, f32[16,32,1024]{2,1,0:T(8,128)S(1)} %copy-done), custom_call_target="tpu_custom_call" | custom-call | tf_op jit(solution)/shard_map/apply_bank/pallas_call | solution.py:353
  (15 shorter events, 0.3 us)
Async XLA Ops:
  16.9 2.8 %collective-permute-start.1 = (f32[2048,128]{1,0:T(8,128)S(1)}, f32[2048,128]{1,0:T(8,128)S(1)}, u32[]{:S(2)}, u32[]{:S(2)}) collective-permute-start(f32[2048,128]{1,0:T(8,128)S(1)} %get-tuple-element.38), channel_id=1, source_target_pairs={{0,1},{1,0},{2,3},{3,2},{4,5},{5,4},{6,7},{7,6},{8,9},{9,8},{10,11... | collective-permute-start | bytes 3145736 | tf_op jit(solution)/shard_map/ppermute | solution.py:376
  18.9 8.1 %collective-permute-start = (f32[2048,128]{1,0:T(8,128)S(1)}, f32[2048,128]{1,0:T(8,128)S(1)}, u32[]{:S(2)}, u32[]{:S(2)}) collective-permute-start(f32[2048,128]{1,0:T(8,128)S(1)} %get-tuple-element.36), channel_id=1, source_target_pairs={{0,1},{1,0},{2,3},{3,2},{4,5},{5,4},{6,7},{7,6},{8,9},{9,8},{10,11... | collective-permute-start | bytes 3145736 | tf_op jit(solution)/shard_map/ppermute | solution.py:376
  19.8 40.7 %copy-start = (f32[16,32,1024]{2,1,0:T(8,128)S(1)}, f32[16,32,1024]{2,1,0:T(8,128)}, u32[]{:S(2)}) copy-start(f32[16,32,1024]{2,1,0:T(8,128)} %bank.1) | copy-start | bytes 6291460
  19.9 15.2 %collective-permute-start.2 = (f32[1024,128]{1,0:T(8,128)S(1)}, f32[1024,128]{1,0:T(8,128)S(1)}, u32[]{:S(2)}, u32[]{:S(2)}) collective-permute-start(f32[1024,128]{1,0:T(8,128)S(1)} %get-tuple-element.39), channel_id=1, source_target_pairs={{0,2},{2,0},{4,6},{6,4},{8,10},{10,8},{12,14},{14,12},{1,3},{3,1},... | collective-permute-start | bytes 1572872 | tf_op jit(solution)/shard_map/ppermute | solution.py:379
  22.8 17.5 %collective-permute-start.5 = (f32[512,128]{1,0:T(8,128)S(1)}, f32[512,128]{1,0:T(8,128)S(1)}, u32[]{:S(2)}, u32[]{:S(2)}) collective-permute-start(f32[512,128]{1,0:T(8,128)S(1)} %get-tuple-element.46), channel_id=1, source_target_pairs={{0,4},{2,6},{4,0},{6,2},{8,12},{10,14},{12,8},{14,10},{1,5},{3,7},... | collective-permute-start | bytes 786440 | tf_op jit(solution)/shard_map/ppermute | solution.py:379
  24.4 16.0 %collective-permute-start.6 = (f32[512,128]{1,0:T(8,128)S(1)}, f32[512,128]{1,0:T(8,128)S(1)}, u32[]{:S(2)}, u32[]{:S(2)}) collective-permute-start(f32[512,128]{1,0:T(8,128)S(1)} %get-tuple-element.47), channel_id=1, source_target_pairs={{0,8},{2,10},{4,12},{6,14},{8,0},{10,2},{12,4},{14,6},{1,9},{3,11}... | collective-permute-start | bytes 786440 | tf_op jit(solution)/shard_map/ppermute | solution.py:379
  35.1 5.2 %collective-permute-start.3 = (f32[256,128]{1,0:T(8,128)S(1)}, f32[256,128]{1,0:T(8,128)S(1)}, u32[]{:S(2)}, u32[]{:S(2)}) collective-permute-start(f32[256,128]{1,0:T(8,128)S(1)} %get-tuple-element.41), channel_id=1, source_target_pairs={{0,4},{2,6},{4,0},{6,2},{8,12},{10,14},{12,8},{14,10},{1,5},{3,7},... | collective-permute-start | bytes 393224 | tf_op jit(solution)/shard_map/ppermute | solution.py:379
  40.5 11.5 %collective-permute-start.7 = (f32[512,128]{1,0:T(8,128)S(1)}, f32[512,128]{1,0:T(8,128)S(1)}, u32[]{:S(2)}, u32[]{:S(2)}) collective-permute-start(f32[512,128]{1,0:T(8,128)S(1)} %get-tuple-element.49), channel_id=1, source_target_pairs={{0,2},{2,0},{4,6},{6,4},{8,10},{10,8},{12,14},{14,12},{1,3},{3,1},... | collective-permute-start | bytes 786440 | tf_op jit(solution)/shard_map/ppermute | solution.py:379
  42.1 9.3 %collective-permute-start.4 = (f32[256,128]{1,0:T(8,128)S(1)}, f32[256,128]{1,0:T(8,128)S(1)}, u32[]{:S(2)}, u32[]{:S(2)}) collective-permute-start(f32[256,128]{1,0:T(8,128)S(1)} %get-tuple-element.44), channel_id=1, source_target_pairs={{0,8},{2,10},{4,12},{6,14},{8,0},{10,2},{12,4},{14,6},{1,9},{3,11}... | collective-permute-start | bytes 393224 | tf_op jit(solution)/shard_map/ppermute | solution.py:379
  44.7 10.8 %collective-permute-start.10 = (f32[128,128]{1,0:T(8,128)S(1)}, f32[128,128]{1,0:T(8,128)S(1)}, u32[]{:S(2)}, u32[]{:S(2)}) collective-permute-start(f32[128,128]{1,0:T(8,128)S(1)} %get-tuple-element.55), channel_id=1, source_target_pairs={{0,8},{2,10},{4,12},{6,14},{8,0},{10,2},{12,4},{14,6},{1,9},{3,11}... | collective-permute-start | bytes 196616 | tf_op jit(solution)/shard_map/ppermute | solution.py:379
  51.5 4.3 %collective-permute-start.8 = (f32[128,128]{1,0:T(8,128)S(1)}, f32[128,128]{1,0:T(8,128)S(1)}, u32[]{:S(2)}, u32[]{:S(2)}) collective-permute-start(f32[128,128]{1,0:T(8,128)S(1)} %get-tuple-element.53), channel_id=1, source_target_pairs={{0,4},{2,6},{4,0},{6,2},{8,12},{10,14},{12,8},{14,10},{1,5},{3,7},... | collective-permute-start | bytes 196616 | tf_op jit(solution)/shard_map/ppermute | solution.py:379
  52.0 4.5 %collective-permute-start.9 = (f32[128,128]{1,0:T(8,128)S(1)}, f32[128,128]{1,0:T(8,128)S(1)}, u32[]{:S(2)}, u32[]{:S(2)}) collective-permute-start(f32[128,128]{1,0:T(8,128)S(1)} %get-tuple-element.54), channel_id=1, source_target_pairs={{0,4},{2,6},{4,0},{6,2},{8,12},{10,14},{12,8},{14,10},{1,5},{3,7},... | collective-permute-start | bytes 196616 | tf_op jit(solution)/shard_map/ppermute | solution.py:379
  53.6 5.2 %collective-permute-start.11 = (f32[128,128]{1,0:T(8,128)S(1)}, f32[128,128]{1,0:T(8,128)S(1)}, u32[]{:S(2)}, u32[]{:S(2)}) collective-permute-start(f32[128,128]{1,0:T(8,128)S(1)} %get-tuple-element.56), channel_id=1, source_target_pairs={{0,8},{2,10},{4,12},{6,14},{8,0},{10,2},{12,4},{14,6},{1,9},{3,11}... | collective-permute-start | bytes 196616 | tf_op jit(solution)/shard_map/ppermute | solution.py:379
  58.9 1.6 %collective-permute-start.12 = (f32[512,128]{1,0:T(8,128)S(1)}, f32[512,128]{1,0:T(8,128)S(1)}, u32[]{:S(2)}, u32[]{:S(2)}) collective-permute-start(f32[512,128]{1,0:T(8,128)S(1)} %last.1), channel_id=1, source_target_pairs={{0,1},{1,0},{2,3},{3,2},{4,5},{5,4},{6,7},{7,6},{8,9},{9,8},{10,11... | collective-permute-start | bytes 786440 | tf_op jit(solution)/shard_map/ppermute | solution.py:376

commit v17 on v15

--- a/solution.py
+++ b/solution.py
@@ -90,26 +90,12 @@
         square[rows, :] = t * t
         cross[rows, :] = t * img[rows, :].astype(jnp.float32)
 
-    sublane = lax.broadcasted_iota(jnp.int32, (SUB, LANES), 0)
-    bits = [(sublane & (1 << t)) != 0 for t in range(3)]
-
     def stage(p, j, part):
         first = pl.multiple_of((p * n_tile + j) * tile_rows, tile_rows)
         part[...] = proj[pl.ds(first, tile_rows), :].astype(jnp.float32)
 
     def staged(part):
         return [part[pl.ds(k, SUB, stride=SUB), :] for k in range(n_pose)]
-
-    def rolled(p, j):
-        first = (p * n_tile + j) * tile_rows
-        cells = []
-        for c in range(0, SUB, 2):
-            pair = proj[pl.ds(pl.multiple_of(first + c * SUB, 2 * SUB), 2 * SUB), :].astype(jnp.float32)
-            cells += [pair[:SUB], pair[SUB:]]
-        cells = [pltpu.roll(x, c, 0) if c else x for c, x in enumerate(cells)]
-        for t, bit in enumerate(bits):
-            cells = [jnp.where(bit, cells[(i + (1 << t)) % SUB], cells[i]) for i in range(SUB)]
-        return [pltpu.roll(cells[-k % SUB], SUB - k, 0) if k else cells[0] for k in range(n_pose)]
 
     def terms(p, j, cells, weights):
         cell = pl.ds((j * (n_part // SUB) + p // SUB) * tile_rows + p % SUB, SUB, stride=SUB)
@@ -126,27 +112,39 @@
 
     idx_copy.wait()
 
-    @pl.loop(0, n_part)
-    def _(p):
-        proj_copy(p).wait()
-        weights = [jnp.full((SUB, LANES), weight[k, p], jnp.float32) for k in range(n_pose)]
-
-        stage(p, 0, parts[0])
-        stage(p, 1, parts[1])
-
-        @pl.loop(0, n_tile, step=UNROLL, init_carry=tuple(terms(p, 0, staged(parts[0]), weights)))
-        def _(j, values):
+    def spread(p):
+        return [jnp.full((SUB, LANES), weight[k, p], jnp.float32) for k in range(n_pose)]
+
+    proj_copy(0).wait()
+    stage(0, 0, parts[0])
+    stage(0, 1, parts[1])
+
+    @pl.loop(0, n_part, init_carry=tuple(terms(0, 0, staged(parts[0]), spread(0))))
+    def _(p, carry):
+        @pl.when(p + 1 < n_part)
+        def _():
+            proj_copy(p + 1).wait()
+
+        weights = spread(p)
+
+        @pl.loop(0, n_tile, step=UNROLL, init_carry=carry)
+        def done(j, values):
+            ends = j + UNROLL == n_tile
+            next_p = jnp.where(ends, jnp.minimum(p + 1, n_part - 1), p)
+            next_j = jnp.where(ends, 0, j + UNROLL)
+
             def tile(u):
-                return jnp.minimum(j + u, n_tile - 1) if u >= UNROLL else j + u
+                return (p, j + u) if u < UNROLL else (next_p, next_j + u - UNROLL)
 
             for u in range(UNROLL):
-                if (u + 2) % 3 != 2:
-                    stage(p, tile(u + 2), parts[(u + 2) % N_BUF])
-                cells = staged(parts[(u + 1) % N_BUF]) if (u + 1) % 3 != 2 else rolled(p, tile(u + 1))
-                later = terms(p, tile(u + 1), cells, weights)
+                stage(*tile(u + 2), parts[(u + 2) % N_BUF])
+                scale = weights if u + 1 < UNROLL else spread(next_p)
+                later = terms(*tile(u + 1), staged(parts[(u + 1) % N_BUF]), scale)
                 add_rows(p, j + u, values)
                 values = later
             return tuple(values)
+
+        return done
 
     sums = Sums(n_owner, accs)
     sums.pieces_away(sent_away, sent=True)
@@ -206,7 +204,7 @@
     bank_size, n_owner,
 ):
     n_part, n_pose, n_tile, n_cell = projections.shape
-    assert n_cell == SUB * LANES and n_pose == SUB and n_part % SUB == 0 and n_tile % UNROLL == 0 and UNROLL % (3 * N_BUF) == 0
+    assert n_cell == SUB * LANES and n_pose == SUB and n_part % SUB == 0 and n_tile % UNROLL == 0 and UNROLL % N_BUF == 0
     n_row = n_owner * NB_DEV * bank_size * SUB
     n_acc = 4 if n_row * LANES * 4 <= 4 * MIB else 2
     projections = tiles_in_order(jnp.transpose(projections, (0, 2, 1, 3)))
@@ -340,49 +338,63 @@
         own[at : at + size, :] = total
 
 
-def bank_kernel(own, other, bank, out):
+def weigh(source, bank, out):
     bank_size, n_z, n_cell = bank.shape
-    n_half = out.shape[0] // 2
     group = 2 * SUB
 
-    def apply(halves):
-        for c in range(n_cell // LANES):
-            cols = slice(c * LANES, (c + 1) * LANES)
-
-            @pl.loop(0, n_z // group)
-            def _(g):
-                rows = pl.ds(pl.multiple_of(g * group, group), group)
-                weights = [bank[t, rows, cols] for t in range(bank_size)]
-                for b in range(2 * n_half):
-                    total = None
-                    for t in range(bank_size):
-                        value = weights[t] * halves[b // n_half][b % n_half, t, c : c + 1, :]
-                        total = value if total is None else total + value
-                    out[b, rows, cols] = total
-
+    for c in range(n_cell // LANES):
+        cols = slice(c * LANES, (c + 1) * LANES)
+
+        @pl.loop(0, n_z // group)
+        def _(g):
+            rows = pl.ds(pl.multiple_of(g * group, group), group)
+            weights = [bank[t, rows, cols] for t in range(bank_size)]
+            for b in range(out.shape[0]):
+                total = None
+                for t in range(bank_size):
+                    value = weights[t] * source[b, t, c : c + 1, :]
+                    total = value if total is None else total + value
+                out[b, rows, cols] = total
+
+
+def bank_rest_kernel(done, other, bank, out_hbm, block, sem):
+    n_half = block.shape[0]
     rep = position()[0]
-
-    @pl.when(rep == 0)
-    def _():
-        apply((own, other))
-
-    @pl.when(rep == 1)
-    def _():
-        apply((other, own))
+    first = pltpu.make_async_copy(done, out_hbm.at[pl.ds(rep * n_half, n_half)], sem.at[0])
+    first.start()
+    weigh(other, bank, block)
+    second = pltpu.make_async_copy(block, out_hbm.at[pl.ds((1 - rep) * n_half, n_half)], sem.at[1])
+    second.start()
+    first.wait()
+    second.wait()
 
 
 def apply_bank(own, other, weight_bank):
     bank_size, n_z, n_cell = weight_bank.shape
+    n_half = NB_DEV // 2
     vmem = pl.BlockSpec(memory_space=pltpu.VMEM)
-    own, other = [array.reshape(NB_DEV // 2, bank_size, SUB, LANES) for array in (own, other)]
+    own, other = [array.reshape(n_half, bank_size, SUB, LANES) for array in (own, other)]
+    params = pltpu.CompilerParams(vmem_limit_bytes=32 * MIB)
+    done = pl.pallas_call(
+        weigh,
+        out_shape=jax.ShapeDtypeStruct((n_half, n_z, n_cell), jnp.float32),
+        in_specs=[vmem] * 2,
+        out_specs=vmem,
+        compiler_params=params,
+        name="bank_own",
+    )(own, weight_bank)
     return pl.pallas_call(
-        bank_kernel,
+        bank_rest_kernel,
         out_shape=jax.ShapeDtypeStruct((NB_DEV, n_z, n_cell), jnp.float32),
         in_specs=[vmem] * 3,
-        out_specs=vmem,
-        compiler_params=pltpu.CompilerParams(vmem_limit_bytes=32 * MIB),
-        name="apply_bank",
-    )(own, other, weight_bank)
+        out_specs=pl.BlockSpec(memory_space=pl.ANY),
+        scratch_shapes=[
+            pltpu.VMEM((n_half, n_z, n_cell), jnp.float32),
+            pltpu.SemaphoreType.DMA((2,)),
+        ],
+        compiler_params=params,
+        name="bank_rest",
+    )(done, other, weight_bank)
 
 
 def body(

time: 59.5 us -> 58.4 us (0.982)
  waiting for transfers between devices: 25.3 us -> 24.5 us
    ppermute x3, waiting for transfers between devices: 3.73 us -> 2.9 us  [over_rep(): return lax.ppermute(array, 'rep', [(0, 1), (1, 0)])]
    pallas_call x1 -> x2, Pallas kernels: 2.36 us -> 2.44 us  [the longest x1 1.62 us: apply_bank(): pl.pallas_call(bank_rest_kernel, out_shape=jax.ShapeDtypeStruct((NB_DEV,...]
  transfers between devices with their start and end apart: 11 -> 11, of which waited for: 7 -> 7; matrix products, arithmetic and copies ran while one was open for 0% -> 0% of each run, Pallas kernels for 0% -> 2%
where the time goes in v17:
time: 58.4 us; the launch traced here: 58.3 us
  waiting for transfers between devices  24.5 us (42%)
  Pallas kernels  20.5 us (35%)
  starting transfers between devices  13.2 us (23%)
    ppermute x8, waiting for transfers between devices, over_blk(): return lax.ppermute(array, 'blk', [(i, i ^ bits) for i in range(n_blk)])  21.6 us
    pallas_call x1, Pallas kernels, accumulate(): pl.pallas_call(functools.partial(accumulate_kernel, bank_size, n_owner, n...  17.8 us
    ppermute x8, starting transfers between devices, over_blk(): return lax.ppermute(array, 'blk', [(i, i ^ bits) for i in range(n_blk)])  12.5 us
    ppermute x3, waiting for transfers between devices, over_rep(): return lax.ppermute(array, 'rep', [(0, 1), (1, 0)])  2.9 us
    pallas_call x1, Pallas kernels, apply_bank(): pl.pallas_call(bank_rest_kernel, out_shape=jax.ShapeDtypeStruct((NB_DEV,...  1.62 us
  transfers between devices with their start and end apart: 11, of which 7 were waited for; matrix products, arithmetic and copies ran while one was open for 0% of the time, Pallas kernels for 2%

profile of v17, /device:TPU:0, one launch (start us, length us, event | category | flops | bytes accessed | tf_op | source)
XLA Modules:
  0.0 58.3 jit_solution(975254550524354165)
XLA Ops:
  0.0 17.8 %accumulate.1 = (f32[2048,128]{1,0:T(8,128)S(1)}, f32[2048,128]{1,0:T(8,128)S(1)}, f32[2048,128]{1,0:T(8,128)S(1)}, f32[2048,128]{1,0:T(8,128)S(1)}) custom-call(bf16[36864,128]{1,0:T(8,128)(2,1)} %bitcast.29, bf16[4608,128]{1,0:T(8,128)(2,1)} %bitcast.30, bf16[4608,128]{1,0:T(8,128)(2,1)} %bitcast.31, f32[8,16]{1,0:T(8,128)} %bitcast.34, s32[8,16]{1,0:T(8,128)} %bitcast.35, ...), custom_call_target="tpu_custom_call" | custom-call | tf_op jit(solution)/shard_map/accumulate/pallas_call | solution.py:226
  17.8 0.5 collective-permute-start.1
  18.3 0.1 collective-permute-start
  18.4 2.2 %collective-permute-done.1.got = f32[2048,128]{1,0:T(8,128)S(1)} collective-permute-done((f32[2048,128]{1,0:T(8,128)S(1)}, f32[2048,128]{1,0:T(8,128)S(1)}, u32[]{:S(2)}, u32[]{:S(2)}) %collective-permute-start.1) | collective-permute-done | bytes 1048608 | tf_op jit(solution)/shard_map/ppermute | solution.py:413
  20.6 0.1 first.1
  20.7 3.0 %collective-permute-start.2 = (f32[1024,128]{1,0:T(8,128)S(1)}, f32[1024,128]{1,0:T(8,128)S(1)}, u32[]{:S(2)}, u32[]{:S(2)}) collective-permute-start(f32[1024,128]{1,0:T(8,128)S(1)} %get-tuple-element.26), channel_id=1, source_target_pairs={{0,2},{2,0},{4,6},{6,4},{8,10},{10,8},{12,14},{14,12},{1,3},{3,1},... | collective-permute-start | bytes 1572872 | tf_op jit(solution)/shard_map/ppermute | solution.py:416
  23.6 1.6 %collective-permute-start.3 = (f32[512,128]{1,0:T(8,128)S(1)}, f32[512,128]{1,0:T(8,128)S(1)}, u32[]{:S(2)}, u32[]{:S(2)}) collective-permute-start(f32[512,128]{1,0:T(8,128)S(1)} %get-tuple-element.27), channel_id=1, source_target_pairs={{0,4},{2,6},{4,0},{6,2},{8,12},{10,14},{12,8},{14,10},{1,5},{3,7},... | collective-permute-start | bytes 786440 | tf_op jit(solution)/shard_map/ppermute | solution.py:416
  25.2 2.6 %collective-permute-start.4 = (f32[512,128]{1,0:T(8,128)S(1)}, f32[512,128]{1,0:T(8,128)S(1)}, u32[]{:S(2)}, u32[]{:S(2)}) collective-permute-start(f32[512,128]{1,0:T(8,128)S(1)} %get-tuple-element.28), channel_id=1, source_target_pairs={{0,8},{2,10},{4,12},{6,14},{8,0},{10,2},{12,4},{14,6},{1,9},{3,11}... | collective-permute-start | bytes 786440 | tf_op jit(solution)/shard_map/ppermute | solution.py:416
  27.8 9.4 %collective-permute-done.3.got_l = f32[512,128]{1,0:T(8,128)S(1)} collective-permute-done((f32[512,128]{1,0:T(8,128)S(1)}, f32[512,128]{1,0:T(8,128)S(1)}, u32[]{:S(2)}, u32[]{:S(2)}) %collective-permute-start.3) | collective-permute-done | bytes 262176 | tf_op jit(solution)/shard_map/ppermute | solution.py:416
  37.2 2.4 %collective-permute-done.4.rest_0_ = f32[512,128]{1,0:T(8,128)S(1)} collective-permute-done((f32[512,128]{1,0:T(8,128)S(1)}, f32[512,128]{1,0:T(8,128)S(1)}, u32[]{:S(2)}, u32[]{:S(2)}) %collective-permute-start.4) | collective-permute-done | bytes 262176 | tf_op jit(solution)/shard_map/ppermute | solution.py:416
  39.6 0.2 second.1
  39.7 0.6 collective-permute-start.5
  40.3 0.4 collective-permute-start.6
  40.8 2.6 %collective-permute-start.7 = (f32[256,128]{1,0:T(8,128)S(1)}, f32[256,128]{1,0:T(8,128)S(1)}, u32[]{:S(2)}, u32[]{:S(2)}) collective-permute-start(f32[256,128]{1,0:T(8,128)S(1)} %get-tuple-element.35), channel_id=1, source_target_pairs={{0,8},{2,10},{4,12},{6,14},{8,0},{10,2},{12,4},{14,6},{1,9},{3,11}... | collective-permute-start | bytes 393224 | tf_op jit(solution)/shard_map/ppermute | solution.py:416
  43.3 3.8 %collective-permute-done.6.got_l = f32[256,128]{1,0:T(8,128)S(1)} collective-permute-done((f32[256,128]{1,0:T(8,128)S(1)}, f32[256,128]{1,0:T(8,128)S(1)}, u32[]{:S(2)}, u32[]{:S(2)}) %collective-permute-start.6) | collective-permute-done | bytes 131104 | tf_op jit(solution)/shard_map/ppermute | solution.py:416
  47.2 1.1 %collective-permute-done.7.rest_0_ = f32[256,128]{1,0:T(8,128)S(1)} collective-permute-done((f32[256,128]{1,0:T(8,128)S(1)}, f32[256,128]{1,0:T(8,128)S(1)}, u32[]{:S(2)}, u32[]{:S(2)}) %collective-permute-start.7) | collective-permute-done | bytes 131104 | tf_op jit(solution)/shard_map/ppermute | solution.py:416
  48.3 0.1 third.1
  48.3 0.1 collective-permute-start.8
  48.4 1.7 %collective-permute-start.9 = (f32[256,128]{1,0:T(8,128)S(1)}, f32[256,128]{1,0:T(8,128)S(1)}, u32[]{:S(2)}, u32[]{:S(2)}) collective-permute-start(f32[256,128]{1,0:T(8,128)S(1)} %get-tuple-element.38), channel_id=1, source_target_pairs={{0,8},{2,10},{4,12},{6,14},{8,0},{10,2},{12,4},{14,6},{1,9},{3,11}... | collective-permute-start | bytes 393224 | tf_op jit(solution)/shard_map/ppermute | solution.py:416
  50.1 4.9 %collective-permute-done.8.got_l = f32[256,128]{1,0:T(8,128)S(1)} collective-permute-done((f32[256,128]{1,0:T(8,128)S(1)}, f32[256,128]{1,0:T(8,128)S(1)}, u32[]{:S(2)}, u32[]{:S(2)}) %collective-permute-start.8) | collective-permute-done | bytes 131104 | tf_op jit(solution)/shard_map/ppermute | solution.py:416
  55.1 0.1 collective-permute-start.10
  55.2 0.8 %bank_own.1.done = f32[4,32,1024]{2,1,0:T(8,128)S(1)} custom-call(f32[4,16,8,128]{3,2,1,0:T(8,128)S(1)} %bitcast.27, f32[16,32,1024]{2,1,0:T(8,128)S(1)} %copy-done), custom_call_target="tpu_custom_call" | custom-call | tf_op jit(solution)/shard_map/bank_own/pallas_call | solution.py:378
  56.0 0.7 %collective-permute-done.10 = f32[512,128]{1,0:T(8,128)S(1)} collective-permute-done((f32[512,128]{1,0:T(8,128)S(1)}, f32[512,128]{1,0:T(8,128)S(1)}, u32[]{:S(2)}, u32[]{:S(2)}) %collective-permute-start.10) | collective-permute-done | bytes 262176 | tf_op jit(solution)/shard_map/ppermute | solution.py:413
  56.7 1.6 %bank_rest.1 = f32[8,32,1024]{2,1,0:T(8,128)} custom-call(f32[4,32,1024]{2,1,0:T(8,128)S(1)} %bank_own.1.done, f32[4,16,8,128]{3,2,1,0:T(8,128)S(1)} %bitcast.28, f32[16,32,1024]{2,1,0:T(8,128)S(1)} %copy-done), custom_call_target="tpu_custom_call" | custom-call | tf_op jit(solution)/shard_map/bank_rest/pallas_call | solution.py:386
  (7 shorter events, 0.0 us)
Async XLA Ops:
  17.8 2.8 %collective-permute-start.1 = (f32[2048,128]{1,0:T(8,128)S(1)}, f32[2048,128]{1,0:T(8,128)S(1)}, u32[]{:S(2)}, u32[]{:S(2)}) collective-permute-start(f32[2048,128]{1,0:T(8,128)S(1)} %get-tuple-element.25), channel_id=1, source_target_pairs={{0,1},{1,0},{2,3},{3,2},{4,5},{5,4},{6,7},{7,6},{8,9},{9,8},{10,11... | collective-permute-start | bytes 3145736 | tf_op jit(solution)/shard_map/ppermute | solution.py:413
  18.3 9.5 %collective-permute-start = (f32[2048,128]{1,0:T(8,128)S(1)}, f32[2048,128]{1,0:T(8,128)S(1)}, u32[]{:S(2)}, u32[]{:S(2)}) collective-permute-start(f32[2048,128]{1,0:T(8,128)S(1)} %get-tuple-element.23), channel_id=1, source_target_pairs={{0,1},{1,0},{2,3},{3,2},{4,5},{5,4},{6,7},{7,6},{8,9},{9,8},{10,11... | collective-permute-start | bytes 3145736 | tf_op jit(solution)/shard_map/ppermute | solution.py:413
  20.7 18.9 %collective-permute-start.2 = (f32[1024,128]{1,0:T(8,128)S(1)}, f32[1024,128]{1,0:T(8,128)S(1)}, u32[]{:S(2)}, u32[]{:S(2)}) collective-permute-start(f32[1024,128]{1,0:T(8,128)S(1)} %get-tuple-element.26), channel_id=1, source_target_pairs={{0,2},{2,0},{4,6},{6,4},{8,10},{10,8},{12,14},{14,12},{1,3},{3,1},... | collective-permute-start | bytes 1572872 | tf_op jit(solution)/shard_map/ppermute | solution.py:416
  23.6 13.6 %collective-permute-start.3 = (f32[512,128]{1,0:T(8,128)S(1)}, f32[512,128]{1,0:T(8,128)S(1)}, u32[]{:S(2)}, u32[]{:S(2)}) collective-permute-start(f32[512,128]{1,0:T(8,128)S(1)} %get-tuple-element.27), channel_id=1, source_target_pairs={{0,4},{2,6},{4,0},{6,2},{8,12},{10,14},{12,8},{14,10},{1,5},{3,7},... | collective-permute-start | bytes 786440 | tf_op jit(solution)/shard_map/ppermute | solution.py:416
  25.2 14.3 %collective-permute-start.4 = (f32[512,128]{1,0:T(8,128)S(1)}, f32[512,128]{1,0:T(8,128)S(1)}, u32[]{:S(2)}, u32[]{:S(2)}) collective-permute-start(f32[512,128]{1,0:T(8,128)S(1)} %get-tuple-element.28), channel_id=1, source_target_pairs={{0,8},{2,10},{4,12},{6,14},{8,0},{10,2},{12,4},{14,6},{1,9},{3,11}... | collective-permute-start | bytes 786440 | tf_op jit(solution)/shard_map/ppermute | solution.py:416
  39.6 15.6 %copy-start = (f32[16,32,1024]{2,1,0:T(8,128)S(1)}, f32[16,32,1024]{2,1,0:T(8,128)}, u32[]{:S(2)}) copy-start(f32[16,32,1024]{2,1,0:T(8,128)} %bank.3) | copy-start | bytes 6291460
  39.7 8.5 %collective-permute-start.5 = (f32[512,128]{1,0:T(8,128)S(1)}, f32[512,128]{1,0:T(8,128)S(1)}, u32[]{:S(2)}, u32[]{:S(2)}) collective-permute-start(f32[512,128]{1,0:T(8,128)S(1)} %get-tuple-element.33), channel_id=1, source_target_pairs={{0,2},{2,0},{4,6},{6,4},{8,10},{10,8},{12,14},{14,12},{1,3},{3,1},... | collective-permute-start | bytes 786440 | tf_op jit(solution)/shard_map/ppermute | solution.py:416
  40.3 6.9 %collective-permute-start.6 = (f32[256,128]{1,0:T(8,128)S(1)}, f32[256,128]{1,0:T(8,128)S(1)}, u32[]{:S(2)}, u32[]{:S(2)}) collective-permute-start(f32[256,128]{1,0:T(8,128)S(1)} %get-tuple-element.34), channel_id=1, source_target_pairs={{0,4},{2,6},{4,0},{6,2},{8,12},{10,14},{12,8},{14,10},{1,5},{3,7},... | collective-permute-start | bytes 393224 | tf_op jit(solution)/shard_map/ppermute | solution.py:416
  40.8 7.5 %collective-permute-start.7 = (f32[256,128]{1,0:T(8,128)S(1)}, f32[256,128]{1,0:T(8,128)S(1)}, u32[]{:S(2)}, u32[]{:S(2)}) collective-permute-start(f32[256,128]{1,0:T(8,128)S(1)} %get-tuple-element.35), channel_id=1, source_target_pairs={{0,8},{2,10},{4,12},{6,14},{8,0},{10,2},{12,4},{14,6},{1,9},{3,11}... | collective-permute-start | bytes 393224 | tf_op jit(solution)/shard_map/ppermute | solution.py:416
  48.3 6.7 %collective-permute-start.8 = (f32[256,128]{1,0:T(8,128)S(1)}, f32[256,128]{1,0:T(8,128)S(1)}, u32[]{:S(2)}, u32[]{:S(2)}) collective-permute-start(f32[256,128]{1,0:T(8,128)S(1)} %get-tuple-element.37), channel_id=1, source_target_pairs={{0,4},{2,6},{4,0},{6,2},{8,12},{10,14},{12,8},{14,10},{1,5},{3,7},... | collective-permute-start | bytes 393224 | tf_op jit(solution)/shard_map/ppermute | solution.py:416
  48.4 6.6 %collective-permute-start.9 = (f32[256,128]{1,0:T(8,128)S(1)}, f32[256,128]{1,0:T(8,128)S(1)}, u32[]{:S(2)}, u32[]{:S(2)}) collective-permute-start(f32[256,128]{1,0:T(8,128)S(1)} %get-tuple-element.38), channel_id=1, source_target_pairs={{0,8},{2,10},{4,12},{6,14},{8,0},{10,2},{12,4},{14,6},{1,9},{3,11}... | collective-permute-start | bytes 393224 | tf_op jit(solution)/shard_map/ppermute | solution.py:416
  55.1 1.6 %collective-permute-start.10 = (f32[512,128]{1,0:T(8,128)S(1)}, f32[512,128]{1,0:T(8,128)S(1)}, u32[]{:S(2)}, u32[]{:S(2)}) collective-permute-start(f32[512,128]{1,0:T(8,128)S(1)} %last.1), channel_id=1, source_target_pairs={{0,1},{1,0},{2,3},{3,2},{4,5},{5,4},{6,7},{7,6},{8,9},{9,8},{10,11... | collective-permute-start | bytes 786440 | tf_op jit(solution)/shard_map/ppermute | solution.py:413

commit v18 on v17

--- a/solution.py
+++ b/solution.py
@@ -25,11 +25,12 @@
 def accumulate_kernel(
     bank_size, n_owner, n_acc,
     proj_hbm, img_hbm, tra_hbm, w_hbm, pose_hbm, blocks_hbm, tiles_hbm,
-    sent_away, kept_away, sent_stay, kept_stay, *rest,
+    sent_away, *rest,
 ):
+    accs, rest = rest[:n_acc], rest[n_acc:]
     proj, img, tra, weight, pose, blocks, tiles, idx_v, idx_s, square, cross = rest[:11]
-    parts, accs = rest[11 : 11 + N_BUF], rest[11 + N_BUF : 11 + N_BUF + n_acc]
-    proj_sem, small_sem, table_sem, idx_sem = rest[11 + N_BUF + n_acc :]
+    parts = rest[11 : 11 + N_BUF]
+    proj_sem, small_sem, table_sem, idx_sem = rest[11 + N_BUF :]
     n_pose, n_part = pose.shape
     n_tile, n_table = blocks.shape
     n_row = accs[0].shape[0]
@@ -112,45 +113,27 @@
 
     idx_copy.wait()
 
-    def spread(p):
-        return [jnp.full((SUB, LANES), weight[k, p], jnp.float32) for k in range(n_pose)]
-
-    proj_copy(0).wait()
-    stage(0, 0, parts[0])
-    stage(0, 1, parts[1])
-
-    @pl.loop(0, n_part, init_carry=tuple(terms(0, 0, staged(parts[0]), spread(0))))
-    def _(p, carry):
-        @pl.when(p + 1 < n_part)
-        def _():
-            proj_copy(p + 1).wait()
-
-        weights = spread(p)
-
-        @pl.loop(0, n_tile, step=UNROLL, init_carry=carry)
-        def done(j, values):
-            ends = j + UNROLL == n_tile
-            next_p = jnp.where(ends, jnp.minimum(p + 1, n_part - 1), p)
-            next_j = jnp.where(ends, 0, j + UNROLL)
-
+    @pl.loop(0, n_part)
+    def _(p):
+        proj_copy(p).wait()
+        weights = [jnp.full((SUB, LANES), weight[k, p], jnp.float32) for k in range(n_pose)]
+
+        stage(p, 0, parts[0])
+        stage(p, 1, parts[1])
+
+        @pl.loop(0, n_tile, step=UNROLL, init_carry=tuple(terms(p, 0, staged(parts[0]), weights)))
+        def _(j, values):
             def tile(u):
-                return (p, j + u) if u < UNROLL else (next_p, next_j + u - UNROLL)
+                return jnp.minimum(j + u, n_tile - 1) if u >= UNROLL else j + u
 
             for u in range(UNROLL):
-                stage(*tile(u + 2), parts[(u + 2) % N_BUF])
-                scale = weights if u + 1 < UNROLL else spread(next_p)
-                later = terms(*tile(u + 1), staged(parts[(u + 1) % N_BUF]), scale)
+                stage(p, tile(u + 2), parts[(u + 2) % N_BUF])
+                later = terms(p, tile(u + 1), staged(parts[(u + 1) % N_BUF]), weights)
                 add_rows(p, j + u, values)
                 values = later
             return tuple(values)
 
-        return done
-
-    sums = Sums(n_owner, accs)
-    sums.pieces_away(sent_away, sent=True)
-    sums.pieces_away(kept_away, sent=False)
-    sums.pieces_stay(sent_stay, sent=True)
-    sums.pieces_stay(kept_stay, sent=False)
+    Sums(n_owner, accs).pieces_away(sent_away, sent=True)
 
 
 class Sums:
@@ -162,24 +145,29 @@
     def pieces(self, out, begin, part, firsts, sent):
         rep, near, low, high = position()
         order = ORDERS[part]
-        inner = self.sizes[order[1]] * self.sizes[order[2]]
+        n_second, n_third = self.sizes[order[1]], self.sizes[order[2]]
         size = PART_ROWS[part] * SUB
         within = sum(PART_ROWS[:part]) * SUB
         half = 1 - rep if sent else rep
 
-        @pl.loop(0, len(firsts) * inner)
-        def _(i):
-            off = {order[0]: firsts[0] + i // inner}
-            off[order[1]] = i % inner // self.sizes[order[2]]
-            off[order[2]] = i % self.sizes[order[2]]
+        def piece(x, y, z):
+            off = {order[0]: firsts[0] + x, order[1]: y, order[2]: z}
             owner = ((high ^ off["h"]) * 2 + (low ^ off["l"])) * 2 + (near ^ off["y"])
             first = pl.multiple_of((owner * 2 + half) * self.half_rows + within, SUB)
             total = self.accs[0][pl.ds(first, size), :]
             for acc in self.accs[1:]:
                 total += acc[pl.ds(first, size), :]
-            out[pl.ds(pl.multiple_of(begin + i * size, SUB), size), :] = total
-
-        return begin + len(firsts) * inner * size
+            at = begin + ((x * n_second + y) * n_third + z) * size
+            out[pl.ds(pl.multiple_of(at, SUB), size), :] = total
+
+        @pl.loop(0, len(firsts))
+        def _(x):
+            @pl.loop(0, n_second)
+            def _(y):
+                for z in range(n_third):
+                    piece(x, y, z)
+
+        return begin + len(firsts) * n_second * n_third * size
 
     def pieces_away(self, out, sent):
         begin = 0
@@ -190,6 +178,14 @@
         begin = 0
         for part in range(len(ORDERS)):
             begin = self.pieces(out, begin, part, range(1), sent)
+
+
+def rest_kernel(n_owner, *refs):
+    accs, (kept_away, sent_stay, kept_stay) = refs[:-3], refs[-3:]
+    sums = Sums(n_owner, accs)
+    sums.pieces_away(kept_away, sent=False)
+    sums.pieces_stay(sent_stay, sent=True)
+    sums.pieces_stay(kept_stay, sent=False)
 
 
 def tiles_in_order(array):
@@ -218,16 +214,15 @@
     assert sum(PART_ROWS) == NB_DEV // 2 * bank_size
 
     away = 2 * n_high * (a + d + b) + 4 * (n_high - 1) * e
-    stays = 2 * n_high * (a + d + b) + 4 * e
 
     def out(rows):
         return jax.ShapeDtypeStruct((rows, LANES), jnp.float32)
 
-    return pl.pallas_call(
+    sent_away, *accs = pl.pallas_call(
         functools.partial(accumulate_kernel, bank_size, n_owner, n_acc),
-        out_shape=[out(away)] * 2 + [out(stays)] * 2,
+        out_shape=[out(away)] + [out(n_row)] * n_acc,
         in_specs=[hbm] * 7,
-        out_specs=[vmem] * 4,
+        out_specs=[vmem] * (1 + n_acc),
         scratch_shapes=[
             pltpu.VMEM(projections.shape, jnp.bfloat16),
             pltpu.VMEM(images.shape, jnp.bfloat16),
@@ -242,19 +237,20 @@
             pltpu.VMEM(transfer.shape, jnp.float32),
         ]
         + [pltpu.VMEM((n_pose * SUB, LANES), jnp.float32)] * N_BUF
-        + [pltpu.VMEM((n_row, LANES), jnp.float32)] * n_acc
         + [
             pltpu.SemaphoreType.DMA((n_part,)),
             pltpu.SemaphoreType.DMA((3,)),
             pltpu.SemaphoreType.DMA((3,)),
             pltpu.SemaphoreType.DMA,
         ],
-        compiler_params=pltpu.CompilerParams(vmem_limit_bytes=(40 if n_acc == 4 else 56) * MIB),
+        compiler_params=pltpu.CompilerParams(vmem_limit_bytes=24 * MIB),
         name="accumulate",
     )(
         stay(projections), stay(images), stay(transfer),
         stay(pose_weights.T), stay(pose_of.T), stay(pose_blocks.T), stay(pose_tiles.T),
     )
+    rows = 2 * n_high * (a + d + b) + 4 * e
+    return sent_away, *in_vmem(functools.partial(rest_kernel, n_owner), "rest", [away, rows, rows], *accs)
 
 
 def in_vmem(kernel, name, rows, *operands):

time: 58.4 us -> 57.3 us (0.981)
  waiting for transfers between devices: 24.5 us -> 23.7 us
    pallas_call x1, Pallas kernels: 17.8 us -> 16.7 us  [accumulate(): pl.pallas_call(functools.partial(accumulate_kernel, bank_size, n_owner, n...]
    ppermute x3, waiting for transfers between devices: 2.9 us -> 2.14 us  [over_rep(): return lax.ppermute(array, 'rep', [(0, 1), (1, 0)])]
    pallas_call x4 -> x5, Pallas kernels: 0.34 us -> 1.06 us  [in_vmem(): pl.pallas_call(kernel, out_shape=[jax.ShapeDtypeStruct((n, LANES), jnp.fl...]
  transfers between devices with their start and end apart: 11 -> 11, of which waited for: 7 -> 7; matrix products, arithmetic and copies ran while one was open for 0% -> 0% of each run, Pallas kernels for 2% -> 3%
where the time goes in v18:
time: 57.3 us; the launch traced here: 57.2 us
  waiting for transfers between devices  23.7 us (41%)
  Pallas kernels  20.2 us (35%)
  starting transfers between devices  13.2 us (23%)
    ppermute x8, waiting for transfers between devices, over_blk(): return lax.ppermute(array, 'blk', [(i, i ^ bits) for i in range(n_blk)])  21.6 us
    pallas_call x1, Pallas kernels, accumulate(): pl.pallas_call(functools.partial(accumulate_kernel, bank_size, n_owner, n...  16.7 us
    ppermute x8, starting transfers between devices, over_blk(): return lax.ppermute(array, 'blk', [(i, i ^ bits) for i in range(n_blk)])  12.5 us
    ppermute x3, waiting for transfers between devices, over_rep(): return lax.ppermute(array, 'rep', [(0, 1), (1, 0)])  2.14 us
    pallas_call x1, Pallas kernels, apply_bank(): pl.pallas_call(bank_rest_kernel, out_shape=jax.ShapeDtypeStruct((NB_DEV,...  1.62 us
  transfers between devices with their start and end apart: 11, of which 7 were waited for; matrix products, arithmetic and copies ran while one was open for 0% of the time, Pallas kernels for 3%

profile of v18, /device:TPU:0, one launch (start us, length us, event | category | flops | bytes accessed | tf_op | source)
XLA Modules:
  0.0 57.2 jit_solution(625894485582933385)
XLA Ops:
  0.0 16.7 %accumulate.1 = (f32[2048,128]{1,0:T(8,128)S(1)}, f32[8192,128]{1,0:T(8,128)S(1)}, f32[8192,128]{1,0:T(8,128)S(1)}, f32[8192,128]{1,0:T(8,128)S(1)}, f32[8192,128]{1,0:T(8,128)S(1)}) custom-call(bf16[36864,128]{1,0:T(8,128)(2,1)} %bitcast.29, bf16[4608,128]{1,0:T(8,128)(2,1)} %bitcast.30, bf16[4608,128]{1,0:T(8,128)(2,1)} %bitcast.31, f32[8,16]{1,0:T(8,128)} %bitcast.34, ...), custom_call_target="tpu_custom_call" | custom-call | tf_op jit(solution)/shard_map/accumulate/pallas_call | solution.py:221
  16.7 0.6 collective-permute-start.1
  17.2 0.7 %rest.1 = (f32[2048,128]{1,0:T(8,128)S(1)}, f32[2048,128]{1,0:T(8,128)S(1)}, f32[2048,128]{1,0:T(8,128)S(1)}) custom-call(f32[8192,128]{1,0:T(8,128)S(1)} %get-tuple-element.26.refs_0_, f32[8192,128]{1,0:T(8,128)S(1)} %get-tuple-element.27.refs_1_, f32[8192,128]{1,0:T(8,128)S(1)} %get-tuple-element.28.refs_2_, f32[8192,128]{1,0:T(8,128)S(1)} %get-tuple-element.29.refs_3_), custom_call_target="tpu_custom_call" | custom-call | tf_op jit(solution)/shard_map/rest/pallas_call | solution.py:258
  18.0 0.1 collective-permute-start
  18.1 1.4 %collective-permute-done.1.got = f32[2048,128]{1,0:T(8,128)S(1)} collective-permute-done((f32[2048,128]{1,0:T(8,128)S(1)}, f32[2048,128]{1,0:T(8,128)S(1)}, u32[]{:S(2)}, u32[]{:S(2)}) %collective-permute-start.1) | collective-permute-done | bytes 1048608 | tf_op jit(solution)/shard_map/ppermute | solution.py:409
  19.5 0.1 first.1
  19.6 2.9 %collective-permute-start.2 = (f32[1024,128]{1,0:T(8,128)S(1)}, f32[1024,128]{1,0:T(8,128)S(1)}, u32[]{:S(2)}, u32[]{:S(2)}) collective-permute-start(f32[1024,128]{1,0:T(8,128)S(1)} %get-tuple-element.34), channel_id=1, source_target_pairs={{0,2},{2,0},{4,6},{6,4},{8,10},{10,8},{12,14},{14,12},{1,3},{3,1},... | collective-permute-start | bytes 1572872 | tf_op jit(solution)/shard_map/ppermute | solution.py:412
  22.5 1.6 %collective-permute-start.3 = (f32[512,128]{1,0:T(8,128)S(1)}, f32[512,128]{1,0:T(8,128)S(1)}, u32[]{:S(2)}, u32[]{:S(2)}) collective-permute-start(f32[512,128]{1,0:T(8,128)S(1)} %get-tuple-element.35), channel_id=1, source_target_pairs={{0,4},{2,6},{4,0},{6,2},{8,12},{10,14},{12,8},{14,10},{1,5},{3,7},... | collective-permute-start | bytes 786440 | tf_op jit(solution)/shard_map/ppermute | solution.py:412
  24.1 2.6 %collective-permute-start.4 = (f32[512,128]{1,0:T(8,128)S(1)}, f32[512,128]{1,0:T(8,128)S(1)}, u32[]{:S(2)}, u32[]{:S(2)}) collective-permute-start(f32[512,128]{1,0:T(8,128)S(1)} %get-tuple-element.36), channel_id=1, source_target_pairs={{0,8},{2,10},{4,12},{6,14},{8,0},{10,2},{12,4},{14,6},{1,9},{3,11}... | collective-permute-start | bytes 786440 | tf_op jit(solution)/shard_map/ppermute | solution.py:412
  26.7 9.4 %collective-permute-done.3.got_l = f32[512,128]{1,0:T(8,128)S(1)} collective-permute-done((f32[512,128]{1,0:T(8,128)S(1)}, f32[512,128]{1,0:T(8,128)S(1)}, u32[]{:S(2)}, u32[]{:S(2)}) %collective-permute-start.3) | collective-permute-done | bytes 262176 | tf_op jit(solution)/shard_map/ppermute | solution.py:412
  36.1 2.3 %collective-permute-done.4.rest_0_ = f32[512,128]{1,0:T(8,128)S(1)} collective-permute-done((f32[512,128]{1,0:T(8,128)S(1)}, f32[512,128]{1,0:T(8,128)S(1)}, u32[]{:S(2)}, u32[]{:S(2)}) %collective-permute-start.4) | collective-permute-done | bytes 262176 | tf_op jit(solution)/shard_map/ppermute | solution.py:412
  38.5 0.2 second.1
  38.6 0.6 collective-permute-start.5
  39.2 0.5 collective-permute-start.6
  39.7 2.6 %collective-permute-start.7 = (f32[256,128]{1,0:T(8,128)S(1)}, f32[256,128]{1,0:T(8,128)S(1)}, u32[]{:S(2)}, u32[]{:S(2)}) collective-permute-start(f32[256,128]{1,0:T(8,128)S(1)} %get-tuple-element.43), channel_id=1, source_target_pairs={{0,8},{2,10},{4,12},{6,14},{8,0},{10,2},{12,4},{14,6},{1,9},{3,11}... | collective-permute-start | bytes 393224 | tf_op jit(solution)/shard_map/ppermute | solution.py:412
  42.2 3.8 %collective-permute-done.6.got_l = f32[256,128]{1,0:T(8,128)S(1)} collective-permute-done((f32[256,128]{1,0:T(8,128)S(1)}, f32[256,128]{1,0:T(8,128)S(1)}, u32[]{:S(2)}, u32[]{:S(2)}) %collective-permute-start.6) | collective-permute-done | bytes 131104 | tf_op jit(solution)/shard_map/ppermute | solution.py:412
  46.0 1.1 %collective-permute-done.7.rest_0_ = f32[256,128]{1,0:T(8,128)S(1)} collective-permute-done((f32[256,128]{1,0:T(8,128)S(1)}, f32[256,128]{1,0:T(8,128)S(1)}, u32[]{:S(2)}, u32[]{:S(2)}) %collective-permute-start.7) | collective-permute-done | bytes 131104 | tf_op jit(solution)/shard_map/ppermute | solution.py:412
  47.2 0.1 collective-permute-start.8
  47.3 1.7 %collective-permute-start.9 = (f32[256,128]{1,0:T(8,128)S(1)}, f32[256,128]{1,0:T(8,128)S(1)}, u32[]{:S(2)}, u32[]{:S(2)}) collective-permute-start(f32[256,128]{1,0:T(8,128)S(1)} %get-tuple-element.46), channel_id=1, source_target_pairs={{0,8},{2,10},{4,12},{6,14},{8,0},{10,2},{12,4},{14,6},{1,9},{3,11}... | collective-permute-start | bytes 393224 | tf_op jit(solution)/shard_map/ppermute | solution.py:412
  49.0 4.9 %collective-permute-done.8.got_l = f32[256,128]{1,0:T(8,128)S(1)} collective-permute-done((f32[256,128]{1,0:T(8,128)S(1)}, f32[256,128]{1,0:T(8,128)S(1)}, u32[]{:S(2)}, u32[]{:S(2)}) %collective-permute-start.8) | collective-permute-done | bytes 131104 | tf_op jit(solution)/shard_map/ppermute | solution.py:412
  54.0 0.1 collective-permute-start.10
  54.1 0.8 %bank_own.1.done = f32[4,32,1024]{2,1,0:T(8,128)S(1)} custom-call(f32[4,16,8,128]{3,2,1,0:T(8,128)S(1)} %bitcast.27, f32[16,32,1024]{2,1,0:T(8,128)S(1)} %copy-done), custom_call_target="tpu_custom_call" | custom-call | tf_op jit(solution)/shard_map/bank_own/pallas_call | solution.py:374
  54.9 0.7 %collective-permute-done.10 = f32[512,128]{1,0:T(8,128)S(1)} collective-permute-done((f32[512,128]{1,0:T(8,128)S(1)}, f32[512,128]{1,0:T(8,128)S(1)}, u32[]{:S(2)}, u32[]{:S(2)}) %collective-permute-start.10) | collective-permute-done | bytes 262176 | tf_op jit(solution)/shard_map/ppermute | solution.py:409
  55.6 1.6 %bank_rest.1 = f32[8,32,1024]{2,1,0:T(8,128)} custom-call(f32[4,32,1024]{2,1,0:T(8,128)S(1)} %bank_own.1.done, f32[4,16,8,128]{3,2,1,0:T(8,128)S(1)} %bitcast.28, f32[16,32,1024]{2,1,0:T(8,128)S(1)} %copy-done), custom_call_target="tpu_custom_call" | custom-call | tf_op jit(solution)/shard_map/bank_rest/pallas_call | solution.py:382
  (8 shorter events, 0.1 us)
Async XLA Ops:
  16.7 2.8 %collective-permute-start.1 = (f32[2048,128]{1,0:T(8,128)S(1)}, f32[2048,128]{1,0:T(8,128)S(1)}, u32[]{:S(2)}, u32[]{:S(2)}) collective-permute-start(f32[2048,128]{1,0:T(8,128)S(1)} %get-tuple-element.33), channel_id=1, source_target_pairs={{0,1},{1,0},{2,3},{3,2},{4,5},{5,4},{6,7},{7,6},{8,9},{9,8},{10,11... | collective-permute-start | bytes 3145736 | tf_op jit(solution)/shard_map/ppermute | solution.py:409
  18.0 36.1 %copy-start = (f32[16,32,1024]{2,1,0:T(8,128)S(1)}, f32[16,32,1024]{2,1,0:T(8,128)}, u32[]{:S(2)}) copy-start(f32[16,32,1024]{2,1,0:T(8,128)} %bank.3) | copy-start | bytes 6291460
  18.0 8.7 %collective-permute-start = (f32[2048,128]{1,0:T(8,128)S(1)}, f32[2048,128]{1,0:T(8,128)S(1)}, u32[]{:S(2)}, u32[]{:S(2)}) collective-permute-start(f32[2048,128]{1,0:T(8,128)S(1)} %get-tuple-element.31), channel_id=1, source_target_pairs={{0,1},{1,0},{2,3},{3,2},{4,5},{5,4},{6,7},{7,6},{8,9},{9,8},{10,11... | collective-permute-start | bytes 3145736 | tf_op jit(solution)/shard_map/ppermute | solution.py:409
  19.6 18.8 %collective-permute-start.2 = (f32[1024,128]{1,0:T(8,128)S(1)}, f32[1024,128]{1,0:T(8,128)S(1)}, u32[]{:S(2)}, u32[]{:S(2)}) collective-permute-start(f32[1024,128]{1,0:T(8,128)S(1)} %get-tuple-element.34), channel_id=1, source_target_pairs={{0,2},{2,0},{4,6},{6,4},{8,10},{10,8},{12,14},{14,12},{1,3},{3,1},... | collective-permute-start | bytes 1572872 | tf_op jit(solution)/shard_map/ppermute | solution.py:412
  22.5 13.6 %collective-permute-start.3 = (f32[512,128]{1,0:T(8,128)S(1)}, f32[512,128]{1,0:T(8,128)S(1)}, u32[]{:S(2)}, u32[]{:S(2)}) collective-permute-start(f32[512,128]{1,0:T(8,128)S(1)} %get-tuple-element.35), channel_id=1, source_target_pairs={{0,4},{2,6},{4,0},{6,2},{8,12},{10,14},{12,8},{14,10},{1,5},{3,7},... | collective-permute-start | bytes 786440 | tf_op jit(solution)/shard_map/ppermute | solution.py:412
  24.1 14.3 %collective-permute-start.4 = (f32[512,128]{1,0:T(8,128)S(1)}, f32[512,128]{1,0:T(8,128)S(1)}, u32[]{:S(2)}, u32[]{:S(2)}) collective-permute-start(f32[512,128]{1,0:T(8,128)S(1)} %get-tuple-element.36), channel_id=1, source_target_pairs={{0,8},{2,10},{4,12},{6,14},{8,0},{10,2},{12,4},{14,6},{1,9},{3,11}... | collective-permute-start | bytes 786440 | tf_op jit(solution)/shard_map/ppermute | solution.py:412
  38.6 8.5 %collective-permute-start.5 = (f32[512,128]{1,0:T(8,128)S(1)}, f32[512,128]{1,0:T(8,128)S(1)}, u32[]{:S(2)}, u32[]{:S(2)}) collective-permute-start(f32[512,128]{1,0:T(8,128)S(1)} %get-tuple-element.41), channel_id=1, source_target_pairs={{0,2},{2,0},{4,6},{6,4},{8,10},{10,8},{12,14},{14,12},{1,3},{3,1},... | collective-permute-start | bytes 786440 | tf_op jit(solution)/shard_map/ppermute | solution.py:412
  39.2 6.8 %collective-permute-start.6 = (f32[256,128]{1,0:T(8,128)S(1)}, f32[256,128]{1,0:T(8,128)S(1)}, u32[]{:S(2)}, u32[]{:S(2)}) collective-permute-start(f32[256,128]{1,0:T(8,128)S(1)} %get-tuple-element.42), channel_id=1, source_target_pairs={{0,4},{2,6},{4,0},{6,2},{8,12},{10,14},{12,8},{14,10},{1,5},{3,7},... | collective-permute-start | bytes 393224 | tf_op jit(solution)/shard_map/ppermute | solution.py:412
  39.7 7.5 %collective-permute-start.7 = (f32[256,128]{1,0:T(8,128)S(1)}, f32[256,128]{1,0:T(8,128)S(1)}, u32[]{:S(2)}, u32[]{:S(2)}) collective-permute-start(f32[256,128]{1,0:T(8,128)S(1)} %get-tuple-element.43), channel_id=1, source_target_pairs={{0,8},{2,10},{4,12},{6,14},{8,0},{10,2},{12,4},{14,6},{1,9},{3,11}... | collective-permute-start | bytes 393224 | tf_op jit(solution)/shard_map/ppermute | solution.py:412
  47.2 6.7 %collective-permute-start.8 = (f32[256,128]{1,0:T(8,128)S(1)}, f32[256,128]{1,0:T(8,128)S(1)}, u32[]{:S(2)}, u32[]{:S(2)}) collective-permute-start(f32[256,128]{1,0:T(8,128)S(1)} %get-tuple-element.45), channel_id=1, source_target_pairs={{0,4},{2,6},{4,0},{6,2},{8,12},{10,14},{12,8},{14,10},{1,5},{3,7},... | collective-permute-start | bytes 393224 | tf_op jit(solution)/shard_map/ppermute | solution.py:412
  47.3 6.6 %collective-permute-start.9 = (f32[256,128]{1,0:T(8,128)S(1)}, f32[256,128]{1,0:T(8,128)S(1)}, u32[]{:S(2)}, u32[]{:S(2)}) collective-permute-start(f32[256,128]{1,0:T(8,128)S(1)} %get-tuple-element.46), channel_id=1, source_target_pairs={{0,8},{2,10},{4,12},{6,14},{8,0},{10,2},{12,4},{14,6},{1,9},{3,11}... | collective-permute-start | bytes 393224 | tf_op jit(solution)/shard_map/ppermute | solution.py:412
  54.0 1.6 %collective-permute-start.10 = (f32[512,128]{1,0:T(8,128)S(1)}, f32[512,128]{1,0:T(8,128)S(1)}, u32[]{:S(2)}, u32[]{:S(2)}) collective-permute-start(f32[512,128]{1,0:T(8,128)S(1)} %last.1), channel_id=1, source_target_pairs={{0,1},{1,0},{2,3},{3,2},{4,5},{5,4},{6,7},{7,6},{8,9},{9,8},{10,11... | collective-permute-start | bytes 786440 | tf_op jit(solution)/shard_map/ppermute | solution.py:409

commit v19 on v18

--- a/solution.py
+++ b/solution.py
@@ -113,25 +113,39 @@
 
     idx_copy.wait()
 
-    @pl.loop(0, n_part)
-    def _(p):
-        proj_copy(p).wait()
-        weights = [jnp.full((SUB, LANES), weight[k, p], jnp.float32) for k in range(n_pose)]
-
-        stage(p, 0, parts[0])
-        stage(p, 1, parts[1])
-
-        @pl.loop(0, n_tile, step=UNROLL, init_carry=tuple(terms(p, 0, staged(parts[0]), weights)))
-        def _(j, values):
+    def spread(p):
+        return [jnp.full((SUB, LANES), weight[k, p], jnp.float32) for k in range(n_pose)]
+
+    proj_copy(0).wait()
+    stage(0, 0, parts[0])
+    stage(0, 1, parts[1])
+
+    @pl.loop(0, n_part, init_carry=tuple(terms(0, 0, staged(parts[0]), spread(0))))
+    def _(p, carry):
+        @pl.when(p + 1 < n_part)
+        def _():
+            proj_copy(p + 1).wait()
+
+        weights = spread(p)
+
+        @pl.loop(0, n_tile, step=UNROLL, init_carry=carry)
+        def done(j, values):
+            ends = j + UNROLL == n_tile
+            next_p = jnp.where(ends, jnp.minimum(p + 1, n_part - 1), p)
+            next_j = jnp.where(ends, 0, j + UNROLL)
+
             def tile(u):
-                return jnp.minimum(j + u, n_tile - 1) if u >= UNROLL else j + u
+                return (p, j + u) if u < UNROLL else (next_p, next_j + u - UNROLL)
 
             for u in range(UNROLL):
-                stage(p, tile(u + 2), parts[(u + 2) % N_BUF])
-                later = terms(p, tile(u + 1), staged(parts[(u + 1) % N_BUF]), weights)
+                stage(*tile(u + 2), parts[(u + 2) % N_BUF])
+                scale = weights if u + 1 < UNROLL else spread(next_p)
+                later = terms(*tile(u + 1), staged(parts[(u + 1) % N_BUF]), scale)
                 add_rows(p, j + u, values)
                 values = later
             return tuple(values)
+
+        return done
 
     Sums(n_owner, accs).pieces_away(sent_away, sent=True)
 

time: 57.3 us -> 57.8 us (level)
  no operation moved by 1% of the time
where the time goes in v19:
time: 57.8 us; the launch traced here: 57.6 us
  waiting for transfers between devices  23.7 us (41%)
  Pallas kernels  20.6 us (36%)
  starting transfers between devices  13.2 us (23%)
    ppermute x8, waiting for transfers between devices, over_blk(): return lax.ppermute(array, 'blk', [(i, i ^ bits) for i in range(n_blk)])  21.6 us
    pallas_call x1, Pallas kernels, accumulate(): pl.pallas_call(functools.partial(accumulate_kernel, bank_size, n_owner, n...  17.1 us
    ppermute x8, starting transfers between devices, over_blk(): return lax.ppermute(array, 'blk', [(i, i ^ bits) for i in range(n_blk)])  12.5 us
    ppermute x3, waiting for transfers between devices, over_rep(): return lax.ppermute(array, 'rep', [(0, 1), (1, 0)])  2.12 us
    pallas_call x1, Pallas kernels, apply_bank(): pl.pallas_call(bank_rest_kernel, out_shape=jax.ShapeDtypeStruct((NB_DEV,...  1.62 us
  transfers between devices with their start and end apart: 11, of which 7 were waited for; matrix products, arithmetic and copies ran while one was open for 0% of the time, Pallas kernels for 3%

profile of v19, /device:TPU:0, one launch (start us, length us, event | category | flops | bytes accessed | tf_op | source)
XLA Modules:
  0.0 57.6 jit_solution(5427345767971202097)
XLA Ops:
  0.0 17.1 %accumulate.1 = (f32[2048,128]{1,0:T(8,128)S(1)}, f32[8192,128]{1,0:T(8,128)S(1)}, f32[8192,128]{1,0:T(8,128)S(1)}, f32[8192,128]{1,0:T(8,128)S(1)}, f32[8192,128]{1,0:T(8,128)S(1)}) custom-call(bf16[36864,128]{1,0:T(8,128)(2,1)} %bitcast.29, bf16[4608,128]{1,0:T(8,128)(2,1)} %bitcast.30, bf16[4608,128]{1,0:T(8,128)(2,1)} %bitcast.31, f32[8,16]{1,0:T(8,128)} %bitcast.34, ...), custom_call_target="tpu_custom_call" | custom-call | tf_op jit(solution)/shard_map/accumulate/pallas_call | solution.py:235
  17.1 0.5 collective-permute-start.1
  17.6 0.7 %rest.1 = (f32[2048,128]{1,0:T(8,128)S(1)}, f32[2048,128]{1,0:T(8,128)S(1)}, f32[2048,128]{1,0:T(8,128)S(1)}) custom-call(f32[8192,128]{1,0:T(8,128)S(1)} %get-tuple-element.26.refs_0_, f32[8192,128]{1,0:T(8,128)S(1)} %get-tuple-element.27.refs_1_, f32[8192,128]{1,0:T(8,128)S(1)} %get-tuple-element.28.refs_2_, f32[8192,128]{1,0:T(8,128)S(1)} %get-tuple-element.29.refs_3_), custom_call_target="tpu_custom_call" | custom-call | tf_op jit(solution)/shard_map/rest/pallas_call | solution.py:272
  18.4 0.1 collective-permute-start
  18.5 1.4 %collective-permute-done.1.got = f32[2048,128]{1,0:T(8,128)S(1)} collective-permute-done((f32[2048,128]{1,0:T(8,128)S(1)}, f32[2048,128]{1,0:T(8,128)S(1)}, u32[]{:S(2)}, u32[]{:S(2)}) %collective-permute-start.1) | collective-permute-done | bytes 1048608 | tf_op jit(solution)/shard_map/ppermute | solution.py:423
  19.9 0.1 first.1
  20.0 3.0 %collective-permute-start.2 = (f32[1024,128]{1,0:T(8,128)S(1)}, f32[1024,128]{1,0:T(8,128)S(1)}, u32[]{:S(2)}, u32[]{:S(2)}) collective-permute-start(f32[1024,128]{1,0:T(8,128)S(1)} %get-tuple-element.34), channel_id=1, source_target_pairs={{0,2},{2,0},{4,6},{6,4},{8,10},{10,8},{12,14},{14,12},{1,3},{3,1},... | collective-permute-start | bytes 1572872 | tf_op jit(solution)/shard_map/ppermute | solution.py:426
  23.0 1.6 %collective-permute-start.3 = (f32[512,128]{1,0:T(8,128)S(1)}, f32[512,128]{1,0:T(8,128)S(1)}, u32[]{:S(2)}, u32[]{:S(2)}) collective-permute-start(f32[512,128]{1,0:T(8,128)S(1)} %get-tuple-element.35), channel_id=1, source_target_pairs={{0,4},{2,6},{4,0},{6,2},{8,12},{10,14},{12,8},{14,10},{1,5},{3,7},... | collective-permute-start | bytes 786440 | tf_op jit(solution)/shard_map/ppermute | solution.py:426
  24.6 2.6 %collective-permute-start.4 = (f32[512,128]{1,0:T(8,128)S(1)}, f32[512,128]{1,0:T(8,128)S(1)}, u32[]{:S(2)}, u32[]{:S(2)}) collective-permute-start(f32[512,128]{1,0:T(8,128)S(1)} %get-tuple-element.36), channel_id=1, source_target_pairs={{0,8},{2,10},{4,12},{6,14},{8,0},{10,2},{12,4},{14,6},{1,9},{3,11}... | collective-permute-start | bytes 786440 | tf_op jit(solution)/shard_map/ppermute | solution.py:426
  27.2 9.4 %collective-permute-done.3.got_l = f32[512,128]{1,0:T(8,128)S(1)} collective-permute-done((f32[512,128]{1,0:T(8,128)S(1)}, f32[512,128]{1,0:T(8,128)S(1)}, u32[]{:S(2)}, u32[]{:S(2)}) %collective-permute-start.3) | collective-permute-done | bytes 262176 | tf_op jit(solution)/shard_map/ppermute | solution.py:426
  36.6 2.3 %collective-permute-done.4.rest_0_ = f32[512,128]{1,0:T(8,128)S(1)} collective-permute-done((f32[512,128]{1,0:T(8,128)S(1)}, f32[512,128]{1,0:T(8,128)S(1)}, u32[]{:S(2)}, u32[]{:S(2)}) %collective-permute-start.4) | collective-permute-done | bytes 262176 | tf_op jit(solution)/shard_map/ppermute | solution.py:426
  38.9 0.2 second.1
  39.1 0.6 collective-permute-start.5
  39.7 0.5 collective-permute-start.6
  40.1 2.6 %collective-permute-start.7 = (f32[256,128]{1,0:T(8,128)S(1)}, f32[256,128]{1,0:T(8,128)S(1)}, u32[]{:S(2)}, u32[]{:S(2)}) collective-permute-start(f32[256,128]{1,0:T(8,128)S(1)} %get-tuple-element.43), channel_id=1, source_target_pairs={{0,8},{2,10},{4,12},{6,14},{8,0},{10,2},{12,4},{14,6},{1,9},{3,11}... | collective-permute-start | bytes 393224 | tf_op jit(solution)/shard_map/ppermute | solution.py:426
  42.7 3.8 %collective-permute-done.6.got_l = f32[256,128]{1,0:T(8,128)S(1)} collective-permute-done((f32[256,128]{1,0:T(8,128)S(1)}, f32[256,128]{1,0:T(8,128)S(1)}, u32[]{:S(2)}, u32[]{:S(2)}) %collective-permute-start.6) | collective-permute-done | bytes 131104 | tf_op jit(solution)/shard_map/ppermute | solution.py:426
  46.5 1.1 %collective-permute-done.7.rest_0_ = f32[256,128]{1,0:T(8,128)S(1)} collective-permute-done((f32[256,128]{1,0:T(8,128)S(1)}, f32[256,128]{1,0:T(8,128)S(1)}, u32[]{:S(2)}, u32[]{:S(2)}) %collective-permute-start.7) | collective-permute-done | bytes 131104 | tf_op jit(solution)/shard_map/ppermute | solution.py:426
  47.7 0.1 collective-permute-start.8
  47.8 1.7 %collective-permute-start.9 = (f32[256,128]{1,0:T(8,128)S(1)}, f32[256,128]{1,0:T(8,128)S(1)}, u32[]{:S(2)}, u32[]{:S(2)}) collective-permute-start(f32[256,128]{1,0:T(8,128)S(1)} %get-tuple-element.46), channel_id=1, source_target_pairs={{0,8},{2,10},{4,12},{6,14},{8,0},{10,2},{12,4},{14,6},{1,9},{3,11}... | collective-permute-start | bytes 393224 | tf_op jit(solution)/shard_map/ppermute | solution.py:426
  49.5 4.9 %collective-permute-done.8.got_l = f32[256,128]{1,0:T(8,128)S(1)} collective-permute-done((f32[256,128]{1,0:T(8,128)S(1)}, f32[256,128]{1,0:T(8,128)S(1)}, u32[]{:S(2)}, u32[]{:S(2)}) %collective-permute-start.8) | collective-permute-done | bytes 131104 | tf_op jit(solution)/shard_map/ppermute | solution.py:426
  54.4 0.1 collective-permute-start.10
  54.5 0.8 %bank_own.1.done = f32[4,32,1024]{2,1,0:T(8,128)S(1)} custom-call(f32[4,16,8,128]{3,2,1,0:T(8,128)S(1)} %bitcast.27, f32[16,32,1024]{2,1,0:T(8,128)S(1)} %copy-done), custom_call_target="tpu_custom_call" | custom-call | tf_op jit(solution)/shard_map/bank_own/pallas_call | solution.py:388
  55.3 0.7 %collective-permute-done.10 = f32[512,128]{1,0:T(8,128)S(1)} collective-permute-done((f32[512,128]{1,0:T(8,128)S(1)}, f32[512,128]{1,0:T(8,128)S(1)}, u32[]{:S(2)}, u32[]{:S(2)}) %collective-permute-start.10) | collective-permute-done | bytes 262176 | tf_op jit(solution)/shard_map/ppermute | solution.py:423
  56.0 1.6 %bank_rest.1 = f32[8,32,1024]{2,1,0:T(8,128)} custom-call(f32[4,32,1024]{2,1,0:T(8,128)S(1)} %bank_own.1.done, f32[4,16,8,128]{3,2,1,0:T(8,128)S(1)} %bitcast.28, f32[16,32,1024]{2,1,0:T(8,128)S(1)} %copy-done), custom_call_target="tpu_custom_call" | custom-call | tf_op jit(solution)/shard_map/bank_rest/pallas_call | solution.py:396
  (8 shorter events, 0.1 us)
Async XLA Ops:
  17.1 2.8 %collective-permute-start.1 = (f32[2048,128]{1,0:T(8,128)S(1)}, f32[2048,128]{1,0:T(8,128)S(1)}, u32[]{:S(2)}, u32[]{:S(2)}) collective-permute-start(f32[2048,128]{1,0:T(8,128)S(1)} %get-tuple-element.33), channel_id=1, source_target_pairs={{0,1},{1,0},{2,3},{3,2},{4,5},{5,4},{6,7},{7,6},{8,9},{9,8},{10,11... | collective-permute-start | bytes 3145736 | tf_op jit(solution)/shard_map/ppermute | solution.py:423
  18.4 36.1 %copy-start = (f32[16,32,1024]{2,1,0:T(8,128)S(1)}, f32[16,32,1024]{2,1,0:T(8,128)}, u32[]{:S(2)}) copy-start(f32[16,32,1024]{2,1,0:T(8,128)} %bank.3) | copy-start | bytes 6291460
  18.4 8.8 %collective-permute-start = (f32[2048,128]{1,0:T(8,128)S(1)}, f32[2048,128]{1,0:T(8,128)S(1)}, u32[]{:S(2)}, u32[]{:S(2)}) collective-permute-start(f32[2048,128]{1,0:T(8,128)S(1)} %get-tuple-element.31), channel_id=1, source_target_pairs={{0,1},{1,0},{2,3},{3,2},{4,5},{5,4},{6,7},{7,6},{8,9},{9,8},{10,11... | collective-permute-start | bytes 3145736 | tf_op jit(solution)/shard_map/ppermute | solution.py:423
  20.0 18.9 %collective-permute-start.2 = (f32[1024,128]{1,0:T(8,128)S(1)}, f32[1024,128]{1,0:T(8,128)S(1)}, u32[]{:S(2)}, u32[]{:S(2)}) collective-permute-start(f32[1024,128]{1,0:T(8,128)S(1)} %get-tuple-element.34), channel_id=1, source_target_pairs={{0,2},{2,0},{4,6},{6,4},{8,10},{10,8},{12,14},{14,12},{1,3},{3,1},... | collective-permute-start | bytes 1572872 | tf_op jit(solution)/shard_map/ppermute | solution.py:426
  23.0 13.6 %collective-permute-start.3 = (f32[512,128]{1,0:T(8,128)S(1)}, f32[512,128]{1,0:T(8,128)S(1)}, u32[]{:S(2)}, u32[]{:S(2)}) collective-permute-start(f32[512,128]{1,0:T(8,128)S(1)} %get-tuple-element.35), channel_id=1, source_target_pairs={{0,4},{2,6},{4,0},{6,2},{8,12},{10,14},{12,8},{14,10},{1,5},{3,7},... | collective-permute-start | bytes 786440 | tf_op jit(solution)/shard_map/ppermute | solution.py:426
  24.6 14.4 %collective-permute-start.4 = (f32[512,128]{1,0:T(8,128)S(1)}, f32[512,128]{1,0:T(8,128)S(1)}, u32[]{:S(2)}, u32[]{:S(2)}) collective-permute-start(f32[512,128]{1,0:T(8,128)S(1)} %get-tuple-element.36), channel_id=1, source_target_pairs={{0,8},{2,10},{4,12},{6,14},{8,0},{10,2},{12,4},{14,6},{1,9},{3,11}... | collective-permute-start | bytes 786440 | tf_op jit(solution)/shard_map/ppermute | solution.py:426
  39.1 8.6 %collective-permute-start.5 = (f32[512,128]{1,0:T(8,128)S(1)}, f32[512,128]{1,0:T(8,128)S(1)}, u32[]{:S(2)}, u32[]{:S(2)}) collective-permute-start(f32[512,128]{1,0:T(8,128)S(1)} %get-tuple-element.41), channel_id=1, source_target_pairs={{0,2},{2,0},{4,6},{6,4},{8,10},{10,8},{12,14},{14,12},{1,3},{3,1},... | collective-permute-start | bytes 786440 | tf_op jit(solution)/shard_map/ppermute | solution.py:426
  39.7 6.8 %collective-permute-start.6 = (f32[256,128]{1,0:T(8,128)S(1)}, f32[256,128]{1,0:T(8,128)S(1)}, u32[]{:S(2)}, u32[]{:S(2)}) collective-permute-start(f32[256,128]{1,0:T(8,128)S(1)} %get-tuple-element.42), channel_id=1, source_target_pairs={{0,4},{2,6},{4,0},{6,2},{8,12},{10,14},{12,8},{14,10},{1,5},{3,7},... | collective-permute-start | bytes 393224 | tf_op jit(solution)/shard_map/ppermute | solution.py:426
  40.1 7.5 %collective-permute-start.7 = (f32[256,128]{1,0:T(8,128)S(1)}, f32[256,128]{1,0:T(8,128)S(1)}, u32[]{:S(2)}, u32[]{:S(2)}) collective-permute-start(f32[256,128]{1,0:T(8,128)S(1)} %get-tuple-element.43), channel_id=1, source_target_pairs={{0,8},{2,10},{4,12},{6,14},{8,0},{10,2},{12,4},{14,6},{1,9},{3,11}... | collective-permute-start | bytes 393224 | tf_op jit(solution)/shard_map/ppermute | solution.py:426
  47.7 6.7 %collective-permute-start.8 = (f32[256,128]{1,0:T(8,128)S(1)}, f32[256,128]{1,0:T(8,128)S(1)}, u32[]{:S(2)}, u32[]{:S(2)}) collective-permute-start(f32[256,128]{1,0:T(8,128)S(1)} %get-tuple-element.45), channel_id=1, source_target_pairs={{0,4},{2,6},{4,0},{6,2},{8,12},{10,14},{12,8},{14,10},{1,5},{3,7},... | collective-permute-start | bytes 393224 | tf_op jit(solution)/shard_map/ppermute | solution.py:426
  47.8 6.6 %collective-permute-start.9 = (f32[256,128]{1,0:T(8,128)S(1)}, f32[256,128]{1,0:T(8,128)S(1)}, u32[]{:S(2)}, u32[]{:S(2)}) collective-permute-start(f32[256,128]{1,0:T(8,128)S(1)} %get-tuple-element.46), channel_id=1, source_target_pairs={{0,8},{2,10},{4,12},{6,14},{8,0},{10,2},{12,4},{14,6},{1,9},{3,11}... | collective-permute-start | bytes 393224 | tf_op jit(solution)/shard_map/ppermute | solution.py:426
  54.4 1.6 %collective-permute-start.10 = (f32[512,128]{1,0:T(8,128)S(1)}, f32[512,128]{1,0:T(8,128)S(1)}, u32[]{:S(2)}, u32[]{:S(2)}) collective-permute-start(f32[512,128]{1,0:T(8,128)S(1)} %last.1), channel_id=1, source_target_pairs={{0,1},{1,0},{2,3},{3,2},{4,5},{5,4},{6,7},{7,6},{8,9},{9,8},{10,11... | collective-permute-start | bytes 786440 | tf_op jit(solution)/shard_map/ppermute | solution.py:423

commit v20 on v18

--- a/solution.py
+++ b/solution.py
@@ -11,7 +11,7 @@
 LANES = 128
 SUB = 8
 MIB = 1 << 20
-UNROLL = 12
+UNROLL = 36
 N_BUF = 4
 ORDERS = ("ylh", "yhl", "lyh", "hyl")
 PART_ROWS = (16, 16, 16, 16)

time: 57.3 us -> 54.8 us (0.956)
  Pallas kernels: 20.2 us -> 17.6 us
    pallas_call x1, Pallas kernels: 16.7 us -> 14.1 us  [accumulate(): pl.pallas_call(functools.partial(accumulate_kernel, bank_size, n_owner, n...]
where the time goes in v20:
time: 54.8 us; the launch traced here: 54.6 us
  waiting for transfers between devices  23.8 us (43%)
  Pallas kernels  17.6 us (32%)
  starting transfers between devices  13.2 us (24%)
    ppermute x8, waiting for transfers between devices, over_blk(): return lax.ppermute(array, 'blk', [(i, i ^ bits) for i in range(n_blk)])  21.6 us
    pallas_call x1, Pallas kernels, accumulate(): pl.pallas_call(functools.partial(accumulate_kernel, bank_size, n_owner, n...  14.1 us
    ppermute x8, starting transfers between devices, over_blk(): return lax.ppermute(array, 'blk', [(i, i ^ bits) for i in range(n_blk)])  12.5 us
    ppermute x3, waiting for transfers between devices, over_rep(): return lax.ppermute(array, 'rep', [(0, 1), (1, 0)])  2.13 us
    pallas_call x1, Pallas kernels, apply_bank(): pl.pallas_call(bank_rest_kernel, out_shape=jax.ShapeDtypeStruct((NB_DEV,...  1.62 us
  transfers between devices with their start and end apart: 11, of which 7 were waited for; matrix products, arithmetic and copies ran while one was open for 0% of the time, Pallas kernels for 3%

profile of v20, /device:TPU:0, one launch (start us, length us, event | category | flops | bytes accessed | tf_op | source)
XLA Modules:
  0.0 54.6 jit_solution(6092649682317978772)
XLA Ops:
  0.0 14.1 %accumulate.1 = (f32[2048,128]{1,0:T(8,128)S(1)}, f32[8192,128]{1,0:T(8,128)S(1)}, f32[8192,128]{1,0:T(8,128)S(1)}, f32[8192,128]{1,0:T(8,128)S(1)}, f32[8192,128]{1,0:T(8,128)S(1)}) custom-call(bf16[36864,128]{1,0:T(8,128)(2,1)} %bitcast.29, bf16[4608,128]{1,0:T(8,128)(2,1)} %bitcast.30, bf16[4608,128]{1,0:T(8,128)(2,1)} %bitcast.31, f32[8,16]{1,0:T(8,128)} %bitcast.34, ...), custom_call_target="tpu_custom_call" | custom-call | tf_op jit(solution)/shard_map/accumulate/pallas_call | solution.py:221
  14.1 0.5 collective-permute-start.1
  14.6 0.7 %rest.1 = (f32[2048,128]{1,0:T(8,128)S(1)}, f32[2048,128]{1,0:T(8,128)S(1)}, f32[2048,128]{1,0:T(8,128)S(1)}) custom-call(f32[8192,128]{1,0:T(8,128)S(1)} %get-tuple-element.26.refs_0_, f32[8192,128]{1,0:T(8,128)S(1)} %get-tuple-element.27.refs_1_, f32[8192,128]{1,0:T(8,128)S(1)} %get-tuple-element.28.refs_2_, f32[8192,128]{1,0:T(8,128)S(1)} %get-tuple-element.29.refs_3_), custom_call_target="tpu_custom_call" | custom-call | tf_op jit(solution)/shard_map/rest/pallas_call | solution.py:258
  15.4 0.1 collective-permute-start
  15.5 1.4 %collective-permute-done.1.got = f32[2048,128]{1,0:T(8,128)S(1)} collective-permute-done((f32[2048,128]{1,0:T(8,128)S(1)}, f32[2048,128]{1,0:T(8,128)S(1)}, u32[]{:S(2)}, u32[]{:S(2)}) %collective-permute-start.1) | collective-permute-done | bytes 1048608 | tf_op jit(solution)/shard_map/ppermute | solution.py:409
  16.9 0.1 first.1
  17.0 3.0 %collective-permute-start.2 = (f32[1024,128]{1,0:T(8,128)S(1)}, f32[1024,128]{1,0:T(8,128)S(1)}, u32[]{:S(2)}, u32[]{:S(2)}) collective-permute-start(f32[1024,128]{1,0:T(8,128)S(1)} %get-tuple-element.34), channel_id=1, source_target_pairs={{0,2},{2,0},{4,6},{6,4},{8,10},{10,8},{12,14},{14,12},{1,3},{3,1},... | collective-permute-start | bytes 1572872 | tf_op jit(solution)/shard_map/ppermute | solution.py:412
  20.0 1.5 %collective-permute-start.3 = (f32[512,128]{1,0:T(8,128)S(1)}, f32[512,128]{1,0:T(8,128)S(1)}, u32[]{:S(2)}, u32[]{:S(2)}) collective-permute-start(f32[512,128]{1,0:T(8,128)S(1)} %get-tuple-element.35), channel_id=1, source_target_pairs={{0,4},{2,6},{4,0},{6,2},{8,12},{10,14},{12,8},{14,10},{1,5},{3,7},... | collective-permute-start | bytes 786440 | tf_op jit(solution)/shard_map/ppermute | solution.py:412
  21.6 2.6 %collective-permute-start.4 = (f32[512,128]{1,0:T(8,128)S(1)}, f32[512,128]{1,0:T(8,128)S(1)}, u32[]{:S(2)}, u32[]{:S(2)}) collective-permute-start(f32[512,128]{1,0:T(8,128)S(1)} %get-tuple-element.36), channel_id=1, source_target_pairs={{0,8},{2,10},{4,12},{6,14},{8,0},{10,2},{12,4},{14,6},{1,9},{3,11}... | collective-permute-start | bytes 786440 | tf_op jit(solution)/shard_map/ppermute | solution.py:412
  24.2 9.4 %collective-permute-done.3.got_l = f32[512,128]{1,0:T(8,128)S(1)} collective-permute-done((f32[512,128]{1,0:T(8,128)S(1)}, f32[512,128]{1,0:T(8,128)S(1)}, u32[]{:S(2)}, u32[]{:S(2)}) %collective-permute-start.3) | collective-permute-done | bytes 262176 | tf_op jit(solution)/shard_map/ppermute | solution.py:412
  33.6 2.3 %collective-permute-done.4.rest_0_ = f32[512,128]{1,0:T(8,128)S(1)} collective-permute-done((f32[512,128]{1,0:T(8,128)S(1)}, f32[512,128]{1,0:T(8,128)S(1)}, u32[]{:S(2)}, u32[]{:S(2)}) %collective-permute-start.4) | collective-permute-done | bytes 262176 | tf_op jit(solution)/shard_map/ppermute | solution.py:412
  35.9 0.2 second.1
  36.1 0.6 %collective-permute-start.5 = (f32[512,128]{1,0:T(8,128)S(1)}, f32[512,128]{1,0:T(8,128)S(1)}, u32[]{:S(2)}, u32[]{:S(2)}) collective-permute-start(f32[512,128]{1,0:T(8,128)S(1)} %get-tuple-element.41), channel_id=1, source_target_pairs={{0,2},{2,0},{4,6},{6,4},{8,10},{10,8},{12,14},{14,12},{1,3},{3,1},... | collective-permute-start | bytes 786440 | tf_op jit(solution)/shard_map/ppermute | solution.py:412
  36.7 0.5 collective-permute-start.6
  37.1 2.6 %collective-permute-start.7 = (f32[256,128]{1,0:T(8,128)S(1)}, f32[256,128]{1,0:T(8,128)S(1)}, u32[]{:S(2)}, u32[]{:S(2)}) collective-permute-start(f32[256,128]{1,0:T(8,128)S(1)} %get-tuple-element.43), channel_id=1, source_target_pairs={{0,8},{2,10},{4,12},{6,14},{8,0},{10,2},{12,4},{14,6},{1,9},{3,11}... | collective-permute-start | bytes 393224 | tf_op jit(solution)/shard_map/ppermute | solution.py:412
  39.7 3.8 %collective-permute-done.6.got_l = f32[256,128]{1,0:T(8,128)S(1)} collective-permute-done((f32[256,128]{1,0:T(8,128)S(1)}, f32[256,128]{1,0:T(8,128)S(1)}, u32[]{:S(2)}, u32[]{:S(2)}) %collective-permute-start.6) | collective-permute-done | bytes 131104 | tf_op jit(solution)/shard_map/ppermute | solution.py:412
  43.5 1.1 %collective-permute-done.7.rest_0_ = f32[256,128]{1,0:T(8,128)S(1)} collective-permute-done((f32[256,128]{1,0:T(8,128)S(1)}, f32[256,128]{1,0:T(8,128)S(1)}, u32[]{:S(2)}, u32[]{:S(2)}) %collective-permute-start.7) | collective-permute-done | bytes 131104 | tf_op jit(solution)/shard_map/ppermute | solution.py:412
  44.7 0.1 collective-permute-start.8
  44.8 1.7 %collective-permute-start.9 = (f32[256,128]{1,0:T(8,128)S(1)}, f32[256,128]{1,0:T(8,128)S(1)}, u32[]{:S(2)}, u32[]{:S(2)}) collective-permute-start(f32[256,128]{1,0:T(8,128)S(1)} %get-tuple-element.46), channel_id=1, source_target_pairs={{0,8},{2,10},{4,12},{6,14},{8,0},{10,2},{12,4},{14,6},{1,9},{3,11}... | collective-permute-start | bytes 393224 | tf_op jit(solution)/shard_map/ppermute | solution.py:412
  46.5 4.9 %collective-permute-done.8.got_l = f32[256,128]{1,0:T(8,128)S(1)} collective-permute-done((f32[256,128]{1,0:T(8,128)S(1)}, f32[256,128]{1,0:T(8,128)S(1)}, u32[]{:S(2)}, u32[]{:S(2)}) %collective-permute-start.8) | collective-permute-done | bytes 131104 | tf_op jit(solution)/shard_map/ppermute | solution.py:412
  51.4 0.1 collective-permute-start.10
  51.5 0.8 %bank_own.1.done = f32[4,32,1024]{2,1,0:T(8,128)S(1)} custom-call(f32[4,16,8,128]{3,2,1,0:T(8,128)S(1)} %bitcast.27, f32[16,32,1024]{2,1,0:T(8,128)S(1)} %copy-done), custom_call_target="tpu_custom_call" | custom-call | tf_op jit(solution)/shard_map/bank_own/pallas_call | solution.py:374
  52.3 0.7 %collective-permute-done.10 = f32[512,128]{1,0:T(8,128)S(1)} collective-permute-done((f32[512,128]{1,0:T(8,128)S(1)}, f32[512,128]{1,0:T(8,128)S(1)}, u32[]{:S(2)}, u32[]{:S(2)}) %collective-permute-start.10) | collective-permute-done | bytes 262176 | tf_op jit(solution)/shard_map/ppermute | solution.py:409
  53.0 1.6 %bank_rest.1 = f32[8,32,1024]{2,1,0:T(8,128)} custom-call(f32[4,32,1024]{2,1,0:T(8,128)S(1)} %bank_own.1.done, f32[4,16,8,128]{3,2,1,0:T(8,128)S(1)} %bitcast.28, f32[16,32,1024]{2,1,0:T(8,128)S(1)} %copy-done), custom_call_target="tpu_custom_call" | custom-call | tf_op jit(solution)/shard_map/bank_rest/pallas_call | solution.py:382
  (8 shorter events, 0.1 us)
Async XLA Ops:
  14.1 2.8 %collective-permute-start.1 = (f32[2048,128]{1,0:T(8,128)S(1)}, f32[2048,128]{1,0:T(8,128)S(1)}, u32[]{:S(2)}, u32[]{:S(2)}) collective-permute-start(f32[2048,128]{1,0:T(8,128)S(1)} %get-tuple-element.33), channel_id=1, source_target_pairs={{0,1},{1,0},{2,3},{3,2},{4,5},{5,4},{6,7},{7,6},{8,9},{9,8},{10,11... | collective-permute-start | bytes 3145736 | tf_op jit(solution)/shard_map/ppermute | solution.py:409
  15.4 36.1 %copy-start = (f32[16,32,1024]{2,1,0:T(8,128)S(1)}, f32[16,32,1024]{2,1,0:T(8,128)}, u32[]{:S(2)}) copy-start(f32[16,32,1024]{2,1,0:T(8,128)} %bank.3) | copy-start | bytes 6291460
  15.4 8.8 %collective-permute-start = (f32[2048,128]{1,0:T(8,128)S(1)}, f32[2048,128]{1,0:T(8,128)S(1)}, u32[]{:S(2)}, u32[]{:S(2)}) collective-permute-start(f32[2048,128]{1,0:T(8,128)S(1)} %get-tuple-element.31), channel_id=1, source_target_pairs={{0,1},{1,0},{2,3},{3,2},{4,5},{5,4},{6,7},{7,6},{8,9},{9,8},{10,11... | collective-permute-start | bytes 3145736 | tf_op jit(solution)/shard_map/ppermute | solution.py:409
  17.0 18.9 %collective-permute-start.2 = (f32[1024,128]{1,0:T(8,128)S(1)}, f32[1024,128]{1,0:T(8,128)S(1)}, u32[]{:S(2)}, u32[]{:S(2)}) collective-permute-start(f32[1024,128]{1,0:T(8,128)S(1)} %get-tuple-element.34), channel_id=1, source_target_pairs={{0,2},{2,0},{4,6},{6,4},{8,10},{10,8},{12,14},{14,12},{1,3},{3,1},... | collective-permute-start | bytes 1572872 | tf_op jit(solution)/shard_map/ppermute | solution.py:412
  20.0 13.6 %collective-permute-start.3 = (f32[512,128]{1,0:T(8,128)S(1)}, f32[512,128]{1,0:T(8,128)S(1)}, u32[]{:S(2)}, u32[]{:S(2)}) collective-permute-start(f32[512,128]{1,0:T(8,128)S(1)} %get-tuple-element.35), channel_id=1, source_target_pairs={{0,4},{2,6},{4,0},{6,2},{8,12},{10,14},{12,8},{14,10},{1,5},{3,7},... | collective-permute-start | bytes 786440 | tf_op jit(solution)/shard_map/ppermute | solution.py:412
  21.6 14.4 %collective-permute-start.4 = (f32[512,128]{1,0:T(8,128)S(1)}, f32[512,128]{1,0:T(8,128)S(1)}, u32[]{:S(2)}, u32[]{:S(2)}) collective-permute-start(f32[512,128]{1,0:T(8,128)S(1)} %get-tuple-element.36), channel_id=1, source_target_pairs={{0,8},{2,10},{4,12},{6,14},{8,0},{10,2},{12,4},{14,6},{1,9},{3,11}... | collective-permute-start | bytes 786440 | tf_op jit(solution)/shard_map/ppermute | solution.py:412
  36.1 8.5 %collective-permute-start.5 = (f32[512,128]{1,0:T(8,128)S(1)}, f32[512,128]{1,0:T(8,128)S(1)}, u32[]{:S(2)}, u32[]{:S(2)}) collective-permute-start(f32[512,128]{1,0:T(8,128)S(1)} %get-tuple-element.41), channel_id=1, source_target_pairs={{0,2},{2,0},{4,6},{6,4},{8,10},{10,8},{12,14},{14,12},{1,3},{3,1},... | collective-permute-start | bytes 786440 | tf_op jit(solution)/shard_map/ppermute | solution.py:412
  36.7 6.9 %collective-permute-start.6 = (f32[256,128]{1,0:T(8,128)S(1)}, f32[256,128]{1,0:T(8,128)S(1)}, u32[]{:S(2)}, u32[]{:S(2)}) collective-permute-start(f32[256,128]{1,0:T(8,128)S(1)} %get-tuple-element.42), channel_id=1, source_target_pairs={{0,4},{2,6},{4,0},{6,2},{8,12},{10,14},{12,8},{14,10},{1,5},{3,7},... | collective-permute-start | bytes 393224 | tf_op jit(solution)/shard_map/ppermute | solution.py:412
  37.1 7.5 %collective-permute-start.7 = (f32[256,128]{1,0:T(8,128)S(1)}, f32[256,128]{1,0:T(8,128)S(1)}, u32[]{:S(2)}, u32[]{:S(2)}) collective-permute-start(f32[256,128]{1,0:T(8,128)S(1)} %get-tuple-element.43), channel_id=1, source_target_pairs={{0,8},{2,10},{4,12},{6,14},{8,0},{10,2},{12,4},{14,6},{1,9},{3,11}... | collective-permute-start | bytes 393224 | tf_op jit(solution)/shard_map/ppermute | solution.py:412
  44.7 6.7 %collective-permute-start.8 = (f32[256,128]{1,0:T(8,128)S(1)}, f32[256,128]{1,0:T(8,128)S(1)}, u32[]{:S(2)}, u32[]{:S(2)}) collective-permute-start(f32[256,128]{1,0:T(8,128)S(1)} %get-tuple-element.45), channel_id=1, source_target_pairs={{0,4},{2,6},{4,0},{6,2},{8,12},{10,14},{12,8},{14,10},{1,5},{3,7},... | collective-permute-start | bytes 393224 | tf_op jit(solution)/shard_map/ppermute | solution.py:412
  44.8 6.6 %collective-permute-start.9 = (f32[256,128]{1,0:T(8,128)S(1)}, f32[256,128]{1,0:T(8,128)S(1)}, u32[]{:S(2)}, u32[]{:S(2)}) collective-permute-start(f32[256,128]{1,0:T(8,128)S(1)} %get-tuple-element.46), channel_id=1, source_target_pairs={{0,8},{2,10},{4,12},{6,14},{8,0},{10,2},{12,4},{14,6},{1,9},{3,11}... | collective-permute-start | bytes 393224 | tf_op jit(solution)/shard_map/ppermute | solution.py:412
  51.4 1.6 %collective-permute-start.10 = (f32[512,128]{1,0:T(8,128)S(1)}, f32[512,128]{1,0:T(8,128)S(1)}, u32[]{:S(2)}, u32[]{:S(2)}) collective-permute-start(f32[512,128]{1,0:T(8,128)S(1)} %last.1), channel_id=1, source_target_pairs={{0,1},{1,0},{2,3},{3,2},{4,5},{5,4},{6,7},{7,6},{8,9},{9,8},{10,11... | collective-permute-start | bytes 786440 | tf_op jit(solution)/shard_map/ppermute | solution.py:409
